TPU v7x, 256 devices: a whole 4x4x8 slice. The times are simulated.
256 devices in a mesh: slab: 16 (over z, core), cross: 16 (over y, x).
Axes of the slice: x: 4, y: 4, z: 8, core: 2. Of those that a mesh axis runs over, the one named last changes fastest.
Arguments:
- forcing: float32 [2, 64, 1024, 512], P(None, 'slab', 'cross'), may hold values from -6 to 6
- viscosity: float32 [64, 1024, 512], P('slab', 'cross'), may hold values from 0.1 to 10
- owner_slot: int32 [512], replicated, may hold values from 0 to 511, each once
Outputs:
- velocity: float32 [2, 64, 1024, 512], P(None, 'slab', 'cross')
- pressure: float32 [64, 512], P('slab', 'cross')
All inputs are finite; a program needn't handle non-finite values.
Results may differ from a plain program's by a relative error of at most 0.00013.
Values sent between devices are 32-bit elements; how exact they have to be, the bound alone decides.
No kernel may reach another device: no remote copies, remote signals or barrier semaphores. Data moves between devices by JAX's collectives and lax.ppermute only.
A program may use at most 64 MiB of HBM per device.

v0:
```python
import jax
import jax.numpy as jnp
from jax import lax
from jax.sharding import PartitionSpec as P

OUTER = 2
DEGREE = 3


cheb_theta = 1.025
cheb_delta = 0.975


def extended(x, sides, width):
    edges = {}
    for axis, dim in sides:
        peers, length = (lax.axis_size(axis), x.shape[dim])
        up = [(i, (i + 1) % peers) for i in range(peers - 1)]
        last = lax.slice_in_dim(x, length - width, length, axis=dim)
        initial = lax.slice_in_dim(x, 0, width, axis=dim)
        edges[dim] = (
            lax.ppermute(last, axis, up),
            lax.ppermute(initial, axis, [(b, a) for a, b in up]),
        )
    done = []
    for _, dim in sides:
        low, high = edges[dim]
        around = [(width, width) if d in done else (0, 0) for d in range(x.ndim)]
        x = jnp.concatenate([jnp.pad(low, around), x, jnp.pad(high, around)], axis=dim)
        done.append(dim)
    return x


def passed_along(block, axis, distance):
    devices = range(lax.axis_size(axis))
    route = [(i - distance, i) for i in devices if i - distance in devices]
    return lax.ppermute(block, axis, route)


def sent_to_all(x, axis):
    peers = lax.axis_size(axis)
    return lax.all_to_all(jnp.broadcast_to(x[None], (peers, *x.shape)), axis, 0, 0, tiled=True)


def of_everyone(x, axis):
    everything = sent_to_all(x, axis)
    return jnp.sum(everything, axis=0)


def face_parts(viscosity):
    rim = extended(viscosity, (("slab", 0), ("cross", 1)), 1)
    rim = jnp.pad(rim, ((0, 0), (0, 0), (1, 1)))
    centre = rim[1:-1, 1:-1, 1:-1]
    neighbours = [
        rim[2:, 1:-1, 1:-1],
        rim[:-2, 1:-1, 1:-1],
        rim[1:-1, 2:, 1:-1],
        rim[1:-1, :-2, 1:-1],
        rim[1:-1, 1:-1, 2:],
        rim[1:-1, 1:-1, :-2],
    ]
    faces = [0.5 * (centre + nb) for nb in neighbours]
    diag = faces[0] + faces[1] + faces[2] + faces[3] + faces[4] + faces[5]
    return (faces, diag)


def apply_op(field, faces):
    padded = extended(field, (("slab", 1), ("cross", 2)), 1)
    padded = jnp.pad(padded, ((0, 0), (0, 0), (0, 0), (1, 1)))
    neighbours = [
        padded[:, 2:, 1:-1, 1:-1],
        padded[:, :-2, 1:-1, 1:-1],
        padded[:, 1:-1, 2:, 1:-1],
        padded[:, 1:-1, :-2, 1:-1],
        padded[:, 1:-1, 1:-1, 2:],
        padded[:, 1:-1, 1:-1, :-2],
    ]
    result = jnp.zeros_like(field)
    for face, nb in zip(faces, neighbours):
        result = result + face[None] * (field - nb)
    return result


def velocity_solve(rhs, faces, diag):
    sigma = cheb_theta / cheb_delta
    solved = rhs / (cheb_theta * diag[None])
    change = solved
    rho_prev = 1.0 / sigma
    for step in range(DEGREE - 1):
        resid = rhs - apply_op(solved, faces)
        rho = 1.0 / (2.0 * sigma - rho_prev)
        change = rho * rho_prev * change + 2.0 * rho / cheb_delta * resid / diag[None]
        solved = solved + change
        rho_prev = rho
    return solved


def diverge(field, onehot):
    col_x = jnp.sum(field[0], axis=1)
    col_z = jnp.sum(field[1], axis=1)
    prior = passed_along(col_x[-1:], "slab", 1)
    below = jnp.concatenate([prior, col_x[:-1]], 0)
    behind = jnp.pad(col_z[:, :-1], ((0, 0), (1, 0)))
    local = col_x - below + col_z - behind
    ordered = jnp.dot(local, onehot, precision=lax.Precision.HIGHEST)
    return of_everyone(ordered, "cross")


def gradient(press, onehot, ny):
    column = jnp.dot(press, onehot.T, precision=lax.Precision.HIGHEST)
    after = passed_along(column[:1], "slab", -1)
    grad_x = column - jnp.concatenate([column[1:], after], 0)
    grad_z = column - jnp.pad(column[:, 1:], ((0, 0), (0, 1)))
    both = jnp.stack([grad_x, grad_z])[:, :, None, :]
    return jnp.broadcast_to(both, (2, column.shape[0], ny, column.shape[1]))


def total(value):
    return of_everyone(value, "slab")


def shards(forcing, viscosity, owner_slot):
    faces, diag = face_parts(viscosity)
    ny = viscosity.shape[1]
    depth = owner_slot.shape[0]
    onehot = (owner_slot[:, None] == jnp.arange(depth, dtype=jnp.int32)[None, :]).astype(
        jnp.float32
    )
    target = diverge(velocity_solve(forcing, faces, diag), onehot)
    pressure = jnp.zeros_like(target)
    resid = target
    dirn = target
    rr = total(jnp.sum(resid * resid))
    for step in range(OUTER):
        image = diverge(velocity_solve(gradient(dirn, onehot, ny), faces, diag), onehot)
        alpha = rr / total(jnp.sum(dirn * image))
        pressure = pressure + alpha * dirn
        if step + 1 < OUTER:
            resid = resid - alpha * image
            fresh = total(jnp.sum(resid * resid))
            dirn = resid + fresh / rr * dirn
            rr = fresh
    velocity = velocity_solve(forcing - gradient(pressure, onehot, ny), faces, diag)
    width = depth // lax.axis_size("cross")
    owned_cols = lax.dynamic_slice_in_dim(pressure, lax.axis_index("cross") * width, width, 1)
    return (velocity, owned_cols)


def solution(mesh):
    in_specs = (P(None, "slab", "cross", None), P("slab", "cross", None), P())
    out_specs = (P(None, "slab", "cross", None), P("slab", "cross"))
    return jax.shard_map(shards, mesh=mesh, in_specs=in_specs, out_specs=out_specs, check_vma=False)
```

profile of v0, /device:TPU:16, one launch (start us, length us, event | category | flops | bytes accessed | tf_op | source)
XLA Modules:
  0.0 307.1 jit_solution(11184726605143092699)
XLA Ops:
  4.3 4.6 %collective-permute-start.2 = (f32[4,1,512]{2,1,0:T(1,128)S(1)}, f32[4,1,512]{2,1,0:T(1,128)S(1)}, u32[]{:S(2)}, u32[]{:S(2)}) collective-permute-start(f32[4,1,512]{2,1,0:T(1,128)S(1)} %get-tuple-element.59), channel_id=1, source_target_pairs={{1,0},{2,1},{3,2},{4,3},{5,4},{6,5},{7,6},{8,7},{9,8},{10,9},{11,1... | collective-permute-start | bytes 24584 | tf_op jit(solution)/shard_map/ppermute | solution.py:23
  12.2 4.4 %collective-permute-done.3 = f32[4,1,512]{2,1,0:T(1,128)S(1)} collective-permute-done((f32[4,1,512]{2,1,0:T(1,128)S(1)}, f32[4,1,512]{2,1,0:T(1,128)S(1)}, u32[]{:S(2)}, u32[]{:S(2)}) %collective-permute-start.3) | collective-permute-done | bytes 8224 | tf_op jit(solution)/shard_map/ppermute | solution.py:22
  25.9 5.8 %collective-permute-start.6 = (f32[2,4,1,512]{3,2,1,0:T(1,128)S(1)}, f32[2,4,1,512]{3,2,1,0:T(1,128)S(1)}, u32[]{:S(2)}, u32[]{:S(2)}) collective-permute-start(f32[2,4,1,512]{3,2,1,0:T(1,128)S(1)} %get-tuple-element.57), channel_id=1, source_target_pairs={{1,0},{2,1},{3,2},{4,3},{5,4},{6,5},{7,6},{8,7},{9,8},{10,9},{11,1... | collective-permute-start | bytes 49160 | tf_op jit(solution)/shard_map/ppermute | solution.py:23
  33.6 5.8 %collective-permute-done.7 = f32[2,4,1,512]{3,2,1,0:T(1,128)S(1)} collective-permute-done((f32[2,4,1,512]{3,2,1,0:T(1,128)S(1)}, f32[2,4,1,512]{3,2,1,0:T(1,128)S(1)}, u32[]{:S(2)}, u32[]{:S(2)}) %collective-permute-start.7) | collective-permute-done | bytes 16416 | tf_op jit(solution)/shard_map/ppermute | solution.py:22
  48.3 3.9 %collective-permute-start.11 = (f32[2,4,1,512]{3,2,1,0:T(1,128)S(1)}, f32[2,4,1,512]{3,2,1,0:T(1,128)S(1)}, u32[]{:S(2)}, u32[]{:S(2)}) collective-permute-start(f32[2,4,1,512]{3,2,1,0:T(1,128)S(1)} %get-tuple-element.52), channel_id=1, source_target_pairs={{0,1},{1,2},{2,3},{3,4},{4,5},{5,6},{6,7},{7,8},{8,9},{9,10},{10,1... | collective-permute-start | bytes 49160 | tf_op jit(solution)/shard_map/ppermute | solution.py:22
  62.4 10.5 %all_to_all.39 = f32[16,4,512]{2,1,0:T(4,128)S(1)} all-to-all(f32[16,4,512]{2,1,0:T(4,128)S(1)} %broadcast_in_dim.20), channel_id=1, replica_groups=mesh['slab'=16,'cross'=16] {'cross'}, dimensions={0} | all-to-all | bytes 262144 | tf_op jit(solution)/shard_map/all_to_all | solution.py:42
  79.4 6.2 %collective-permute-start.15 = (f32[2,1,64,512]{3,2,1,0:T(8,128)S(1)}, f32[2,1,64,512]{3,2,1,0:T(8,128)S(1)}, u32[]{:S(2)}, u32[]{:S(2)}) collective-permute-start(f32[2,1,64,512]{3,2,1,0:T(8,128)S(1)} %get-tuple-element.46), channel_id=1, source_target_pairs={{0,16},{16,32},{32,48},{48,64},{64,80},{80,96},{96,112},{112,128},... | collective-permute-start | bytes 786440 | tf_op jit(solution)/shard_map/ppermute | solution.py:22
  85.6 4.0 %collective-permute-start.16 = (f32[2,4,1,512]{3,2,1,0:T(1,128)S(1)}, f32[2,4,1,512]{3,2,1,0:T(1,128)S(1)}, u32[]{:S(2)}, u32[]{:S(2)}) collective-permute-start(f32[2,4,1,512]{3,2,1,0:T(1,128)S(1)} %get-tuple-element.49), channel_id=1, source_target_pairs={{1,0},{2,1},{3,2},{4,3},{5,4},{6,5},{7,6},{8,7},{9,8},{10,9},{11,1... | collective-permute-start | bytes 49160 | tf_op jit(solution)/shard_map/ppermute | solution.py:23
  91.6 5.8 %collective-permute-done.17 = f32[2,4,1,512]{3,2,1,0:T(1,128)S(1)} collective-permute-done((f32[2,4,1,512]{3,2,1,0:T(1,128)S(1)}, f32[2,4,1,512]{3,2,1,0:T(1,128)S(1)}, u32[]{:S(2)}, u32[]{:S(2)}) %collective-permute-start.17) | collective-permute-done | bytes 16416 | tf_op jit(solution)/shard_map/ppermute | solution.py:22
  106.2 3.9 %collective-permute-start.21 = (f32[2,4,1,512]{3,2,1,0:T(1,128)S(1)}, f32[2,4,1,512]{3,2,1,0:T(1,128)S(1)}, u32[]{:S(2)}, u32[]{:S(2)}) collective-permute-start(f32[2,4,1,512]{3,2,1,0:T(1,128)S(1)} %get-tuple-element.44), channel_id=1, source_target_pairs={{0,1},{1,2},{2,3},{3,4},{4,5},{5,6},{6,7},{7,8},{8,9},{9,10},{10,1... | collective-permute-start | bytes 49160 | tf_op jit(solution)/shard_map/ppermute | solution.py:22
  120.8 10.4 %all_to_all.40 = f32[16,4,512]{2,1,0:T(4,128)S(1)} all-to-all(f32[16,4,512]{2,1,0:T(4,128)S(1)} %broadcast_in_dim.23), channel_id=1, replica_groups=mesh['slab'=16,'cross'=16] {'cross'}, dimensions={0} | all-to-all | bytes 262144 | tf_op jit(solution)/shard_map/all_to_all | solution.py:42
  132.7 24.4 %all_to_all.41 = f32[16,1,1]{2,1,0:T(1,128)S(1)} all-to-all(f32[16,1,1]{2,1,0:T(1,128)S(1)} %broadcast_in_dim.21), channel_id=1, replica_groups=mesh['slab'=16,'cross'=16] {'slab'}, dimensions={0} | all-to-all | bytes 128 | tf_op jit(solution)/shard_map/all_to_all | solution.py:42
  162.4 6.9 %all-to-all-done.3 = f32[16,1,1]{2,1,0:T(1,128)S(1)} async-done(((f32[16,1,1]{2,1,0:T(1,128)}), f32[16,1,1]{2,1,0:T(1,128)S(1)}, u32[]{:S(2)}, u32[]{:S(2)}) %all-to-all-start.3) | async-done | bytes 96 | tf_op jit(solution)/shard_map/all_to_all | solution.py:42
  172.8 10.1 %all_to_all.42 = f32[16,1,1]{2,1,0:T(1,128)S(1)} all-to-all(f32[16,1,1]{2,1,0:T(1,128)S(1)} %broadcast_in_dim.25), channel_id=1, replica_groups=mesh['slab'=16,'cross'=16] {'slab'}, dimensions={0} | all-to-all | bytes 128 | tf_op jit(solution)/shard_map/all_to_all | solution.py:42
  191.3 4.2 %collective-permute-start.25 = (f32[2,1,64,512]{3,2,1,0:T(8,128)S(1)}, f32[2,1,64,512]{3,2,1,0:T(8,128)S(1)}, u32[]{:S(2)}, u32[]{:S(2)}) collective-permute-start(f32[2,1,64,512]{3,2,1,0:T(8,128)S(1)} %get-tuple-element.38), channel_id=1, source_target_pairs={{0,16},{16,32},{32,48},{48,64},{64,80},{80,96},{96,112},{112,128},... | collective-permute-start | bytes 786440 | tf_op jit(solution)/shard_map/ppermute | solution.py:22
  195.6 3.9 %collective-permute-start.26 = (f32[2,4,1,512]{3,2,1,0:T(1,128)S(1)}, f32[2,4,1,512]{3,2,1,0:T(1,128)S(1)}, u32[]{:S(2)}, u32[]{:S(2)}) collective-permute-start(f32[2,4,1,512]{3,2,1,0:T(1,128)S(1)} %get-tuple-element.41), channel_id=1, source_target_pairs={{1,0},{2,1},{3,2},{4,3},{5,4},{6,5},{7,6},{8,7},{9,8},{10,9},{11,1... | collective-permute-start | bytes 49160 | tf_op jit(solution)/shard_map/ppermute | solution.py:23
  201.5 5.8 %collective-permute-done.27 = f32[2,4,1,512]{3,2,1,0:T(1,128)S(1)} collective-permute-done((f32[2,4,1,512]{3,2,1,0:T(1,128)S(1)}, f32[2,4,1,512]{3,2,1,0:T(1,128)S(1)}, u32[]{:S(2)}, u32[]{:S(2)}) %collective-permute-start.27) | collective-permute-done | bytes 16416 | tf_op jit(solution)/shard_map/ppermute | solution.py:22
  216.1 3.9 %collective-permute-start.31 = (f32[2,4,1,512]{3,2,1,0:T(1,128)S(1)}, f32[2,4,1,512]{3,2,1,0:T(1,128)S(1)}, u32[]{:S(2)}, u32[]{:S(2)}) collective-permute-start(f32[2,4,1,512]{3,2,1,0:T(1,128)S(1)} %get-tuple-element.36), channel_id=1, source_target_pairs={{0,1},{1,2},{2,3},{3,4},{4,5},{5,6},{6,7},{7,8},{8,9},{9,10},{10,1... | collective-permute-start | bytes 49160 | tf_op jit(solution)/shard_map/ppermute | solution.py:22
  230.2 10.7 %all_to_all.43 = f32[16,4,512]{2,1,0:T(4,128)S(1)} all-to-all(f32[16,4,512]{2,1,0:T(4,128)S(1)} %broadcast_in_dim.27), channel_id=1, replica_groups=mesh['slab'=16,'cross'=16] {'cross'}, dimensions={0} | all-to-all | bytes 262144 | tf_op jit(solution)/shard_map/all_to_all | solution.py:42
  242.2 16.4 %all_to_all.44 = f32[16,1,1]{2,1,0:T(1,128)S(1)} all-to-all(f32[16,1,1]{2,1,0:T(1,128)S(1)} %broadcast_in_dim.28), channel_id=1, replica_groups=mesh['slab'=16,'cross'=16] {'slab'}, dimensions={0} | all-to-all | bytes 128 | tf_op jit(solution)/shard_map/all_to_all | solution.py:42
  268.1 4.9 %collective-permute-start.35 = (f32[2,1,64,512]{3,2,1,0:T(8,128)}, f32[2,1,64,512]{3,2,1,0:T(8,128)}, u32[]{:S(2)}, u32[]{:S(2)}) collective-permute-start(f32[2,1,64,512]{3,2,1,0:T(8,128)} %get-tuple-element.30), channel_id=1, source_target_pairs={{0,16},{16,32},{32,48},{48,64},{64,80},{80,96},{96,112},{112,128},... | collective-permute-start | bytes 786440 | tf_op jit(solution)/shard_map/ppermute | solution.py:22
  273.1 3.9 %collective-permute-start.36 = (f32[2,4,1,512]{3,2,1,0:T(1,128)S(1)}, f32[2,4,1,512]{3,2,1,0:T(1,128)S(1)}, u32[]{:S(2)}, u32[]{:S(2)}) collective-permute-start(f32[2,4,1,512]{3,2,1,0:T(1,128)S(1)} %get-tuple-element.33), channel_id=1, source_target_pairs={{1,0},{2,1},{3,2},{4,3},{5,4},{6,5},{7,6},{8,7},{9,8},{10,9},{11,1... | collective-permute-start | bytes 49160 | tf_op jit(solution)/shard_map/ppermute | solution.py:23
  279.0 5.7 %collective-permute-done.37 = f32[2,4,1,512]{3,2,1,0:T(1,128)S(1)} collective-permute-done((f32[2,4,1,512]{3,2,1,0:T(1,128)S(1)}, f32[2,4,1,512]{3,2,1,0:T(1,128)S(1)}, u32[]{:S(2)}, u32[]{:S(2)}) %collective-permute-start.37) | collective-permute-done | bytes 16416 | tf_op jit(solution)/shard_map/ppermute | solution.py:22
  295.9 3.9 %collective-permute-start.41 = (f32[2,4,1,512]{3,2,1,0:T(1,128)S(1)}, f32[2,4,1,512]{3,2,1,0:T(1,128)S(1)}, u32[]{:S(2)}, u32[]{:S(2)}) collective-permute-start(f32[2,4,1,512]{3,2,1,0:T(1,128)S(1)} %get-tuple-element.28), channel_id=1, source_target_pairs={{0,1},{1,2},{2,3},{3,4},{4,5},{5,6},{6,7},{7,8},{8,9},{9,10},{10,1... | collective-permute-start | bytes 49160 | tf_op jit(solution)/shard_map/ppermute | solution.py:22
  (202 shorter events, 131.1 us)
Async XLA Ops:
  1.7 14.9 %collective-permute-start.1 = (f32[1,64,512]{2,1,0:T(8,128)S(1)}, f32[1,64,512]{2,1,0:T(8,128)S(1)}, u32[]{:S(2)}, u32[]{:S(2)}) collective-permute-start(f32[1,64,512]{2,1,0:T(8,128)S(1)} %get-tuple-element.61), channel_id=1, source_target_pairs={{0,16},{16,32},{32,48},{48,64},{64,80},{80,96},{96,112},{112,128},... | collective-permute-start | bytes 393224 | tf_op jit(solution)/shard_map/ppermute | solution.py:22
  4.3 7.8 %collective-permute-start.2 = (f32[4,1,512]{2,1,0:T(1,128)S(1)}, f32[4,1,512]{2,1,0:T(1,128)S(1)}, u32[]{:S(2)}, u32[]{:S(2)}) collective-permute-start(f32[4,1,512]{2,1,0:T(1,128)S(1)} %get-tuple-element.59), channel_id=1, source_target_pairs={{1,0},{2,1},{3,2},{4,3},{5,4},{6,5},{7,6},{8,7},{9,8},{10,9},{11,1... | collective-permute-start | bytes 24584 | tf_op jit(solution)/shard_map/ppermute | solution.py:23
  20.7 18.7 %collective-permute-start.4 = (f32[2,1,64,512]{3,2,1,0:T(8,128)S(1)}, f32[2,1,64,512]{3,2,1,0:T(8,128)S(1)}, u32[]{:S(2)}, u32[]{:S(2)}) collective-permute-start(f32[2,1,64,512]{3,2,1,0:T(8,128)S(1)} %get-tuple-element.55), channel_id=1, source_target_pairs={{16,0},{32,16},{48,32},{64,48},{80,64},{96,80},{112,96},{128,112},... | collective-permute-start | bytes 786440 | tf_op jit(solution)/shard_map/ppermute | solution.py:23
  22.0 17.5 %collective-permute-start.5 = (f32[2,1,64,512]{3,2,1,0:T(8,128)S(1)}, f32[2,1,64,512]{3,2,1,0:T(8,128)S(1)}, u32[]{:S(2)}, u32[]{:S(2)}) collective-permute-start(f32[2,1,64,512]{3,2,1,0:T(8,128)S(1)} %get-tuple-element.54), channel_id=1, source_target_pairs={{0,16},{16,32},{32,48},{48,64},{64,80},{80,96},{96,112},{112,128},... | collective-permute-start | bytes 786440 | tf_op jit(solution)/shard_map/ppermute | solution.py:22
  31.7 7.7 %collective-permute-start.7 = (f32[2,4,1,512]{3,2,1,0:T(1,128)S(1)}, f32[2,4,1,512]{3,2,1,0:T(1,128)S(1)}, u32[]{:S(2)}, u32[]{:S(2)}) collective-permute-start(f32[2,4,1,512]{3,2,1,0:T(1,128)S(1)} %get-tuple-element.56), channel_id=1, source_target_pairs={{0,1},{1,2},{2,3},{3,4},{4,5},{5,6},{6,7},{7,8},{8,9},{9,10},{10,1... | collective-permute-start | bytes 49160 | tf_op jit(solution)/shard_map/ppermute | solution.py:22
  42.0 14.1 %collective-permute-start.8 = (f32[2,1,64,512]{3,2,1,0:T(8,128)S(1)}, f32[2,1,64,512]{3,2,1,0:T(8,128)S(1)}, u32[]{:S(2)}, u32[]{:S(2)}) collective-permute-start(f32[2,1,64,512]{3,2,1,0:T(8,128)S(1)} %get-tuple-element.51), channel_id=1, source_target_pairs={{16,0},{32,16},{48,32},{64,48},{80,64},{96,80},{112,96},{128,112},... | collective-permute-start | bytes 786440 | tf_op jit(solution)/shard_map/ppermute | solution.py:23
  43.3 12.8 %collective-permute-start.9 = (f32[2,1,64,512]{3,2,1,0:T(8,128)S(1)}, f32[2,1,64,512]{3,2,1,0:T(8,128)S(1)}, u32[]{:S(2)}, u32[]{:S(2)}) collective-permute-start(f32[2,1,64,512]{3,2,1,0:T(8,128)S(1)} %get-tuple-element.50), channel_id=1, source_target_pairs={{0,16},{16,32},{32,48},{48,64},{64,80},{80,96},{96,112},{112,128},... | collective-permute-start | bytes 786440 | tf_op jit(solution)/shard_map/ppermute | solution.py:22
  48.3 7.7 %collective-permute-start.11 = (f32[2,4,1,512]{3,2,1,0:T(1,128)S(1)}, f32[2,4,1,512]{3,2,1,0:T(1,128)S(1)}, u32[]{:S(2)}, u32[]{:S(2)}) collective-permute-start(f32[2,4,1,512]{3,2,1,0:T(1,128)S(1)} %get-tuple-element.52), channel_id=1, source_target_pairs={{0,1},{1,2},{2,3},{3,4},{4,5},{5,6},{6,7},{7,8},{8,9},{9,10},{10,1... | collective-permute-start | bytes 49160 | tf_op jit(solution)/shard_map/ppermute | solution.py:22
  78.0 19.4 %collective-permute-start.14 = (f32[2,1,64,512]{3,2,1,0:T(8,128)S(1)}, f32[2,1,64,512]{3,2,1,0:T(8,128)S(1)}, u32[]{:S(2)}, u32[]{:S(2)}) collective-permute-start(f32[2,1,64,512]{3,2,1,0:T(8,128)S(1)} %get-tuple-element.47), channel_id=1, source_target_pairs={{16,0},{32,16},{48,32},{64,48},{80,64},{96,80},{112,96},{128,112},... | collective-permute-start | bytes 786440 | tf_op jit(solution)/shard_map/ppermute | solution.py:23
  79.4 18.0 %collective-permute-start.15 = (f32[2,1,64,512]{3,2,1,0:T(8,128)S(1)}, f32[2,1,64,512]{3,2,1,0:T(8,128)S(1)}, u32[]{:S(2)}, u32[]{:S(2)}) collective-permute-start(f32[2,1,64,512]{3,2,1,0:T(8,128)S(1)} %get-tuple-element.46), channel_id=1, source_target_pairs={{0,16},{16,32},{32,48},{48,64},{64,80},{80,96},{96,112},{112,128},... | collective-permute-start | bytes 786440 | tf_op jit(solution)/shard_map/ppermute | solution.py:22
  89.6 7.7 %collective-permute-start.17 = (f32[2,4,1,512]{3,2,1,0:T(1,128)S(1)}, f32[2,4,1,512]{3,2,1,0:T(1,128)S(1)}, u32[]{:S(2)}, u32[]{:S(2)}) collective-permute-start(f32[2,4,1,512]{3,2,1,0:T(1,128)S(1)} %get-tuple-element.48), channel_id=1, source_target_pairs={{0,1},{1,2},{2,3},{3,4},{4,5},{5,6},{6,7},{7,8},{8,9},{9,10},{10,1... | collective-permute-start | bytes 49160 | tf_op jit(solution)/shard_map/ppermute | solution.py:22
  99.9 14.1 %collective-permute-start.18 = (f32[2,1,64,512]{3,2,1,0:T(8,128)S(1)}, f32[2,1,64,512]{3,2,1,0:T(8,128)S(1)}, u32[]{:S(2)}, u32[]{:S(2)}) collective-permute-start(f32[2,1,64,512]{3,2,1,0:T(8,128)S(1)} %get-tuple-element.43), channel_id=1, source_target_pairs={{16,0},{32,16},{48,32},{64,48},{80,64},{96,80},{112,96},{128,112},... | collective-permute-start | bytes 786440 | tf_op jit(solution)/shard_map/ppermute | solution.py:23
  101.2 12.8 %collective-permute-start.19 = (f32[2,1,64,512]{3,2,1,0:T(8,128)S(1)}, f32[2,1,64,512]{3,2,1,0:T(8,128)S(1)}, u32[]{:S(2)}, u32[]{:S(2)}) collective-permute-start(f32[2,1,64,512]{3,2,1,0:T(8,128)S(1)} %get-tuple-element.42), channel_id=1, source_target_pairs={{0,16},{16,32},{32,48},{48,64},{64,80},{80,96},{96,112},{112,128},... | collective-permute-start | bytes 786440 | tf_op jit(solution)/shard_map/ppermute | solution.py:22
  158.3 11.0 %all-to-all-start.3 = ((f32[16,1,1]{2,1,0:T(1,128)}), f32[16,1,1]{2,1,0:T(1,128)S(1)}, u32[]{:S(2)}, u32[]{:S(2)}) async-start(f32[16,1,1]{2,1,0:T(1,128)} %broadcast_in_dim.24), calls=%async_computation.3 | async-start | bytes 16384 | tf_op jit(solution)/shard_map/all_to_all | solution.py:42
  189.9 17.4 %collective-permute-start.24 = (f32[2,1,64,512]{3,2,1,0:T(8,128)S(1)}, f32[2,1,64,512]{3,2,1,0:T(8,128)S(1)}, u32[]{:S(2)}, u32[]{:S(2)}) collective-permute-start(f32[2,1,64,512]{3,2,1,0:T(8,128)S(1)} %get-tuple-element.39), channel_id=1, source_target_pairs={{16,0},{32,16},{48,32},{64,48},{80,64},{96,80},{112,96},{128,112},... | collective-permute-start | bytes 786440 | tf_op jit(solution)/shard_map/ppermute | solution.py:23
  191.3 16.0 %collective-permute-start.25 = (f32[2,1,64,512]{3,2,1,0:T(8,128)S(1)}, f32[2,1,64,512]{3,2,1,0:T(8,128)S(1)}, u32[]{:S(2)}, u32[]{:S(2)}) collective-permute-start(f32[2,1,64,512]{3,2,1,0:T(8,128)S(1)} %get-tuple-element.38), channel_id=1, source_target_pairs={{0,16},{16,32},{32,48},{48,64},{64,80},{80,96},{96,112},{112,128},... | collective-permute-start | bytes 786440 | tf_op jit(solution)/shard_map/ppermute | solution.py:22
  209.8 14.1 %collective-permute-start.28 = (f32[2,1,64,512]{3,2,1,0:T(8,128)S(1)}, f32[2,1,64,512]{3,2,1,0:T(8,128)S(1)}, u32[]{:S(2)}, u32[]{:S(2)}) collective-permute-start(f32[2,1,64,512]{3,2,1,0:T(8,128)S(1)} %get-tuple-element.35), channel_id=1, source_target_pairs={{16,0},{32,16},{48,32},{64,48},{80,64},{96,80},{112,96},{128,112},... | collective-permute-start | bytes 786440 | tf_op jit(solution)/shard_map/ppermute | solution.py:23
  211.1 12.8 %collective-permute-start.29 = (f32[2,1,64,512]{3,2,1,0:T(8,128)S(1)}, f32[2,1,64,512]{3,2,1,0:T(8,128)S(1)}, u32[]{:S(2)}, u32[]{:S(2)}) collective-permute-start(f32[2,1,64,512]{3,2,1,0:T(8,128)S(1)} %get-tuple-element.34), channel_id=1, source_target_pairs={{0,16},{16,32},{32,48},{48,64},{64,80},{80,96},{96,112},{112,128},... | collective-permute-start | bytes 786440 | tf_op jit(solution)/shard_map/ppermute | solution.py:22
  216.1 7.7 %collective-permute-start.31 = (f32[2,4,1,512]{3,2,1,0:T(1,128)S(1)}, f32[2,4,1,512]{3,2,1,0:T(1,128)S(1)}, u32[]{:S(2)}, u32[]{:S(2)}) collective-permute-start(f32[2,4,1,512]{3,2,1,0:T(1,128)S(1)} %get-tuple-element.36), channel_id=1, source_target_pairs={{0,1},{1,2},{2,3},{3,4},{4,5},{5,6},{6,7},{7,8},{8,9},{9,10},{10,1... | collective-permute-start | bytes 49160 | tf_op jit(solution)/shard_map/ppermute | solution.py:22
  266.8 18.0 %collective-permute-start.34 = (f32[2,1,64,512]{3,2,1,0:T(8,128)}, f32[2,1,64,512]{3,2,1,0:T(8,128)S(1)}, u32[]{:S(2)}, u32[]{:S(2)}) collective-permute-start(f32[2,1,64,512]{3,2,1,0:T(8,128)} %get-tuple-element.31), channel_id=1, source_target_pairs={{16,0},{32,16},{48,32},{64,48},{80,64},{96,80},{112,96},{128,112},... | collective-permute-start | bytes 786440 | tf_op jit(solution)/shard_map/ppermute | solution.py:23
  268.1 16.7 %collective-permute-start.35 = (f32[2,1,64,512]{3,2,1,0:T(8,128)}, f32[2,1,64,512]{3,2,1,0:T(8,128)}, u32[]{:S(2)}, u32[]{:S(2)}) collective-permute-start(f32[2,1,64,512]{3,2,1,0:T(8,128)} %get-tuple-element.30), channel_id=1, source_target_pairs={{0,16},{16,32},{32,48},{48,64},{64,80},{80,96},{96,112},{112,128},... | collective-permute-start | bytes 786440 | tf_op jit(solution)/shard_map/ppermute | solution.py:22
  289.5 14.1 %collective-permute-start.38 = (f32[2,1,64,512]{3,2,1,0:T(8,128)S(1)}, f32[2,1,64,512]{3,2,1,0:T(8,128)S(1)}, u32[]{:S(2)}, u32[]{:S(2)}) collective-permute-start(f32[2,1,64,512]{3,2,1,0:T(8,128)S(1)} %get-tuple-element.27), channel_id=1, source_target_pairs={{16,0},{32,16},{48,32},{64,48},{80,64},{96,80},{112,96},{128,112},... | collective-permute-start | bytes 786440 | tf_op jit(solution)/shard_map/ppermute | solution.py:23
  290.8 12.8 %collective-permute-start.39 = (f32[2,1,64,512]{3,2,1,0:T(8,128)S(1)}, f32[2,1,64,512]{3,2,1,0:T(8,128)S(1)}, u32[]{:S(2)}, u32[]{:S(2)}) collective-permute-start(f32[2,1,64,512]{3,2,1,0:T(8,128)S(1)} %get-tuple-element.26), channel_id=1, source_target_pairs={{0,16},{16,32},{32,48},{48,64},{64,80},{80,96},{96,112},{112,128},... | collective-permute-start | bytes 786440 | tf_op jit(solution)/shard_map/ppermute | solution.py:22
  295.9 7.8 %collective-permute-start.41 = (f32[2,4,1,512]{3,2,1,0:T(1,128)S(1)}, f32[2,4,1,512]{3,2,1,0:T(1,128)S(1)}, u32[]{:S(2)}, u32[]{:S(2)}) collective-permute-start(f32[2,4,1,512]{3,2,1,0:T(1,128)S(1)} %get-tuple-element.28), channel_id=1, source_target_pairs={{0,1},{1,2},{2,3},{3,4},{4,5},{5,6},{6,7},{7,8},{8,9},{9,10},{10,1... | collective-permute-start | bytes 49160 | tf_op jit(solution)/shard_map/ppermute | solution.py:22
  (32 other events, 277.6 us)
where the time goes:
time: 310 us; the launch traced here: 307 us
  starting transfers between devices  115 us (37%)
  blocking collectives  82.5 us (27%)
  waiting for transfers between devices  56.2 us (18%)
  other arithmetic  33.4 us (11%)
  local copies, waits for them, and re-layouts  10.5 us (3%)
  between operations  6.01 us (2%)
  matrix products  3.35 us (1%)
    all_to_all x6, blocking collectives, sent_to_all(): lax.all_to_all(jnp.broadcast_to(x[None], (peers, *x.shape)), axis, 0, 0,...  82.5 us
    ppermute x18, starting transfers between devices, extended(): lax.ppermute(last, axis, up)  58.5 us
    ppermute x18, waiting for transfers between devices, extended(): lax.ppermute(last, axis, up)  42 us
    ppermute x18, starting transfers between devices, extended(): lax.ppermute(initial, axis, [(b, a) for a, b in up])  41.7 us
    add x8, other arithmetic, velocity_solve(): solved = solved + change  14.8 us
    ppermute x6, starting transfers between devices, passed_along(): return lax.ppermute(block, axis, route)  11.5 us
    concatenate x9, other arithmetic, extended(): jnp.concatenate([jnp.pad(low, around), x, jnp.pad(high, around)], axis=dim)  8.57 us
    ppermute x6, waiting for transfers between devices, passed_along(): return lax.ppermute(block, axis, route)  7.22 us
  transfers between devices with their start and end apart: 43, of which 16 were waited for; matrix products, arithmetic and copies ran while one was open for 1% of the time, Pallas kernels for 0%

commit v1 on v0

v1 whole, which is shorter than its diff:
```python
import functools

import jax
import jax.numpy as jnp
from jax import lax
from jax.experimental import pallas as pl
from jax.experimental.pallas import tpu as pltpu
from jax.sharding import PartitionSpec as P

OUTER = 2
DEGREE = 3
cheb_theta = 1.025
cheb_delta = 0.975


def series():
    sigma = cheb_theta / cheb_delta
    rho0 = 1.0 / sigma
    rho1 = 1.0 / (2.0 * sigma - rho0)
    rho2 = 1.0 / (2.0 * sigma - rho1)
    g1, g2 = 2.0 * rho1 / cheb_delta, 2.0 * rho2 / cheb_delta
    p0, p1 = (1.0 + rho1 * rho0) / cheb_theta + g1, -g1 / cheb_theta
    q = rho2 * rho1
    c0 = (1.0 + q) * p0 - q / cheb_theta + g2
    c1 = (1.0 + q) * p1 - g2 * p0
    c2 = -g2 * p1
    return c0 + c1 + c2, -c1 - 2.0 * c2, c2


E0, E1, E2 = (2.0 * e for e in series())

NY, NZ = 64, 512
ROWS = 4
FRAME = 80
LO, HI = 8, 72
FORWARD = ((0, 0), (0, 1), (0, 2), (1, -1), (1, 0), (1, 1), (2, 0))
PAYLOAD = 40


def up_z(x):
    return pltpu.roll(x, NZ - 1, x.ndim - 1)


def down_z(x):
    return pltpu.roll(x, 1, x.ndim - 1)


def lane(shape):
    return lax.broadcasted_iota(jnp.int32, shape, len(shape) - 1)


def fill_viscosity(par, v, own, od, ev, lo, hi, od_c, ev_c):
    v[...] = jnp.zeros_like(v)
    v[3:7, LO:HI] = own[...]
    v[3:7, LO - 3 : LO] = lo[:, 0:3]
    v[3:7, HI : HI + 3] = hi[:, 0:3]
    od_at = par * 7
    ev_at = 7 - par * 7
    v[pl.ds(od_at, 3), LO:HI] = od[...]
    v[pl.ds(ev_at, 3), LO:HI] = ev[...]
    for at, c in ((od_at, od_c), (ev_at, ev_c)):
        v[pl.ds(at, 3), LO - 3 : LO] = c[:, 0:3]
        v[pl.ds(at, 3), HI : HI + 3] = c[:, 7:10]


def fill_inverse(v, d, fz):
    ids = lane((FRAME, NZ))

    def layer(r, _):
        mid = v[r + 1]
        nxt = jnp.where(ids == NZ - 1, 0.0, up_z(mid))
        prv = jnp.where(ids == 0, 0.0, down_z(mid))
        total = 6.0 * mid + v[r] + v[r + 2] + nxt + prv
        total = total + pltpu.roll(mid, 1, 0) + pltpu.roll(mid, FRAME - 1, 0)
        d[r] = jnp.where(mid > 0.0, 1.0 / total, 0.0)
        fz[r] = jnp.where(ids == NZ - 1, 0.0, mid + nxt)
        return 0

    lax.fori_loop(0, 8, layer, 0)


def stencil_kernel(par_ref, own, od, ev, lo, hi, od_c, ev_c, f, out, v, d, fz, h0, ex, ez, ezm, acc):
    fill_viscosity(par_ref[0], v, own, od, ev, lo, hi, od_c, ev_c)
    fill_inverse(v, d, fz)

    def edges(r, _):
        dm, vm = d[r], v[r + 1]
        ex[r] = E2 * dm * (vm + v[r + 2]) * d[r + 1]
        dy = pltpu.roll(dm, FRAME - 1, 0)
        ey = E2 * dm * (vm + pltpu.roll(vm, FRAME - 1, 0)) * dy
        h0[r] = E1 * dm + ey + pltpu.roll(ey, 1, 0)
        e = E2 * dm * fz[r] * up_z(dm)
        ez[r] = e
        ezm[r] = down_z(e)
        return 0

    lax.fori_loop(0, 7, edges, 0)

    acc[...] = jnp.zeros_like(acc)
    own_rows = slice(LO, HI)
    above = slice(LO + 1, HI + 1)
    under = slice(LO - 1, HI - 1)

    def layer(i, _):
        r = i + 2
        vm = v[r + 1, own_rows]
        fyp = vm + v[r + 1, above]
        fym = vm + v[r + 1, under]
        fxp = vm + v[r + 2, own_rows]
        fxm = vm + v[r, own_rows]
        fzp = fz[r, own_rows]
        fzm = down_z(fzp)
        dm = d[r, own_rows]
        u0, u1 = dm * f[0, i], dm * f[1, i]

        def weigh(di, dk, s):
            for c, u in ((0, u0), (1, u1)):
                row = jnp.sum(u * s, axis=0, keepdims=True)
                if dk:
                    row = pltpu.roll(row, dk % NZ, 1)
                at = pl.ds(16 * c + i + di + 2, 1)
                acc[at] = acc[at] + row[None]
            if (di, dk) in FORWARD:
                out[FORWARD.index((di, dk)), pl.ds(i, 1)] = jnp.sum(dm * s, axis=0, keepdims=True)

        exi, exm = ex[r, own_rows], ex[r - 1, own_rows]
        ezi, ezmi = ez[r, own_rows], ezm[r, own_rows]
        h = h0[r, own_rows]
        weigh(
            0,
            0,
            E0
            + fyp * h0[r, above]
            + fym * h0[r, under]
            + fxp * exi
            + fxm * exm
            + fzp * ezi
            + fzm * ezmi,
        )
        weigh(1, 0, fyp * ex[r, above] + fym * ex[r, under] + fxp * h0[r + 1, own_rows])
        weigh(-1, 0, fyp * ex[r - 1, above] + fym * ex[r - 1, under] + fxm * h0[r - 1, own_rows])
        weigh(0, 1, fyp * ez[r, above] + fym * ez[r, under] + fzp * up_z(h))
        weigh(0, -1, fyp * ezm[r, above] + fym * ezm[r, under] + fzm * down_z(h))
        weigh(2, 0, fxp * ex[r + 1, own_rows])
        weigh(-2, 0, fxm * ex[r - 2, own_rows])
        weigh(0, 2, fzp * up_z(ezi))
        weigh(0, -2, fzm * down_z(ezmi))
        weigh(1, 1, fxp * ez[r + 1, own_rows] + fzp * up_z(exi))
        weigh(1, -1, fxp * ezm[r + 1, own_rows] + fzm * down_z(exi))
        weigh(-1, 1, fxm * ez[r - 1, own_rows] + fzp * up_z(exm))
        weigh(-1, -1, fxm * ezm[r - 1, own_rows] + fzm * down_z(exm))
        return 0

    lax.fori_loop(0, ROWS, layer, 0)

    cx = acc[0:16, 0]
    cz = acc[16:32, 0]
    zero = lane((16, NZ)) == 0
    e = cx - pltpu.roll(cx, 1, 0) + cz - jnp.where(zero, 0.0, down_z(cz))
    out[7:9] = e[0:8].reshape(2, 4, NZ)
    out[9, 0:1] = e[8:9]
    out[9, 1:4] = jnp.zeros((3, NZ), jnp.float32)


def krylov_kernel(par_ref, mine, mate, below_mine, below_mate, above_mine, above_mate, basis, dots, s_ref, g_ref):
    par, chip = par_ref[0], par_ref[1]
    odd = par == 1

    def pair(a, b):
        return lax.select(odd, b, a), lax.select(odd, a, b)

    slabs = []
    for a, b in ((below_mine, below_mate), (mine, mate), (above_mine, above_mate)):
        slabs += pair(a[...], b[...])
    W = 24
    g_ref[...] = jnp.zeros_like(g_ref)
    for n, slab in enumerate(slabs):
        for o in range(7):
            s_ref[o, 4 * n : 4 * n + 4] = slab[o]
        flat = slab[7:10].reshape(12, NZ)[0:9]
        at = 8 + 4 * n - 2
        g_ref[at : at + 9] = g_ref[at : at + 9] + flat
    ids = lane((W, NZ))
    layer = lax.broadcasted_iota(jnp.int32, (W, NZ), 0) - 8 + 8 * chip
    inside = jnp.logical_and(layer >= 0, layer < 64)

    def next_layer(x, n=1):
        return pltpu.roll(x, (W - n) % W, 0)

    def shift(x, di, dk):
        if di:
            x = pltpu.roll(x, (-di) % W, 0)
        if dk:
            x = pltpu.roll(x, (-dk) % NZ, 1)
        return x

    def spread(q):
        qx = q - next_layer(q)
        qz = q - jnp.where(ids == NZ - 1, 0.0, up_z(q))
        return qx, qz

    def times_s(b):
        total = None
        for n, (di, dk) in enumerate(FORWARD):
            s = s_ref[n]
            if n == 0:
                total = s * b
            else:
                total = total + s * shift(b, di, dk) + shift(s * b, -di, -dk)
        return total

    g = jnp.where(inside, g_ref[8 : 8 + W], 0.0)
    gx, gz = spread(g)
    tx, tz = times_s(gx), times_s(gz)
    h = tx - pltpu.roll(tx, 1, 0) + tz - jnp.where(ids == 0, 0.0, down_z(tz))
    h = jnp.where(inside, h, 0.0)
    hx, hz = spread(h)
    energy = hx * times_s(hx) + hz * times_s(hz)

    def own(x):
        return lax.select(odd, pltpu.roll(x, W - 4, 0), x)

    for n, x in enumerate((gx, gz, hx, hz)):
        basis[8 * n : 8 * n + 8] = own(x)[6:14]
    basis[32:40] = own(g)[8:16]
    basis[40:48] = own(h)[8:16]
    rows = []
    for x in (g * g, g * h, h * h, energy):
        part = x[8:16]
        part = part[:, 0:128] + part[:, 128:256] + part[:, 256:384] + part[:, 384:512]
        rows.append(jnp.sum(part, axis=0, keepdims=True))
    dots[...] = jnp.concatenate(rows + [jnp.zeros((4, 128), jnp.float32)], 0)


def velocity_kernel(
    par_ref, own, od, ev, lo, hi, od_c, ev_c, f, od_f, ev_f, basis, dots, onehot, vel, press, v, d, fz, u, t, b
):
    par = par_ref[0]
    fill_viscosity(par, v, own, od, ev, lo, hi, od_c, ev_c)
    fill_inverse(v, d, fz)

    sums = jnp.sum(jnp.sum(dots[...], axis=0), axis=1, keepdims=True)
    gg, gh, hh, hkh = sums[0:1], sums[1:2], sums[2:3], sums[3:4]
    alpha0 = gg / gh
    fresh = gg - 2.0 * alpha0 * gh + alpha0 * alpha0 * hh
    beta = fresh / gg
    grow = 1.0 + beta
    alpha1 = fresh / (grow * grow * gh - 2.0 * grow * alpha0 * hh + alpha0 * alpha0 * hkh)
    on_g = alpha0 + alpha1 * grow
    on_h = alpha1 * alpha0
    b[0:16] = on_g * basis[0:16] - on_h * basis[16:32]
    p = on_g * basis[32:40] - on_h * basis[40:48]
    press[...] = jnp.dot(
        p, onehot[...], precision=lax.Precision.HIGHEST, preferred_element_type=jnp.float32
    )[0:4]

    u[...] = jnp.zeros_like(u)
    od_at, ev_at = par * 6, 6 - par * 6
    for c in range(2):
        u[c, 2:6, LO:HI] = f[c]
        u[c, 2:6, LO - 2 : LO] = lo[:, 3 + 2 * c : 5 + 2 * c]
        u[c, 2:6, HI : HI + 2] = hi[:, 3 + 2 * c : 5 + 2 * c]
        u[c, pl.ds(od_at, 2), LO:HI] = od_f[c]
        u[c, pl.ds(ev_at, 2), LO:HI] = ev_f[c]
        for at, first, corner in ((od_at, 1 - par, od_c), (ev_at, par, ev_c)):
            u[c, pl.ds(at, 2), LO - 2 : LO] = corner[pl.ds(first, 2), 3 + 2 * c : 5 + 2 * c]
            u[c, pl.ds(at, 2), HI : HI + 2] = corner[pl.ds(first, 2), 10 + 2 * c : 12 + 2 * c]

    def scale(r, _):
        dm = d[r]
        u[0, r] = dm * (u[0, r] - b[pl.ds(r, 1)])
        u[1, r] = dm * (u[1, r] - b[pl.ds(8 + r, 1)])
        return 0

    lax.fori_loop(0, 8, scale, 0)

    def first(r, _):
        vm = v[r + 1]
        fy = vm + pltpu.roll(vm, FRAME - 1, 0)
        fxp, fxm = vm + v[r + 2], vm + v[r]
        fzp, dm = fz[r], d[r]
        for c in range(2):
            x = u[c, r]
            y = fy * pltpu.roll(x, FRAME - 1, 0) + pltpu.roll(fy * x, 1, 0)
            y = y + fxp * u[c, r + 1] + fxm * u[c, r - 1]
            y = y + fzp * up_z(x) + down_z(fzp * x)
            t[c, r] = E1 * x + E2 * (dm * y)
        return 0

    lax.fori_loop(1, 7, first, 0)

    own_rows = slice(LO, HI)
    above = slice(LO + 1, HI + 1)
    under = slice(LO - 1, HI - 1)

    def second(i, _):
        r = i + 2
        vm = v[r + 1, own_rows]
        fyp = vm + v[r + 1, above]
        fym = vm + v[r + 1, under]
        fxp, fxm = vm + v[r + 2, own_rows], vm + v[r, own_rows]
        fzp, dm = fz[r, own_rows], d[r, own_rows]
        for c in range(2):
            x = t[c, r, own_rows]
            y = fyp * t[c, r, above] + fym * t[c, r, under]
            y = y + fxp * t[c, r + 1, own_rows] + fxm * t[c, r - 1, own_rows]
            y = y + fzp * up_z(x) + down_z(fzp * x)
            vel[c, i] = E0 * u[c, r, own_rows] + dm * y
        return 0

    lax.fori_loop(0, ROWS, second, 0)


def call(kernel, out_shape, scratch, args, smem=1):
    vmem = pl.BlockSpec(memory_space=pltpu.VMEM)
    specs = [pl.BlockSpec(memory_space=pltpu.SMEM)] * smem + [vmem] * (len(args) - smem)
    return pl.pallas_call(
        kernel,
        out_shape=out_shape,
        in_specs=specs,
        out_specs=jax.tree.map(lambda _: vmem, out_shape),
        scratch_shapes=[pltpu.VMEM(s, jnp.float32) for s in scratch],
        compiler_params=pltpu.CompilerParams(vmem_limit_bytes=48 * 1024 * 1024),
    )(*args)


def f32(*shape):
    return jax.ShapeDtypeStruct(shape, jnp.float32)


def shards(forcing, viscosity, owner_slot):
    slabs, cross = lax.axis_size("slab"), lax.axis_size("cross")
    slab = lax.axis_index("slab")
    par = slab % 2
    where = jnp.stack([par, slab // 2]).astype(jnp.int32)
    mates = [(i, i ^ 1) for i in range(slabs)]
    others = [(i, i + 1) for i in range(1, slabs - 1, 2)]
    others = others + [(b, a) for a, b in others]
    up = [(i, i + 1) for i in range(cross - 1)]
    down = [(b, a) for a, b in up]
    chips = slabs // 2
    chip_up = [(i, (i + 2) % slabs) for i in range(slabs) if i + 2 < slabs]
    chip_down = [(b, a) for a, b in chip_up]

    def sides(x, n):
        last, initial = x[..., x.shape[-3] - n :, :, :], x[..., :n, :, :]
        odd = par == 1
        return jnp.where(odd, last, initial), jnp.where(odd, initial, last)

    to_od, to_ev = sides(viscosity, 3)
    od = lax.ppermute(to_od, "slab", others)
    ev = lax.ppermute(to_ev, "slab", mates)
    edge_hi = jnp.concatenate([viscosity[:, -3:], forcing[0, :, -2:], forcing[1, :, -2:]], 1)
    edge_lo = jnp.concatenate([viscosity[:, :3], forcing[0, :, :2], forcing[1, :, :2]], 1)
    lo = lax.ppermute(edge_hi, "cross", up)
    hi = lax.ppermute(edge_lo, "cross", down)
    to_od, to_ev = sides(jnp.concatenate([lo, hi], 1), 3)
    od_c = lax.ppermute(to_od, "slab", others)
    ev_c = lax.ppermute(to_ev, "slab", mates)

    grid = (viscosity, od, ev, lo, hi, od_c, ev_c)
    part = call(
        stencil_kernel,
        f32(10, 4, NZ),
        [(10, FRAME, NZ)] + [(8, FRAME, NZ)] * 2 + [(7, FRAME, NZ)] * 4 + [(32, 1, NZ)],
        (where, *grid, forcing),
    )

    part, forced = lax.optimization_barrier((part, forcing))
    to_od, to_ev = sides(forced, 2)
    od_f = lax.ppermute(to_od, "slab", others)
    ev_f = lax.ppermute(to_ev, "slab", mates)

    for step in (1, 4):
        part = sum(
            (lax.ppermute(part, "cross", [(i, i ^ (n * step)) for i in range(cross)]) for n in (1, 2, 3)), part
        )

    mate = lax.ppermute(part, "slab", mates)
    both = jnp.stack([part, mate])
    below = lax.ppermute(both, "slab", chip_up)
    above = lax.ppermute(both, "slab", chip_down)
    basis, dots = call(
        krylov_kernel,
        (f32(48, NZ), f32(8, 128)),
        [(7, 24, NZ), (40, NZ)],
        (where, part, mate, below[0], below[1], above[0], above[1]),
    )
    groups = [[2 * z + c for z in range(chips)] for c in range(2)]
    dots = lax.all_to_all(
        jnp.broadcast_to(dots[None], (chips, 8, 128)), "slab", 0, 0, tiled=True, axis_index_groups=groups
    )

    width = owner_slot.shape[0] // cross
    column = lax.axis_index("cross") * width + jnp.arange(width, dtype=jnp.int32)
    onehot = (owner_slot[:, None] == column[None, :]).astype(jnp.float32)
    return call(
        velocity_kernel,
        (f32(2, ROWS, NY, NZ), f32(ROWS, width)),
        [(10, FRAME, NZ)] + [(8, FRAME, NZ)] * 2 + [(2, 8, FRAME, NZ)] * 2 + [(16, NZ)],
        (where, *grid, forcing, od_f, ev_f, basis, dots, onehot),
    )


def solution(mesh):
    in_specs = (P(None, "slab", "cross", None), P("slab", "cross", None), P())
    out_specs = (P(None, "slab", "cross", None), P("slab", "cross"))
    return jax.shard_map(shards, mesh=mesh, in_specs=in_specs, out_specs=out_specs, check_vma=False)
```

time: 310 us -> 100 us (0.32)
  the two profiles are of different devices: /device:TPU:16 before, /device:TPU:1 now
where the time goes in v1:
time: 100 us; the launch traced here: 99.5 us
  starting transfers between devices  46.8 us (47%)
  waiting for transfers between devices  27.4 us (27%)
  Pallas kernels  16.9 us (17%)
  local copies, waits for them, and re-layouts  4.01 us (4%)
  other arithmetic  3.58 us (4%)
    pallas_call x3, Pallas kernels, call(): pl.pallas_call(kernel, out_shape=out_shape, in_specs=specs, out_specs=jax...  16.9 us
    all_to_all x1, starting transfers between devices, shards(): lax.all_to_all(jnp.broadcast_to(dots[None], (chips, 8, 128)), 'slab', 0,...  11.2 us
    ppermute x6, starting transfers between devices, shards(): lax.ppermute(part, 'cross', [(i, i ^ n * step) for i in range(cross)])  8.47 us
    ppermute x1, starting transfers between devices, shards(): od_f = lax.ppermute(to_od, 'slab', others)  8.2 us
    ppermute x6, waiting for transfers between devices, shards(): lax.ppermute(part, 'cross', [(i, i ^ n * step) for i in range(cross)])  7.24 us
    all_to_all x1, waiting for transfers between devices, shards(): lax.all_to_all(jnp.broadcast_to(dots[None], (chips, 8, 128)), 'slab', 0,...  6.73 us
    ppermute x1, waiting for transfers between devices, shards(): below = lax.ppermute(both, 'slab', chip_up)  6.25 us
    ppermute x1, starting transfers between devices, shards(): od_c = lax.ppermute(to_od, 'slab', others)  4.13 us
  transfers between devices with their start and end apart: 18, of which 9 were waited for; matrix products, arithmetic and copies ran while one was open for 4% of the time, Pallas kernels for 1%

profile of v1, /device:TPU:1, one launch (start us, length us, event | category | flops | bytes accessed | tf_op | source)
XLA Modules:
  0.0 99.5 jit_solution(3752084469434434457)
XLA Ops:
  2.5 3.9 %collective-permute-start.2 = (f32[4,7,512]{2,1,0:T(8,128)S(1)}, f32[4,7,512]{2,1,0:T(8,128)S(1)}, u32[]{:S(2)}, u32[]{:S(2)}) collective-permute-start(f32[4,7,512]{2,1,0:T(8,128)S(1)} %pad_maximum_fusion.2), channel_id=1, source_target_pairs={{0,1},{1,2},{2,3},{3,4},{4,5},{5,6},{6,7},{7,8},{8,9},{9,10},{10,1... | collective-permute-start | bytes 172040 | tf_op jit(solution)/shard_map/ppermute | solution.py:355
  6.5 2.1 %slice_select_fusion.2 = (f32[3,64,512]{2,1,0:T(8,128)}, f32[3,64,512]{2,1,0:T(8,128)S(1)}) fusion(f32[4,64,512]{2,1,0:T(8,128)} %own.3, pred[]{:T(512)S(6)} %eq.10), kind=kLoop, calls=%fused_computation.2 | loop fusion | flops 196608 | bytes 1572865 | tf_op jit(solution)/shard_map/jit(_where)/select_n | solution.py:348
  9.5 3.4 %collective-permute-start = (f32[3,64,512]{2,1,0:T(8,128)S(1)}, f32[3,64,512]{2,1,0:T(8,128)S(1)}, u32[]{:S(2)}, u32[]{:S(2)}) collective-permute-start(f32[3,64,512]{2,1,0:T(8,128)S(1)} %get-tuple-element.19), channel_id=1, source_target_pairs={{16,32},{48,64},{80,96},{112,128},{144,160},{176,192},{208,224},{3... | collective-permute-start | bytes 1179656 | tf_op jit(solution)/shard_map/ppermute | solution.py:351
  13.0 1.3 %collective-permute-start.3 = (f32[4,7,512]{2,1,0:T(8,128)S(1)}, f32[4,7,512]{2,1,0:T(8,128)S(1)}, u32[]{:S(2)}, u32[]{:S(2)}) collective-permute-start(f32[4,7,512]{2,1,0:T(8,128)S(1)} %pad_maximum_fusion.3), channel_id=1, source_target_pairs={{1,0},{2,1},{3,2},{4,3},{5,4},{6,5},{7,6},{8,7},{9,8},{10,9},{11,1... | collective-permute-start | bytes 172040 | tf_op jit(solution)/shard_map/ppermute | solution.py:356
  14.3 3.7 %collective-permute-done.3.hi = f32[4,7,512]{2,1,0:T(8,128)S(1)} collective-permute-done((f32[4,7,512]{2,1,0:T(8,128)S(1)}, f32[4,7,512]{2,1,0:T(8,128)S(1)}, u32[]{:S(2)}, u32[]{:S(2)}) %collective-permute-start.3) | collective-permute-done | bytes 57376 | tf_op jit(solution)/shard_map/ppermute | solution.py:356
  18.1 4.1 %collective-permute-start.4 = (f32[3,14,512]{2,1,0:T(8,128)S(1)}, f32[3,14,512]{2,1,0:T(8,128)S(1)}, u32[]{:S(2)}, u32[]{:S(2)}) collective-permute-start(f32[3,14,512]{2,1,0:T(8,128)S(1)} %get-tuple-element.25), channel_id=1, source_target_pairs={{16,32},{48,64},{80,96},{112,128},{144,160},{176,192},{208,224},{3... | collective-permute-start | bytes 258056 | tf_op jit(solution)/shard_map/ppermute | solution.py:358
  22.4 2.2 %collective-permute-done.4.od_c = f32[3,14,512]{2,1,0:T(8,128)S(1)} collective-permute-done((f32[3,14,512]{2,1,0:T(8,128)S(1)}, f32[3,14,512]{2,1,0:T(8,128)S(1)}, u32[]{:S(2)}, u32[]{:S(2)}) %collective-permute-start.4) | collective-permute-done | bytes 86048 | tf_op jit(solution)/shard_map/ppermute | solution.py:358
  24.6 7.9 %shard_map.50 = f32[10,4,512]{2,1,0:T(4,128)S(1)} custom-call(s32[2]{0:T(128)S(1)} %pad_add_fusion.par_ref, f32[4,64,512]{2,1,0:T(8,128)S(1)} %copy-done.1, f32[3,64,512]{2,1,0:T(8,128)S(1)} %collective-permute-done.od, f32[3,64,512]{2,1,0:T(8,128)S(1)} %collective-permute-done.1.ev, f32[4,7,512]{2,1,0:T(8,128)S(1)} %collective-permute-done.2.lo, ...), custom_call_target="tpu_custom_call" | custom-call | tf_op jit(solution)/shard_map/pallas_call | solution.py:317
  32.5 4.5 %collective-permute-start.10 = (f32[10,4,512]{2,1,0:T(4,128)S(1)}, f32[10,4,512]{2,1,0:T(4,128)S(1)}, u32[]{:S(2)}, u32[]{:S(2)}) collective-permute-start(f32[10,4,512]{2,1,0:T(4,128)S(1)} %shard_map.50), channel_id=1, source_target_pairs={{0,3},{1,2},{2,1},{3,0},{4,7},{5,6},{6,5},{7,4},{8,11},{9,10},{10,... | collective-permute-start | bytes 245768 | tf_op jit(solution)/shard_map/ppermute | solution.py:376
  37.7 1.6 %collective-permute-done.10 = f32[10,4,512]{2,1,0:T(4,128)S(1)} collective-permute-done((f32[10,4,512]{2,1,0:T(4,128)S(1)}, f32[10,4,512]{2,1,0:T(4,128)S(1)}, u32[]{:S(2)}, u32[]{:S(2)}) %collective-permute-start.10) | collective-permute-done | bytes 81952 | tf_op jit(solution)/shard_map/ppermute | solution.py:376
  39.3 2.5 %collective-permute-done.9 = f32[10,4,512]{2,1,0:T(4,128)S(1)} collective-permute-done((f32[10,4,512]{2,1,0:T(4,128)S(1)}, f32[10,4,512]{2,1,0:T(4,128)S(1)}, u32[]{:S(2)}, u32[]{:S(2)}) %collective-permute-start.9) | collective-permute-done | bytes 81952 | tf_op jit(solution)/shard_map/ppermute | solution.py:376
  41.9 3.1 %collective-permute-start.12 = (f32[10,4,512]{2,1,0:T(4,128)S(1)}, f32[10,4,512]{2,1,0:T(4,128)S(1)}, u32[]{:S(2)}, u32[]{:S(2)}) collective-permute-start(f32[10,4,512]{2,1,0:T(4,128)S(1)} %bitcast.36), channel_id=1, source_target_pairs={{0,8},{1,9},{2,10},{3,11},{4,12},{5,13},{6,14},{7,15},{8,0},{9,1},... | collective-permute-start | bytes 245768 | tf_op jit(solution)/shard_map/ppermute | solution.py:376
  45.2 2.1 %collective-permute-done.13 = f32[10,4,512]{2,1,0:T(4,128)S(1)} collective-permute-done((f32[10,4,512]{2,1,0:T(4,128)S(1)}, f32[10,4,512]{2,1,0:T(4,128)S(1)}, u32[]{:S(2)}, u32[]{:S(2)}) %collective-permute-start.13) | collective-permute-done | bytes 81952 | tf_op jit(solution)/shard_map/ppermute | solution.py:376
  47.3 1.0 collective-permute-done.11
  48.4 1.3 %collective-permute-done.14.mate = f32[10,4,512]{2,1,0:T(4,128)S(1)} collective-permute-done((f32[10,4,512]{2,1,0:T(4,128)S(1)}, f32[10,4,512]{2,1,0:T(4,128)S(1)}, u32[]{:S(2)}, u32[]{:S(2)}) %collective-permute-start.14) | collective-permute-done | bytes 81952 | tf_op jit(solution)/shard_map/ppermute | solution.py:379
  49.7 1.3 %collective-permute-start.16 = (f32[2,10,4,512]{3,2,1,0:T(4,128)S(1)}, f32[2,10,4,512]{3,2,1,0:T(4,128)S(1)}, u32[]{:S(2)}, u32[]{:S(2)}) collective-permute-start(f32[2,10,4,512]{3,2,1,0:T(4,128)S(1)} %pad_maximum_fusion), channel_id=1, source_target_pairs={{32,0},{48,16},{64,32},{80,48},{96,64},{112,80},{128,96},{144,112}... | collective-permute-start | bytes 491528 | tf_op jit(solution)/shard_map/ppermute | solution.py:382
  51.0 1.1 %slice_select_fusion = (f32[2,2,64,512]{3,2,1,0:T(8,128)}, f32[2,2,64,512]{3,2,1,0:T(8,128)}) fusion(f32[2,4,64,512]{3,2,1,0:T(8,128)S(1)} %copy-done, pred[]{:T(512)S(6)} %eq.10), kind=kLoop, calls=%fused_computation | loop fusion | flops 262144 | bytes 2097153 | tf_op jit(solution)/shard_map/jit(_where)/select_n | solution.py:348
  52.3 8.2 %collective-permute-start.6 = (f32[2,2,64,512]{3,2,1,0:T(8,128)}, f32[2,2,64,512]{3,2,1,0:T(8,128)}, u32[]{:S(2)}, u32[]{:S(2)}) collective-permute-start(f32[2,2,64,512]{3,2,1,0:T(8,128)} %get-tuple-element.11), channel_id=1, source_target_pairs={{16,32},{48,64},{80,96},{112,128},{144,160},{176,192},{208,224},{3... | collective-permute-start | bytes 1572872 | tf_op jit(solution)/shard_map/ppermute | solution.py:371
  60.5 3.5 %collective-permute-start.15 = (f32[2,10,4,512]{3,2,1,0:T(4,128)S(1)}, f32[2,10,4,512]{3,2,1,0:T(4,128)S(1)}, u32[]{:S(2)}, u32[]{:S(2)}) collective-permute-start(f32[2,10,4,512]{3,2,1,0:T(4,128)S(1)} %pad_maximum_fusion), channel_id=1, source_target_pairs={{0,32},{16,48},{32,64},{48,80},{64,96},{80,112},{96,128},{112,144}... | collective-permute-start | bytes 491528 | tf_op jit(solution)/shard_map/ppermute | solution.py:381
  64.1 6.2 %collective-permute-done.15 = f32[2,10,4,512]{3,2,1,0:T(4,128)S(1)} collective-permute-done((f32[2,10,4,512]{3,2,1,0:T(4,128)S(1)}, f32[2,10,4,512]{3,2,1,0:T(4,128)S(1)}, u32[]{:S(2)}, u32[]{:S(2)}) %collective-permute-start.15) | collective-permute-done | bytes 163872 | tf_op jit(solution)/shard_map/ppermute | solution.py:381
  70.4 1.2 %shard_map.51 = (f32[48,512]{1,0:T(8,128)S(1)}, f32[8,128]{1,0:T(8,128)S(1)}) custom-call(s32[2]{0:T(128)S(1)} %pad_add_fusion.par_ref, f32[10,4,512]{2,1,0:T(4,128)S(1)} %bitcast.32, f32[10,4,512]{2,1,0:T(4,128)S(1)} %collective-permute-done.14.mate, f32[10,4,512]{2,1,0:T(4,128)S(1)} %get-tuple-element.23.below_mine, ...), custom_call_target="tpu_custom_call" | custom-call | tf_op jit(solution)/shard_map/pallas_call | solution.py:317
  72.8 11.2 %all-to-all-start = ((f32[8,8,128]{2,1,0:T(8,128)}), f32[8,8,128]{2,1,0:T(8,128)S(1)}, u32[]{:S(2)}, u32[]{:S(2)}) async-start(f32[8,8,128]{2,1,0:T(8,128)} %broadcast_in_dim.2), calls=%async_computation | async-start | bytes 65536 | tf_op jit(solution)/shard_map/all_to_all | solution.py:390
  84.1 6.7 %all-to-all-done.dots = f32[8,8,128]{2,1,0:T(8,128)S(1)} async-done(((f32[8,8,128]{2,1,0:T(8,128)}), f32[8,8,128]{2,1,0:T(8,128)S(1)}, u32[]{:S(2)}, u32[]{:S(2)}) %all-to-all-start) | async-done | bytes 32800 | tf_op jit(solution)/shard_map/all_to_all | solution.py:390
  91.8 7.8 %shard_map.52 = (f32[2,4,64,512]{3,2,1,0:T(8,128)}, f32[4,32]{1,0:T(4,128)}) custom-call(s32[2]{0:T(128)S(1)} %pad_add_fusion.par_ref, f32[4,64,512]{2,1,0:T(8,128)S(1)} %copy-done.1, f32[3,64,512]{2,1,0:T(8,128)S(1)} %collective-permute-done.od, f32[3,64,512]{2,1,0:T(8,128)S(1)} %collective-permute-done.1.ev, f32[4,7,512]{2,1,0:T(8,128)S(1)} %collective-permute-done.2.lo, ...), custom_call_target="tpu_custom_call" | custom-call | tf_op jit(solution)/shard_map/pallas_call | solution.py:317
  (41 shorter events, 6.7 us)
Async XLA Ops:
  2.5 11.8 %collective-permute-start.2 = (f32[4,7,512]{2,1,0:T(8,128)S(1)}, f32[4,7,512]{2,1,0:T(8,128)S(1)}, u32[]{:S(2)}, u32[]{:S(2)}) collective-permute-start(f32[4,7,512]{2,1,0:T(8,128)S(1)} %pad_maximum_fusion.2), channel_id=1, source_target_pairs={{0,1},{1,2},{2,3},{3,4},{4,5},{5,6},{6,7},{7,8},{8,9},{9,10},{10,1... | collective-permute-start | bytes 172040 | tf_op jit(solution)/shard_map/ppermute | solution.py:355
  6.5 18.1 %copy-start = (f32[2,4,64,512]{3,2,1,0:T(8,128)S(1)}, f32[2,4,64,512]{3,2,1,0:T(8,128)}, u32[]{:S(2)}) copy-start(f32[2,4,64,512]{3,2,1,0:T(8,128)} %f.3) | copy-start | bytes 3145732
  6.5 18.1 %copy-start.1 = (f32[4,64,512]{2,1,0:T(8,128)S(1)}, f32[4,64,512]{2,1,0:T(8,128)}, u32[]{:S(2)}) copy-start(f32[4,64,512]{2,1,0:T(8,128)} %own.3) | copy-start | bytes 1572868
  8.6 16.0 %collective-permute-start.1 = (f32[3,64,512]{2,1,0:T(8,128)}, f32[3,64,512]{2,1,0:T(8,128)S(1)}, u32[]{:S(2)}, u32[]{:S(2)}) collective-permute-start(f32[3,64,512]{2,1,0:T(8,128)} %get-tuple-element.18), channel_id=1, source_target_pairs={{0,16},{16,0},{32,48},{48,32},{64,80},{80,64},{96,112},{112,96},{1... | collective-permute-start | bytes 1179656 | tf_op jit(solution)/shard_map/ppermute | solution.py:352
  9.5 15.0 %collective-permute-start = (f32[3,64,512]{2,1,0:T(8,128)S(1)}, f32[3,64,512]{2,1,0:T(8,128)S(1)}, u32[]{:S(2)}, u32[]{:S(2)}) collective-permute-start(f32[3,64,512]{2,1,0:T(8,128)S(1)} %get-tuple-element.19), channel_id=1, source_target_pairs={{16,32},{48,64},{80,96},{112,128},{144,160},{176,192},{208,224},{3... | collective-permute-start | bytes 1179656 | tf_op jit(solution)/shard_map/ppermute | solution.py:351
  13.0 5.0 %collective-permute-start.3 = (f32[4,7,512]{2,1,0:T(8,128)S(1)}, f32[4,7,512]{2,1,0:T(8,128)S(1)}, u32[]{:S(2)}, u32[]{:S(2)}) collective-permute-start(f32[4,7,512]{2,1,0:T(8,128)S(1)} %pad_maximum_fusion.3), channel_id=1, source_target_pairs={{1,0},{2,1},{3,2},{4,3},{5,4},{6,5},{7,6},{8,7},{9,8},{10,9},{11,1... | collective-permute-start | bytes 172040 | tf_op jit(solution)/shard_map/ppermute | solution.py:356
  18.0 4.3 %collective-permute-start.5 = (f32[3,14,512]{2,1,0:T(8,128)S(1)}, f32[3,14,512]{2,1,0:T(8,128)S(1)}, u32[]{:S(2)}, u32[]{:S(2)}) collective-permute-start(f32[3,14,512]{2,1,0:T(8,128)S(1)} %get-tuple-element.24), channel_id=1, source_target_pairs={{0,16},{16,0},{32,48},{48,32},{64,80},{80,64},{96,112},{112,96},{1... | collective-permute-start | bytes 258056 | tf_op jit(solution)/shard_map/ppermute | solution.py:359
  18.1 6.4 %collective-permute-start.4 = (f32[3,14,512]{2,1,0:T(8,128)S(1)}, f32[3,14,512]{2,1,0:T(8,128)S(1)}, u32[]{:S(2)}, u32[]{:S(2)}) collective-permute-start(f32[3,14,512]{2,1,0:T(8,128)S(1)} %get-tuple-element.25), channel_id=1, source_target_pairs={{16,32},{48,64},{80,96},{112,128},{144,160},{176,192},{208,224},{3... | collective-permute-start | bytes 258056 | tf_op jit(solution)/shard_map/ppermute | solution.py:358
  32.5 6.7 %collective-permute-start.10 = (f32[10,4,512]{2,1,0:T(4,128)S(1)}, f32[10,4,512]{2,1,0:T(4,128)S(1)}, u32[]{:S(2)}, u32[]{:S(2)}) collective-permute-start(f32[10,4,512]{2,1,0:T(4,128)S(1)} %shard_map.50), channel_id=1, source_target_pairs={{0,3},{1,2},{2,1},{3,0},{4,7},{5,6},{6,5},{7,4},{8,11},{9,10},{10,... | collective-permute-start | bytes 245768 | tf_op jit(solution)/shard_map/ppermute | solution.py:376
  37.0 4.8 %collective-permute-start.9 = (f32[10,4,512]{2,1,0:T(4,128)S(1)}, f32[10,4,512]{2,1,0:T(4,128)S(1)}, u32[]{:S(2)}, u32[]{:S(2)}) collective-permute-start(f32[10,4,512]{2,1,0:T(4,128)S(1)} %shard_map.50), channel_id=1, source_target_pairs={{0,2},{1,3},{2,0},{3,1},{4,6},{5,7},{6,4},{7,5},{8,10},{9,11},{10,... | collective-permute-start | bytes 245768 | tf_op jit(solution)/shard_map/ppermute | solution.py:376
  37.0 4.8 %collective-permute-start.8 = (f32[10,4,512]{2,1,0:T(4,128)S(1)}, f32[10,4,512]{2,1,0:T(4,128)S(1)}, u32[]{:S(2)}, u32[]{:S(2)}) collective-permute-start(f32[10,4,512]{2,1,0:T(4,128)S(1)} %shard_map.50), channel_id=1, source_target_pairs={{0,1},{1,0},{2,3},{3,2},{4,5},{5,4},{6,7},{7,6},{8,9},{9,8},{10,11... | collective-permute-start | bytes 245768 | tf_op jit(solution)/shard_map/ppermute | solution.py:376
  41.8 5.5 %collective-permute-start.13 = (f32[10,4,512]{2,1,0:T(4,128)S(1)}, f32[10,4,512]{2,1,0:T(4,128)S(1)}, u32[]{:S(2)}, u32[]{:S(2)}) collective-permute-start(f32[10,4,512]{2,1,0:T(4,128)S(1)} %bitcast.35), channel_id=1, source_target_pairs={{0,12},{1,13},{2,14},{3,15},{4,8},{5,9},{6,10},{7,11},{8,4},{9,5},... | collective-permute-start | bytes 245768 | tf_op jit(solution)/shard_map/ppermute | solution.py:376
  41.9 5.4 %collective-permute-start.12 = (f32[10,4,512]{2,1,0:T(4,128)S(1)}, f32[10,4,512]{2,1,0:T(4,128)S(1)}, u32[]{:S(2)}, u32[]{:S(2)}) collective-permute-start(f32[10,4,512]{2,1,0:T(4,128)S(1)} %bitcast.36), channel_id=1, source_target_pairs={{0,8},{1,9},{2,10},{3,11},{4,12},{5,13},{6,14},{7,15},{8,0},{9,1},... | collective-permute-start | bytes 245768 | tf_op jit(solution)/shard_map/ppermute | solution.py:376
  45.0 3.3 %collective-permute-start.11 = (f32[10,4,512]{2,1,0:T(4,128)S(1)}, f32[10,4,512]{2,1,0:T(4,128)S(1)}, u32[]{:S(2)}, u32[]{:S(2)}) collective-permute-start(f32[10,4,512]{2,1,0:T(4,128)S(1)} %bitcast.37), channel_id=1, source_target_pairs={{0,4},{1,5},{2,6},{3,7},{4,0},{5,1},{6,2},{7,3},{8,12},{9,13},{10,... | collective-permute-start | bytes 245768 | tf_op jit(solution)/shard_map/ppermute | solution.py:376
  48.3 1.4 %collective-permute-start.14 = (f32[10,4,512]{2,1,0:T(4,128)S(1)}, f32[10,4,512]{2,1,0:T(4,128)S(1)}, u32[]{:S(2)}, u32[]{:S(2)}) collective-permute-start(f32[10,4,512]{2,1,0:T(4,128)S(1)} %bitcast.30), channel_id=1, source_target_pairs={{0,16},{16,0},{32,48},{48,32},{64,80},{80,64},{96,112},{112,96},{1... | collective-permute-start | bytes 245768 | tf_op jit(solution)/shard_map/ppermute | solution.py:379
  49.7 14.4 %collective-permute-start.16 = (f32[2,10,4,512]{3,2,1,0:T(4,128)S(1)}, f32[2,10,4,512]{3,2,1,0:T(4,128)S(1)}, u32[]{:S(2)}, u32[]{:S(2)}) collective-permute-start(f32[2,10,4,512]{3,2,1,0:T(4,128)S(1)} %pad_maximum_fusion), channel_id=1, source_target_pairs={{32,0},{48,16},{64,32},{80,48},{96,64},{112,80},{128,96},{144,112}... | collective-permute-start | bytes 491528 | tf_op jit(solution)/shard_map/ppermute | solution.py:382
  52.2 38.7 %collective-permute-start.7 = (f32[2,2,64,512]{3,2,1,0:T(8,128)}, f32[2,2,64,512]{3,2,1,0:T(8,128)S(1)}, u32[]{:S(2)}, u32[]{:S(2)}) collective-permute-start(f32[2,2,64,512]{3,2,1,0:T(8,128)} %get-tuple-element.10), channel_id=1, source_target_pairs={{0,16},{16,0},{32,48},{48,32},{64,80},{80,64},{96,112},{112,96},{1... | collective-permute-start | bytes 1572872 | tf_op jit(solution)/shard_map/ppermute | solution.py:372
  52.3 38.5 %collective-permute-start.6 = (f32[2,2,64,512]{3,2,1,0:T(8,128)}, f32[2,2,64,512]{3,2,1,0:T(8,128)}, u32[]{:S(2)}, u32[]{:S(2)}) collective-permute-start(f32[2,2,64,512]{3,2,1,0:T(8,128)} %get-tuple-element.11), channel_id=1, source_target_pairs={{16,32},{48,64},{80,96},{112,128},{144,160},{176,192},{208,224},{3... | collective-permute-start | bytes 1572872 | tf_op jit(solution)/shard_map/ppermute | solution.py:371
  60.5 9.8 %collective-permute-start.15 = (f32[2,10,4,512]{3,2,1,0:T(4,128)S(1)}, f32[2,10,4,512]{3,2,1,0:T(4,128)S(1)}, u32[]{:S(2)}, u32[]{:S(2)}) collective-permute-start(f32[2,10,4,512]{3,2,1,0:T(4,128)S(1)} %pad_maximum_fusion), channel_id=1, source_target_pairs={{0,32},{16,48},{32,64},{48,80},{64,96},{80,112},{96,128},{112,144}... | collective-permute-start | bytes 491528 | tf_op jit(solution)/shard_map/ppermute | solution.py:381
  71.5 0.6 copy-start.2
  72.8 11.2 %copy-start.4 = (s32[512]{0:T(512)S(1)}, s32[512]{0:T(512)}, u32[]{:S(2)}) copy-start(s32[512]{0:T(512)} %param.5) | copy-start | bytes 6148
  72.8 18.1 %all-to-all-start = ((f32[8,8,128]{2,1,0:T(8,128)}), f32[8,8,128]{2,1,0:T(8,128)S(1)}, u32[]{:S(2)}, u32[]{:S(2)}) async-start(f32[8,8,128]{2,1,0:T(8,128)} %broadcast_in_dim.2), calls=%async_computation | async-start | bytes 65536 | tf_op jit(solution)/shard_map/all_to_all | solution.py:390
  90.9 0.9 copy-start.3

commit v2 on v1

--- a/solution.py
+++ b/solution.py
@@ -49,18 +49,19 @@
     return lax.broadcasted_iota(jnp.int32, shape, len(shape) - 1)
 
 
-def fill_viscosity(par, v, own, od, ev, lo, hi, od_c, ev_c):
-    v[...] = jnp.zeros_like(v)
-    v[3:7, LO:HI] = own[...]
+def fill_viscosity(par, v, own, od, ev, lo, hi, od_c, ev_c, sems):
+    copies = [pltpu.make_async_copy(own, v.at[3:7, LO:HI], sems.at[0])]
+    for n, at, first, x in ((1, par * 7, 1 - par, od), (2, 7 - par * 7, par, ev)):
+        copies.append(pltpu.make_async_copy(x.at[pl.ds(first, 3)], v.at[pl.ds(at, 3), LO:HI], sems.at[n]))
+    for copy in copies:
+        copy.start()
     v[3:7, LO - 3 : LO] = lo[:, 0:3]
     v[3:7, HI : HI + 3] = hi[:, 0:3]
-    od_at = par * 7
-    ev_at = 7 - par * 7
-    v[pl.ds(od_at, 3), LO:HI] = od[...]
-    v[pl.ds(ev_at, 3), LO:HI] = ev[...]
-    for at, c in ((od_at, od_c), (ev_at, ev_c)):
-        v[pl.ds(at, 3), LO - 3 : LO] = c[:, 0:3]
-        v[pl.ds(at, 3), HI : HI + 3] = c[:, 7:10]
+    for at, first, c in ((par * 7, 1 - par, od_c), (7 - par * 7, par, ev_c)):
+        v[pl.ds(at, 3), LO - 3 : LO] = c[pl.ds(first, 3), 0:3]
+        v[pl.ds(at, 3), HI : HI + 3] = c[pl.ds(first, 3), 7:10]
+    for copy in copies:
+        copy.wait()
 
 
 def fill_inverse(v, d, fz):
@@ -79,8 +80,20 @@
     lax.fori_loop(0, 8, layer, 0)
 
 
-def stencil_kernel(par_ref, own, od, ev, lo, hi, od_c, ev_c, f, out, v, d, fz, h0, ex, ez, ezm, acc):
-    fill_viscosity(par_ref[0], v, own, od, ev, lo, hi, od_c, ev_c)
+def stencil_kernel(
+    par_ref, own, od, ev, lo, hi, od_c, ev_c, f_hbm, out, to_od, to_ev, *rest
+):
+    kept_hbm, (v, d, fz, h0, ex, ez, ezm, acc, f, sems) = rest[:6], rest[6:]
+    par = par_ref[0]
+    moves = [
+        pltpu.make_async_copy(f_hbm, f, sems.at[3]),
+        pltpu.make_async_copy(f_hbm.at[:, pl.ds(2 * par, 2)], to_od, sems.at[4]),
+        pltpu.make_async_copy(f_hbm.at[:, pl.ds(2 - 2 * par, 2)], to_ev, sems.at[5]),
+    ]
+    moves[0].start()
+    fill_viscosity(par, v, own, od, ev, lo, hi, od_c, ev_c, sems)
+    moves[1].start()
+    moves[2].start()
     fill_inverse(v, d, fz)
 
     def edges(r, _):
@@ -96,6 +109,10 @@
 
     lax.fori_loop(0, 7, edges, 0)
 
+    saves = [pltpu.make_async_copy(x, y, sems.at[6 + n]) for n, (x, y) in enumerate(zip((v, d, fz, h0, ex, ez), kept_hbm))]
+    for copy in saves:
+        copy.start()
+    moves[0].wait()
     acc[...] = jnp.zeros_like(acc)
     own_rows = slice(LO, HI)
     above = slice(LO + 1, HI + 1)
@@ -160,6 +177,8 @@
     out[7:9] = e[0:8].reshape(2, 4, NZ)
     out[9, 0:1] = e[8:9]
     out[9, 1:4] = jnp.zeros((3, NZ), jnp.float32)
+    for copy in moves[1:] + saves:
+        copy.wait()
 
 
 def krylov_kernel(par_ref, mine, mate, below_mine, below_mate, above_mine, above_mate, basis, dots, s_ref, g_ref):
@@ -229,47 +248,34 @@
         part = x[8:16]
         part = part[:, 0:128] + part[:, 128:256] + part[:, 256:384] + part[:, 384:512]
         rows.append(jnp.sum(part, axis=0, keepdims=True))
-    dots[...] = jnp.concatenate(rows + [jnp.zeros((4, 128), jnp.float32)], 0)
-
-
-def velocity_kernel(
-    par_ref, own, od, ev, lo, hi, od_c, ev_c, f, od_f, ev_f, basis, dots, onehot, vel, press, v, d, fz, u, t, b
+    packed = jnp.concatenate(rows + [jnp.zeros((4, 128), jnp.float32)], 0)
+    dots[...] = jnp.broadcast_to(packed[None], dots.shape)
+
+
+def forced_kernel(
+    par_ref, f, od_f, ev_f, lo, hi, od_c, ev_c, v_hbm, d_hbm, fz_hbm, out, v, d, fz, u, t, sems
 ):
     par = par_ref[0]
-    fill_viscosity(par, v, own, od, ev, lo, hi, od_c, ev_c)
-    fill_inverse(v, d, fz)
-
-    sums = jnp.sum(jnp.sum(dots[...], axis=0), axis=1, keepdims=True)
-    gg, gh, hh, hkh = sums[0:1], sums[1:2], sums[2:3], sums[3:4]
-    alpha0 = gg / gh
-    fresh = gg - 2.0 * alpha0 * gh + alpha0 * alpha0 * hh
-    beta = fresh / gg
-    grow = 1.0 + beta
-    alpha1 = fresh / (grow * grow * gh - 2.0 * grow * alpha0 * hh + alpha0 * alpha0 * hkh)
-    on_g = alpha0 + alpha1 * grow
-    on_h = alpha1 * alpha0
-    b[0:16] = on_g * basis[0:16] - on_h * basis[16:32]
-    p = on_g * basis[32:40] - on_h * basis[40:48]
-    press[...] = jnp.dot(
-        p, onehot[...], precision=lax.Precision.HIGHEST, preferred_element_type=jnp.float32
-    )[0:4]
-
-    u[...] = jnp.zeros_like(u)
-    od_at, ev_at = par * 6, 6 - par * 6
+    copies = [pltpu.make_async_copy(x, y, sems.at[n]) for n, (x, y) in enumerate(((d_hbm, d), (v_hbm, v), (fz_hbm, fz)))]
     for c in range(2):
-        u[c, 2:6, LO:HI] = f[c]
+        copies.append(pltpu.make_async_copy(f.at[c], u.at[c, 2:6, LO:HI], sems.at[3 + c]))
+    copies.append(pltpu.make_async_copy(od_f, u.at[:, pl.ds(par * 6, 2), LO:HI], sems.at[5]))
+    copies.append(pltpu.make_async_copy(ev_f, u.at[:, pl.ds(6 - par * 6, 2), LO:HI], sems.at[6]))
+    for copy in copies:
+        copy.start()
+    for c in range(2):
         u[c, 2:6, LO - 2 : LO] = lo[:, 3 + 2 * c : 5 + 2 * c]
         u[c, 2:6, HI : HI + 2] = hi[:, 3 + 2 * c : 5 + 2 * c]
-        u[c, pl.ds(od_at, 2), LO:HI] = od_f[c]
-        u[c, pl.ds(ev_at, 2), LO:HI] = ev_f[c]
-        for at, first, corner in ((od_at, 1 - par, od_c), (ev_at, par, ev_c)):
+        for at, first, corner in ((par * 6, 2 - 2 * par, od_c), (6 - par * 6, 2 * par, ev_c)):
             u[c, pl.ds(at, 2), LO - 2 : LO] = corner[pl.ds(first, 2), 3 + 2 * c : 5 + 2 * c]
             u[c, pl.ds(at, 2), HI : HI + 2] = corner[pl.ds(first, 2), 10 + 2 * c : 12 + 2 * c]
+    for copy in copies:
+        copy.wait()
 
     def scale(r, _):
         dm = d[r]
-        u[0, r] = dm * (u[0, r] - b[pl.ds(r, 1)])
-        u[1, r] = dm * (u[1, r] - b[pl.ds(8 + r, 1)])
+        u[0, r] = dm * u[0, r]
+        u[1, r] = dm * u[1, r]
         return 0
 
     lax.fori_loop(0, 8, scale, 0)
@@ -289,39 +295,96 @@
 
     lax.fori_loop(1, 7, first, 0)
 
+    def second(i, _):
+        couple(i, v, d, fz, t, lambda c, y: store(c, i, y))
+        return 0
+
+    def store(c, i, y):
+        out[c, i] = E0 * u[c, i + 2, LO:HI] + y
+
+    lax.fori_loop(0, ROWS, second, 0)
+
+
+def couple(i, v, d, fz, t, done):
     own_rows = slice(LO, HI)
     above = slice(LO + 1, HI + 1)
     under = slice(LO - 1, HI - 1)
+    r = i + 2
+    vm = v[r + 1, own_rows]
+    fyp = vm + v[r + 1, above]
+    fym = vm + v[r + 1, under]
+    fxp, fxm = vm + v[r + 2, own_rows], vm + v[r, own_rows]
+    fzp, dm = fz[r, own_rows], d[r, own_rows]
+    for c in range(2):
+        x = t[c, r, own_rows]
+        y = fyp * t[c, r, above] + fym * t[c, r, under]
+        y = y + fxp * t[c, r + 1, own_rows] + fxm * t[c, r - 1, own_rows]
+        y = y + fzp * up_z(x) + down_z(fzp * x)
+        done(c, dm * y)
+
+
+def velocity_kernel(basis, dots, onehot, v, d, fz, h0, ex, ez, forced, vel, press, t, b, bz):
+    sums = jnp.sum(jnp.sum(dots[...], axis=0), axis=1, keepdims=True)
+    gg, gh, hh, hkh = sums[0:1], sums[1:2], sums[2:3], sums[3:4]
+    alpha0 = gg / gh
+    fresh = gg - 2.0 * alpha0 * gh + alpha0 * alpha0 * hh
+    beta = fresh / gg
+    grow = 1.0 + beta
+    alpha1 = fresh / (grow * grow * gh - 2.0 * grow * alpha0 * hh + alpha0 * alpha0 * hkh)
+    on_g = alpha0 + alpha1 * grow
+    on_h = alpha1 * alpha0
+    grad = on_g * basis[0:16] - on_h * basis[16:32]
+    b[...] = grad
+    bz[0:16] = up_z(grad)
+    bz[16:32] = down_z(grad)
+    p = on_g * basis[32:40] - on_h * basis[40:48]
+    press[...] = jnp.dot(
+        p, onehot[...], precision=lax.Precision.HIGHEST, preferred_element_type=jnp.float32
+    )[0:4]
+
+    def first(r, _):
+        h, exi, exm, ezi = h0[r], ex[r], ex[r - 1], ez[r]
+        ezm = down_z(ezi)
+        for c in range(2):
+            at = 8 * c + r
+            y = h * b[pl.ds(at, 1)] + exi * b[pl.ds(at + 1, 1)] + exm * b[pl.ds(at - 1, 1)]
+            t[c, r] = y + ezi * bz[pl.ds(at, 1)] + ezm * bz[pl.ds(16 + at, 1)]
+        return 0
+
+    lax.fori_loop(1, 7, first, 0)
 
     def second(i, _):
-        r = i + 2
-        vm = v[r + 1, own_rows]
-        fyp = vm + v[r + 1, above]
-        fym = vm + v[r + 1, under]
-        fxp, fxm = vm + v[r + 2, own_rows], vm + v[r, own_rows]
-        fzp, dm = fz[r, own_rows], d[r, own_rows]
-        for c in range(2):
-            x = t[c, r, own_rows]
-            y = fyp * t[c, r, above] + fym * t[c, r, under]
-            y = y + fxp * t[c, r + 1, own_rows] + fxm * t[c, r - 1, own_rows]
-            y = y + fzp * up_z(x) + down_z(fzp * x)
-            vel[c, i] = E0 * u[c, r, own_rows] + dm * y
-        return 0
+        couple(i, v, d, fz, t, lambda c, y: store(c, i, y))
+        return 0
+
+    def store(c, i, y):
+        own = E0 * (d[i + 2, LO:HI] * b[pl.ds(8 * c + i + 2, 1)])
+        vel[c, i] = forced[c, i] - (own + y)
 
     lax.fori_loop(0, ROWS, second, 0)
 
 
-def call(kernel, out_shape, scratch, args, smem=1):
-    vmem = pl.BlockSpec(memory_space=pltpu.VMEM)
-    specs = [pl.BlockSpec(memory_space=pltpu.SMEM)] * smem + [vmem] * (len(args) - smem)
+VMEM = pl.BlockSpec(memory_space=pltpu.VMEM)
+SMEM = pl.BlockSpec(memory_space=pltpu.SMEM)
+ANY = pl.BlockSpec(memory_space=pl.ANY)
+HBM = pl.BlockSpec(memory_space=pltpu.HBM)
+
+
+def call(kernel, out_shape, scratch, args, in_specs, out_specs=None, micros=1.0, sems=0, mib=16):
     return pl.pallas_call(
         kernel,
         out_shape=out_shape,
-        in_specs=specs,
-        out_specs=jax.tree.map(lambda _: vmem, out_shape),
-        scratch_shapes=[pltpu.VMEM(s, jnp.float32) for s in scratch],
-        compiler_params=pltpu.CompilerParams(vmem_limit_bytes=48 * 1024 * 1024),
+        in_specs=in_specs,
+        out_specs=out_specs or jax.tree.map(lambda _: VMEM, out_shape),
+        scratch_shapes=[pltpu.VMEM(s, jnp.float32) for s in scratch]
+        + ([pltpu.SemaphoreType.DMA((sems,))] if sems else []),
+        compiler_params=pltpu.CompilerParams(vmem_limit_bytes=mib * 1024 * 1024),
+        cost_estimate=pl.CostEstimate(flops=0, transcendentals=0, bytes_accessed=int(micros * 3.6e6)),
     )(*args)
+
+
+def in_hbm(x):
+    return pltpu.with_memory_space_constraint(x, pltpu.HBM)
 
 
 def f32(*shape):
@@ -342,39 +405,53 @@
     chip_up = [(i, (i + 2) % slabs) for i in range(slabs) if i + 2 < slabs]
     chip_down = [(b, a) for a, b in chip_up]
 
-    def sides(x, n):
-        last, initial = x[..., x.shape[-3] - n :, :, :], x[..., :n, :, :]
-        odd = par == 1
-        return jnp.where(odd, last, initial), jnp.where(odd, initial, last)
-
-    to_od, to_ev = sides(viscosity, 3)
-    od = lax.ppermute(to_od, "slab", others)
-    ev = lax.ppermute(to_ev, "slab", mates)
+    od = lax.ppermute(viscosity, "slab", others)
+    ev = lax.ppermute(viscosity, "slab", mates)
     edge_hi = jnp.concatenate([viscosity[:, -3:], forcing[0, :, -2:], forcing[1, :, -2:]], 1)
     edge_lo = jnp.concatenate([viscosity[:, :3], forcing[0, :, :2], forcing[1, :, :2]], 1)
     lo = lax.ppermute(edge_hi, "cross", up)
     hi = lax.ppermute(edge_lo, "cross", down)
-    to_od, to_ev = sides(jnp.concatenate([lo, hi], 1), 3)
-    od_c = lax.ppermute(to_od, "slab", others)
-    ev_c = lax.ppermute(to_ev, "slab", mates)
-
-    grid = (viscosity, od, ev, lo, hi, od_c, ev_c)
-    part = call(
+    edges = jnp.concatenate([lo, hi], 1)
+    od_c = lax.ppermute(edges, "slab", others)
+    ev_c = lax.ppermute(edges, "slab", mates)
+
+    margins = (lo, hi, od_c, ev_c)
+    kept = (f32(10, FRAME, NZ), f32(8, FRAME, NZ), f32(8, FRAME, NZ)) + (f32(7, FRAME, NZ),) * 3
+    part, to_od, to_ev, v, d, fz, h0, ex, ez = call(
         stencil_kernel,
-        f32(10, 4, NZ),
-        [(10, FRAME, NZ)] + [(8, FRAME, NZ)] * 2 + [(7, FRAME, NZ)] * 4 + [(32, 1, NZ)],
-        (where, *grid, forcing),
+        (f32(10, 4, NZ), f32(2, 2, NY, NZ), f32(2, 2, NY, NZ), *[pltpu.HBM(x.shape, x.dtype) for x in kept]),
+        [x.shape for x in kept] + [(7, FRAME, NZ), (32, 1, NZ), (2, ROWS, NY, NZ)],
+        (where, in_hbm(viscosity), od, ev, *margins, in_hbm(forcing)),
+        in_specs=[SMEM, ANY, ANY, ANY] + [VMEM] * 4 + [ANY],
+        out_specs=(VMEM,) + (HBM,) * 8,
+        micros=6,
+        sems=12,
     )
 
-    part, forced = lax.optimization_barrier((part, forcing))
-    to_od, to_ev = sides(forced, 2)
+    width = owner_slot.shape[0] // cross
+    column = lax.axis_index("cross") * width + jnp.arange(width, dtype=jnp.int32)
+    onehot = (owner_slot[:, None] == column[None, :]).astype(jnp.float32)
+
+    def among(x, step):
+        return [lax.ppermute(x, "cross", [(i, i ^ (n * step)) for i in range(cross)]) for n in (1, 2, 3)]
+
+    got = among(part, 1)
     od_f = lax.ppermute(to_od, "slab", others)
     ev_f = lax.ppermute(to_ev, "slab", mates)
-
-    for step in (1, 4):
-        part = sum(
-            (lax.ppermute(part, "cross", [(i, i ^ (n * step)) for i in range(cross)]) for n in (1, 2, 3)), part
-        )
+    got, od_f, ev_f, onehot = lax.optimization_barrier((got, od_f, ev_f, onehot))
+    part = part + got[0] + got[1] + got[2]
+    got = among(part, 4)
+    forced = call(
+        forced_kernel,
+        f32(2, ROWS, NY, NZ),
+        [x.shape for x in kept[:3]] + [(2, 8, FRAME, NZ)] * 2,
+        (where, in_hbm(forcing), od_f, ev_f, *margins, in_hbm(v), in_hbm(d), in_hbm(fz)),
+        in_specs=[SMEM] + [ANY] * 3 + [VMEM] * 4 + [ANY] * 3,
+        micros=5,
+        sems=7,
+    )
+    got, forced = lax.optimization_barrier((got, forced))
+    part = part + got[0] + got[1] + got[2]
 
     mate = lax.ppermute(part, "slab", mates)
     both = jnp.stack([part, mate])
@@ -382,23 +459,22 @@
     above = lax.ppermute(both, "slab", chip_down)
     basis, dots = call(
         krylov_kernel,
-        (f32(48, NZ), f32(8, 128)),
+        (f32(48, NZ), f32(chips, 8, 128)),
         [(7, 24, NZ), (40, NZ)],
         (where, part, mate, below[0], below[1], above[0], above[1]),
+        in_specs=[SMEM] + [VMEM] * 6,
+        mib=4,
     )
     groups = [[2 * z + c for z in range(chips)] for c in range(2)]
-    dots = lax.all_to_all(
-        jnp.broadcast_to(dots[None], (chips, 8, 128)), "slab", 0, 0, tiled=True, axis_index_groups=groups
-    )
-
-    width = owner_slot.shape[0] // cross
-    column = lax.axis_index("cross") * width + jnp.arange(width, dtype=jnp.int32)
-    onehot = (owner_slot[:, None] == column[None, :]).astype(jnp.float32)
+    dots = lax.all_to_all(dots, "slab", 0, 0, tiled=True, axis_index_groups=groups)
+
     return call(
         velocity_kernel,
         (f32(2, ROWS, NY, NZ), f32(ROWS, width)),
-        [(10, FRAME, NZ)] + [(8, FRAME, NZ)] * 2 + [(2, 8, FRAME, NZ)] * 2 + [(16, NZ)],
-        (where, *grid, forcing, od_f, ev_f, basis, dots, onehot),
+        [(2, 8, FRAME, NZ), (16, NZ), (32, NZ)],
+        (basis, dots, onehot, v, d, fz, h0, ex, ez, forced),
+        in_specs=[VMEM] * 10,
+        micros=4,
     )
 
 

time: 100 us -> 93.3 us (0.933)
  the two profiles are of different devices: /device:TPU:1 before, /device:TPU:16 now
where the time goes in v2:
time: 93.3 us; the launch traced here: 92.6 us
  starting transfers between devices  36 us (39%)
  Pallas kernels  20.6 us (22%)
  blocking collectives  20.2 us (22%)
  waiting for transfers between devices  12.6 us (14%)
  local copies, waits for them, and re-layouts  1.9 us (2%)
    pallas_call x4, Pallas kernels, call(): pl.pallas_call(kernel, out_shape=out_shape, in_specs=in_specs, out_specs=...  20.6 us
    all_to_all x1, blocking collectives, shards(): lax.all_to_all(dots, 'slab', 0, 0, tiled=True, axis_index_groups=groups)  20.2 us
    ppermute x6, starting transfers between devices, among(): lax.ppermute(x, 'cross', [(i, i ^ n * step) for i in range(cross)])  9.15 us
    ppermute x1, starting transfers between devices, shards(): ev_f = lax.ppermute(to_ev, 'slab', mates)  8.6 us
    ppermute x6, waiting for transfers between devices, among(): lax.ppermute(x, 'cross', [(i, i ^ n * step) for i in range(cross)])  5.57 us
    ppermute x1, starting transfers between devices, shards(): below = lax.ppermute(both, 'slab', chip_up)  4.56 us
    ppermute x1, starting transfers between devices, shards(): hi = lax.ppermute(edge_lo, 'cross', down)  4.55 us
    ppermute x1, starting transfers between devices, shards(): lo = lax.ppermute(edge_hi, 'cross', up)  3.4 us
  transfers between devices with their start and end apart: 17, of which 8 were waited for; matrix products, arithmetic and copies ran while one was open for 2% of the time, Pallas kernels for 7%

profile of v2, /device:TPU:16, one launch (start us, length us, event | category | flops | bytes accessed | tf_op | source)
XLA Modules:
  0.0 92.6 jit_solution(2831835502608853491)
XLA Ops:
  0.7 0.7 collective-permute-start
  1.4 0.9 fusion
  2.3 1.0 %slice_bitcast_fusion.5 = (f32[4,2,512]{2,1,0:T(2,128)S(1)}, f32[4,2,512]{2,1,0:T(2,128)S(1)}, f32[4,2,512]{2,1,0:T(2,128)S(1)}, f32[4,2,512]{2,1,0:T(2,128)S(1)}) fusion(f32[2,4,64,512]{3,2,1,0:T(8,128)} %f.1), kind=kLoop, calls=%fused_computation.12 | loop fusion | bytes 131072 | tf_op jit(solution)/shard_map/squeeze | solution.py:411
  3.3 3.4 %collective-permute-start.2 = (f32[4,7,512]{2,1,0:T(8,128)S(1)}, f32[4,7,512]{2,1,0:T(8,128)S(1)}, u32[]{:S(2)}, u32[]{:S(2)}) collective-permute-start(f32[4,7,512]{2,1,0:T(8,128)S(1)} %pad_maximum_fusion.2), channel_id=1, source_target_pairs={{0,1},{1,2},{2,3},{3,4},{4,5},{5,6},{6,7},{7,8},{8,9},{9,10},{10,1... | collective-permute-start | bytes 172040 | tf_op jit(solution)/shard_map/ppermute | solution.py:412
  6.8 4.6 %collective-permute-start.3 = (f32[4,7,512]{2,1,0:T(8,128)S(1)}, f32[4,7,512]{2,1,0:T(8,128)S(1)}, u32[]{:S(2)}, u32[]{:S(2)}) collective-permute-start(f32[4,7,512]{2,1,0:T(8,128)S(1)} %pad_maximum_fusion.3), channel_id=1, source_target_pairs={{1,0},{2,1},{3,2},{4,3},{5,4},{6,5},{7,6},{8,7},{9,8},{10,9},{11,1... | collective-permute-start | bytes 172040 | tf_op jit(solution)/shard_map/ppermute | solution.py:413
  11.6 1.6 %collective-permute-done.3.hi = f32[4,7,512]{2,1,0:T(8,128)S(1)} collective-permute-done((f32[4,7,512]{2,1,0:T(8,128)S(1)}, f32[4,7,512]{2,1,0:T(8,128)S(1)}, u32[]{:S(2)}, u32[]{:S(2)}) %collective-permute-start.3) | collective-permute-done | bytes 57376 | tf_op jit(solution)/shard_map/ppermute | solution.py:413
  13.2 2.2 %collective-permute-start.5 = (f32[4,14,512]{2,1,0:T(8,128)S(1)}, f32[4,14,512]{2,1,0:T(8,128)S(1)}, u32[]{:S(2)}, u32[]{:S(2)}) collective-permute-start(f32[4,14,512]{2,1,0:T(8,128)S(1)} %pad_maximum_fusion.1), channel_id=1, source_target_pairs={{0,16},{16,0},{32,48},{48,32},{64,80},{80,64},{96,112},{112,96},{1... | collective-permute-start | bytes 344072 | tf_op jit(solution)/shard_map/ppermute | solution.py:416
  16.5 9.3 %shard_map.50 = (f32[10,4,512]{2,1,0:T(4,128)S(1)}, f32[2,2,64,512]{3,2,1,0:T(8,128)S(1)}, f32[2,2,64,512]{3,2,1,0:T(8,128)S(1)}, f32[10,80,512]{2,1,0:T(8,128)}...) custom-call(s32[2]{0:T(128)S(1)} %pad_add_fusion.par_ref, ...), custom_call_target="tpu_custom_call" | custom-call | bytes 21600000 | tf_op jit(solution)/shard_map/pallas_call | solution.py:374
  26.4 8.6 %collective-permute-start.10 = (f32[2,2,64,512]{3,2,1,0:T(8,128)S(1)}, f32[2,2,64,512]{3,2,1,0:T(8,128)S(1)}, u32[]{:S(2)}, u32[]{:S(2)}) collective-permute-start(f32[2,2,64,512]{3,2,1,0:T(8,128)S(1)} %get-tuple-element.25), channel_id=1, source_target_pairs={{0,16},{16,0},{32,48},{48,32},{64,80},{80,64},{96,112},{112,96},{1... | collective-permute-start | bytes 1572872 | tf_op jit(solution)/shard_map/ppermute | solution.py:440
  35.0 4.1 %collective-permute-start.8 = (f32[10,4,512]{2,1,0:T(4,128)S(1)}, f32[10,4,512]{2,1,0:T(4,128)S(1)}, u32[]{:S(2)}, u32[]{:S(2)}) collective-permute-start(f32[10,4,512]{2,1,0:T(4,128)S(1)} %get-tuple-element.23), channel_id=1, source_target_pairs={{0,3},{1,2},{2,1},{3,0},{4,7},{5,6},{6,5},{7,4},{8,11},{9,10},{10,... | collective-permute-start | bytes 245768 | tf_op jit(solution)/shard_map/ppermute | solution.py:436
  39.1 0.9 collective-permute-start.6
  40.1 2.8 %collective-permute-done.8 = f32[10,4,512]{2,1,0:T(4,128)S(1)} collective-permute-done((f32[10,4,512]{2,1,0:T(4,128)S(1)}, f32[10,4,512]{2,1,0:T(4,128)S(1)}, u32[]{:S(2)}, u32[]{:S(2)}) %collective-permute-start.8) | collective-permute-done | bytes 81952 | tf_op jit(solution)/shard_map/ppermute | solution.py:436
  42.9 2.8 %collective-permute-done.7 = f32[10,4,512]{2,1,0:T(4,128)S(1)} collective-permute-done((f32[10,4,512]{2,1,0:T(4,128)S(1)}, f32[10,4,512]{2,1,0:T(4,128)S(1)}, u32[]{:S(2)}, u32[]{:S(2)}) %collective-permute-start.7) | collective-permute-done | bytes 81952 | tf_op jit(solution)/shard_map/ppermute | solution.py:436
  45.7 0.8 collective-permute-start.13
  46.6 3.3 %collective-permute-start.11 = (f32[10,4,512]{2,1,0:T(4,128)S(1)}, f32[10,4,512]{2,1,0:T(4,128)S(1)}, u32[]{:S(2)}, u32[]{:S(2)}) collective-permute-start(f32[10,4,512]{2,1,0:T(4,128)S(1)} %bitcast.37), channel_id=1, source_target_pairs={{0,4},{1,5},{2,6},{3,7},{4,0},{5,1},{6,2},{7,3},{8,12},{9,13},{10,... | collective-permute-start | bytes 245768 | tf_op jit(solution)/shard_map/ppermute | solution.py:436
  50.0 6.8 %shard_map.51.forced = f32[2,4,64,512]{3,2,1,0:T(8,128)S(1)} custom-call(s32[2]{0:T(128)S(1)} %pad_add_fusion.par_ref, f32[2,4,64,512]{3,2,1,0:T(8,128)} %f.1, f32[2,2,64,512]{3,2,1,0:T(8,128)S(1)} %collective-permute-done.9.od_f, f32[2,2,64,512]{3,2,1,0:T(8,128)S(1)} %collective-permute-done.10.ev_f, f32[4,7,512]{2,1,0:T(8,128)S(1)} %collective-permute-done.2.lo, ...), custom_call_target="tpu_custom_call" | custom-call | bytes 18000000 | tf_op jit(solution)/shard_map/pallas_call | solution.py:374
  56.9 1.3 %collective-permute-done.14.mate = f32[10,4,512]{2,1,0:T(4,128)S(1)} collective-permute-done((f32[10,4,512]{2,1,0:T(4,128)S(1)}, f32[10,4,512]{2,1,0:T(4,128)S(1)}, u32[]{:S(2)}, u32[]{:S(2)}) %collective-permute-start.14) | collective-permute-done | bytes 81952 | tf_op jit(solution)/shard_map/ppermute | solution.py:456
  58.2 1.3 %collective-permute-start.16 = (f32[2,10,4,512]{3,2,1,0:T(4,128)S(1)}, f32[2,10,4,512]{3,2,1,0:T(4,128)S(1)}, u32[]{:S(2)}, u32[]{:S(2)}) collective-permute-start(f32[2,10,4,512]{3,2,1,0:T(4,128)S(1)} %pad_maximum_fusion), channel_id=1, source_target_pairs={{32,0},{48,16},{64,32},{80,48},{96,64},{112,80},{128,96},{144,112}... | collective-permute-start | bytes 491528 | tf_op jit(solution)/shard_map/ppermute | solution.py:459
  59.5 4.6 %collective-permute-start.15 = (f32[2,10,4,512]{3,2,1,0:T(4,128)S(1)}, f32[2,10,4,512]{3,2,1,0:T(4,128)S(1)}, u32[]{:S(2)}, u32[]{:S(2)}) collective-permute-start(f32[2,10,4,512]{3,2,1,0:T(4,128)S(1)} %pad_maximum_fusion), channel_id=1, source_target_pairs={{0,32},{16,48},{32,64},{48,80},{64,96},{80,112},{96,128},{112,144}... | collective-permute-start | bytes 491528 | tf_op jit(solution)/shard_map/ppermute | solution.py:458
  64.1 2.5 %collective-permute-done.16 = f32[2,10,4,512]{3,2,1,0:T(4,128)S(1)} collective-permute-done((f32[2,10,4,512]{3,2,1,0:T(4,128)S(1)}, f32[2,10,4,512]{3,2,1,0:T(4,128)S(1)}, u32[]{:S(2)}, u32[]{:S(2)}) %collective-permute-start.16) | collective-permute-done | bytes 163872 | tf_op jit(solution)/shard_map/ppermute | solution.py:459
  66.6 1.2 %collective-permute-done.15 = f32[2,10,4,512]{3,2,1,0:T(4,128)S(1)} collective-permute-done((f32[2,10,4,512]{3,2,1,0:T(4,128)S(1)}, f32[2,10,4,512]{3,2,1,0:T(4,128)S(1)}, u32[]{:S(2)}, u32[]{:S(2)}) %collective-permute-start.15) | collective-permute-done | bytes 163872 | tf_op jit(solution)/shard_map/ppermute | solution.py:458
  67.8 1.2 %shard_map.52 = (f32[48,512]{1,0:T(8,128)S(1)}, f32[8,8,128]{2,1,0:T(8,128)S(1)}) custom-call(s32[2]{0:T(128)S(1)} %pad_add_fusion.par_ref, f32[10,4,512]{2,1,0:T(4,128)S(1)} %bitcast.32, f32[10,4,512]{2,1,0:T(4,128)S(1)} %collective-permute-done.14.mate, f32[10,4,512]{2,1,0:T(4,128)S(1)} %get-tuple-element.53.below_mine, ...), custom_call_target="tpu_custom_call" | custom-call | bytes 3600000 | tf_op jit(solution)/shard_map/pallas_call | solution.py:374
  69.0 20.2 %all_to_all.5.dots = f32[8,8,128]{2,1,0:T(8,128)S(1)} all-to-all(f32[8,8,128]{2,1,0:T(8,128)S(1)} %get-tuple-element.38), channel_id=1, replica_groups={{0,32,64,96,128,160,192,224},{16,48,80,112,144,176,208,240},{1,33,65,97..., dimensions={0} | all-to-all | bytes 65536 | tf_op jit(solution)/shard_map/all_to_all | solution.py:469
  89.2 3.4 %shard_map.53 = (f32[2,4,64,512]{3,2,1,0:T(8,128)}, f32[4,32]{1,0:T(4,128)}) custom-call(f32[48,512]{1,0:T(8,128)S(1)} %get-tuple-element.37.basis, f32[8,8,128]{2,1,0:T(8,128)S(1)} %all_to_all.5.dots, f32[512,32]{1,0:T(8,128)S(1)} %compare_convert_fusion.onehot, f32[10,80,512]{2,1,0:T(8,128)S(1)} %copy-done, f32[8,80,512]{2,1,0:T(8,128)S(1)} %copy-done.1, ...), custom_call_target="tpu_custom_call" | custom-call | bytes 14400000 | tf_op jit(solution)/shard_map/pallas_call | solution.py:374
  (42 shorter events, 2.5 us)
Async XLA Ops:
  0.6 15.8 %collective-permute-start.1 = (f32[4,64,512]{2,1,0:T(8,128)}, f32[4,64,512]{2,1,0:T(8,128)S(1)}, u32[]{:S(2)}, u32[]{:S(2)}) collective-permute-start(f32[4,64,512]{2,1,0:T(8,128)} %own.1), channel_id=1, source_target_pairs={{0,16},{16,0},{32,48},{48,32},{64,80},{80,64},{96,112},{112,96},{1... | collective-permute-start | bytes 1572872 | tf_op jit(solution)/shard_map/ppermute | solution.py:409
  0.7 15.7 %collective-permute-start = (f32[4,64,512]{2,1,0:T(8,128)}, f32[4,64,512]{2,1,0:T(8,128)S(1)}, u32[]{:S(2)}, u32[]{:S(2)}) collective-permute-start(f32[4,64,512]{2,1,0:T(8,128)} %own.1), channel_id=1, source_target_pairs={{16,32},{48,64},{80,96},{112,128},{144,160},{176,192},{208,224},{3... | collective-permute-start | bytes 1572872 | tf_op jit(solution)/shard_map/ppermute | solution.py:408
  3.3 8.3 %collective-permute-start.2 = (f32[4,7,512]{2,1,0:T(8,128)S(1)}, f32[4,7,512]{2,1,0:T(8,128)S(1)}, u32[]{:S(2)}, u32[]{:S(2)}) collective-permute-start(f32[4,7,512]{2,1,0:T(8,128)S(1)} %pad_maximum_fusion.2), channel_id=1, source_target_pairs={{0,1},{1,2},{2,3},{3,4},{4,5},{5,6},{6,7},{7,8},{8,9},{9,10},{10,1... | collective-permute-start | bytes 172040 | tf_op jit(solution)/shard_map/ppermute | solution.py:412
  6.8 6.4 %collective-permute-start.3 = (f32[4,7,512]{2,1,0:T(8,128)S(1)}, f32[4,7,512]{2,1,0:T(8,128)S(1)}, u32[]{:S(2)}, u32[]{:S(2)}) collective-permute-start(f32[4,7,512]{2,1,0:T(8,128)S(1)} %pad_maximum_fusion.3), channel_id=1, source_target_pairs={{1,0},{2,1},{3,2},{4,3},{5,4},{6,5},{7,6},{8,7},{9,8},{10,9},{11,1... | collective-permute-start | bytes 172040 | tf_op jit(solution)/shard_map/ppermute | solution.py:413
  13.2 3.2 %collective-permute-start.5 = (f32[4,14,512]{2,1,0:T(8,128)S(1)}, f32[4,14,512]{2,1,0:T(8,128)S(1)}, u32[]{:S(2)}, u32[]{:S(2)}) collective-permute-start(f32[4,14,512]{2,1,0:T(8,128)S(1)} %pad_maximum_fusion.1), channel_id=1, source_target_pairs={{0,16},{16,0},{32,48},{48,32},{64,80},{80,64},{96,112},{112,96},{1... | collective-permute-start | bytes 344072 | tf_op jit(solution)/shard_map/ppermute | solution.py:416
  15.5 1.0 %collective-permute-start.4 = (f32[4,14,512]{2,1,0:T(8,128)S(1)}, f32[4,14,512]{2,1,0:T(8,128)S(1)}, u32[]{:S(2)}, u32[]{:S(2)}) collective-permute-start(f32[4,14,512]{2,1,0:T(8,128)S(1)} %pad_maximum_fusion.1), channel_id=1, source_target_pairs={{16,32},{48,64},{80,96},{112,128},{144,160},{176,192},{208,224},{3... | collective-permute-start | bytes 344072 | tf_op jit(solution)/shard_map/ppermute | solution.py:415
  16.2 23.8 %copy-start.6 = (s32[512]{0:T(512)S(1)}, s32[512]{0:T(512)}, u32[]{:S(2)}) copy-start(s32[512]{0:T(512)} %param.5) | copy-start | bytes 6148
  25.7 20.0 %collective-permute-start.9 = (f32[2,2,64,512]{3,2,1,0:T(8,128)S(1)}, f32[2,2,64,512]{3,2,1,0:T(8,128)S(1)}, u32[]{:S(2)}, u32[]{:S(2)}) collective-permute-start(f32[2,2,64,512]{3,2,1,0:T(8,128)S(1)} %get-tuple-element.24), channel_id=1, source_target_pairs={{16,32},{48,64},{80,96},{112,128},{144,160},{176,192},{208,224},{3... | collective-permute-start | bytes 1572872 | tf_op jit(solution)/shard_map/ppermute | solution.py:439
  26.4 19.3 %collective-permute-start.10 = (f32[2,2,64,512]{3,2,1,0:T(8,128)S(1)}, f32[2,2,64,512]{3,2,1,0:T(8,128)S(1)}, u32[]{:S(2)}, u32[]{:S(2)}) collective-permute-start(f32[2,2,64,512]{3,2,1,0:T(8,128)S(1)} %get-tuple-element.25), channel_id=1, source_target_pairs={{0,16},{16,0},{32,48},{48,32},{64,80},{80,64},{96,112},{112,96},{1... | collective-permute-start | bytes 1572872 | tf_op jit(solution)/shard_map/ppermute | solution.py:440
  35.0 7.9 %collective-permute-start.8 = (f32[10,4,512]{2,1,0:T(4,128)S(1)}, f32[10,4,512]{2,1,0:T(4,128)S(1)}, u32[]{:S(2)}, u32[]{:S(2)}) collective-permute-start(f32[10,4,512]{2,1,0:T(4,128)S(1)} %get-tuple-element.23), channel_id=1, source_target_pairs={{0,3},{1,2},{2,1},{3,0},{4,7},{5,6},{6,5},{7,4},{8,11},{9,10},{10,... | collective-permute-start | bytes 245768 | tf_op jit(solution)/shard_map/ppermute | solution.py:436
  39.1 6.6 %collective-permute-start.7 = (f32[10,4,512]{2,1,0:T(4,128)S(1)}, f32[10,4,512]{2,1,0:T(4,128)S(1)}, u32[]{:S(2)}, u32[]{:S(2)}) collective-permute-start(f32[10,4,512]{2,1,0:T(4,128)S(1)} %get-tuple-element.23), channel_id=1, source_target_pairs={{0,2},{1,3},{2,0},{3,1},{4,6},{5,7},{6,4},{7,5},{8,10},{9,11},{10,... | collective-permute-start | bytes 245768 | tf_op jit(solution)/shard_map/ppermute | solution.py:436
  39.1 6.6 %collective-permute-start.6 = (f32[10,4,512]{2,1,0:T(4,128)S(1)}, f32[10,4,512]{2,1,0:T(4,128)S(1)}, u32[]{:S(2)}, u32[]{:S(2)}) collective-permute-start(f32[10,4,512]{2,1,0:T(4,128)S(1)} %get-tuple-element.23), channel_id=1, source_target_pairs={{0,1},{1,0},{2,3},{3,2},{4,5},{5,4},{6,7},{7,6},{8,9},{9,8},{10,11... | collective-permute-start | bytes 245768 | tf_op jit(solution)/shard_map/ppermute | solution.py:436
  45.7 11.0 %collective-permute-start.13 = (f32[10,4,512]{2,1,0:T(4,128)S(1)}, f32[10,4,512]{2,1,0:T(4,128)S(1)}, u32[]{:S(2)}, u32[]{:S(2)}) collective-permute-start(f32[10,4,512]{2,1,0:T(4,128)S(1)} %bitcast.35), channel_id=1, source_target_pairs={{0,12},{1,13},{2,14},{3,15},{4,8},{5,9},{6,10},{7,11},{8,4},{9,5},... | collective-permute-start | bytes 245768 | tf_op jit(solution)/shard_map/ppermute | solution.py:436
  46.6 10.2 %collective-permute-start.12 = (f32[10,4,512]{2,1,0:T(4,128)S(1)}, f32[10,4,512]{2,1,0:T(4,128)S(1)}, u32[]{:S(2)}, u32[]{:S(2)}) collective-permute-start(f32[10,4,512]{2,1,0:T(4,128)S(1)} %bitcast.36), channel_id=1, source_target_pairs={{0,8},{1,9},{2,10},{3,11},{4,12},{5,13},{6,14},{7,15},{8,0},{9,1},... | collective-permute-start | bytes 245768 | tf_op jit(solution)/shard_map/ppermute | solution.py:436
  46.6 10.2 %collective-permute-start.11 = (f32[10,4,512]{2,1,0:T(4,128)S(1)}, f32[10,4,512]{2,1,0:T(4,128)S(1)}, u32[]{:S(2)}, u32[]{:S(2)}) collective-permute-start(f32[10,4,512]{2,1,0:T(4,128)S(1)} %bitcast.37), channel_id=1, source_target_pairs={{0,4},{1,5},{2,6},{3,7},{4,0},{5,1},{6,2},{7,3},{8,12},{9,13},{10,... | collective-permute-start | bytes 245768 | tf_op jit(solution)/shard_map/ppermute | solution.py:436
  49.9 39.2 %copy-start.1 = (f32[8,80,512]{2,1,0:T(8,128)S(1)}, f32[8,80,512]{2,1,0:T(8,128)}, u32[]{:S(2)}) copy-start(f32[8,80,512]{2,1,0:T(8,128)} %get-tuple-element.32.d_hbm.d) | copy-start | bytes 3932164
  49.9 39.2 %copy-start.2 = (f32[8,80,512]{2,1,0:T(8,128)S(1)}, f32[8,80,512]{2,1,0:T(8,128)}, u32[]{:S(2)}) copy-start(f32[8,80,512]{2,1,0:T(8,128)} %get-tuple-element.33.fz_hbm.fz) | copy-start | bytes 3932164
  49.9 39.2 %copy-start.3 = (f32[7,80,512]{2,1,0:T(8,128)S(1)}, f32[7,80,512]{2,1,0:T(8,128)}, u32[]{:S(2)}) copy-start(f32[7,80,512]{2,1,0:T(8,128)} %get-tuple-element.40.h0) | copy-start | bytes 3440644
  49.9 39.2 %copy-start.4 = (f32[7,80,512]{2,1,0:T(8,128)S(1)}, f32[7,80,512]{2,1,0:T(8,128)}, u32[]{:S(2)}) copy-start(f32[7,80,512]{2,1,0:T(8,128)} %get-tuple-element.41.ex) | copy-start | bytes 3440644
  49.9 39.2 %copy-start.5 = (f32[7,80,512]{2,1,0:T(8,128)S(1)}, f32[7,80,512]{2,1,0:T(8,128)}, u32[]{:S(2)}) copy-start(f32[7,80,512]{2,1,0:T(8,128)} %get-tuple-element.42.ez) | copy-start | bytes 3440644
  56.8 32.4 %copy-start = (f32[10,80,512]{2,1,0:T(8,128)S(1)}, f32[10,80,512]{2,1,0:T(8,128)}, u32[]{:S(2)}) copy-start(f32[10,80,512]{2,1,0:T(8,128)} %get-tuple-element.31.v_hbm.v) | copy-start | bytes 4915204
  56.8 1.4 %collective-permute-start.14 = (f32[10,4,512]{2,1,0:T(4,128)S(1)}, f32[10,4,512]{2,1,0:T(4,128)S(1)}, u32[]{:S(2)}, u32[]{:S(2)}) collective-permute-start(f32[10,4,512]{2,1,0:T(4,128)S(1)} %bitcast.30), channel_id=1, source_target_pairs={{0,16},{16,0},{32,48},{48,32},{64,80},{80,64},{96,112},{112,96},{1... | collective-permute-start | bytes 245768 | tf_op jit(solution)/shard_map/ppermute | solution.py:456
  58.2 8.3 %collective-permute-start.16 = (f32[2,10,4,512]{3,2,1,0:T(4,128)S(1)}, f32[2,10,4,512]{3,2,1,0:T(4,128)S(1)}, u32[]{:S(2)}, u32[]{:S(2)}) collective-permute-start(f32[2,10,4,512]{3,2,1,0:T(4,128)S(1)} %pad_maximum_fusion), channel_id=1, source_target_pairs={{32,0},{48,16},{64,32},{80,48},{96,64},{112,80},{128,96},{144,112}... | collective-permute-start | bytes 491528 | tf_op jit(solution)/shard_map/ppermute | solution.py:459
  59.5 8.2 %collective-permute-start.15 = (f32[2,10,4,512]{3,2,1,0:T(4,128)S(1)}, f32[2,10,4,512]{3,2,1,0:T(4,128)S(1)}, u32[]{:S(2)}, u32[]{:S(2)}) collective-permute-start(f32[2,10,4,512]{3,2,1,0:T(4,128)S(1)} %pad_maximum_fusion), channel_id=1, source_target_pairs={{0,32},{16,48},{32,64},{48,80},{64,96},{80,112},{96,128},{112,144}... | collective-permute-start | bytes 491528 | tf_op jit(solution)/shard_map/ppermute | solution.py:458

commit v3 on v2

--- a/solution.py
+++ b/solution.py
@@ -49,17 +49,56 @@
     return lax.broadcasted_iota(jnp.int32, shape, len(shape) - 1)
 
 
-def fill_viscosity(par, v, own, od, ev, lo, hi, od_c, ev_c, sems):
+def edge_kernel(par_ref, own, f, out, low_v, high_v, low_f, high_f, sems):
+    copies = [
+        pltpu.make_async_copy(own.at[:, 0:8], low_v, sems.at[0]),
+        pltpu.make_async_copy(own.at[:, NY - 8 : NY], high_v, sems.at[1]),
+        pltpu.make_async_copy(f.at[:, :, 0:8], low_f, sems.at[2]),
+        pltpu.make_async_copy(f.at[:, :, NY - 8 : NY], high_f, sems.at[3]),
+    ]
+    for copy in copies:
+        copy.start()
+    for copy in copies:
+        copy.wait()
+    out[:, 0:3] = low_v[:, 0:3]
+    out[:, 7:10] = high_v[:, 5:8]
+    for c in range(2):
+        out[:, 3 + 2 * c : 5 + 2 * c] = low_f[c, :, 0:2]
+        out[:, 10 + 2 * c : 12 + 2 * c] = high_f[c, :, 6:8]
+
+
+def corner_kernel(par_ref, own, od, ev, low, high):
+    odd = par_ref[0] == 1
+    below = lax.select(odd, ev[2:4], od[2:4])
+    above = lax.select(odd, od[0:2], ev[0:2])
+    for out, near, forced, base in ((low, (0, 2), 0, 0), (high, (1, 3), 1, 7)):
+        for n in range(4):
+            out[7 * n : 7 * n + 7] = own[n, base : base + 7]
+        for at, x, far, far_at in ((28, below[1], below[0], 36), (32, above[0], above[1], 37)):
+            out[at : at + 2] = x[base + near[0] : base + near[1]]
+            for c in range(2):
+                row = base + 3 + 2 * c + forced
+                out[at + 2 + c : at + 3 + c] = x[row : row + 1]
+            row = base + 2 * forced
+            out[far_at : far_at + 1] = far[row : row + 1]
+        out[38:40] = jnp.zeros((2, NZ), jnp.float32)
+
+
+def fill_viscosity(par, v, own, od, ev, lo, hi, sems):
     copies = [pltpu.make_async_copy(own, v.at[3:7, LO:HI], sems.at[0])]
     for n, at, first, x in ((1, par * 7, 1 - par, od), (2, 7 - par * 7, par, ev)):
         copies.append(pltpu.make_async_copy(x.at[pl.ds(first, 3)], v.at[pl.ds(at, 3), LO:HI], sems.at[n]))
     for copy in copies:
         copy.start()
-    v[3:7, LO - 3 : LO] = lo[:, 0:3]
-    v[3:7, HI : HI + 3] = hi[:, 0:3]
-    for at, first, c in ((par * 7, 1 - par, od_c), (7 - par * 7, par, ev_c)):
-        v[pl.ds(at, 3), LO - 3 : LO] = c[pl.ds(first, 3), 0:3]
-        v[pl.ds(at, 3), HI : HI + 3] = c[pl.ds(first, 3), 7:10]
+    for n in range(4):
+        v[3 + n, LO - 3 : LO] = lo[7 * n : 7 * n + 3]
+        v[3 + n, HI : HI + 3] = hi[7 * n : 7 * n + 3]
+    for r, at in ((2, 28), (7, 32)):
+        v[r, LO - 2 : LO] = lo[at : at + 2]
+        v[r, HI : HI + 2] = hi[at : at + 2]
+    for r, at in ((1, 36), (8, 37)):
+        v[r, LO - 1 : LO] = lo[at : at + 1]
+        v[r, HI : HI + 1] = hi[at : at + 1]
     for copy in copies:
         copy.wait()
 
@@ -80,20 +119,18 @@
     lax.fori_loop(0, 8, layer, 0)
 
 
-def stencil_kernel(
-    par_ref, own, od, ev, lo, hi, od_c, ev_c, f_hbm, out, to_od, to_ev, *rest
-):
+def stencil_kernel(par_ref, own, od, ev, lo, hi, f_hbm, out, to_od, to_ev, *rest):
     kept_hbm, (v, d, fz, h0, ex, ez, ezm, acc, f, sems) = rest[:6], rest[6:]
     par = par_ref[0]
+    load = pltpu.make_async_copy(f_hbm, f, sems.at[3])
+    load.start()
+    fill_viscosity(par, v, own, od, ev, lo, hi, sems)
     moves = [
-        pltpu.make_async_copy(f_hbm, f, sems.at[3]),
-        pltpu.make_async_copy(f_hbm.at[:, pl.ds(2 * par, 2)], to_od, sems.at[4]),
-        pltpu.make_async_copy(f_hbm.at[:, pl.ds(2 - 2 * par, 2)], to_ev, sems.at[5]),
+        pltpu.make_async_copy(f_hbm.at[:, pl.ds(2 * par, 2)], to_od, sems.at[10]),
+        pltpu.make_async_copy(f_hbm.at[:, pl.ds(2 - 2 * par, 2)], to_ev, sems.at[11]),
     ]
-    moves[0].start()
-    fill_viscosity(par, v, own, od, ev, lo, hi, od_c, ev_c, sems)
-    moves[1].start()
-    moves[2].start()
+    for copy in moves:
+        copy.start()
     fill_inverse(v, d, fz)
 
     def edges(r, _):
@@ -109,10 +146,10 @@
 
     lax.fori_loop(0, 7, edges, 0)
 
-    saves = [pltpu.make_async_copy(x, y, sems.at[6 + n]) for n, (x, y) in enumerate(zip((v, d, fz, h0, ex, ez), kept_hbm))]
+    saves = [pltpu.make_async_copy(x, y, sems.at[4 + n]) for n, (x, y) in enumerate(zip((v, d, fz, h0, ex, ez), kept_hbm))]
     for copy in saves:
         copy.start()
-    moves[0].wait()
+    load.wait()
     acc[...] = jnp.zeros_like(acc)
     own_rows = slice(LO, HI)
     above = slice(LO + 1, HI + 1)
@@ -177,7 +214,7 @@
     out[7:9] = e[0:8].reshape(2, 4, NZ)
     out[9, 0:1] = e[8:9]
     out[9, 1:4] = jnp.zeros((3, NZ), jnp.float32)
-    for copy in moves[1:] + saves:
+    for copy in moves + saves:
         copy.wait()
 
 
@@ -252,23 +289,22 @@
     dots[...] = jnp.broadcast_to(packed[None], dots.shape)
 
 
-def forced_kernel(
-    par_ref, f, od_f, ev_f, lo, hi, od_c, ev_c, v_hbm, d_hbm, fz_hbm, out, v, d, fz, u, t, sems
-):
+def forced_kernel(par_ref, f, od_f, ev_f, lo, hi, v_hbm, d_hbm, fz_hbm, out_hbm, v, d, fz, u, t, out, sems):
     par = par_ref[0]
     copies = [pltpu.make_async_copy(x, y, sems.at[n]) for n, (x, y) in enumerate(((d_hbm, d), (v_hbm, v), (fz_hbm, fz)))]
     for c in range(2):
         copies.append(pltpu.make_async_copy(f.at[c], u.at[c, 2:6, LO:HI], sems.at[3 + c]))
-    copies.append(pltpu.make_async_copy(od_f, u.at[:, pl.ds(par * 6, 2), LO:HI], sems.at[5]))
-    copies.append(pltpu.make_async_copy(ev_f, u.at[:, pl.ds(6 - par * 6, 2), LO:HI], sems.at[6]))
+    for n, at, x in ((5, par * 6, od_f), (6, 6 - par * 6, ev_f)):
+        copies.append(pltpu.make_async_copy(x, u.at[:, pl.ds(at, 2), LO:HI], sems.at[n]))
     for copy in copies:
         copy.start()
     for c in range(2):
-        u[c, 2:6, LO - 2 : LO] = lo[:, 3 + 2 * c : 5 + 2 * c]
-        u[c, 2:6, HI : HI + 2] = hi[:, 3 + 2 * c : 5 + 2 * c]
-        for at, first, corner in ((par * 6, 2 - 2 * par, od_c), (6 - par * 6, 2 * par, ev_c)):
-            u[c, pl.ds(at, 2), LO - 2 : LO] = corner[pl.ds(first, 2), 3 + 2 * c : 5 + 2 * c]
-            u[c, pl.ds(at, 2), HI : HI + 2] = corner[pl.ds(first, 2), 10 + 2 * c : 12 + 2 * c]
+        for n in range(4):
+            u[c, 2 + n, LO - 2 : LO] = lo[7 * n + 3 + 2 * c : 7 * n + 5 + 2 * c]
+            u[c, 2 + n, HI : HI + 2] = hi[7 * n + 3 + 2 * c : 7 * n + 5 + 2 * c]
+        for r, at in ((1, 30), (6, 34)):
+            u[c, r, LO - 1 : LO] = lo[at + c : at + c + 1]
+            u[c, r, HI : HI + 1] = hi[at + c : at + c + 1]
     for copy in copies:
         copy.wait()
 
@@ -295,14 +331,16 @@
 
     lax.fori_loop(1, 7, first, 0)
 
-    def second(i, _):
-        couple(i, v, d, fz, t, lambda c, y: store(c, i, y))
-        return 0
-
     def store(c, i, y):
         out[c, i] = E0 * u[c, i + 2, LO:HI] + y
 
-    lax.fori_loop(0, ROWS, second, 0)
+    saves = []
+    for i in range(ROWS):
+        couple(i, v, d, fz, t, lambda c, y: store(c, i, y))
+        saves.append(pltpu.make_async_copy(out.at[:, i], out_hbm.at[:, i], sems.at[7 + i]))
+        saves[-1].start()
+    for copy in saves:
+        copy.wait()
 
 
 def couple(i, v, d, fz, t, done):
@@ -323,7 +361,12 @@
         done(c, dm * y)
 
 
-def velocity_kernel(basis, dots, onehot, v, d, fz, h0, ex, ez, forced, vel, press, t, b, bz):
+def velocity_kernel(basis, dots, onehot, *rest):
+    inputs, (vel_hbm, press), scratch, (vel, t, b, bz, sems) = rest[:7], rest[7:9], rest[9:16], rest[16:]
+    h0, ex, ez, v, d, fz, forced = scratch
+    loads = [pltpu.make_async_copy(x, y, sems.at[n]) for n, (x, y) in enumerate(zip(inputs, scratch))]
+    for copy in loads:
+        copy.start()
     sums = jnp.sum(jnp.sum(dots[...], axis=0), axis=1, keepdims=True)
     gg, gh, hh, hkh = sums[0:1], sums[1:2], sums[2:3], sums[3:4]
     alpha0 = gg / gh
@@ -342,6 +385,9 @@
         p, onehot[...], precision=lax.Precision.HIGHEST, preferred_element_type=jnp.float32
     )[0:4]
 
+    for copy in loads[:3]:
+        copy.wait()
+
     def first(r, _):
         h, exi, exm, ezi = h0[r], ex[r], ex[r - 1], ez[r]
         ezm = down_z(ezi)
@@ -353,15 +399,20 @@
 
     lax.fori_loop(1, 7, first, 0)
 
-    def second(i, _):
-        couple(i, v, d, fz, t, lambda c, y: store(c, i, y))
-        return 0
+    for copy in loads[3:]:
+        copy.wait()
 
     def store(c, i, y):
         own = E0 * (d[i + 2, LO:HI] * b[pl.ds(8 * c + i + 2, 1)])
         vel[c, i] = forced[c, i] - (own + y)
 
-    lax.fori_loop(0, ROWS, second, 0)
+    saves = []
+    for i in range(ROWS):
+        couple(i, v, d, fz, t, lambda c, y: store(c, i, y))
+        saves.append(pltpu.make_async_copy(vel.at[:, i], vel_hbm.at[:, i], sems.at[7 + i]))
+        saves[-1].start()
+    for copy in saves:
+        copy.wait()
 
 
 VMEM = pl.BlockSpec(memory_space=pltpu.VMEM)
@@ -405,24 +456,33 @@
     chip_up = [(i, (i + 2) % slabs) for i in range(slabs) if i + 2 < slabs]
     chip_down = [(b, a) for a, b in chip_up]
 
-    od = lax.ppermute(viscosity, "slab", others)
-    ev = lax.ppermute(viscosity, "slab", mates)
-    edge_hi = jnp.concatenate([viscosity[:, -3:], forcing[0, :, -2:], forcing[1, :, -2:]], 1)
-    edge_lo = jnp.concatenate([viscosity[:, :3], forcing[0, :, :2], forcing[1, :, :2]], 1)
-    lo = lax.ppermute(edge_hi, "cross", up)
-    hi = lax.ppermute(edge_lo, "cross", down)
-    edges = jnp.concatenate([lo, hi], 1)
-    od_c = lax.ppermute(edges, "slab", others)
-    ev_c = lax.ppermute(edges, "slab", mates)
-
-    margins = (lo, hi, od_c, ev_c)
+    edges = call(
+        edge_kernel,
+        f32(ROWS, 14, NZ),
+        [(ROWS, 8, NZ)] * 2 + [(2, ROWS, 8, NZ)] * 2,
+        (where, in_hbm(viscosity), in_hbm(forcing)),
+        in_specs=[SMEM, ANY, ANY],
+        sems=4,
+        mib=4,
+    )
+    od_e = lax.ppermute(edges, "slab", others)
+    ev_e = lax.ppermute(edges, "slab", mates)
+    od_e, ev_e, late = lax.optimization_barrier((od_e, ev_e, viscosity))
+    od = lax.ppermute(late, "slab", others)
+    ev = lax.ppermute(late, "slab", mates)
+    low, high = call(
+        corner_kernel, (f32(40, NZ), f32(40, NZ)), [], (where, edges, od_e, ev_e), in_specs=[SMEM] + [VMEM] * 3, mib=4
+    )
+    lo = lax.ppermute(high, "cross", up)
+    hi = lax.ppermute(low, "cross", down)
+
     kept = (f32(10, FRAME, NZ), f32(8, FRAME, NZ), f32(8, FRAME, NZ)) + (f32(7, FRAME, NZ),) * 3
     part, to_od, to_ev, v, d, fz, h0, ex, ez = call(
         stencil_kernel,
-        (f32(10, 4, NZ), f32(2, 2, NY, NZ), f32(2, 2, NY, NZ), *[pltpu.HBM(x.shape, x.dtype) for x in kept]),
+        (f32(10, 4, NZ), *[pltpu.HBM((2, 2, NY, NZ), jnp.float32)] * 2, *[pltpu.HBM(x.shape, x.dtype) for x in kept]),
         [x.shape for x in kept] + [(7, FRAME, NZ), (32, 1, NZ), (2, ROWS, NY, NZ)],
-        (where, in_hbm(viscosity), od, ev, *margins, in_hbm(forcing)),
-        in_specs=[SMEM, ANY, ANY, ANY] + [VMEM] * 4 + [ANY],
+        (where, in_hbm(viscosity), od, ev, lo, hi, in_hbm(forcing)),
+        in_specs=[SMEM, ANY, ANY, ANY, VMEM, VMEM, ANY],
         out_specs=(VMEM,) + (HBM,) * 8,
         micros=6,
         sems=12,
@@ -435,22 +495,14 @@
     def among(x, step):
         return [lax.ppermute(x, "cross", [(i, i ^ (n * step)) for i in range(cross)]) for n in (1, 2, 3)]
 
+    part, onehot = lax.optimization_barrier((part, onehot))
     got = among(part, 1)
+    part = part + got[0] + got[1] + got[2]
+    part, to_od, to_ev = lax.optimization_barrier((part, to_od, to_ev))
     od_f = lax.ppermute(to_od, "slab", others)
     ev_f = lax.ppermute(to_ev, "slab", mates)
-    got, od_f, ev_f, onehot = lax.optimization_barrier((got, od_f, ev_f, onehot))
-    part = part + got[0] + got[1] + got[2]
     got = among(part, 4)
-    forced = call(
-        forced_kernel,
-        f32(2, ROWS, NY, NZ),
-        [x.shape for x in kept[:3]] + [(2, 8, FRAME, NZ)] * 2,
-        (where, in_hbm(forcing), od_f, ev_f, *margins, in_hbm(v), in_hbm(d), in_hbm(fz)),
-        in_specs=[SMEM] + [ANY] * 3 + [VMEM] * 4 + [ANY] * 3,
-        micros=5,
-        sems=7,
-    )
-    got, forced = lax.optimization_barrier((got, forced))
+    got, od_f, ev_f = lax.optimization_barrier((got, od_f, ev_f))
     part = part + got[0] + got[1] + got[2]
 
     mate = lax.ppermute(part, "slab", mates)
@@ -465,16 +517,31 @@
         in_specs=[SMEM] + [VMEM] * 6,
         mib=4,
     )
+    dots, od_f, ev_f = lax.optimization_barrier((dots, od_f, ev_f))
+    forced = call(
+        forced_kernel,
+        pltpu.HBM((2, ROWS, NY, NZ), jnp.float32),
+        [x.shape for x in kept[:3]] + [(2, 8, FRAME, NZ)] * 2 + [(2, ROWS, NY, NZ)],
+        (where, in_hbm(forcing), in_hbm(od_f), in_hbm(ev_f), lo, hi, in_hbm(v), in_hbm(d), in_hbm(fz)),
+        in_specs=[SMEM] + [ANY] * 3 + [VMEM] * 2 + [ANY] * 3,
+        out_specs=HBM,
+        micros=5,
+        sems=11,
+    )
     groups = [[2 * z + c for z in range(chips)] for c in range(2)]
     dots = lax.all_to_all(dots, "slab", 0, 0, tiled=True, axis_index_groups=groups)
 
+    big = (h0, ex, ez, v, d, fz, forced)
     return call(
         velocity_kernel,
-        (f32(2, ROWS, NY, NZ), f32(ROWS, width)),
-        [(2, 8, FRAME, NZ), (16, NZ), (32, NZ)],
-        (basis, dots, onehot, v, d, fz, h0, ex, ez, forced),
-        in_specs=[VMEM] * 10,
+        (pltpu.HBM((2, ROWS, NY, NZ), jnp.float32), f32(ROWS, width)),
+        [x.shape for x in big] + [(2, ROWS, NY, NZ), (2, 8, FRAME, NZ), (16, NZ), (32, NZ)],
+        (basis, dots, onehot, *[in_hbm(x) for x in big]),
+        in_specs=[VMEM] * 3 + [ANY] * 7,
+        out_specs=(HBM, VMEM),
         micros=4,
+        sems=11,
+        mib=24,
     )
 
 

time: 93.3 us -> 119 us (1.28)
  Pallas kernels: 20.6 us -> 53 us
  blocking collectives: 20.2 us -> 0 us
  starting transfers between devices: 36 us -> 47.5 us
  waiting for transfers between devices: 12.6 us -> 16.9 us
  local copies, waits for them, and re-layouts: 1.9 us -> 0.04 us
    pallas_call x4 -> x6, Pallas kernels: 20.6 us -> 53 us  [call(): pl.pallas_call(kernel, out_shape=out_shape, in_specs=in_specs, out_specs=...]
    all_to_all x1 -> x0, blocking collectives: 20.2 us -> none  [shards(): lax.all_to_all(dots, 'slab', 0, 0, tiled=True, axis_index_groups=groups)]
    all_to_all x0 -> x1, starting transfers between devices: none -> 11.4 us  [shards(): lax.all_to_all(dots, 'slab', 0, 0, tiled=True, axis_index_groups=groups)]
    ppermute x6, waiting for transfers between devices: 5.57 us -> 9.25 us  [among(): lax.ppermute(x, 'cross', [(i, i ^ n * step) for i in range(cross)])]
    ppermute x1, starting transfers between devices: 8.6 us -> 5.16 us  [shards(): ev_f = lax.ppermute(to_ev, 'slab', mates)]
    ppermute x6, starting transfers between devices: 11.6 us -> 14.8 us  [the longest x1 5.43 us: shards(): ev = lax.ppermute(late, 'slab', mates)]
  transfers between devices with their start and end apart: 17 -> 18, of which waited for: 8 -> 12; matrix products, arithmetic and copies ran while one was open for 2% -> 0% of each run, Pallas kernels for 7% -> 7%
where the time goes in v3:
time: 119 us
  Pallas kernels  53 us (45%)
  starting transfers between devices  47.5 us (40%)
  waiting for transfers between devices  16.9 us (14%)
    pallas_call x6, Pallas kernels, call(): pl.pallas_call(kernel, out_shape=out_shape, in_specs=in_specs, out_specs=...  53 us
    all_to_all x1, starting transfers between devices, shards(): lax.all_to_all(dots, 'slab', 0, 0, tiled=True, axis_index_groups=groups)  11.4 us
    ppermute x6, starting transfers between devices, among(): lax.ppermute(x, 'cross', [(i, i ^ n * step) for i in range(cross)])  9.45 us
    ppermute x6, waiting for transfers between devices, among(): lax.ppermute(x, 'cross', [(i, i ^ n * step) for i in range(cross)])  9.25 us
    ppermute x1, starting transfers between devices, shards(): ev = lax.ppermute(late, 'slab', mates)  5.43 us
    ppermute x1, starting transfers between devices, shards(): ev_f = lax.ppermute(to_ev, 'slab', mates)  5.16 us
    ppermute x1, starting transfers between devices, shards(): below = lax.ppermute(both, 'slab', chip_up)  4.56 us
    ppermute x1, starting transfers between devices, shards(): hi = lax.ppermute(low, 'cross', down)  4.55 us
  transfers between devices with their start and end apart: 18, of which 12 were waited for; matrix products, arithmetic and copies ran while one was open for 0% of the time, Pallas kernels for 7%

profile of v3, /device:TPU:16, one launch (start us, length us, event | category | flops | bytes accessed | tf_op | source)
XLA Modules:
  0.0 118.7 jit_solution(17169680927069663535)
XLA Ops:
  0.7 1.7 %shard_map.50.own = f32[4,14,512]{2,1,0:T(8,128)S(1)} custom-call(s32[2]{0:T(128)S(1)} %pad_add_fusion.par_ref, f32[4,64,512]{2,1,0:T(8,128)} %own.3, f32[2,4,64,512]{3,2,1,0:T(8,128)} %f.3), custom_call_target="tpu_custom_call" | custom-call | bytes 3600000 | tf_op jit(solution)/shard_map/pallas_call | solution.py:425
  3.9 5.4 %collective-permute-start.3 = (f32[4,64,512]{2,1,0:T(8,128)S(1)}, f32[4,64,512]{2,1,0:T(8,128)S(1)}, u32[]{:S(2)}, u32[]{:S(2)}) collective-permute-start(f32[4,64,512]{2,1,0:T(8,128)S(1)} %copy-done), channel_id=1, source_target_pairs={{0,16},{16,0},{32,48},{48,32},{64,80},{80,64},{96,112},{112,96},{1... | collective-permute-start | bytes 1572872 | tf_op jit(solution)/shard_map/ppermute | solution.py:472
  10.6 3.4 %collective-permute-start.4 = (f32[40,512]{1,0:T(8,128)S(1)}, f32[40,512]{1,0:T(8,128)S(1)}, u32[]{:S(2)}, u32[]{:S(2)}) collective-permute-start(f32[40,512]{1,0:T(8,128)S(1)} %get-tuple-element.34), channel_id=1, source_target_pairs={{0,1},{1,2},{2,3},{3,4},{4,5},{5,6},{6,7},{7,8},{8,9},{9,10},{10,1... | collective-permute-start | bytes 245768 | tf_op jit(solution)/shard_map/ppermute | solution.py:476
  14.0 4.6 %collective-permute-start.5 = (f32[40,512]{1,0:T(8,128)S(1)}, f32[40,512]{1,0:T(8,128)S(1)}, u32[]{:S(2)}, u32[]{:S(2)}) collective-permute-start(f32[40,512]{1,0:T(8,128)S(1)} %get-tuple-element.35), channel_id=1, source_target_pairs={{1,0},{2,1},{3,2},{4,3},{5,4},{6,5},{7,6},{8,7},{9,8},{10,9},{11,1... | collective-permute-start | bytes 245768 | tf_op jit(solution)/shard_map/ppermute | solution.py:477
  19.0 1.6 %collective-permute-done.5.hi = f32[40,512]{1,0:T(8,128)S(1)} collective-permute-done((f32[40,512]{1,0:T(8,128)S(1)}, f32[40,512]{1,0:T(8,128)S(1)}, u32[]{:S(2)}, u32[]{:S(2)}) %collective-permute-start.5) | collective-permute-done | bytes 81952 | tf_op jit(solution)/shard_map/ppermute | solution.py:477
  20.6 34.9 %shard_map.52 = (f32[10,4,512]{2,1,0:T(4,128)S(1)}, f32[2,2,64,512]{3,2,1,0:T(8,128)}, f32[2,2,64,512]{3,2,1,0:T(8,128)}, f32[10,80,512]{2,1,0:T(8,128)}, f32[8,...) custom-call(s32[2]{0:T(128)S(1)} %pad_add_fusion.par_ref, ...), custom_call_target="tpu_custom_call" | custom-call | bytes 21600000 | tf_op jit(solution)/shard_map/pallas_call | solution.py:425
  55.5 4.4 %collective-permute-start.8 = (f32[10,4,512]{2,1,0:T(4,128)S(1)}, f32[10,4,512]{2,1,0:T(4,128)S(1)}, u32[]{:S(2)}, u32[]{:S(2)}) collective-permute-start(f32[10,4,512]{2,1,0:T(4,128)S(1)} %get-tuple-element.37), channel_id=1, source_target_pairs={{0,3},{1,2},{2,1},{3,0},{4,7},{5,6},{6,5},{7,4},{8,11},{9,10},{10,... | collective-permute-start | bytes 245768 | tf_op jit(solution)/shard_map/ppermute | solution.py:496
  59.9 1.0 collective-permute-start.6
  60.8 2.8 %collective-permute-done.8 = f32[10,4,512]{2,1,0:T(4,128)S(1)} collective-permute-done((f32[10,4,512]{2,1,0:T(4,128)S(1)}, f32[10,4,512]{2,1,0:T(4,128)S(1)}, u32[]{:S(2)}, u32[]{:S(2)}) %collective-permute-start.8) | collective-permute-done | bytes 81952 | tf_op jit(solution)/shard_map/ppermute | solution.py:496
  63.6 2.6 %collective-permute-done.7 = f32[10,4,512]{2,1,0:T(4,128)S(1)} collective-permute-done((f32[10,4,512]{2,1,0:T(4,128)S(1)}, f32[10,4,512]{2,1,0:T(4,128)S(1)}, u32[]{:S(2)}, u32[]{:S(2)}) %collective-permute-start.7) | collective-permute-done | bytes 81952 | tf_op jit(solution)/shard_map/ppermute | solution.py:496
  66.9 5.2 %collective-permute-start.13 = (f32[2,2,64,512]{3,2,1,0:T(8,128)}, f32[2,2,64,512]{3,2,1,0:T(8,128)S(1)}, u32[]{:S(2)}, u32[]{:S(2)}) collective-permute-start(f32[2,2,64,512]{3,2,1,0:T(8,128)} %get-tuple-element.42), channel_id=1, source_target_pairs={{0,16},{16,0},{32,48},{48,32},{64,80},{80,64},{96,112},{112,96},{1... | collective-permute-start | bytes 1572872 | tf_op jit(solution)/shard_map/ppermute | solution.py:503
  72.1 0.7 collective-permute-start.11
  73.0 3.2 %collective-permute-start.9 = (f32[10,4,512]{2,1,0:T(4,128)S(1)}, f32[10,4,512]{2,1,0:T(4,128)S(1)}, u32[]{:S(2)}, u32[]{:S(2)}) collective-permute-start(f32[10,4,512]{2,1,0:T(4,128)S(1)} %bitcast.29), channel_id=1, source_target_pairs={{0,4},{1,5},{2,6},{3,7},{4,0},{5,1},{6,2},{7,3},{8,12},{9,13},{10,... | collective-permute-start | bytes 245768 | tf_op jit(solution)/shard_map/ppermute | solution.py:496
  76.5 2.8 %collective-permute-done.10 = f32[10,4,512]{2,1,0:T(4,128)S(1)} collective-permute-done((f32[10,4,512]{2,1,0:T(4,128)S(1)}, f32[10,4,512]{2,1,0:T(4,128)S(1)}, u32[]{:S(2)}, u32[]{:S(2)}) %collective-permute-start.10) | collective-permute-done | bytes 81952 | tf_op jit(solution)/shard_map/ppermute | solution.py:496
  79.4 0.7 collective-permute-done.9
  80.2 1.3 %collective-permute-done.14.mate = f32[10,4,512]{2,1,0:T(4,128)S(1)} collective-permute-done((f32[10,4,512]{2,1,0:T(4,128)S(1)}, f32[10,4,512]{2,1,0:T(4,128)S(1)}, u32[]{:S(2)}, u32[]{:S(2)}) %collective-permute-start.14) | collective-permute-done | bytes 81952 | tf_op jit(solution)/shard_map/ppermute | solution.py:508
  81.5 1.3 %collective-permute-start.16 = (f32[2,10,4,512]{3,2,1,0:T(4,128)S(1)}, f32[2,10,4,512]{3,2,1,0:T(4,128)S(1)}, u32[]{:S(2)}, u32[]{:S(2)}) collective-permute-start(f32[2,10,4,512]{3,2,1,0:T(4,128)S(1)} %pad_maximum_fusion), channel_id=1, source_target_pairs={{32,0},{48,16},{64,32},{80,48},{96,64},{112,80},{128,96},{144,112}... | collective-permute-start | bytes 491528 | tf_op jit(solution)/shard_map/ppermute | solution.py:511
  82.8 4.6 %collective-permute-start.15 = (f32[2,10,4,512]{3,2,1,0:T(4,128)S(1)}, f32[2,10,4,512]{3,2,1,0:T(4,128)S(1)}, u32[]{:S(2)}, u32[]{:S(2)}) collective-permute-start(f32[2,10,4,512]{3,2,1,0:T(4,128)S(1)} %pad_maximum_fusion), channel_id=1, source_target_pairs={{0,32},{16,48},{32,64},{48,80},{64,96},{80,112},{96,128},{112,144}... | collective-permute-start | bytes 491528 | tf_op jit(solution)/shard_map/ppermute | solution.py:510
  87.4 2.3 %collective-permute-done.16 = f32[2,10,4,512]{3,2,1,0:T(4,128)S(1)} collective-permute-done((f32[2,10,4,512]{3,2,1,0:T(4,128)S(1)}, f32[2,10,4,512]{3,2,1,0:T(4,128)S(1)}, u32[]{:S(2)}, u32[]{:S(2)}) %collective-permute-start.16) | collective-permute-done | bytes 163872 | tf_op jit(solution)/shard_map/ppermute | solution.py:511
  89.7 1.2 collective-permute-done.15
  90.9 1.8 %shard_map.53 = (f32[48,512]{1,0:T(8,128)S(1)}, f32[8,8,128]{2,1,0:T(8,128)}) custom-call(s32[2]{0:T(128)S(1)} %pad_add_fusion.par_ref, f32[10,4,512]{2,1,0:T(4,128)S(1)} %bitcast.24, f32[10,4,512]{2,1,0:T(4,128)S(1)} %collective-permute-done.14.mate, f32[10,4,512]{2,1,0:T(4,128)S(1)} %get-tuple-element.63.below_mine, ...), custom_call_target="tpu_custom_call" | custom-call | bytes 3600000 | tf_op jit(solution)/shard_map/pallas_call | solution.py:425
  92.7 11.4 %all-to-all-start = ((f32[8,8,128]{2,1,0:T(8,128)}), f32[8,8,128]{2,1,0:T(8,128)S(1)}, u32[]{:S(2)}, u32[]{:S(2)}) async-start(f32[8,8,128]{2,1,0:T(8,128)} %get-tuple-element.50), calls=%async_computation | async-start | bytes 65536 | tf_op jit(solution)/shard_map/all_to_all | solution.py:532
  104.1 7.7 %shard_map.54.rest_6_ = f32[2,4,64,512]{3,2,1,0:T(8,128)} custom-call(s32[2]{0:T(128)S(1)} %pad_add_fusion.par_ref, f32[2,4,64,512]{3,2,1,0:T(8,128)} %f.3, f32[2,2,64,512]{3,2,1,0:T(8,128)} %copy-done.1, f32[2,2,64,512]{3,2,1,0:T(8,128)} %copy-done.2, f32[40,512]{1,0:T(8,128)S(1)} %collective-permute-done.4.lo, f32[40,512]{1,0:T(8,128)S(1)} %collective-permute-done.5.hi, ...), custom_call_target="tpu_custom_call" | custom-call | bytes 18000000 | tf_op jit(solution)/shard_map/pallas_call | solution.py:425
  112.1 6.4 %shard_map.55 = (f32[2,4,64,512]{3,2,1,0:T(8,128)}, f32[4,32]{1,0:T(4,128)}) custom-call(f32[48,512]{1,0:T(8,128)S(1)} %get-tuple-element.46.basis, f32[8,8,128]{2,1,0:T(8,128)S(1)} %all-to-all-done.dots, f32[512,32]{1,0:T(8,128)S(1)} %compare_convert_fusion.onehot, f32[7,80,512]{2,1,0:T(8,128)} %get-tuple-element.52.rest_0_, ...), custom_call_target="tpu_custom_call" | custom-call | bytes 14400000 | tf_op jit(solution)/shard_map/pallas_call | solution.py:425
  (34 shorter events, 5.0 us)
Async XLA Ops:
  0.6 3.2 %copy-start = (f32[4,64,512]{2,1,0:T(8,128)S(1)}, f32[4,64,512]{2,1,0:T(8,128)}, u32[]{:S(2)}) copy-start(f32[4,64,512]{2,1,0:T(8,128)} %own.3) | copy-start | bytes 1572868
  0.6 17.9 %copy-start.3 = (s32[512]{0:T(512)S(1)}, s32[512]{0:T(512)}, u32[]{:S(2)}) copy-start(s32[512]{0:T(512)} %param.5) | copy-start | bytes 6148
  2.4 1.4 %collective-permute-start.1 = (f32[4,14,512]{2,1,0:T(8,128)S(1)}, f32[4,14,512]{2,1,0:T(8,128)S(1)}, u32[]{:S(2)}, u32[]{:S(2)}) collective-permute-start(f32[4,14,512]{2,1,0:T(8,128)S(1)} %shard_map.50.own), channel_id=1, source_target_pairs={{0,16},{16,0},{32,48},{48,32},{64,80},{80,64},{96,112},{112,96},{1... | collective-permute-start | bytes 344072 | tf_op jit(solution)/shard_map/ppermute | solution.py:469
  2.5 1.3 %collective-permute-start = (f32[4,14,512]{2,1,0:T(8,128)S(1)}, f32[4,14,512]{2,1,0:T(8,128)S(1)}, u32[]{:S(2)}, u32[]{:S(2)}) collective-permute-start(f32[4,14,512]{2,1,0:T(8,128)S(1)} %shard_map.50.own), channel_id=1, source_target_pairs={{16,32},{48,64},{80,96},{112,128},{144,160},{176,192},{208,224},{3... | collective-permute-start | bytes 344072 | tf_op jit(solution)/shard_map/ppermute | solution.py:468
  3.9 16.7 %collective-permute-start.3 = (f32[4,64,512]{2,1,0:T(8,128)S(1)}, f32[4,64,512]{2,1,0:T(8,128)S(1)}, u32[]{:S(2)}, u32[]{:S(2)}) collective-permute-start(f32[4,64,512]{2,1,0:T(8,128)S(1)} %copy-done), channel_id=1, source_target_pairs={{0,16},{16,0},{32,48},{48,32},{64,80},{80,64},{96,112},{112,96},{1... | collective-permute-start | bytes 1572872 | tf_op jit(solution)/shard_map/ppermute | solution.py:472
  9.3 11.3 %collective-permute-start.2 = (f32[4,64,512]{2,1,0:T(8,128)S(1)}, f32[4,64,512]{2,1,0:T(8,128)S(1)}, u32[]{:S(2)}, u32[]{:S(2)}) collective-permute-start(f32[4,64,512]{2,1,0:T(8,128)S(1)} %copy-done), channel_id=1, source_target_pairs={{16,32},{48,64},{80,96},{112,128},{144,160},{176,192},{208,224},{3... | collective-permute-start | bytes 1572872 | tf_op jit(solution)/shard_map/ppermute | solution.py:471
  10.6 8.4 %collective-permute-start.4 = (f32[40,512]{1,0:T(8,128)S(1)}, f32[40,512]{1,0:T(8,128)S(1)}, u32[]{:S(2)}, u32[]{:S(2)}) collective-permute-start(f32[40,512]{1,0:T(8,128)S(1)} %get-tuple-element.34), channel_id=1, source_target_pairs={{0,1},{1,2},{2,3},{3,4},{4,5},{5,6},{6,7},{7,8},{8,9},{9,10},{10,1... | collective-permute-start | bytes 245768 | tf_op jit(solution)/shard_map/ppermute | solution.py:476
  14.0 6.6 %collective-permute-start.5 = (f32[40,512]{1,0:T(8,128)S(1)}, f32[40,512]{1,0:T(8,128)S(1)}, u32[]{:S(2)}, u32[]{:S(2)}) collective-permute-start(f32[40,512]{1,0:T(8,128)S(1)} %get-tuple-element.35), channel_id=1, source_target_pairs={{1,0},{2,1},{3,2},{4,3},{5,4},{6,5},{7,6},{8,7},{9,8},{10,9},{11,1... | collective-permute-start | bytes 245768 | tf_op jit(solution)/shard_map/ppermute | solution.py:477
  55.5 8.1 %collective-permute-start.8 = (f32[10,4,512]{2,1,0:T(4,128)S(1)}, f32[10,4,512]{2,1,0:T(4,128)S(1)}, u32[]{:S(2)}, u32[]{:S(2)}) collective-permute-start(f32[10,4,512]{2,1,0:T(4,128)S(1)} %get-tuple-element.37), channel_id=1, source_target_pairs={{0,3},{1,2},{2,1},{3,0},{4,7},{5,6},{6,5},{7,4},{8,11},{9,10},{10,... | collective-permute-start | bytes 245768 | tf_op jit(solution)/shard_map/ppermute | solution.py:496
  59.9 6.3 %collective-permute-start.7 = (f32[10,4,512]{2,1,0:T(4,128)S(1)}, f32[10,4,512]{2,1,0:T(4,128)S(1)}, u32[]{:S(2)}, u32[]{:S(2)}) collective-permute-start(f32[10,4,512]{2,1,0:T(4,128)S(1)} %get-tuple-element.37), channel_id=1, source_target_pairs={{0,2},{1,3},{2,0},{3,1},{4,6},{5,7},{6,4},{7,5},{8,10},{9,11},{10,... | collective-permute-start | bytes 245768 | tf_op jit(solution)/shard_map/ppermute | solution.py:496
  59.9 6.3 %collective-permute-start.6 = (f32[10,4,512]{2,1,0:T(4,128)S(1)}, f32[10,4,512]{2,1,0:T(4,128)S(1)}, u32[]{:S(2)}, u32[]{:S(2)}) collective-permute-start(f32[10,4,512]{2,1,0:T(4,128)S(1)} %get-tuple-element.37), channel_id=1, source_target_pairs={{0,1},{1,0},{2,3},{3,2},{4,5},{5,4},{6,7},{7,6},{8,9},{9,8},{10,11... | collective-permute-start | bytes 245768 | tf_op jit(solution)/shard_map/ppermute | solution.py:496
  66.2 13.9 %collective-permute-start.12 = (f32[2,2,64,512]{3,2,1,0:T(8,128)}, f32[2,2,64,512]{3,2,1,0:T(8,128)S(1)}, u32[]{:S(2)}, u32[]{:S(2)}) collective-permute-start(f32[2,2,64,512]{3,2,1,0:T(8,128)} %get-tuple-element.41), channel_id=1, source_target_pairs={{16,32},{48,64},{80,96},{112,128},{144,160},{176,192},{208,224},{3... | collective-permute-start | bytes 1572872 | tf_op jit(solution)/shard_map/ppermute | solution.py:502
  66.9 13.2 %collective-permute-start.13 = (f32[2,2,64,512]{3,2,1,0:T(8,128)}, f32[2,2,64,512]{3,2,1,0:T(8,128)S(1)}, u32[]{:S(2)}, u32[]{:S(2)}) collective-permute-start(f32[2,2,64,512]{3,2,1,0:T(8,128)} %get-tuple-element.42), channel_id=1, source_target_pairs={{0,16},{16,0},{32,48},{48,32},{64,80},{80,64},{96,112},{112,96},{1... | collective-permute-start | bytes 1572872 | tf_op jit(solution)/shard_map/ppermute | solution.py:503
  72.1 4.4 %collective-permute-start.11 = (f32[10,4,512]{2,1,0:T(4,128)S(1)}, f32[10,4,512]{2,1,0:T(4,128)S(1)}, u32[]{:S(2)}, u32[]{:S(2)}) collective-permute-start(f32[10,4,512]{2,1,0:T(4,128)S(1)} %bitcast.27), channel_id=1, source_target_pairs={{0,12},{1,13},{2,14},{3,15},{4,8},{5,9},{6,10},{7,11},{8,4},{9,5},... | collective-permute-start | bytes 245768 | tf_op jit(solution)/shard_map/ppermute | solution.py:496
  72.8 6.6 %collective-permute-start.10 = (f32[10,4,512]{2,1,0:T(4,128)S(1)}, f32[10,4,512]{2,1,0:T(4,128)S(1)}, u32[]{:S(2)}, u32[]{:S(2)}) collective-permute-start(f32[10,4,512]{2,1,0:T(4,128)S(1)} %bitcast.28), channel_id=1, source_target_pairs={{0,8},{1,9},{2,10},{3,11},{4,12},{5,13},{6,14},{7,15},{8,0},{9,1},... | collective-permute-start | bytes 245768 | tf_op jit(solution)/shard_map/ppermute | solution.py:496
  73.0 7.1 %collective-permute-start.9 = (f32[10,4,512]{2,1,0:T(4,128)S(1)}, f32[10,4,512]{2,1,0:T(4,128)S(1)}, u32[]{:S(2)}, u32[]{:S(2)}) collective-permute-start(f32[10,4,512]{2,1,0:T(4,128)S(1)} %bitcast.29), channel_id=1, source_target_pairs={{0,4},{1,5},{2,6},{3,7},{4,0},{5,1},{6,2},{7,3},{8,12},{9,13},{10,... | collective-permute-start | bytes 245768 | tf_op jit(solution)/shard_map/ppermute | solution.py:496
  80.1 24.0 %copy-start.1 = (f32[2,2,64,512]{3,2,1,0:T(8,128)}, f32[2,2,64,512]{3,2,1,0:T(8,128)S(1)}, u32[]{:S(2)}) copy-start(f32[2,2,64,512]{3,2,1,0:T(8,128)S(1)} %collective-permute-done.12.od_f) | copy-start | bytes 1572868
  80.1 24.0 %copy-start.2 = (f32[2,2,64,512]{3,2,1,0:T(8,128)}, f32[2,2,64,512]{3,2,1,0:T(8,128)S(1)}, u32[]{:S(2)}) copy-start(f32[2,2,64,512]{3,2,1,0:T(8,128)S(1)} %collective-permute-done.13.ev_f) | copy-start | bytes 1572868
  80.1 1.4 %collective-permute-start.14 = (f32[10,4,512]{2,1,0:T(4,128)S(1)}, f32[10,4,512]{2,1,0:T(4,128)S(1)}, u32[]{:S(2)}, u32[]{:S(2)}) collective-permute-start(f32[10,4,512]{2,1,0:T(4,128)S(1)} %bitcast.22), channel_id=1, source_target_pairs={{0,16},{16,0},{32,48},{48,32},{64,80},{80,64},{96,112},{112,96},{1... | collective-permute-start | bytes 245768 | tf_op jit(solution)/shard_map/ppermute | solution.py:508
  81.5 8.2 %collective-permute-start.16 = (f32[2,10,4,512]{3,2,1,0:T(4,128)S(1)}, f32[2,10,4,512]{3,2,1,0:T(4,128)S(1)}, u32[]{:S(2)}, u32[]{:S(2)}) collective-permute-start(f32[2,10,4,512]{3,2,1,0:T(4,128)S(1)} %pad_maximum_fusion), channel_id=1, source_target_pairs={{32,0},{48,16},{64,32},{80,48},{96,64},{112,80},{128,96},{144,112}... | collective-permute-start | bytes 491528 | tf_op jit(solution)/shard_map/ppermute | solution.py:511
  82.8 8.0 %collective-permute-start.15 = (f32[2,10,4,512]{3,2,1,0:T(4,128)S(1)}, f32[2,10,4,512]{3,2,1,0:T(4,128)S(1)}, u32[]{:S(2)}, u32[]{:S(2)}) collective-permute-start(f32[2,10,4,512]{3,2,1,0:T(4,128)S(1)} %pad_maximum_fusion), channel_id=1, source_target_pairs={{0,32},{16,48},{32,64},{48,80},{64,96},{80,112},{96,128},{112,144}... | collective-permute-start | bytes 491528 | tf_op jit(solution)/shard_map/ppermute | solution.py:510
  92.7 19.4 %all-to-all-start = ((f32[8,8,128]{2,1,0:T(8,128)}), f32[8,8,128]{2,1,0:T(8,128)S(1)}, u32[]{:S(2)}, u32[]{:S(2)}) async-start(f32[8,8,128]{2,1,0:T(8,128)} %get-tuple-element.50), calls=%async_computation | async-start | bytes 65536 | tf_op jit(solution)/shard_map/all_to_all | solution.py:532

commit v4 on v3

--- a/solution.py
+++ b/solution.py
@@ -67,7 +67,29 @@
         out[:, 10 + 2 * c : 12 + 2 * c] = high_f[c, :, 6:8]
 
 
-def corner_kernel(par_ref, own, od, ev, low, high):
+def pack_kernel(par_ref, own_hbm, f_hbm, to_od, to_ev, own, f, sems):
+    par = par_ref[0]
+    loads = [pltpu.make_async_copy(own_hbm, own, sems.at[0]), pltpu.make_async_copy(f_hbm, f, sems.at[1])]
+    for copy in loads:
+        copy.start()
+    saves = []
+    for n, (out, last) in enumerate(((to_od, par), (to_ev, 1 - par))):
+        saves.append(pltpu.make_async_copy(own.at[pl.ds(last, 3)], out.at[0:3], sems.at[2 + 3 * n]))
+        for c in range(2):
+            saves.append(
+                pltpu.make_async_copy(
+                    f.at[c, pl.ds(2 * last, 2)], out.at[3 + 2 * c : 5 + 2 * c], sems.at[3 + 3 * n + c]
+                )
+            )
+    for copy in loads:
+        copy.wait()
+    for copy in saves:
+        copy.start()
+    for copy in saves:
+        copy.wait()
+
+
+def corner_kernel(par_ref, own, od, ev, first, second, low, high):
     odd = par_ref[0] == 1
     below = lax.select(odd, ev[2:4], od[2:4])
     above = lax.select(odd, od[0:2], ev[0:2])
@@ -82,12 +104,19 @@
             row = base + 2 * forced
             out[far_at : far_at + 1] = far[row : row + 1]
         out[38:40] = jnp.zeros((2, NZ), jnp.float32)
+    odd = par_ref[2] == 1
+    first[...] = lax.select(odd, low[...], high[...])
+    second[...] = lax.select(odd, high[...], low[...])
+
+
+def sides(odd, first, second):
+    return lax.select(odd, first[...], second[...]), lax.select(odd, second[...], first[...])
 
 
 def fill_viscosity(par, v, own, od, ev, lo, hi, sems):
     copies = [pltpu.make_async_copy(own, v.at[3:7, LO:HI], sems.at[0])]
-    for n, at, first, x in ((1, par * 7, 1 - par, od), (2, 7 - par * 7, par, ev)):
-        copies.append(pltpu.make_async_copy(x.at[pl.ds(first, 3)], v.at[pl.ds(at, 3), LO:HI], sems.at[n]))
+    for n, at, x in ((1, par * 7, od), (2, 7 - par * 7, ev)):
+        copies.append(pltpu.make_async_copy(x.at[0:3], v.at[pl.ds(at, 3), LO:HI], sems.at[n]))
     for copy in copies:
         copy.start()
     for n in range(4):
@@ -119,18 +148,13 @@
     lax.fori_loop(0, 8, layer, 0)
 
 
-def stencil_kernel(par_ref, own, od, ev, lo, hi, f_hbm, out, to_od, to_ev, *rest):
+def stencil_kernel(par_ref, own, od, ev, first, second, f_hbm, out, *rest):
     kept_hbm, (v, d, fz, h0, ex, ez, ezm, acc, f, sems) = rest[:6], rest[6:]
     par = par_ref[0]
     load = pltpu.make_async_copy(f_hbm, f, sems.at[3])
     load.start()
+    lo, hi = sides(par_ref[2] == 1, first, second)
     fill_viscosity(par, v, own, od, ev, lo, hi, sems)
-    moves = [
-        pltpu.make_async_copy(f_hbm.at[:, pl.ds(2 * par, 2)], to_od, sems.at[10]),
-        pltpu.make_async_copy(f_hbm.at[:, pl.ds(2 - 2 * par, 2)], to_ev, sems.at[11]),
-    ]
-    for copy in moves:
-        copy.start()
     fill_inverse(v, d, fz)
 
     def edges(r, _):
@@ -214,11 +238,11 @@
     out[7:9] = e[0:8].reshape(2, 4, NZ)
     out[9, 0:1] = e[8:9]
     out[9, 1:4] = jnp.zeros((3, NZ), jnp.float32)
-    for copy in moves + saves:
-        copy.wait()
-
-
-def krylov_kernel(par_ref, mine, mate, below_mine, below_mate, above_mine, above_mate, basis, dots, s_ref, g_ref):
+    for copy in saves:
+        copy.wait()
+
+
+def krylov_kernel(par_ref, mine, mate, first, second, basis, dots, s_ref, g_ref):
     par, chip = par_ref[0], par_ref[1]
     odd = par == 1
 
@@ -226,8 +250,9 @@
         return lax.select(odd, b, a), lax.select(odd, a, b)
 
     slabs = []
-    for a, b in ((below_mine, below_mate), (mine, mate), (above_mine, above_mate)):
-        slabs += pair(a[...], b[...])
+    below, above = sides(par_ref[3] == 1, first, second)
+    for a, b in ((below[0], below[1]), (mine[...], mate[...]), (above[0], above[1])):
+        slabs += pair(a, b)
     W = 24
     g_ref[...] = jnp.zeros_like(g_ref)
     for n, slab in enumerate(slabs):
@@ -289,15 +314,18 @@
     dots[...] = jnp.broadcast_to(packed[None], dots.shape)
 
 
-def forced_kernel(par_ref, f, od_f, ev_f, lo, hi, v_hbm, d_hbm, fz_hbm, out_hbm, v, d, fz, u, t, out, sems):
+def forced_kernel(par_ref, f, od, ev, first, second, v_hbm, d_hbm, fz_hbm, out, v, d, fz, u, t, sems):
     par = par_ref[0]
     copies = [pltpu.make_async_copy(x, y, sems.at[n]) for n, (x, y) in enumerate(((d_hbm, d), (v_hbm, v), (fz_hbm, fz)))]
     for c in range(2):
         copies.append(pltpu.make_async_copy(f.at[c], u.at[c, 2:6, LO:HI], sems.at[3 + c]))
-    for n, at, x in ((5, par * 6, od_f), (6, 6 - par * 6, ev_f)):
-        copies.append(pltpu.make_async_copy(x, u.at[:, pl.ds(at, 2), LO:HI], sems.at[n]))
+        for n, at, x in ((5, par * 6, od), (7, 6 - par * 6, ev)):
+            copies.append(
+                pltpu.make_async_copy(x.at[3 + 2 * c : 5 + 2 * c], u.at[c, pl.ds(at, 2), LO:HI], sems.at[n + c])
+            )
     for copy in copies:
         copy.start()
+    lo, hi = sides(par_ref[2] == 1, first, second)
     for c in range(2):
         for n in range(4):
             u[c, 2 + n, LO - 2 : LO] = lo[7 * n + 3 + 2 * c : 7 * n + 5 + 2 * c]
@@ -334,13 +362,8 @@
     def store(c, i, y):
         out[c, i] = E0 * u[c, i + 2, LO:HI] + y
 
-    saves = []
     for i in range(ROWS):
         couple(i, v, d, fz, t, lambda c, y: store(c, i, y))
-        saves.append(pltpu.make_async_copy(out.at[:, i], out_hbm.at[:, i], sems.at[7 + i]))
-        saves[-1].start()
-    for copy in saves:
-        copy.wait()
 
 
 def couple(i, v, d, fz, t, done):
@@ -361,12 +384,7 @@
         done(c, dm * y)
 
 
-def velocity_kernel(basis, dots, onehot, *rest):
-    inputs, (vel_hbm, press), scratch, (vel, t, b, bz, sems) = rest[:7], rest[7:9], rest[9:16], rest[16:]
-    h0, ex, ez, v, d, fz, forced = scratch
-    loads = [pltpu.make_async_copy(x, y, sems.at[n]) for n, (x, y) in enumerate(zip(inputs, scratch))]
-    for copy in loads:
-        copy.start()
+def velocity_kernel(basis, dots, onehot, h0, ex, ez, v, d, fz, forced, vel_hbm, press, vel, t, b, bz, sems):
     sums = jnp.sum(jnp.sum(dots[...], axis=0), axis=1, keepdims=True)
     gg, gh, hh, hkh = sums[0:1], sums[1:2], sums[2:3], sums[3:4]
     alpha0 = gg / gh
@@ -385,9 +403,6 @@
         p, onehot[...], precision=lax.Precision.HIGHEST, preferred_element_type=jnp.float32
     )[0:4]
 
-    for copy in loads[:3]:
-        copy.wait()
-
     def first(r, _):
         h, exi, exm, ezi = h0[r], ex[r], ex[r - 1], ez[r]
         ezm = down_z(ezi)
@@ -399,9 +414,6 @@
 
     lax.fori_loop(1, 7, first, 0)
 
-    for copy in loads[3:]:
-        copy.wait()
-
     def store(c, i, y):
         own = E0 * (d[i + 2, LO:HI] * b[pl.ds(8 * c + i + 2, 1)])
         vel[c, i] = forced[c, i] - (own + y)
@@ -409,7 +421,7 @@
     saves = []
     for i in range(ROWS):
         couple(i, v, d, fz, t, lambda c, y: store(c, i, y))
-        saves.append(pltpu.make_async_copy(vel.at[:, i], vel_hbm.at[:, i], sems.at[7 + i]))
+        saves.append(pltpu.make_async_copy(vel.at[:, i], vel_hbm.at[:, i], sems.at[i]))
         saves[-1].start()
     for copy in saves:
         copy.wait()
@@ -442,19 +454,20 @@
     return jax.ShapeDtypeStruct(shape, jnp.float32)
 
 
+def pairs(n, first):
+    up = [(i, i + 1) for i in range(first, n - 1, 2)]
+    return up + [(b, a) for a, b in up]
+
+
 def shards(forcing, viscosity, owner_slot):
     slabs, cross = lax.axis_size("slab"), lax.axis_size("cross")
     slab = lax.axis_index("slab")
     par = slab % 2
-    where = jnp.stack([par, slab // 2]).astype(jnp.int32)
-    mates = [(i, i ^ 1) for i in range(slabs)]
-    others = [(i, i + 1) for i in range(1, slabs - 1, 2)]
-    others = others + [(b, a) for a, b in others]
-    up = [(i, i + 1) for i in range(cross - 1)]
-    down = [(b, a) for a, b in up]
+    where = jnp.stack([par, slab // 2, lax.axis_index("cross") % 2, slab // 2 % 2]).astype(jnp.int32)
+    mates, others = pairs(slabs, 0), pairs(slabs, 1)
     chips = slabs // 2
-    chip_up = [(i, (i + 2) % slabs) for i in range(slabs) if i + 2 < slabs]
-    chip_down = [(b, a) for a, b in chip_up]
+    first_chips = [(2 * a + c, 2 * b + c) for a, b in pairs(chips, 0) for c in range(2)]
+    second_chips = [(2 * a + c, 2 * b + c) for a, b in pairs(chips, 1) for c in range(2)]
 
     edges = call(
         edge_kernel,
@@ -467,25 +480,42 @@
     )
     od_e = lax.ppermute(edges, "slab", others)
     ev_e = lax.ppermute(edges, "slab", mates)
-    od_e, ev_e, late = lax.optimization_barrier((od_e, ev_e, viscosity))
-    od = lax.ppermute(late, "slab", others)
-    ev = lax.ppermute(late, "slab", mates)
-    low, high = call(
-        corner_kernel, (f32(40, NZ), f32(40, NZ)), [], (where, edges, od_e, ev_e), in_specs=[SMEM] + [VMEM] * 3, mib=4
-    )
-    lo = lax.ppermute(high, "cross", up)
-    hi = lax.ppermute(low, "cross", down)
+    layers = pltpu.HBM((7, NY, NZ), jnp.float32)
+    to_od, to_ev = call(
+        pack_kernel,
+        (layers, layers),
+        [(ROWS, NY, NZ), (2, ROWS, NY, NZ)],
+        (where, in_hbm(viscosity), in_hbm(forcing)),
+        in_specs=[SMEM, ANY, ANY],
+        out_specs=(HBM, HBM),
+        micros=2,
+        sems=8,
+        mib=4,
+    )
+    od_e, ev_e, to_od, to_ev = lax.optimization_barrier((od_e, ev_e, to_od, to_ev))
+    od = lax.ppermute(to_od, "slab", others)
+    ev = lax.ppermute(to_ev, "slab", mates)
+    first, second = call(
+        corner_kernel,
+        (f32(40, NZ), f32(40, NZ)),
+        [(40, NZ), (40, NZ)],
+        (where, edges, od_e, ev_e),
+        in_specs=[SMEM] + [VMEM] * 3,
+        mib=4,
+    )
+    first = lax.ppermute(first, "cross", pairs(cross, 0))
+    second = lax.ppermute(second, "cross", pairs(cross, 1))
 
     kept = (f32(10, FRAME, NZ), f32(8, FRAME, NZ), f32(8, FRAME, NZ)) + (f32(7, FRAME, NZ),) * 3
-    part, to_od, to_ev, v, d, fz, h0, ex, ez = call(
+    part, v, d, fz, h0, ex, ez = call(
         stencil_kernel,
-        (f32(10, 4, NZ), *[pltpu.HBM((2, 2, NY, NZ), jnp.float32)] * 2, *[pltpu.HBM(x.shape, x.dtype) for x in kept]),
+        (f32(10, 4, NZ), *[pltpu.HBM(x.shape, x.dtype) for x in kept]),
         [x.shape for x in kept] + [(7, FRAME, NZ), (32, 1, NZ), (2, ROWS, NY, NZ)],
-        (where, in_hbm(viscosity), od, ev, lo, hi, in_hbm(forcing)),
+        (where, in_hbm(viscosity), od, ev, first, second, in_hbm(forcing)),
         in_specs=[SMEM, ANY, ANY, ANY, VMEM, VMEM, ANY],
-        out_specs=(VMEM,) + (HBM,) * 8,
+        out_specs=(VMEM,) + (HBM,) * 6,
         micros=6,
-        sems=12,
+        sems=10,
     )
 
     width = owner_slot.shape[0] // cross
@@ -498,50 +528,42 @@
     part, onehot = lax.optimization_barrier((part, onehot))
     got = among(part, 1)
     part = part + got[0] + got[1] + got[2]
-    part, to_od, to_ev = lax.optimization_barrier((part, to_od, to_ev))
-    od_f = lax.ppermute(to_od, "slab", others)
-    ev_f = lax.ppermute(to_ev, "slab", mates)
     got = among(part, 4)
-    got, od_f, ev_f = lax.optimization_barrier((got, od_f, ev_f))
+    forced = call(
+        forced_kernel,
+        f32(2, ROWS, NY, NZ),
+        [x.shape for x in kept[:3]] + [(2, 8, FRAME, NZ)] * 2,
+        (where, in_hbm(forcing), od, ev, first, second, in_hbm(v), in_hbm(d), in_hbm(fz)),
+        in_specs=[SMEM] + [ANY] * 3 + [VMEM] * 2 + [ANY] * 3,
+        micros=5,
+        sems=9,
+    )
+    got, forced = lax.optimization_barrier((got, forced))
     part = part + got[0] + got[1] + got[2]
 
     mate = lax.ppermute(part, "slab", mates)
     both = jnp.stack([part, mate])
-    below = lax.ppermute(both, "slab", chip_up)
-    above = lax.ppermute(both, "slab", chip_down)
+    window = (lax.ppermute(both, "slab", first_chips), lax.ppermute(both, "slab", second_chips))
     basis, dots = call(
         krylov_kernel,
         (f32(48, NZ), f32(chips, 8, 128)),
         [(7, 24, NZ), (40, NZ)],
-        (where, part, mate, below[0], below[1], above[0], above[1]),
-        in_specs=[SMEM] + [VMEM] * 6,
+        (where, part, mate, *window),
+        in_specs=[SMEM] + [VMEM] * 4,
         mib=4,
-    )
-    dots, od_f, ev_f = lax.optimization_barrier((dots, od_f, ev_f))
-    forced = call(
-        forced_kernel,
-        pltpu.HBM((2, ROWS, NY, NZ), jnp.float32),
-        [x.shape for x in kept[:3]] + [(2, 8, FRAME, NZ)] * 2 + [(2, ROWS, NY, NZ)],
-        (where, in_hbm(forcing), in_hbm(od_f), in_hbm(ev_f), lo, hi, in_hbm(v), in_hbm(d), in_hbm(fz)),
-        in_specs=[SMEM] + [ANY] * 3 + [VMEM] * 2 + [ANY] * 3,
-        out_specs=HBM,
-        micros=5,
-        sems=11,
     )
     groups = [[2 * z + c for z in range(chips)] for c in range(2)]
     dots = lax.all_to_all(dots, "slab", 0, 0, tiled=True, axis_index_groups=groups)
 
-    big = (h0, ex, ez, v, d, fz, forced)
     return call(
         velocity_kernel,
         (pltpu.HBM((2, ROWS, NY, NZ), jnp.float32), f32(ROWS, width)),
-        [x.shape for x in big] + [(2, ROWS, NY, NZ), (2, 8, FRAME, NZ), (16, NZ), (32, NZ)],
-        (basis, dots, onehot, *[in_hbm(x) for x in big]),
-        in_specs=[VMEM] * 3 + [ANY] * 7,
+        [(2, ROWS, NY, NZ), (2, 8, FRAME, NZ), (16, NZ), (32, NZ)],
+        (basis, dots, onehot, h0, ex, ez, v, d, fz, forced),
+        in_specs=[VMEM] * 10,
         out_specs=(HBM, VMEM),
         micros=4,
-        sems=11,
-        mib=24,
+        sems=4,
     )
 
 

time: 119 us -> 88.3 us (0.74)
  Pallas kernels: 53 us -> 26.5 us
  starting transfers between devices: 47.5 us -> 26.1 us
  blocking collectives: 0 us -> 19.8 us
  waiting for transfers between devices: 16.9 us -> 14.3 us
    pallas_call x6 -> x7, Pallas kernels: 53 us -> 26.5 us  [call(): pl.pallas_call(kernel, out_shape=out_shape, in_specs=in_specs, out_specs=...]
    all_to_all x0 -> x1, blocking collectives: none -> 19.8 us  [shards(): lax.all_to_all(dots, 'slab', 0, 0, tiled=True, axis_index_groups=groups)]
    ppermute x8 -> x6, starting transfers between devices: 25.8 us -> 13 us  [the longest x1 3.88 us: shards(): second = lax.ppermute(second, 'cross', pairs(cross, 1))]
    all_to_all x1 -> x0, starting transfers between devices: 11.4 us -> none  [shards(): lax.all_to_all(dots, 'slab', 0, 0, tiled=True, axis_index_groups=groups)]
    ppermute x6, waiting for transfers between devices: 9.25 us -> 4.83 us  [among(): lax.ppermute(x, 'cross', [(i, i ^ n * step) for i in range(cross)])]
    ppermute x1, starting transfers between devices: 0.09 us -> 3.36 us  [shards(): ev_e = lax.ppermute(edges, 'slab', mates)]
    ppermute x8 -> x6, waiting for transfers between devices: 5.35 us -> 8.25 us  [the longest x1 4.39 us: shards(): second = lax.ppermute(second, 'cross', pairs(cross, 1))]
  transfers between devices with their start and end apart: 18 -> 15, of which waited for: 12 -> 5; matrix products, arithmetic and copies ran while one was open for 0% -> 0% of each run, Pallas kernels for 7% -> 12%
where the time goes in v4:
time: 88.3 us; the launch traced here: 88 us
  Pallas kernels  26.5 us (30%)
  starting transfers between devices  26.1 us (30%)
  blocking collectives  19.8 us (22%)
  waiting for transfers between devices  14.3 us (16%)
  between operations  0.9 us (1%)
    pallas_call x7, Pallas kernels, call(): pl.pallas_call(kernel, out_shape=out_shape, in_specs=in_specs, out_specs=...  26.5 us
    all_to_all x1, blocking collectives, shards(): lax.all_to_all(dots, 'slab', 0, 0, tiled=True, axis_index_groups=groups)  19.8 us
    ppermute x6, starting transfers between devices, among(): lax.ppermute(x, 'cross', [(i, i ^ n * step) for i in range(cross)])  8.97 us
    ppermute x6, waiting for transfers between devices, among(): lax.ppermute(x, 'cross', [(i, i ^ n * step) for i in range(cross)])  4.83 us
    ppermute x1, waiting for transfers between devices, shards(): second = lax.ppermute(second, 'cross', pairs(cross, 1))  4.39 us
    ppermute x1, starting transfers between devices, shards(): second = lax.ppermute(second, 'cross', pairs(cross, 1))  3.88 us
    ppermute x1, waiting for transfers between devices, shards(): lax.ppermute(both, 'slab', first_chips)  3.85 us
    ppermute x1, starting transfers between devices, shards(): ev_e = lax.ppermute(edges, 'slab', mates)  3.36 us
  transfers between devices with their start and end apart: 15, of which 5 were waited for; matrix products, arithmetic and copies ran while one was open for 0% of the time, Pallas kernels for 12%

profile of v4, /device:TPU:16, one launch (start us, length us, event | category | flops | bytes accessed | tf_op | source)
XLA Modules:
  0.0 88.0 jit_solution(5713444623095576487)
XLA Ops:
  0.7 1.7 %shard_map.50.own = f32[4,14,512]{2,1,0:T(8,128)S(1)} custom-call(s32[4]{0:T(128)S(1)} %pad_add_fusion.par_ref, f32[4,64,512]{2,1,0:T(8,128)} %own.3, f32[2,4,64,512]{3,2,1,0:T(8,128)} %f.3), custom_call_target="tpu_custom_call" | custom-call | bytes 3600000 | tf_op jit(solution)/shard_map/pallas_call | solution.py:437
  2.4 0.7 collective-permute-start
  3.1 3.4 %collective-permute-start.1 = (f32[4,14,512]{2,1,0:T(8,128)S(1)}, f32[4,14,512]{2,1,0:T(8,128)S(1)}, u32[]{:S(2)}, u32[]{:S(2)}) collective-permute-start(f32[4,14,512]{2,1,0:T(8,128)S(1)} %shard_map.50.own), channel_id=1, source_target_pairs={{0,16},{32,48},{64,80},{96,112},{128,144},{160,176},{192,208},{224... | collective-permute-start | bytes 344072 | tf_op jit(solution)/shard_map/ppermute | solution.py:482
  6.5 3.2 %shard_map.51 = (f32[7,64,512]{2,1,0:T(8,128)}, f32[7,64,512]{2,1,0:T(8,128)}) custom-call(s32[4]{0:T(128)S(1)} %pad_add_fusion.par_ref, f32[4,64,512]{2,1,0:T(8,128)} %own.3, f32[2,4,64,512]{3,2,1,0:T(8,128)} %f.3), custom_call_target="tpu_custom_call" | custom-call | bytes 7200000 | tf_op jit(solution)/shard_map/pallas_call | solution.py:437
  9.7 0.7 collective-permute-start.2
  10.5 3.3 %collective-permute-start.3 = (f32[7,64,512]{2,1,0:T(8,128)}, f32[7,64,512]{2,1,0:T(8,128)S(1)}, u32[]{:S(2)}, u32[]{:S(2)}) collective-permute-start(f32[7,64,512]{2,1,0:T(8,128)} %get-tuple-element.28), channel_id=1, source_target_pairs={{0,16},{32,48},{64,80},{96,112},{128,144},{160,176},{192,208},{224... | collective-permute-start | bytes 2752520 | tf_op jit(solution)/shard_map/ppermute | solution.py:497
  14.4 1.6 %collective-permute-start.4 = (f32[40,512]{1,0:T(8,128)S(1)}, f32[40,512]{1,0:T(8,128)S(1)}, u32[]{:S(2)}, u32[]{:S(2)}) collective-permute-start(f32[40,512]{1,0:T(8,128)S(1)} %get-tuple-element.31), channel_id=1, source_target_pairs={{0,1},{2,3},{4,5},{6,7},{8,9},{10,11},{12,13},{14,15},{1,0},{3,2},... | collective-permute-start | bytes 245768 | tf_op jit(solution)/shard_map/ppermute | solution.py:506
  15.9 3.9 %collective-permute-start.5 = (f32[40,512]{1,0:T(8,128)S(1)}, f32[40,512]{1,0:T(8,128)S(1)}, u32[]{:S(2)}, u32[]{:S(2)}) collective-permute-start(f32[40,512]{1,0:T(8,128)S(1)} %get-tuple-element.32), channel_id=1, source_target_pairs={{1,2},{3,4},{5,6},{7,8},{9,10},{11,12},{13,14},{2,1},{4,3},{6,5},{... | collective-permute-start | bytes 245768 | tf_op jit(solution)/shard_map/ppermute | solution.py:507
  20.0 4.4 %collective-permute-done.5.second = f32[40,512]{1,0:T(8,128)S(1)} collective-permute-done((f32[40,512]{1,0:T(8,128)S(1)}, f32[40,512]{1,0:T(8,128)S(1)}, u32[]{:S(2)}, u32[]{:S(2)}) %collective-permute-start.5) | collective-permute-done | bytes 81952 | tf_op jit(solution)/shard_map/ppermute | solution.py:507
  24.4 9.2 %shard_map.53 = (f32[10,4,512]{2,1,0:T(4,128)S(1)}, f32[10,80,512]{2,1,0:T(8,128)}, f32[8,80,512]{2,1,0:T(8,128)}, f32[8,80,512]{2,1,0:T(8,128)}, f32[7,80,512]{...) custom-call(s32[4]{0:T(128)S(1)} %pad_add_fusion.par_ref, f32[4,64,512]{2,1,0:T(8,128)} %own.3, ...), custom_call_target="tpu_custom_call" | custom-call | bytes 21600000 | tf_op jit(solution)/shard_map/pallas_call | solution.py:437
  33.6 2.2 %collective-permute-start.8 = (f32[10,4,512]{2,1,0:T(4,128)S(1)}, f32[10,4,512]{2,1,0:T(4,128)S(1)}, u32[]{:S(2)}, u32[]{:S(2)}) collective-permute-start(f32[10,4,512]{2,1,0:T(4,128)S(1)} %get-tuple-element.34), channel_id=1, source_target_pairs={{0,3},{1,2},{2,1},{3,0},{4,7},{5,6},{6,5},{7,4},{8,11},{9,10},{10,... | collective-permute-start | bytes 245768 | tf_op jit(solution)/shard_map/ppermute | solution.py:526
  35.8 2.0 %collective-permute-start.6 = (f32[10,4,512]{2,1,0:T(4,128)S(1)}, f32[10,4,512]{2,1,0:T(4,128)S(1)}, u32[]{:S(2)}, u32[]{:S(2)}) collective-permute-start(f32[10,4,512]{2,1,0:T(4,128)S(1)} %get-tuple-element.34), channel_id=1, source_target_pairs={{0,1},{1,0},{2,3},{3,2},{4,5},{5,4},{6,7},{7,6},{8,9},{9,8},{10,11... | collective-permute-start | bytes 245768 | tf_op jit(solution)/shard_map/ppermute | solution.py:526
  37.8 2.0 %collective-permute-done.8 = f32[10,4,512]{2,1,0:T(4,128)S(1)} collective-permute-done((f32[10,4,512]{2,1,0:T(4,128)S(1)}, f32[10,4,512]{2,1,0:T(4,128)S(1)}, u32[]{:S(2)}, u32[]{:S(2)}) %collective-permute-start.8) | collective-permute-done | bytes 81952 | tf_op jit(solution)/shard_map/ppermute | solution.py:526
  39.8 2.8 %collective-permute-done.7 = f32[10,4,512]{2,1,0:T(4,128)S(1)} collective-permute-done((f32[10,4,512]{2,1,0:T(4,128)S(1)}, f32[10,4,512]{2,1,0:T(4,128)S(1)}, u32[]{:S(2)}, u32[]{:S(2)}) %collective-permute-start.7) | collective-permute-done | bytes 81952 | tf_op jit(solution)/shard_map/ppermute | solution.py:526
  43.0 2.0 %collective-permute-start.11 = (f32[10,4,512]{2,1,0:T(4,128)S(1)}, f32[10,4,512]{2,1,0:T(4,128)S(1)}, u32[]{:S(2)}, u32[]{:S(2)}) collective-permute-start(f32[10,4,512]{2,1,0:T(4,128)S(1)} %bitcast.22), channel_id=1, source_target_pairs={{0,12},{1,13},{2,14},{3,15},{4,8},{5,9},{6,10},{7,11},{8,4},{9,5},... | collective-permute-start | bytes 245768 | tf_op jit(solution)/shard_map/ppermute | solution.py:526
  45.0 2.4 %collective-permute-start.9 = (f32[10,4,512]{2,1,0:T(4,128)S(1)}, f32[10,4,512]{2,1,0:T(4,128)S(1)}, u32[]{:S(2)}, u32[]{:S(2)}) collective-permute-start(f32[10,4,512]{2,1,0:T(4,128)S(1)} %bitcast.23), channel_id=1, source_target_pairs={{0,4},{1,5},{2,6},{3,7},{4,0},{5,1},{6,2},{7,3},{8,12},{9,13},{10,... | collective-permute-start | bytes 245768 | tf_op jit(solution)/shard_map/ppermute | solution.py:526
  47.4 6.9 %shard_map.54.forced = f32[2,4,64,512]{3,2,1,0:T(8,128)S(1)} custom-call(s32[4]{0:T(128)S(1)} %pad_add_fusion.par_ref, f32[2,4,64,512]{3,2,1,0:T(8,128)} %f.3, f32[7,64,512]{2,1,0:T(8,128)S(1)} %collective-permute-done.2.od, f32[7,64,512]{2,1,0:T(8,128)S(1)} %collective-permute-done.3.ev, f32[40,512]{1,0:T(8,128)S(1)} %collective-permute-done.4.first, ...), custom_call_target="tpu_custom_call" | custom-call | bytes 18000000 | tf_op jit(solution)/shard_map/pallas_call | solution.py:437
  54.5 1.3 %collective-permute-done.12.mate = f32[10,4,512]{2,1,0:T(4,128)S(1)} collective-permute-done((f32[10,4,512]{2,1,0:T(4,128)S(1)}, f32[10,4,512]{2,1,0:T(4,128)S(1)}, u32[]{:S(2)}, u32[]{:S(2)}) %collective-permute-start.12) | collective-permute-done | bytes 81952 | tf_op jit(solution)/shard_map/ppermute | solution.py:544
  55.8 2.9 %collective-permute-start.13 = (f32[2,10,4,512]{3,2,1,0:T(4,128)S(1)}, f32[2,10,4,512]{3,2,1,0:T(4,128)S(1)}, u32[]{:S(2)}, u32[]{:S(2)}) collective-permute-start(f32[2,10,4,512]{3,2,1,0:T(4,128)S(1)} %pad_maximum_fusion), channel_id=1, source_target_pairs={{0,32},{16,48},{64,96},{80,112},{128,160},{144,176},{192,224},{208... | collective-permute-start | bytes 491528 | tf_op jit(solution)/shard_map/ppermute | solution.py:546
  58.7 0.7 collective-permute-start.14
  59.3 3.9 %collective-permute-done.13.first = f32[2,10,4,512]{3,2,1,0:T(4,128)S(1)} collective-permute-done((f32[2,10,4,512]{3,2,1,0:T(4,128)S(1)}, f32[2,10,4,512]{3,2,1,0:T(4,128)S(1)}, u32[]{:S(2)}, u32[]{:S(2)}) %collective-permute-start.13) | collective-permute-done | bytes 163872 | tf_op jit(solution)/shard_map/ppermute | solution.py:546
  63.2 1.2 %shard_map.55 = (f32[48,512]{1,0:T(8,128)S(1)}, f32[8,8,128]{2,1,0:T(8,128)S(1)}) custom-call(s32[4]{0:T(128)S(1)} %pad_add_fusion.par_ref, f32[10,4,512]{2,1,0:T(4,128)S(1)} %bitcast.18, f32[10,4,512]{2,1,0:T(4,128)S(1)} %collective-permute-done.12.mate, f32[2,10,4,512]{3,2,1,0:T(4,128)S(1)} %collective-permute-done.13.first, ...), custom_call_target="tpu_custom_call" | custom-call | bytes 3600000 | tf_op jit(solution)/shard_map/pallas_call | solution.py:437
  64.4 19.8 %all_to_all.5.dots = f32[8,8,128]{2,1,0:T(8,128)S(1)} all-to-all(f32[8,8,128]{2,1,0:T(8,128)S(1)} %get-tuple-element.42), channel_id=1, replica_groups={{0,32,64,96,128,160,192,224},{16,48,80,112,144,176,208,240},{1,33,65,97..., dimensions={0} | all-to-all | bytes 65536 | tf_op jit(solution)/shard_map/all_to_all | solution.py:556
  84.2 3.8 %shard_map.56 = (f32[2,4,64,512]{3,2,1,0:T(8,128)}, f32[4,32]{1,0:T(4,128)}) custom-call(f32[48,512]{1,0:T(8,128)S(1)} %get-tuple-element.41.basis, f32[8,8,128]{2,1,0:T(8,128)S(1)} %all_to_all.5.dots, f32[512,32]{1,0:T(8,128)S(1)} %compare_convert_fusion.onehot, f32[7,80,512]{2,1,0:T(8,128)S(1)} %copy-done.3, f32[7,80,512]{2,1,0:T(8,128)S(1)} %copy-done.4, ...), custom_call_target="tpu_custom_call" | custom-call | bytes 14400000 | tf_op jit(solution)/shard_map/pallas_call | solution.py:437
  (34 shorter events, 1.5 us)
Async XLA Ops:
  2.4 17.4 %copy-start.6 = (s32[512]{0:T(512)S(1)}, s32[512]{0:T(512)}, u32[]{:S(2)}) copy-start(s32[512]{0:T(512)} %param.5) | copy-start | bytes 6148
  2.4 7.3 %collective-permute-start = (f32[4,14,512]{2,1,0:T(8,128)S(1)}, f32[4,14,512]{2,1,0:T(8,128)S(1)}, u32[]{:S(2)}, u32[]{:S(2)}) collective-permute-start(f32[4,14,512]{2,1,0:T(8,128)S(1)} %shard_map.50.own), channel_id=1, source_target_pairs={{16,32},{48,64},{80,96},{112,128},{144,160},{176,192},{208,224},{3... | collective-permute-start | bytes 344072 | tf_op jit(solution)/shard_map/ppermute | solution.py:481
  3.1 6.6 %collective-permute-start.1 = (f32[4,14,512]{2,1,0:T(8,128)S(1)}, f32[4,14,512]{2,1,0:T(8,128)S(1)}, u32[]{:S(2)}, u32[]{:S(2)}) collective-permute-start(f32[4,14,512]{2,1,0:T(8,128)S(1)} %shard_map.50.own), channel_id=1, source_target_pairs={{0,16},{32,48},{64,80},{96,112},{128,144},{160,176},{192,208},{224... | collective-permute-start | bytes 344072 | tf_op jit(solution)/shard_map/ppermute | solution.py:482
  9.7 14.7 %collective-permute-start.2 = (f32[7,64,512]{2,1,0:T(8,128)}, f32[7,64,512]{2,1,0:T(8,128)S(1)}, u32[]{:S(2)}, u32[]{:S(2)}) collective-permute-start(f32[7,64,512]{2,1,0:T(8,128)} %get-tuple-element.27), channel_id=1, source_target_pairs={{16,32},{48,64},{80,96},{112,128},{144,160},{176,192},{208,224},{3... | collective-permute-start | bytes 2752520 | tf_op jit(solution)/shard_map/ppermute | solution.py:496
  10.5 13.9 %collective-permute-start.3 = (f32[7,64,512]{2,1,0:T(8,128)}, f32[7,64,512]{2,1,0:T(8,128)S(1)}, u32[]{:S(2)}, u32[]{:S(2)}) collective-permute-start(f32[7,64,512]{2,1,0:T(8,128)} %get-tuple-element.28), channel_id=1, source_target_pairs={{0,16},{32,48},{64,80},{96,112},{128,144},{160,176},{192,208},{224... | collective-permute-start | bytes 2752520 | tf_op jit(solution)/shard_map/ppermute | solution.py:497
  14.4 5.6 %collective-permute-start.4 = (f32[40,512]{1,0:T(8,128)S(1)}, f32[40,512]{1,0:T(8,128)S(1)}, u32[]{:S(2)}, u32[]{:S(2)}) collective-permute-start(f32[40,512]{1,0:T(8,128)S(1)} %get-tuple-element.31), channel_id=1, source_target_pairs={{0,1},{2,3},{4,5},{6,7},{8,9},{10,11},{12,13},{14,15},{1,0},{3,2},... | collective-permute-start | bytes 245768 | tf_op jit(solution)/shard_map/ppermute | solution.py:506
  15.9 8.4 %collective-permute-start.5 = (f32[40,512]{1,0:T(8,128)S(1)}, f32[40,512]{1,0:T(8,128)S(1)}, u32[]{:S(2)}, u32[]{:S(2)}) collective-permute-start(f32[40,512]{1,0:T(8,128)S(1)} %get-tuple-element.32), channel_id=1, source_target_pairs={{1,2},{3,4},{5,6},{7,8},{9,10},{11,12},{13,14},{2,1},{4,3},{6,5},{... | collective-permute-start | bytes 245768 | tf_op jit(solution)/shard_map/ppermute | solution.py:507
  33.6 6.2 %collective-permute-start.8 = (f32[10,4,512]{2,1,0:T(4,128)S(1)}, f32[10,4,512]{2,1,0:T(4,128)S(1)}, u32[]{:S(2)}, u32[]{:S(2)}) collective-permute-start(f32[10,4,512]{2,1,0:T(4,128)S(1)} %get-tuple-element.34), channel_id=1, source_target_pairs={{0,3},{1,2},{2,1},{3,0},{4,7},{5,6},{6,5},{7,4},{8,11},{9,10},{10,... | collective-permute-start | bytes 245768 | tf_op jit(solution)/shard_map/ppermute | solution.py:526
  35.8 6.8 %collective-permute-start.7 = (f32[10,4,512]{2,1,0:T(4,128)S(1)}, f32[10,4,512]{2,1,0:T(4,128)S(1)}, u32[]{:S(2)}, u32[]{:S(2)}) collective-permute-start(f32[10,4,512]{2,1,0:T(4,128)S(1)} %get-tuple-element.34), channel_id=1, source_target_pairs={{0,2},{1,3},{2,0},{3,1},{4,6},{5,7},{6,4},{7,5},{8,10},{9,11},{10,... | collective-permute-start | bytes 245768 | tf_op jit(solution)/shard_map/ppermute | solution.py:526
  35.8 6.8 %collective-permute-start.6 = (f32[10,4,512]{2,1,0:T(4,128)S(1)}, f32[10,4,512]{2,1,0:T(4,128)S(1)}, u32[]{:S(2)}, u32[]{:S(2)}) collective-permute-start(f32[10,4,512]{2,1,0:T(4,128)S(1)} %get-tuple-element.34), channel_id=1, source_target_pairs={{0,1},{1,0},{2,3},{3,2},{4,5},{5,4},{6,7},{7,6},{8,9},{9,8},{10,11... | collective-permute-start | bytes 245768 | tf_op jit(solution)/shard_map/ppermute | solution.py:526
  42.6 11.7 %collective-permute-start.10 = (f32[10,4,512]{2,1,0:T(4,128)S(1)}, f32[10,4,512]{2,1,0:T(4,128)S(1)}, u32[]{:S(2)}, u32[]{:S(2)}) collective-permute-start(f32[10,4,512]{2,1,0:T(4,128)S(1)} %bitcast.21), channel_id=1, source_target_pairs={{0,8},{1,9},{2,10},{3,11},{4,12},{5,13},{6,14},{7,15},{8,0},{9,1},... | collective-permute-start | bytes 245768 | tf_op jit(solution)/shard_map/ppermute | solution.py:526
  43.0 11.3 %collective-permute-start.11 = (f32[10,4,512]{2,1,0:T(4,128)S(1)}, f32[10,4,512]{2,1,0:T(4,128)S(1)}, u32[]{:S(2)}, u32[]{:S(2)}) collective-permute-start(f32[10,4,512]{2,1,0:T(4,128)S(1)} %bitcast.22), channel_id=1, source_target_pairs={{0,12},{1,13},{2,14},{3,15},{4,8},{5,9},{6,10},{7,11},{8,4},{9,5},... | collective-permute-start | bytes 245768 | tf_op jit(solution)/shard_map/ppermute | solution.py:526
  45.0 9.3 %collective-permute-start.9 = (f32[10,4,512]{2,1,0:T(4,128)S(1)}, f32[10,4,512]{2,1,0:T(4,128)S(1)}, u32[]{:S(2)}, u32[]{:S(2)}) collective-permute-start(f32[10,4,512]{2,1,0:T(4,128)S(1)} %bitcast.23), channel_id=1, source_target_pairs={{0,4},{1,5},{2,6},{3,7},{4,0},{5,1},{6,2},{7,3},{8,12},{9,13},{10,... | collective-permute-start | bytes 245768 | tf_op jit(solution)/shard_map/ppermute | solution.py:526
  47.4 36.8 %copy-start = (f32[10,80,512]{2,1,0:T(8,128)S(1)}, f32[10,80,512]{2,1,0:T(8,128)}, u32[]{:S(2)}) copy-start(f32[10,80,512]{2,1,0:T(8,128)} %get-tuple-element.35.v_hbm.v) | copy-start | bytes 4915204
  47.4 36.8 %copy-start.2 = (f32[8,80,512]{2,1,0:T(8,128)S(1)}, f32[8,80,512]{2,1,0:T(8,128)}, u32[]{:S(2)}) copy-start(f32[8,80,512]{2,1,0:T(8,128)} %get-tuple-element.37.fz_hbm.fz) | copy-start | bytes 3932164
  47.4 36.8 %copy-start.3 = (f32[7,80,512]{2,1,0:T(8,128)S(1)}, f32[7,80,512]{2,1,0:T(8,128)}, u32[]{:S(2)}) copy-start(f32[7,80,512]{2,1,0:T(8,128)} %get-tuple-element.44.h0) | copy-start | bytes 3440644
  47.4 36.8 %copy-start.4 = (f32[7,80,512]{2,1,0:T(8,128)S(1)}, f32[7,80,512]{2,1,0:T(8,128)}, u32[]{:S(2)}) copy-start(f32[7,80,512]{2,1,0:T(8,128)} %get-tuple-element.45.ex) | copy-start | bytes 3440644
  47.4 36.8 %copy-start.5 = (f32[7,80,512]{2,1,0:T(8,128)S(1)}, f32[7,80,512]{2,1,0:T(8,128)}, u32[]{:S(2)}) copy-start(f32[7,80,512]{2,1,0:T(8,128)} %get-tuple-element.46.ez) | copy-start | bytes 3440644
  54.3 29.9 %copy-start.1 = (f32[8,80,512]{2,1,0:T(8,128)S(1)}, f32[8,80,512]{2,1,0:T(8,128)}, u32[]{:S(2)}) copy-start(f32[8,80,512]{2,1,0:T(8,128)} %get-tuple-element.36.d_hbm.d) | copy-start | bytes 3932164
  54.4 1.4 %collective-permute-start.12 = (f32[10,4,512]{2,1,0:T(4,128)S(1)}, f32[10,4,512]{2,1,0:T(4,128)S(1)}, u32[]{:S(2)}, u32[]{:S(2)}) collective-permute-start(f32[10,4,512]{2,1,0:T(4,128)S(1)} %bitcast.16), channel_id=1, source_target_pairs={{0,16},{32,48},{64,80},{96,112},{128,144},{160,176},{192,208},{224... | collective-permute-start | bytes 245768 | tf_op jit(solution)/shard_map/ppermute | solution.py:544
  55.8 7.4 %collective-permute-start.13 = (f32[2,10,4,512]{3,2,1,0:T(4,128)S(1)}, f32[2,10,4,512]{3,2,1,0:T(4,128)S(1)}, u32[]{:S(2)}, u32[]{:S(2)}) collective-permute-start(f32[2,10,4,512]{3,2,1,0:T(4,128)S(1)} %pad_maximum_fusion), channel_id=1, source_target_pairs={{0,32},{16,48},{64,96},{80,112},{128,160},{144,176},{192,224},{208... | collective-permute-start | bytes 491528 | tf_op jit(solution)/shard_map/ppermute | solution.py:546
  58.7 4.5 %collective-permute-start.14 = (f32[2,10,4,512]{3,2,1,0:T(4,128)S(1)}, f32[2,10,4,512]{3,2,1,0:T(4,128)S(1)}, u32[]{:S(2)}, u32[]{:S(2)}) collective-permute-start(f32[2,10,4,512]{3,2,1,0:T(4,128)S(1)} %pad_maximum_fusion), channel_id=1, source_target_pairs={{32,64},{48,80},{96,128},{112,144},{160,192},{176,208},{64,32},{80... | collective-permute-start | bytes 491528 | tf_op jit(solution)/shard_map/ppermute | solution.py:546

commit v5 on v4

--- a/solution.py
+++ b/solution.py
@@ -69,23 +69,20 @@
 
 def pack_kernel(par_ref, own_hbm, f_hbm, to_od, to_ev, own, f, sems):
     par = par_ref[0]
-    loads = [pltpu.make_async_copy(own_hbm, own, sems.at[0]), pltpu.make_async_copy(f_hbm, f, sems.at[1])]
-    for copy in loads:
-        copy.start()
-    saves = []
+    copies = []
     for n, (out, last) in enumerate(((to_od, par), (to_ev, 1 - par))):
-        saves.append(pltpu.make_async_copy(own.at[pl.ds(last, 3)], out.at[0:3], sems.at[2 + 3 * n]))
+        copies.append(pltpu.make_async_copy(own_hbm.at[pl.ds(last, 3)], out.at[0:3], sems.at[3 * n]))
         for c in range(2):
-            saves.append(
+            copies.append(
                 pltpu.make_async_copy(
-                    f.at[c, pl.ds(2 * last, 2)], out.at[3 + 2 * c : 5 + 2 * c], sems.at[3 + 3 * n + c]
+                    f_hbm.at[c, pl.ds(2 * last, 2)], out.at[3 + 2 * c : 5 + 2 * c], sems.at[1 + 3 * n + c]
                 )
             )
-    for copy in loads:
-        copy.wait()
-    for copy in saves:
+    copies.append(pltpu.make_async_copy(own_hbm, own, sems.at[6]))
+    copies.append(pltpu.make_async_copy(f_hbm, f, sems.at[7]))
+    for copy in copies:
         copy.start()
-    for copy in saves:
+    for copy in copies:
         copy.wait()
 
 
@@ -148,11 +145,8 @@
     lax.fori_loop(0, 8, layer, 0)
 
 
-def stencil_kernel(par_ref, own, od, ev, first, second, f_hbm, out, *rest):
-    kept_hbm, (v, d, fz, h0, ex, ez, ezm, acc, f, sems) = rest[:6], rest[6:]
+def stencil_kernel(par_ref, own, od, ev, first, second, f, out, v, d, fz, h0, ex, ez, ezm, acc, sems):
     par = par_ref[0]
-    load = pltpu.make_async_copy(f_hbm, f, sems.at[3])
-    load.start()
     lo, hi = sides(par_ref[2] == 1, first, second)
     fill_viscosity(par, v, own, od, ev, lo, hi, sems)
     fill_inverse(v, d, fz)
@@ -170,10 +164,6 @@
 
     lax.fori_loop(0, 7, edges, 0)
 
-    saves = [pltpu.make_async_copy(x, y, sems.at[4 + n]) for n, (x, y) in enumerate(zip((v, d, fz, h0, ex, ez), kept_hbm))]
-    for copy in saves:
-        copy.start()
-    load.wait()
     acc[...] = jnp.zeros_like(acc)
     own_rows = slice(LO, HI)
     above = slice(LO + 1, HI + 1)
@@ -238,8 +228,6 @@
     out[7:9] = e[0:8].reshape(2, 4, NZ)
     out[9, 0:1] = e[8:9]
     out[9, 1:4] = jnp.zeros((3, NZ), jnp.float32)
-    for copy in saves:
-        copy.wait()
 
 
 def krylov_kernel(par_ref, mine, mate, first, second, basis, dots, s_ref, g_ref):
@@ -314,35 +302,28 @@
     dots[...] = jnp.broadcast_to(packed[None], dots.shape)
 
 
-def forced_kernel(par_ref, f, od, ev, first, second, v_hbm, d_hbm, fz_hbm, out, v, d, fz, u, t, sems):
+def forced_kernel(par_ref, f, od, ev, first, second, v, d, fz, out, u, t):
     par = par_ref[0]
-    copies = [pltpu.make_async_copy(x, y, sems.at[n]) for n, (x, y) in enumerate(((d_hbm, d), (v_hbm, v), (fz_hbm, fz)))]
-    for c in range(2):
-        copies.append(pltpu.make_async_copy(f.at[c], u.at[c, 2:6, LO:HI], sems.at[3 + c]))
-        for n, at, x in ((5, par * 6, od), (7, 6 - par * 6, ev)):
-            copies.append(
-                pltpu.make_async_copy(x.at[3 + 2 * c : 5 + 2 * c], u.at[c, pl.ds(at, 2), LO:HI], sems.at[n + c])
-            )
-    for copy in copies:
-        copy.start()
     lo, hi = sides(par_ref[2] == 1, first, second)
+
+    def scale(i, _):
+        dm = d[i + 2, LO:HI]
+        for c in range(2):
+            u[c, i + 2, LO:HI] = dm * f[c, i]
+        return 0
+
+    lax.fori_loop(0, ROWS, scale, 0)
+    for at, x in ((par * 6, od), (6 - par * 6, ev)):
+        dm = d[pl.ds(at, 2), LO:HI]
+        for c in range(2):
+            u[c, pl.ds(at, 2), LO:HI] = dm * x[3 + 2 * c : 5 + 2 * c]
     for c in range(2):
         for n in range(4):
-            u[c, 2 + n, LO - 2 : LO] = lo[7 * n + 3 + 2 * c : 7 * n + 5 + 2 * c]
-            u[c, 2 + n, HI : HI + 2] = hi[7 * n + 3 + 2 * c : 7 * n + 5 + 2 * c]
+            u[c, 2 + n, LO - 2 : LO] = d[2 + n, LO - 2 : LO] * lo[7 * n + 3 + 2 * c : 7 * n + 5 + 2 * c]
+            u[c, 2 + n, HI : HI + 2] = d[2 + n, HI : HI + 2] * hi[7 * n + 3 + 2 * c : 7 * n + 5 + 2 * c]
         for r, at in ((1, 30), (6, 34)):
-            u[c, r, LO - 1 : LO] = lo[at + c : at + c + 1]
-            u[c, r, HI : HI + 1] = hi[at + c : at + c + 1]
-    for copy in copies:
-        copy.wait()
-
-    def scale(r, _):
-        dm = d[r]
-        u[0, r] = dm * u[0, r]
-        u[1, r] = dm * u[1, r]
-        return 0
-
-    lax.fori_loop(0, 8, scale, 0)
+            u[c, r, LO - 1 : LO] = d[r, LO - 1 : LO] * lo[at + c : at + c + 1]
+            u[c, r, HI : HI + 1] = d[r, HI : HI + 1] * hi[at + c : at + c + 1]
 
     def first(r, _):
         vm = v[r + 1]
@@ -446,6 +427,10 @@
     )(*args)
 
 
+def in_vmem(x):
+    return pltpu.with_memory_space_constraint(x, pltpu.VMEM)
+
+
 def in_hbm(x):
     return pltpu.with_memory_space_constraint(x, pltpu.HBM)
 
@@ -480,14 +465,13 @@
     )
     od_e = lax.ppermute(edges, "slab", others)
     ev_e = lax.ppermute(edges, "slab", mates)
-    layers = pltpu.HBM((7, NY, NZ), jnp.float32)
-    to_od, to_ev = call(
+    layers = pltpu.VMEM((7, NY, NZ), jnp.float32)
+    to_od, to_ev, own, f = call(
         pack_kernel,
-        (layers, layers),
-        [(ROWS, NY, NZ), (2, ROWS, NY, NZ)],
+        (layers, layers, pltpu.VMEM(viscosity.shape, jnp.float32), pltpu.VMEM(forcing.shape, jnp.float32)),
+        [],
         (where, in_hbm(viscosity), in_hbm(forcing)),
         in_specs=[SMEM, ANY, ANY],
-        out_specs=(HBM, HBM),
         micros=2,
         sems=8,
         mib=4,
@@ -499,7 +483,7 @@
         corner_kernel,
         (f32(40, NZ), f32(40, NZ)),
         [(40, NZ), (40, NZ)],
-        (where, edges, od_e, ev_e),
+        (where, in_vmem(edges), in_vmem(od_e), in_vmem(ev_e)),
         in_specs=[SMEM] + [VMEM] * 3,
         mib=4,
     )
@@ -509,13 +493,13 @@
     kept = (f32(10, FRAME, NZ), f32(8, FRAME, NZ), f32(8, FRAME, NZ)) + (f32(7, FRAME, NZ),) * 3
     part, v, d, fz, h0, ex, ez = call(
         stencil_kernel,
-        (f32(10, 4, NZ), *[pltpu.HBM(x.shape, x.dtype) for x in kept]),
-        [x.shape for x in kept] + [(7, FRAME, NZ), (32, 1, NZ), (2, ROWS, NY, NZ)],
-        (where, in_hbm(viscosity), od, ev, first, second, in_hbm(forcing)),
-        in_specs=[SMEM, ANY, ANY, ANY, VMEM, VMEM, ANY],
-        out_specs=(VMEM,) + (HBM,) * 6,
+        (f32(10, 4, NZ), *[pltpu.VMEM(x.shape, x.dtype) for x in kept]),
+        [(7, FRAME, NZ), (32, 1, NZ)],
+        (where, in_vmem(own), in_vmem(od), in_vmem(ev), first, second, in_vmem(f)),
+        in_specs=[SMEM] + [VMEM] * 6,
         micros=6,
-        sems=10,
+        sems=4,
+        mib=6,
     )
 
     width = owner_slot.shape[0] // cross
@@ -531,12 +515,12 @@
     got = among(part, 4)
     forced = call(
         forced_kernel,
-        f32(2, ROWS, NY, NZ),
-        [x.shape for x in kept[:3]] + [(2, 8, FRAME, NZ)] * 2,
-        (where, in_hbm(forcing), od, ev, first, second, in_hbm(v), in_hbm(d), in_hbm(fz)),
-        in_specs=[SMEM] + [ANY] * 3 + [VMEM] * 2 + [ANY] * 3,
+        pltpu.VMEM((2, ROWS, NY, NZ), jnp.float32),
+        [(2, 8, FRAME, NZ)] * 2,
+        (where, in_vmem(f), in_vmem(od), in_vmem(ev), first, second, in_vmem(v), in_vmem(d), in_vmem(fz)),
+        in_specs=[SMEM] + [VMEM] * 8,
         micros=5,
-        sems=9,
+        mib=8,
     )
     got, forced = lax.optimization_barrier((got, forced))
     part = part + got[0] + got[1] + got[2]
@@ -559,11 +543,12 @@
         velocity_kernel,
         (pltpu.HBM((2, ROWS, NY, NZ), jnp.float32), f32(ROWS, width)),
         [(2, ROWS, NY, NZ), (2, 8, FRAME, NZ), (16, NZ), (32, NZ)],
-        (basis, dots, onehot, h0, ex, ez, v, d, fz, forced),
+        (basis, dots, onehot, *[in_vmem(x) for x in (h0, ex, ez, v, d, fz, forced)]),
         in_specs=[VMEM] * 10,
         out_specs=(HBM, VMEM),
         micros=4,
         sems=4,
+        mib=8,
     )
 
 

time: 88.3 us -> 86.8 us (0.983)
  local copies, waits for them, and re-layouts: 0.03 us -> 3.1 us
  Pallas kernels: 26.5 us -> 24.4 us
  blocking collectives: 19.8 us -> 18.9 us
  starting transfers between devices: 26.1 us -> 25.2 us
    unnamed x14 -> x10, local copies, waits for them, and re-layouts: 0.03 us -> 3.1 us
    pallas_call x7, Pallas kernels: 26.5 us -> 24.4 us  [call(): pl.pallas_call(kernel, out_shape=out_shape, in_specs=in_specs, out_specs=...]
    all_to_all x1, blocking collectives: 19.8 us -> 18.9 us  [shards(): lax.all_to_all(dots, 'slab', 0, 0, tiled=True, axis_index_groups=groups)]
  transfers between devices with their start and end apart: 15 -> 15, of which waited for: 5 -> 5; matrix products, arithmetic and copies ran while one was open for 0% -> 0% of each run, Pallas kernels for 12% -> 10%
where the time goes in v5:
time: 86.8 us; the launch traced here: 86.5 us
  starting transfers between devices  25.2 us (29%)
  Pallas kernels  24.4 us (28%)
  blocking collectives  18.9 us (22%)
  waiting for transfers between devices  13.7 us (16%)
  local copies, waits for them, and re-layouts  3.1 us (4%)
    pallas_call x7, Pallas kernels, call(): pl.pallas_call(kernel, out_shape=out_shape, in_specs=in_specs, out_specs=...  24.4 us
    all_to_all x1, blocking collectives, shards(): lax.all_to_all(dots, 'slab', 0, 0, tiled=True, axis_index_groups=groups)  18.9 us
    ppermute x6, starting transfers between devices, among(): lax.ppermute(x, 'cross', [(i, i ^ n * step) for i in range(cross)])  8.97 us
    ppermute x1, waiting for transfers between devices, shards(): second = lax.ppermute(second, 'cross', pairs(cross, 1))  4.39 us
    ppermute x6, waiting for transfers between devices, among(): lax.ppermute(x, 'cross', [(i, i ^ n * step) for i in range(cross)])  4.18 us
    ppermute x1, starting transfers between devices, shards(): second = lax.ppermute(second, 'cross', pairs(cross, 1))  3.88 us
    ppermute x1, waiting for transfers between devices, shards(): lax.ppermute(both, 'slab', first_chips)  3.85 us
    ppermute x1, starting transfers between devices, shards(): ev_e = lax.ppermute(edges, 'slab', mates)  3.36 us
  transfers between devices with their start and end apart: 15, of which 5 were waited for; matrix products, arithmetic and copies ran while one was open for 0% of the time, Pallas kernels for 10%

profile of v5, /device:TPU:16, one launch (start us, length us, event | category | flops | bytes accessed | tf_op | source)
XLA Modules:
  0.0 86.5 jit_solution(8209133762424977348)
XLA Ops:
  0.7 1.7 %shard_map.51.own = f32[4,14,512]{2,1,0:T(8,128)S(1)} custom-call(s32[4]{0:T(128)S(1)} %pad_add_fusion.par_ref, f32[4,64,512]{2,1,0:T(8,128)} %own.1, f32[2,4,64,512]{3,2,1,0:T(8,128)} %f.1), custom_call_target="tpu_custom_call" | custom-call | bytes 3600000 | tf_op jit(solution)/shard_map/pallas_call | solution.py:418
  3.1 3.4 %collective-permute-start.1 = (f32[4,14,512]{2,1,0:T(8,128)S(1)}, f32[4,14,512]{2,1,0:T(8,128)S(1)}, u32[]{:S(2)}, u32[]{:S(2)}) collective-permute-start(f32[4,14,512]{2,1,0:T(8,128)S(1)} %shard_map.51.own), channel_id=1, source_target_pairs={{0,16},{32,48},{64,80},{96,112},{128,144},{160,176},{192,208},{224... | collective-permute-start | bytes 344072 | tf_op jit(solution)/shard_map/ppermute | solution.py:467
  6.5 3.8 %shard_map.50 = (f32[7,64,512]{2,1,0:T(8,128)}, f32[7,64,512]{2,1,0:T(8,128)}, f32[4,64,512]{2,1,0:T(8,128)S(1)}, f32[2,4,64,512]{3,2,1,0:T(8,128)S(1)}) custom-call(s32[4]{0:T(128)S(1)} %pad_add_fusion.par_ref, f32[4,64,512]{2,1,0:T(8,128)} %own.1, f32[2,4,64,512]{3,2,1,0:T(8,128)} %f.1), custom_call_target="tpu_custom_call" | custom-call | bytes 7200000 | tf_op jit(solution)/shard_map/pallas_call | solution.py:418
  11.6 0.7 collective-permute-start.2
  12.3 3.3 %collective-permute-start.3 = (f32[7,64,512]{2,1,0:T(8,128)}, f32[7,64,512]{2,1,0:T(8,128)S(1)}, u32[]{:S(2)}, u32[]{:S(2)}) collective-permute-start(f32[7,64,512]{2,1,0:T(8,128)} %get-tuple-element.31), channel_id=1, source_target_pairs={{0,16},{32,48},{64,80},{96,112},{128,144},{160,176},{192,208},{224... | collective-permute-start | bytes 2752520 | tf_op jit(solution)/shard_map/ppermute | solution.py:481
  15.7 0.9 %copy-done.1 = f32[4,14,512]{2,1,0:T(8,128)S(1)} copy-done((f32[4,14,512]{2,1,0:T(8,128)S(1)}, f32[4,14,512]{2,1,0:T(8,128)}, u32[]{:S(2)}) %copy-start.1) | copy-done | bytes 114712
  16.6 0.9 %copy-done.3 = f32[4,14,512]{2,1,0:T(8,128)S(1)} copy-done((f32[4,14,512]{2,1,0:T(8,128)S(1)}, f32[4,14,512]{2,1,0:T(8,128)}, u32[]{:S(2)}) %copy-start.3) | copy-done | bytes 114712
  18.1 1.6 %collective-permute-start.4 = (f32[40,512]{1,0:T(8,128)S(1)}, f32[40,512]{1,0:T(8,128)S(1)}, u32[]{:S(2)}, u32[]{:S(2)}) collective-permute-start(f32[40,512]{1,0:T(8,128)S(1)} %get-tuple-element.34), channel_id=1, source_target_pairs={{0,1},{2,3},{4,5},{6,7},{8,9},{10,11},{12,13},{14,15},{1,0},{3,2},... | collective-permute-start | bytes 245768 | tf_op jit(solution)/shard_map/ppermute | solution.py:490
  19.6 3.9 %collective-permute-start.5 = (f32[40,512]{1,0:T(8,128)S(1)}, f32[40,512]{1,0:T(8,128)S(1)}, u32[]{:S(2)}, u32[]{:S(2)}) collective-permute-start(f32[40,512]{1,0:T(8,128)S(1)} %get-tuple-element.35), channel_id=1, source_target_pairs={{1,2},{3,4},{5,6},{7,8},{9,10},{11,12},{13,14},{2,1},{4,3},{6,5},{... | collective-permute-start | bytes 245768 | tf_op jit(solution)/shard_map/ppermute | solution.py:491
  23.7 4.4 %collective-permute-done.5.second = f32[40,512]{1,0:T(8,128)S(1)} collective-permute-done((f32[40,512]{1,0:T(8,128)S(1)}, f32[40,512]{1,0:T(8,128)S(1)}, u32[]{:S(2)}, u32[]{:S(2)}) %collective-permute-start.5) | collective-permute-done | bytes 81952 | tf_op jit(solution)/shard_map/ppermute | solution.py:491
  28.1 8.6 %shard_map.53 = (f32[10,4,512]{2,1,0:T(4,128)S(1)}, f32[10,80,512]{2,1,0:T(8,128)S(1)}, f32[8,80,512]{2,1,0:T(8,128)S(1)}, f32[8,80,512]{2,1,0:T(8,128)S(1)}, f3...) custom-call(s32[4]{0:T(128)S(1)} %pad_add_fusion.par_ref, ...), custom_call_target="tpu_custom_call" | custom-call | bytes 21600000 | tf_op jit(solution)/shard_map/pallas_call | solution.py:418
  36.7 2.2 %collective-permute-start.8 = (f32[10,4,512]{2,1,0:T(4,128)S(1)}, f32[10,4,512]{2,1,0:T(4,128)S(1)}, u32[]{:S(2)}, u32[]{:S(2)}) collective-permute-start(f32[10,4,512]{2,1,0:T(4,128)S(1)} %get-tuple-element.38), channel_id=1, source_target_pairs={{0,3},{1,2},{2,1},{3,0},{4,7},{5,6},{6,5},{7,4},{8,11},{9,10},{10,... | collective-permute-start | bytes 245768 | tf_op jit(solution)/shard_map/ppermute | solution.py:510
  38.9 2.0 %collective-permute-start.6 = (f32[10,4,512]{2,1,0:T(4,128)S(1)}, f32[10,4,512]{2,1,0:T(4,128)S(1)}, u32[]{:S(2)}, u32[]{:S(2)}) collective-permute-start(f32[10,4,512]{2,1,0:T(4,128)S(1)} %get-tuple-element.38), channel_id=1, source_target_pairs={{0,1},{1,0},{2,3},{3,2},{4,5},{5,4},{6,7},{7,6},{8,9},{9,8},{10,11... | collective-permute-start | bytes 245768 | tf_op jit(solution)/shard_map/ppermute | solution.py:510
  40.9 1.6 %collective-permute-done.8 = f32[10,4,512]{2,1,0:T(4,128)S(1)} collective-permute-done((f32[10,4,512]{2,1,0:T(4,128)S(1)}, f32[10,4,512]{2,1,0:T(4,128)S(1)}, u32[]{:S(2)}, u32[]{:S(2)}) %collective-permute-start.8) | collective-permute-done | bytes 81952 | tf_op jit(solution)/shard_map/ppermute | solution.py:510
  42.4 2.6 %collective-permute-done.7 = f32[10,4,512]{2,1,0:T(4,128)S(1)} collective-permute-done((f32[10,4,512]{2,1,0:T(4,128)S(1)}, f32[10,4,512]{2,1,0:T(4,128)S(1)}, u32[]{:S(2)}, u32[]{:S(2)}) %collective-permute-start.7) | collective-permute-done | bytes 81952 | tf_op jit(solution)/shard_map/ppermute | solution.py:510
  45.5 1.6 %collective-permute-start.11 = (f32[10,4,512]{2,1,0:T(4,128)S(1)}, f32[10,4,512]{2,1,0:T(4,128)S(1)}, u32[]{:S(2)}, u32[]{:S(2)}) collective-permute-start(f32[10,4,512]{2,1,0:T(4,128)S(1)} %bitcast.22), channel_id=1, source_target_pairs={{0,12},{1,13},{2,14},{3,15},{4,8},{5,9},{6,10},{7,11},{8,4},{9,5},... | collective-permute-start | bytes 245768 | tf_op jit(solution)/shard_map/ppermute | solution.py:510
  47.0 2.8 %collective-permute-start.9 = (f32[10,4,512]{2,1,0:T(4,128)S(1)}, f32[10,4,512]{2,1,0:T(4,128)S(1)}, u32[]{:S(2)}, u32[]{:S(2)}) collective-permute-start(f32[10,4,512]{2,1,0:T(4,128)S(1)} %bitcast.23), channel_id=1, source_target_pairs={{0,4},{1,5},{2,6},{3,7},{4,0},{5,1},{6,2},{7,3},{8,12},{9,13},{10,... | collective-permute-start | bytes 245768 | tf_op jit(solution)/shard_map/ppermute | solution.py:510
  49.8 4.5 %shard_map.54.forced = f32[2,4,64,512]{3,2,1,0:T(8,128)S(1)} custom-call(s32[4]{0:T(128)S(1)} %pad_add_fusion.par_ref, f32[2,4,64,512]{3,2,1,0:T(8,128)S(1)} %get-tuple-element.36.f, f32[7,64,512]{2,1,0:T(8,128)S(1)} %collective-permute-done.2.od, f32[7,64,512]{2,1,0:T(8,128)S(1)} %collective-permute-done.3.ev, f32[40,512]{1,0:T(8,128)S(1)} %collective-permute-done.4.first, ...), custom_call_target="tpu_custom_call" | custom-call | bytes 18000000 | tf_op jit(solution)/shard_map/pallas_call | solution.py:418
  54.5 1.3 %collective-permute-done.12.mate = f32[10,4,512]{2,1,0:T(4,128)S(1)} collective-permute-done((f32[10,4,512]{2,1,0:T(4,128)S(1)}, f32[10,4,512]{2,1,0:T(4,128)S(1)}, u32[]{:S(2)}, u32[]{:S(2)}) %collective-permute-start.12) | collective-permute-done | bytes 81952 | tf_op jit(solution)/shard_map/ppermute | solution.py:528
  55.8 2.0 %collective-permute-start.13 = (f32[2,10,4,512]{3,2,1,0:T(4,128)S(1)}, f32[2,10,4,512]{3,2,1,0:T(4,128)S(1)}, u32[]{:S(2)}, u32[]{:S(2)}) collective-permute-start(f32[2,10,4,512]{3,2,1,0:T(4,128)S(1)} %pad_maximum_fusion), channel_id=1, source_target_pairs={{0,32},{16,48},{64,96},{80,112},{128,160},{144,176},{192,224},{208... | collective-permute-start | bytes 491528 | tf_op jit(solution)/shard_map/ppermute | solution.py:530
  58.5 3.9 %collective-permute-done.13.first = f32[2,10,4,512]{3,2,1,0:T(4,128)S(1)} collective-permute-done((f32[2,10,4,512]{3,2,1,0:T(4,128)S(1)}, f32[2,10,4,512]{3,2,1,0:T(4,128)S(1)}, u32[]{:S(2)}, u32[]{:S(2)}) %collective-permute-start.13) | collective-permute-done | bytes 163872 | tf_op jit(solution)/shard_map/ppermute | solution.py:530
  62.4 1.2 %shard_map.55 = (f32[48,512]{1,0:T(8,128)S(1)}, f32[8,8,128]{2,1,0:T(8,128)S(1)}) custom-call(s32[4]{0:T(128)S(1)} %pad_add_fusion.par_ref, f32[10,4,512]{2,1,0:T(4,128)S(1)} %bitcast.18, f32[10,4,512]{2,1,0:T(4,128)S(1)} %collective-permute-done.12.mate, f32[2,10,4,512]{3,2,1,0:T(4,128)S(1)} %collective-permute-done.13.first, ...), custom_call_target="tpu_custom_call" | custom-call | bytes 3600000 | tf_op jit(solution)/shard_map/pallas_call | solution.py:418
  63.5 18.9 %all_to_all.5.dots = f32[8,8,128]{2,1,0:T(8,128)S(1)} all-to-all(f32[8,8,128]{2,1,0:T(8,128)S(1)} %get-tuple-element.46), channel_id=1, replica_groups={{0,32,64,96,128,160,192,224},{16,48,80,112,144,176,208,240},{1,33,65,97..., dimensions={0} | all-to-all | bytes 65536 | tf_op jit(solution)/shard_map/all_to_all | solution.py:540
  82.5 4.0 %shard_map.56 = (f32[2,4,64,512]{3,2,1,0:T(8,128)}, f32[4,32]{1,0:T(4,128)}) custom-call(f32[48,512]{1,0:T(8,128)S(1)} %get-tuple-element.45.basis, f32[8,8,128]{2,1,0:T(8,128)S(1)} %all_to_all.5.dots, f32[512,32]{1,0:T(8,128)S(1)} %compare_convert_fusion.onehot, f32[7,80,512]{2,1,0:T(8,128)S(1)} %get-tuple-element.48.h0, ...), custom_call_target="tpu_custom_call" | custom-call | bytes 14400000 | tf_op jit(solution)/shard_map/pallas_call | solution.py:418
  (30 shorter events, 4.1 us)
Async XLA Ops:
  2.4 21.1 %copy-start.4 = (s32[512]{0:T(512)S(1)}, s32[512]{0:T(512)}, u32[]{:S(2)}) copy-start(s32[512]{0:T(512)} %param.5) | copy-start | bytes 6148
  2.4 7.9 %collective-permute-start = (f32[4,14,512]{2,1,0:T(8,128)S(1)}, f32[4,14,512]{2,1,0:T(8,128)S(1)}, u32[]{:S(2)}, u32[]{:S(2)}) collective-permute-start(f32[4,14,512]{2,1,0:T(8,128)S(1)} %shard_map.51.own), channel_id=1, source_target_pairs={{16,32},{48,64},{80,96},{112,128},{144,160},{176,192},{208,224},{3... | collective-permute-start | bytes 344072 | tf_op jit(solution)/shard_map/ppermute | solution.py:466
  3.1 7.9 %collective-permute-start.1 = (f32[4,14,512]{2,1,0:T(8,128)S(1)}, f32[4,14,512]{2,1,0:T(8,128)S(1)}, u32[]{:S(2)}, u32[]{:S(2)}) collective-permute-start(f32[4,14,512]{2,1,0:T(8,128)S(1)} %shard_map.51.own), channel_id=1, source_target_pairs={{0,16},{32,48},{64,80},{96,112},{128,144},{160,176},{192,208},{224... | collective-permute-start | bytes 344072 | tf_op jit(solution)/shard_map/ppermute | solution.py:467
  10.3 0.6 copy-start
  11.0 0.7 copy-start.2
  11.6 16.5 %collective-permute-start.2 = (f32[7,64,512]{2,1,0:T(8,128)}, f32[7,64,512]{2,1,0:T(8,128)S(1)}, u32[]{:S(2)}, u32[]{:S(2)}) collective-permute-start(f32[7,64,512]{2,1,0:T(8,128)} %get-tuple-element.30), channel_id=1, source_target_pairs={{16,32},{48,64},{80,96},{112,128},{144,160},{176,192},{208,224},{3... | collective-permute-start | bytes 2752520 | tf_op jit(solution)/shard_map/ppermute | solution.py:480
  12.3 15.7 %collective-permute-start.3 = (f32[7,64,512]{2,1,0:T(8,128)}, f32[7,64,512]{2,1,0:T(8,128)S(1)}, u32[]{:S(2)}, u32[]{:S(2)}) collective-permute-start(f32[7,64,512]{2,1,0:T(8,128)} %get-tuple-element.31), channel_id=1, source_target_pairs={{0,16},{32,48},{64,80},{96,112},{128,144},{160,176},{192,208},{224... | collective-permute-start | bytes 2752520 | tf_op jit(solution)/shard_map/ppermute | solution.py:481
  15.7 0.9 %copy-start.1 = (f32[4,14,512]{2,1,0:T(8,128)S(1)}, f32[4,14,512]{2,1,0:T(8,128)}, u32[]{:S(2)}) copy-start(f32[4,14,512]{2,1,0:T(8,128)} %copy-done) | copy-start | bytes 344068
  16.6 0.9 %copy-start.3 = (f32[4,14,512]{2,1,0:T(8,128)S(1)}, f32[4,14,512]{2,1,0:T(8,128)}, u32[]{:S(2)}) copy-start(f32[4,14,512]{2,1,0:T(8,128)} %copy-done.2) | copy-start | bytes 344068
  18.1 5.6 %collective-permute-start.4 = (f32[40,512]{1,0:T(8,128)S(1)}, f32[40,512]{1,0:T(8,128)S(1)}, u32[]{:S(2)}, u32[]{:S(2)}) collective-permute-start(f32[40,512]{1,0:T(8,128)S(1)} %get-tuple-element.34), channel_id=1, source_target_pairs={{0,1},{2,3},{4,5},{6,7},{8,9},{10,11},{12,13},{14,15},{1,0},{3,2},... | collective-permute-start | bytes 245768 | tf_op jit(solution)/shard_map/ppermute | solution.py:490
  19.6 8.4 %collective-permute-start.5 = (f32[40,512]{1,0:T(8,128)S(1)}, f32[40,512]{1,0:T(8,128)S(1)}, u32[]{:S(2)}, u32[]{:S(2)}) collective-permute-start(f32[40,512]{1,0:T(8,128)S(1)} %get-tuple-element.35), channel_id=1, source_target_pairs={{1,2},{3,4},{5,6},{7,8},{9,10},{11,12},{13,14},{2,1},{4,3},{6,5},{... | collective-permute-start | bytes 245768 | tf_op jit(solution)/shard_map/ppermute | solution.py:491
  36.7 5.7 %collective-permute-start.8 = (f32[10,4,512]{2,1,0:T(4,128)S(1)}, f32[10,4,512]{2,1,0:T(4,128)S(1)}, u32[]{:S(2)}, u32[]{:S(2)}) collective-permute-start(f32[10,4,512]{2,1,0:T(4,128)S(1)} %get-tuple-element.38), channel_id=1, source_target_pairs={{0,3},{1,2},{2,1},{3,0},{4,7},{5,6},{6,5},{7,4},{8,11},{9,10},{10,... | collective-permute-start | bytes 245768 | tf_op jit(solution)/shard_map/ppermute | solution.py:510
  38.9 6.2 %collective-permute-start.7 = (f32[10,4,512]{2,1,0:T(4,128)S(1)}, f32[10,4,512]{2,1,0:T(4,128)S(1)}, u32[]{:S(2)}, u32[]{:S(2)}) collective-permute-start(f32[10,4,512]{2,1,0:T(4,128)S(1)} %get-tuple-element.38), channel_id=1, source_target_pairs={{0,2},{1,3},{2,0},{3,1},{4,6},{5,7},{6,4},{7,5},{8,10},{9,11},{10,... | collective-permute-start | bytes 245768 | tf_op jit(solution)/shard_map/ppermute | solution.py:510
  38.9 6.2 %collective-permute-start.6 = (f32[10,4,512]{2,1,0:T(4,128)S(1)}, f32[10,4,512]{2,1,0:T(4,128)S(1)}, u32[]{:S(2)}, u32[]{:S(2)}) collective-permute-start(f32[10,4,512]{2,1,0:T(4,128)S(1)} %get-tuple-element.38), channel_id=1, source_target_pairs={{0,1},{1,0},{2,3},{3,2},{4,5},{5,4},{6,7},{7,6},{8,9},{9,8},{10,11... | collective-permute-start | bytes 245768 | tf_op jit(solution)/shard_map/ppermute | solution.py:510
  45.1 9.3 %collective-permute-start.10 = (f32[10,4,512]{2,1,0:T(4,128)S(1)}, f32[10,4,512]{2,1,0:T(4,128)S(1)}, u32[]{:S(2)}, u32[]{:S(2)}) collective-permute-start(f32[10,4,512]{2,1,0:T(4,128)S(1)} %bitcast.21), channel_id=1, source_target_pairs={{0,8},{1,9},{2,10},{3,11},{4,12},{5,13},{6,14},{7,15},{8,0},{9,1},... | collective-permute-start | bytes 245768 | tf_op jit(solution)/shard_map/ppermute | solution.py:510
  45.5 8.9 %collective-permute-start.11 = (f32[10,4,512]{2,1,0:T(4,128)S(1)}, f32[10,4,512]{2,1,0:T(4,128)S(1)}, u32[]{:S(2)}, u32[]{:S(2)}) collective-permute-start(f32[10,4,512]{2,1,0:T(4,128)S(1)} %bitcast.22), channel_id=1, source_target_pairs={{0,12},{1,13},{2,14},{3,15},{4,8},{5,9},{6,10},{7,11},{8,4},{9,5},... | collective-permute-start | bytes 245768 | tf_op jit(solution)/shard_map/ppermute | solution.py:510
  47.0 7.4 %collective-permute-start.9 = (f32[10,4,512]{2,1,0:T(4,128)S(1)}, f32[10,4,512]{2,1,0:T(4,128)S(1)}, u32[]{:S(2)}, u32[]{:S(2)}) collective-permute-start(f32[10,4,512]{2,1,0:T(4,128)S(1)} %bitcast.23), channel_id=1, source_target_pairs={{0,4},{1,5},{2,6},{3,7},{4,0},{5,1},{6,2},{7,3},{8,12},{9,13},{10,... | collective-permute-start | bytes 245768 | tf_op jit(solution)/shard_map/ppermute | solution.py:510
  54.4 1.4 %collective-permute-start.12 = (f32[10,4,512]{2,1,0:T(4,128)S(1)}, f32[10,4,512]{2,1,0:T(4,128)S(1)}, u32[]{:S(2)}, u32[]{:S(2)}) collective-permute-start(f32[10,4,512]{2,1,0:T(4,128)S(1)} %bitcast.16), channel_id=1, source_target_pairs={{0,16},{32,48},{64,80},{96,112},{128,144},{160,176},{192,208},{224... | collective-permute-start | bytes 245768 | tf_op jit(solution)/shard_map/ppermute | solution.py:528
  55.8 6.5 %collective-permute-start.13 = (f32[2,10,4,512]{3,2,1,0:T(4,128)S(1)}, f32[2,10,4,512]{3,2,1,0:T(4,128)S(1)}, u32[]{:S(2)}, u32[]{:S(2)}) collective-permute-start(f32[2,10,4,512]{3,2,1,0:T(4,128)S(1)} %pad_maximum_fusion), channel_id=1, source_target_pairs={{0,32},{16,48},{64,96},{80,112},{128,160},{144,176},{192,224},{208... | collective-permute-start | bytes 491528 | tf_op jit(solution)/shard_map/ppermute | solution.py:530
  57.8 4.5 %collective-permute-start.14 = (f32[2,10,4,512]{3,2,1,0:T(4,128)S(1)}, f32[2,10,4,512]{3,2,1,0:T(4,128)S(1)}, u32[]{:S(2)}, u32[]{:S(2)}) collective-permute-start(f32[2,10,4,512]{3,2,1,0:T(4,128)S(1)} %pad_maximum_fusion), channel_id=1, source_target_pairs={{32,64},{48,80},{96,128},{112,144},{160,192},{176,208},{64,32},{80... | collective-permute-start | bytes 491528 | tf_op jit(solution)/shard_map/ppermute | solution.py:530

commit v6 on v5

--- a/solution.py
+++ b/solution.py
@@ -49,44 +49,36 @@
     return lax.broadcasted_iota(jnp.int32, shape, len(shape) - 1)
 
 
-def edge_kernel(par_ref, own, f, out, low_v, high_v, low_f, high_f, sems):
-    copies = [
-        pltpu.make_async_copy(own.at[:, 0:8], low_v, sems.at[0]),
-        pltpu.make_async_copy(own.at[:, NY - 8 : NY], high_v, sems.at[1]),
-        pltpu.make_async_copy(f.at[:, :, 0:8], low_f, sems.at[2]),
-        pltpu.make_async_copy(f.at[:, :, NY - 8 : NY], high_f, sems.at[3]),
-    ]
+def edge_kernel(own_hbm, f_hbm, out, own, f, sems):
+    copies = [pltpu.make_async_copy(own_hbm, own, sems.at[0]), pltpu.make_async_copy(f_hbm, f, sems.at[1])]
     for copy in copies:
         copy.start()
-    for copy in copies:
-        copy.wait()
-    out[:, 0:3] = low_v[:, 0:3]
-    out[:, 7:10] = high_v[:, 5:8]
+    copies[0].wait()
+    out[:, 0:3] = own[:, 0:3]
+    out[:, 7:10] = own[:, NY - 3 : NY]
+    copies[1].wait()
     for c in range(2):
-        out[:, 3 + 2 * c : 5 + 2 * c] = low_f[c, :, 0:2]
-        out[:, 10 + 2 * c : 12 + 2 * c] = high_f[c, :, 6:8]
-
-
-def pack_kernel(par_ref, own_hbm, f_hbm, to_od, to_ev, own, f, sems):
-    par = par_ref[0]
+        out[:, 3 + 2 * c : 5 + 2 * c] = f[c, :, 0:2]
+        out[:, 10 + 2 * c : 12 + 2 * c] = f[c, :, NY - 2 : NY]
+
+
+def pack(par, own, f, to_od, to_ev, sems):
     copies = []
     for n, (out, last) in enumerate(((to_od, par), (to_ev, 1 - par))):
-        copies.append(pltpu.make_async_copy(own_hbm.at[pl.ds(last, 3)], out.at[0:3], sems.at[3 * n]))
+        copies.append(pltpu.make_async_copy(own.at[pl.ds(last, 3)], out.at[0:3], sems.at[3 * n]))
         for c in range(2):
             copies.append(
                 pltpu.make_async_copy(
-                    f_hbm.at[c, pl.ds(2 * last, 2)], out.at[3 + 2 * c : 5 + 2 * c], sems.at[1 + 3 * n + c]
+                    f.at[c, pl.ds(2 * last, 2)], out.at[3 + 2 * c : 5 + 2 * c], sems.at[1 + 3 * n + c]
                 )
             )
-    copies.append(pltpu.make_async_copy(own_hbm, own, sems.at[6]))
-    copies.append(pltpu.make_async_copy(f_hbm, f, sems.at[7]))
+    return copies
+
+
+def corner_kernel(par_ref, own, od, ev, own_all, f_all, first, second, to_od, to_ev, low, high, sems):
+    copies = pack(par_ref[0], own_all, f_all, to_od, to_ev, sems)
     for copy in copies:
         copy.start()
-    for copy in copies:
-        copy.wait()
-
-
-def corner_kernel(par_ref, own, od, ev, first, second, low, high):
     odd = par_ref[0] == 1
     below = lax.select(odd, ev[2:4], od[2:4])
     above = lax.select(odd, od[0:2], ev[0:2])
@@ -104,6 +96,8 @@
     odd = par_ref[2] == 1
     first[...] = lax.select(odd, low[...], high[...])
     second[...] = lax.select(odd, high[...], low[...])
+    for copy in copies:
+        copy.wait()
 
 
 def sides(odd, first, second):
@@ -145,11 +139,13 @@
     lax.fori_loop(0, 8, layer, 0)
 
 
-def stencil_kernel(par_ref, own, od, ev, first, second, f, out, v, d, fz, h0, ex, ez, ezm, acc, sems):
+def stencil_kernel(par_ref, own, od, ev, first, second, f, out, v, d, fz, h0, ex, ez, ezm, acc, s_acc, sems):
     par = par_ref[0]
     lo, hi = sides(par_ref[2] == 1, first, second)
     fill_viscosity(par, v, own, od, ev, lo, hi, sems)
     fill_inverse(v, d, fz)
+
+    ex[0] = E2 * d[0] * (v[1] + v[2]) * d[1]
 
     def edges(r, _):
         dm, vm = d[r], v[r + 1]
@@ -162,7 +158,7 @@
         ezm[r] = down_z(e)
         return 0
 
-    lax.fori_loop(0, 7, edges, 0)
+    lax.fori_loop(1, 7, edges, 0)
 
     acc[...] = jnp.zeros_like(acc)
     own_rows = slice(LO, HI)
@@ -181,15 +177,15 @@
         dm = d[r, own_rows]
         u0, u1 = dm * f[0, i], dm * f[1, i]
 
+        def fold(x):
+            return jnp.sum(x.reshape(8, 8, NZ), axis=0)
+
         def weigh(di, dk, s):
             for c, u in ((0, u0), (1, u1)):
-                row = jnp.sum(u * s, axis=0, keepdims=True)
-                if dk:
-                    row = pltpu.roll(row, dk % NZ, 1)
-                at = pl.ds(16 * c + i + di + 2, 1)
-                acc[at] = acc[at] + row[None]
+                at = i + di + 2
+                acc[dk + 2, c, at] = acc[dk + 2, c, at] + fold(u * s)
             if (di, dk) in FORWARD:
-                out[FORWARD.index((di, dk)), pl.ds(i, 1)] = jnp.sum(dm * s, axis=0, keepdims=True)
+                s_acc[FORWARD.index((di, dk)), i] = fold(dm * s)
 
         exi, exm = ex[r, own_rows], ex[r - 1, own_rows]
         ezi, ezmi = ez[r, own_rows], ezm[r, own_rows]
@@ -221,8 +217,16 @@
 
     lax.fori_loop(0, ROWS, layer, 0)
 
-    cx = acc[0:16, 0]
-    cz = acc[16:32, 0]
+    for n in range(7):
+        out[n] = jnp.sum(s_acc[n], axis=1)
+
+    def columns(c):
+        total = jnp.sum(acc[2, c], axis=1)
+        for dk in (-2, -1, 1, 2):
+            total = total + pltpu.roll(jnp.sum(acc[dk + 2, c], axis=1), dk % NZ, 1)
+        return jnp.concatenate([total, jnp.zeros((8, NZ), jnp.float32)], 0)
+
+    cx, cz = columns(0), columns(1)
     zero = lane((16, NZ)) == 0
     e = cx - pltpu.roll(cx, 1, 0) + cz - jnp.where(zero, 0.0, down_z(cz))
     out[7:9] = e[0:8].reshape(2, 4, NZ)
@@ -454,39 +458,33 @@
     first_chips = [(2 * a + c, 2 * b + c) for a, b in pairs(chips, 0) for c in range(2)]
     second_chips = [(2 * a + c, 2 * b + c) for a, b in pairs(chips, 1) for c in range(2)]
 
-    edges = call(
+    edges, own, f = call(
         edge_kernel,
-        f32(ROWS, 14, NZ),
-        [(ROWS, 8, NZ)] * 2 + [(2, ROWS, 8, NZ)] * 2,
-        (where, in_hbm(viscosity), in_hbm(forcing)),
-        in_specs=[SMEM, ANY, ANY],
-        sems=4,
+        (
+            pltpu.VMEM((ROWS, 14, NZ), jnp.float32),
+            pltpu.VMEM(viscosity.shape, jnp.float32),
+            pltpu.VMEM(forcing.shape, jnp.float32),
+        ),
+        [],
+        (in_hbm(viscosity), in_hbm(forcing)),
+        in_specs=[ANY, ANY],
+        sems=2,
         mib=4,
     )
     od_e = lax.ppermute(edges, "slab", others)
     ev_e = lax.ppermute(edges, "slab", mates)
     layers = pltpu.VMEM((7, NY, NZ), jnp.float32)
-    to_od, to_ev, own, f = call(
-        pack_kernel,
-        (layers, layers, pltpu.VMEM(viscosity.shape, jnp.float32), pltpu.VMEM(forcing.shape, jnp.float32)),
-        [],
-        (where, in_hbm(viscosity), in_hbm(forcing)),
-        in_specs=[SMEM, ANY, ANY],
-        micros=2,
-        sems=8,
+    first, second, to_od, to_ev = call(
+        corner_kernel,
+        (f32(40, NZ), f32(40, NZ), layers, layers),
+        [(40, NZ), (40, NZ)],
+        (where, in_vmem(edges), in_vmem(od_e), in_vmem(ev_e), in_vmem(own), in_vmem(f)),
+        in_specs=[SMEM] + [VMEM] * 5,
+        sems=6,
         mib=4,
     )
-    od_e, ev_e, to_od, to_ev = lax.optimization_barrier((od_e, ev_e, to_od, to_ev))
     od = lax.ppermute(to_od, "slab", others)
     ev = lax.ppermute(to_ev, "slab", mates)
-    first, second = call(
-        corner_kernel,
-        (f32(40, NZ), f32(40, NZ)),
-        [(40, NZ), (40, NZ)],
-        (where, in_vmem(edges), in_vmem(od_e), in_vmem(ev_e)),
-        in_specs=[SMEM] + [VMEM] * 3,
-        mib=4,
-    )
     first = lax.ppermute(first, "cross", pairs(cross, 0))
     second = lax.ppermute(second, "cross", pairs(cross, 1))
 
@@ -494,12 +492,12 @@
     part, v, d, fz, h0, ex, ez = call(
         stencil_kernel,
         (f32(10, 4, NZ), *[pltpu.VMEM(x.shape, x.dtype) for x in kept]),
-        [(7, FRAME, NZ), (32, 1, NZ)],
+        [(7, FRAME, NZ), (5, 2, 8, 8, NZ), (7, ROWS, 8, NZ)],
         (where, in_vmem(own), in_vmem(od), in_vmem(ev), first, second, in_vmem(f)),
         in_specs=[SMEM] + [VMEM] * 6,
         micros=6,
         sems=4,
-        mib=6,
+        mib=8,
     )
 
     width = owner_slot.shape[0] // cross

time: 86.8 us -> 87 us (level)
  Pallas kernels: 24.4 us -> 20.9 us
  starting transfers between devices: 25.2 us -> 27.7 us
  local copies, waits for them, and re-layouts: 3.1 us -> 0.63 us
  blocking collectives: 18.9 us -> 20.8 us
  waiting for transfers between devices: 13.7 us -> 15.5 us
    pallas_call x7 -> x6, Pallas kernels: 24.4 us -> 20.9 us  [call(): pl.pallas_call(kernel, out_shape=out_shape, in_specs=in_specs, out_specs=...]
    unnamed x10 -> x4, local copies, waits for them, and re-layouts: 3.1 us -> 0.63 us
    all_to_all x1, blocking collectives: 18.9 us -> 20.8 us  [shards(): lax.all_to_all(dots, 'slab', 0, 0, tiled=True, axis_index_groups=groups)]
    ppermute x1, starting transfers between devices: 2 us -> 3.29 us  [shards(): lax.ppermute(both, 'slab', first_chips)]
    ppermute x1, starting transfers between devices: 3.31 us -> 4.58 us  [shards(): ev = lax.ppermute(to_ev, 'slab', mates)]
    ppermute x6, waiting for transfers between devices: 4.18 us -> 5.09 us  [among(): lax.ppermute(x, 'cross', [(i, i ^ n * step) for i in range(cross)])]
    ppermute x1, waiting for transfers between devices: 0.01 us -> 0.91 us  [shards(): ev_e = lax.ppermute(edges, 'slab', mates)]
  transfers between devices with their start and end apart: 15 -> 15, of which waited for: 5 -> 7; matrix products, arithmetic and copies ran while one was open for 0% -> 0% of each run, Pallas kernels for 10% -> 5%
where the time goes in v6:
time: 87 us; the launch traced here: 86.7 us
  starting transfers between devices  27.7 us (32%)
  Pallas kernels  20.9 us (24%)
  blocking collectives  20.8 us (24%)
  waiting for transfers between devices  15.5 us (18%)
    pallas_call x6, Pallas kernels, call(): pl.pallas_call(kernel, out_shape=out_shape, in_specs=in_specs, out_specs=...  20.9 us
    all_to_all x1, blocking collectives, shards(): lax.all_to_all(dots, 'slab', 0, 0, tiled=True, axis_index_groups=groups)  20.8 us
    ppermute x6, starting transfers between devices, among(): lax.ppermute(x, 'cross', [(i, i ^ n * step) for i in range(cross)])  8.96 us
    ppermute x6, waiting for transfers between devices, among(): lax.ppermute(x, 'cross', [(i, i ^ n * step) for i in range(cross)])  5.09 us
    ppermute x1, starting transfers between devices, shards(): ev = lax.ppermute(to_ev, 'slab', mates)  4.58 us
    ppermute x1, waiting for transfers between devices, shards(): second = lax.ppermute(second, 'cross', pairs(cross, 1))  4.39 us
    ppermute x1, starting transfers between devices, shards(): second = lax.ppermute(second, 'cross', pairs(cross, 1))  3.88 us
    ppermute x1, waiting for transfers between devices, shards(): lax.ppermute(both, 'slab', first_chips)  3.85 us
  transfers between devices with their start and end apart: 15, of which 7 were waited for; matrix products, arithmetic and copies ran while one was open for 0% of the time, Pallas kernels for 5%

profile of v6, /device:TPU:16, one launch (start us, length us, event | category | flops | bytes accessed | tf_op | source)
XLA Modules:
  0.0 86.7 jit_solution(12174589782249430262)
XLA Ops:
  0.6 1.4 %shard_map.50 = (f32[4,14,512]{2,1,0:T(8,128)S(1)}, f32[4,64,512]{2,1,0:T(8,128)S(1)}, f32[2,4,64,512]{3,2,1,0:T(8,128)S(1)}) custom-call(f32[4,64,512]{2,1,0:T(8,128)} %own_hbm.1, f32[2,4,64,512]{3,2,1,0:T(8,128)} %f_hbm.1), custom_call_target="tpu_custom_call" | custom-call | bytes 3600000 | tf_op jit(solution)/shard_map/pallas_call | solution.py:422
  2.8 3.4 %collective-permute-start.1 = (f32[4,14,512]{2,1,0:T(8,128)S(1)}, f32[4,14,512]{2,1,0:T(8,128)S(1)}, u32[]{:S(2)}, u32[]{:S(2)}) collective-permute-start(f32[4,14,512]{2,1,0:T(8,128)S(1)} %get-tuple-element.25.own), channel_id=1, source_target_pairs={{0,16},{32,48},{64,80},{96,112},{128,144},{160,176},{192,208},{224... | collective-permute-start | bytes 344072 | tf_op jit(solution)/shard_map/ppermute | solution.py:475
  6.2 0.9 %collective-permute-done.1.ev = f32[4,14,512]{2,1,0:T(8,128)S(1)} collective-permute-done((f32[4,14,512]{2,1,0:T(8,128)S(1)}, f32[4,14,512]{2,1,0:T(8,128)S(1)}, u32[]{:S(2)}, u32[]{:S(2)}) %collective-permute-start.1) | collective-permute-done | bytes 114720 | tf_op jit(solution)/shard_map/ppermute | solution.py:475
  7.1 2.3 %shard_map.51 = (f32[40,512]{1,0:T(8,128)S(1)}, f32[40,512]{1,0:T(8,128)S(1)}, f32[7,64,512]{2,1,0:T(8,128)}, f32[7,64,512]{2,1,0:T(8,128)}) custom-call(s32[4]{0:T(128)S(1)} %pad_add_fusion.par_ref, f32[4,14,512]{2,1,0:T(8,128)S(1)} %get-tuple-element.25.own, f32[4,14,512]{2,1,0:T(8,128)S(1)} %collective-permute-done.od, ...), custom_call_target="tpu_custom_call" | custom-call | bytes 3600000 | tf_op jit(solution)/shard_map/pallas_call | solution.py:422
  10.1 0.7 collective-permute-start.2
  10.8 4.6 %collective-permute-start.3 = (f32[7,64,512]{2,1,0:T(8,128)}, f32[7,64,512]{2,1,0:T(8,128)S(1)}, u32[]{:S(2)}, u32[]{:S(2)}) collective-permute-start(f32[7,64,512]{2,1,0:T(8,128)} %get-tuple-element.28), channel_id=1, source_target_pairs={{0,16},{32,48},{64,80},{96,112},{128,144},{160,176},{192,208},{224... | collective-permute-start | bytes 2752520 | tf_op jit(solution)/shard_map/ppermute | solution.py:487
  15.4 1.5 %collective-permute-start.4 = (f32[40,512]{1,0:T(8,128)}, f32[40,512]{1,0:T(8,128)S(1)}, u32[]{:S(2)}, u32[]{:S(2)}) collective-permute-start(f32[40,512]{1,0:T(8,128)} %copy-done), channel_id=1, source_target_pairs={{0,1},{2,3},{4,5},{6,7},{8,9},{10,11},{12,13},{14,15},{1,0},{3,2},... | collective-permute-start | bytes 245768 | tf_op jit(solution)/shard_map/ppermute | solution.py:488
  16.9 3.9 %collective-permute-start.5 = (f32[40,512]{1,0:T(8,128)S(1)}, f32[40,512]{1,0:T(8,128)S(1)}, u32[]{:S(2)}, u32[]{:S(2)}) collective-permute-start(f32[40,512]{1,0:T(8,128)S(1)} %get-tuple-element.30), channel_id=1, source_target_pairs={{1,2},{3,4},{5,6},{7,8},{9,10},{11,12},{13,14},{2,1},{4,3},{6,5},{... | collective-permute-start | bytes 245768 | tf_op jit(solution)/shard_map/ppermute | solution.py:489
  20.9 4.4 %collective-permute-done.5.second = f32[40,512]{1,0:T(8,128)S(1)} collective-permute-done((f32[40,512]{1,0:T(8,128)S(1)}, f32[40,512]{1,0:T(8,128)S(1)}, u32[]{:S(2)}, u32[]{:S(2)}) %collective-permute-start.5) | collective-permute-done | bytes 81952 | tf_op jit(solution)/shard_map/ppermute | solution.py:489
  25.3 7.5 %shard_map.52 = (f32[10,4,512]{2,1,0:T(4,128)S(1)}, f32[10,80,512]{2,1,0:T(8,128)S(1)}, f32[8,80,512]{2,1,0:T(8,128)S(1)}, f32[8,80,512]{2,1,0:T(8,128)S(1)}, f3...) custom-call(s32[4]{0:T(128)S(1)} %pad_add_fusion.par_ref, ...), custom_call_target="tpu_custom_call" | custom-call | bytes 21600000 | tf_op jit(solution)/shard_map/pallas_call | solution.py:422
  32.8 2.2 %collective-permute-start.8 = (f32[10,4,512]{2,1,0:T(4,128)S(1)}, f32[10,4,512]{2,1,0:T(4,128)S(1)}, u32[]{:S(2)}, u32[]{:S(2)}) collective-permute-start(f32[10,4,512]{2,1,0:T(4,128)S(1)} %get-tuple-element.32), channel_id=1, source_target_pairs={{0,3},{1,2},{2,1},{3,0},{4,7},{5,6},{6,5},{7,4},{8,11},{9,10},{10,... | collective-permute-start | bytes 245768 | tf_op jit(solution)/shard_map/ppermute | solution.py:508
  35.0 2.0 %collective-permute-start.6 = (f32[10,4,512]{2,1,0:T(4,128)S(1)}, f32[10,4,512]{2,1,0:T(4,128)S(1)}, u32[]{:S(2)}, u32[]{:S(2)}) collective-permute-start(f32[10,4,512]{2,1,0:T(4,128)S(1)} %get-tuple-element.32), channel_id=1, source_target_pairs={{0,1},{1,0},{2,3},{3,2},{4,5},{5,4},{6,7},{7,6},{8,9},{9,8},{10,11... | collective-permute-start | bytes 245768 | tf_op jit(solution)/shard_map/ppermute | solution.py:508
  37.0 2.1 %collective-permute-done.8 = f32[10,4,512]{2,1,0:T(4,128)S(1)} collective-permute-done((f32[10,4,512]{2,1,0:T(4,128)S(1)}, f32[10,4,512]{2,1,0:T(4,128)S(1)}, u32[]{:S(2)}, u32[]{:S(2)}) %collective-permute-start.8) | collective-permute-done | bytes 81952 | tf_op jit(solution)/shard_map/ppermute | solution.py:508
  39.1 2.1 %collective-permute-done.7 = f32[10,4,512]{2,1,0:T(4,128)S(1)} collective-permute-done((f32[10,4,512]{2,1,0:T(4,128)S(1)}, f32[10,4,512]{2,1,0:T(4,128)S(1)}, u32[]{:S(2)}, u32[]{:S(2)}) %collective-permute-start.7) | collective-permute-done | bytes 81952 | tf_op jit(solution)/shard_map/ppermute | solution.py:508
  41.2 0.9 %collective-permute-done.6 = f32[10,4,512]{2,1,0:T(4,128)S(1)} collective-permute-done((f32[10,4,512]{2,1,0:T(4,128)S(1)}, f32[10,4,512]{2,1,0:T(4,128)S(1)}, u32[]{:S(2)}, u32[]{:S(2)}) %collective-permute-start.6) | collective-permute-done | bytes 81952 | tf_op jit(solution)/shard_map/ppermute | solution.py:508
  42.2 2.7 %collective-permute-start.11 = (f32[10,4,512]{2,1,0:T(4,128)S(1)}, f32[10,4,512]{2,1,0:T(4,128)S(1)}, u32[]{:S(2)}, u32[]{:S(2)}) collective-permute-start(f32[10,4,512]{2,1,0:T(4,128)S(1)} %bitcast.22), channel_id=1, source_target_pairs={{0,12},{1,13},{2,14},{3,15},{4,8},{5,9},{6,10},{7,11},{8,4},{9,5},... | collective-permute-start | bytes 245768 | tf_op jit(solution)/shard_map/ppermute | solution.py:508
  44.9 2.0 %collective-permute-start.9 = (f32[10,4,512]{2,1,0:T(4,128)S(1)}, f32[10,4,512]{2,1,0:T(4,128)S(1)}, u32[]{:S(2)}, u32[]{:S(2)}) collective-permute-start(f32[10,4,512]{2,1,0:T(4,128)S(1)} %bitcast.23), channel_id=1, source_target_pairs={{0,4},{1,5},{2,6},{3,7},{4,0},{5,1},{6,2},{7,3},{8,12},{9,13},{10,... | collective-permute-start | bytes 245768 | tf_op jit(solution)/shard_map/ppermute | solution.py:508
  46.9 4.5 %shard_map.53.forced = f32[2,4,64,512]{3,2,1,0:T(8,128)S(1)} custom-call(s32[4]{0:T(128)S(1)} %pad_add_fusion.par_ref, f32[2,4,64,512]{3,2,1,0:T(8,128)S(1)} %get-tuple-element.26.f_all.f, f32[7,64,512]{2,1,0:T(8,128)S(1)} %collective-permute-done.2.od, f32[7,64,512]{2,1,0:T(8,128)S(1)} %collective-permute-done.3.ev, ...), custom_call_target="tpu_custom_call" | custom-call | bytes 18000000 | tf_op jit(solution)/shard_map/pallas_call | solution.py:422
  51.6 1.3 %collective-permute-done.12.mate = f32[10,4,512]{2,1,0:T(4,128)S(1)} collective-permute-done((f32[10,4,512]{2,1,0:T(4,128)S(1)}, f32[10,4,512]{2,1,0:T(4,128)S(1)}, u32[]{:S(2)}, u32[]{:S(2)}) %collective-permute-start.12) | collective-permute-done | bytes 81952 | tf_op jit(solution)/shard_map/ppermute | solution.py:526
  52.9 3.3 %collective-permute-start.13 = (f32[2,10,4,512]{3,2,1,0:T(4,128)S(1)}, f32[2,10,4,512]{3,2,1,0:T(4,128)S(1)}, u32[]{:S(2)}, u32[]{:S(2)}) collective-permute-start(f32[2,10,4,512]{3,2,1,0:T(4,128)S(1)} %pad_maximum_fusion), channel_id=1, source_target_pairs={{0,32},{16,48},{64,96},{80,112},{128,160},{144,176},{192,224},{208... | collective-permute-start | bytes 491528 | tf_op jit(solution)/shard_map/ppermute | solution.py:528
  56.8 3.9 %collective-permute-done.13.first = f32[2,10,4,512]{3,2,1,0:T(4,128)S(1)} collective-permute-done((f32[2,10,4,512]{3,2,1,0:T(4,128)S(1)}, f32[2,10,4,512]{3,2,1,0:T(4,128)S(1)}, u32[]{:S(2)}, u32[]{:S(2)}) %collective-permute-start.13) | collective-permute-done | bytes 163872 | tf_op jit(solution)/shard_map/ppermute | solution.py:528
  60.7 1.2 %shard_map.54 = (f32[48,512]{1,0:T(8,128)S(1)}, f32[8,8,128]{2,1,0:T(8,128)S(1)}) custom-call(s32[4]{0:T(128)S(1)} %pad_add_fusion.par_ref, f32[10,4,512]{2,1,0:T(4,128)S(1)} %bitcast.18, f32[10,4,512]{2,1,0:T(4,128)S(1)} %collective-permute-done.12.mate, f32[2,10,4,512]{3,2,1,0:T(4,128)S(1)} %collective-permute-done.13.first, ...), custom_call_target="tpu_custom_call" | custom-call | bytes 3600000 | tf_op jit(solution)/shard_map/pallas_call | solution.py:422
  61.9 20.8 %all_to_all.5.dots = f32[8,8,128]{2,1,0:T(8,128)S(1)} all-to-all(f32[8,8,128]{2,1,0:T(8,128)S(1)} %get-tuple-element.40), channel_id=1, replica_groups={{0,32,64,96,128,160,192,224},{16,48,80,112,144,176,208,240},{1,33,65,97..., dimensions={0} | all-to-all | bytes 65536 | tf_op jit(solution)/shard_map/all_to_all | solution.py:538
  82.7 4.0 %shard_map.55 = (f32[2,4,64,512]{3,2,1,0:T(8,128)}, f32[4,32]{1,0:T(4,128)}) custom-call(f32[48,512]{1,0:T(8,128)S(1)} %get-tuple-element.39.basis, f32[8,8,128]{2,1,0:T(8,128)S(1)} %all_to_all.5.dots, f32[512,32]{1,0:T(8,128)S(1)} %compare_convert_fusion.onehot, f32[7,80,512]{2,1,0:T(8,128)S(1)} %get-tuple-element.42.h0, ...), custom_call_target="tpu_custom_call" | custom-call | bytes 14400000 | tf_op jit(solution)/shard_map/pallas_call | solution.py:422
  (23 shorter events, 2.5 us)
Async XLA Ops:
  2.1 18.7 %copy-start.1 = (s32[512]{0:T(512)S(1)}, s32[512]{0:T(512)}, u32[]{:S(2)}) copy-start(s32[512]{0:T(512)} %param.5) | copy-start | bytes 6148
  2.1 4.1 %collective-permute-start = (f32[4,14,512]{2,1,0:T(8,128)S(1)}, f32[4,14,512]{2,1,0:T(8,128)S(1)}, u32[]{:S(2)}, u32[]{:S(2)}) collective-permute-start(f32[4,14,512]{2,1,0:T(8,128)S(1)} %get-tuple-element.25.own), channel_id=1, source_target_pairs={{16,32},{48,64},{80,96},{112,128},{144,160},{176,192},{208,224},{3... | collective-permute-start | bytes 344072 | tf_op jit(solution)/shard_map/ppermute | solution.py:474
  2.8 4.3 %collective-permute-start.1 = (f32[4,14,512]{2,1,0:T(8,128)S(1)}, f32[4,14,512]{2,1,0:T(8,128)S(1)}, u32[]{:S(2)}, u32[]{:S(2)}) collective-permute-start(f32[4,14,512]{2,1,0:T(8,128)S(1)} %get-tuple-element.25.own), channel_id=1, source_target_pairs={{0,16},{32,48},{64,80},{96,112},{128,144},{160,176},{192,208},{224... | collective-permute-start | bytes 344072 | tf_op jit(solution)/shard_map/ppermute | solution.py:475
  9.5 0.6 copy-start
  10.1 15.2 %collective-permute-start.2 = (f32[7,64,512]{2,1,0:T(8,128)}, f32[7,64,512]{2,1,0:T(8,128)S(1)}, u32[]{:S(2)}, u32[]{:S(2)}) collective-permute-start(f32[7,64,512]{2,1,0:T(8,128)} %get-tuple-element.27), channel_id=1, source_target_pairs={{16,32},{48,64},{80,96},{112,128},{144,160},{176,192},{208,224},{3... | collective-permute-start | bytes 2752520 | tf_op jit(solution)/shard_map/ppermute | solution.py:486
  10.8 14.5 %collective-permute-start.3 = (f32[7,64,512]{2,1,0:T(8,128)}, f32[7,64,512]{2,1,0:T(8,128)S(1)}, u32[]{:S(2)}, u32[]{:S(2)}) collective-permute-start(f32[7,64,512]{2,1,0:T(8,128)} %get-tuple-element.28), channel_id=1, source_target_pairs={{0,16},{32,48},{64,80},{96,112},{128,144},{160,176},{192,208},{224... | collective-permute-start | bytes 2752520 | tf_op jit(solution)/shard_map/ppermute | solution.py:487
  15.4 5.5 %collective-permute-start.4 = (f32[40,512]{1,0:T(8,128)}, f32[40,512]{1,0:T(8,128)S(1)}, u32[]{:S(2)}, u32[]{:S(2)}) collective-permute-start(f32[40,512]{1,0:T(8,128)} %copy-done), channel_id=1, source_target_pairs={{0,1},{2,3},{4,5},{6,7},{8,9},{10,11},{12,13},{14,15},{1,0},{3,2},... | collective-permute-start | bytes 245768 | tf_op jit(solution)/shard_map/ppermute | solution.py:488
  16.9 8.4 %collective-permute-start.5 = (f32[40,512]{1,0:T(8,128)S(1)}, f32[40,512]{1,0:T(8,128)S(1)}, u32[]{:S(2)}, u32[]{:S(2)}) collective-permute-start(f32[40,512]{1,0:T(8,128)S(1)} %get-tuple-element.30), channel_id=1, source_target_pairs={{1,2},{3,4},{5,6},{7,8},{9,10},{11,12},{13,14},{2,1},{4,3},{6,5},{... | collective-permute-start | bytes 245768 | tf_op jit(solution)/shard_map/ppermute | solution.py:489
  32.8 6.3 %collective-permute-start.8 = (f32[10,4,512]{2,1,0:T(4,128)S(1)}, f32[10,4,512]{2,1,0:T(4,128)S(1)}, u32[]{:S(2)}, u32[]{:S(2)}) collective-permute-start(f32[10,4,512]{2,1,0:T(4,128)S(1)} %get-tuple-element.32), channel_id=1, source_target_pairs={{0,3},{1,2},{2,1},{3,0},{4,7},{5,6},{6,5},{7,4},{8,11},{9,10},{10,... | collective-permute-start | bytes 245768 | tf_op jit(solution)/shard_map/ppermute | solution.py:508
  35.0 6.2 %collective-permute-start.7 = (f32[10,4,512]{2,1,0:T(4,128)S(1)}, f32[10,4,512]{2,1,0:T(4,128)S(1)}, u32[]{:S(2)}, u32[]{:S(2)}) collective-permute-start(f32[10,4,512]{2,1,0:T(4,128)S(1)} %get-tuple-element.32), channel_id=1, source_target_pairs={{0,2},{1,3},{2,0},{3,1},{4,6},{5,7},{6,4},{7,5},{8,10},{9,11},{10,... | collective-permute-start | bytes 245768 | tf_op jit(solution)/shard_map/ppermute | solution.py:508
  35.0 7.1 %collective-permute-start.6 = (f32[10,4,512]{2,1,0:T(4,128)S(1)}, f32[10,4,512]{2,1,0:T(4,128)S(1)}, u32[]{:S(2)}, u32[]{:S(2)}) collective-permute-start(f32[10,4,512]{2,1,0:T(4,128)S(1)} %get-tuple-element.32), channel_id=1, source_target_pairs={{0,1},{1,0},{2,3},{3,2},{4,5},{5,4},{6,7},{7,6},{8,9},{9,8},{10,11... | collective-permute-start | bytes 245768 | tf_op jit(solution)/shard_map/ppermute | solution.py:508
  42.1 9.3 %collective-permute-start.10 = (f32[10,4,512]{2,1,0:T(4,128)S(1)}, f32[10,4,512]{2,1,0:T(4,128)S(1)}, u32[]{:S(2)}, u32[]{:S(2)}) collective-permute-start(f32[10,4,512]{2,1,0:T(4,128)S(1)} %bitcast.21), channel_id=1, source_target_pairs={{0,8},{1,9},{2,10},{3,11},{4,12},{5,13},{6,14},{7,15},{8,0},{9,1},... | collective-permute-start | bytes 245768 | tf_op jit(solution)/shard_map/ppermute | solution.py:508
  42.2 9.2 %collective-permute-start.11 = (f32[10,4,512]{2,1,0:T(4,128)S(1)}, f32[10,4,512]{2,1,0:T(4,128)S(1)}, u32[]{:S(2)}, u32[]{:S(2)}) collective-permute-start(f32[10,4,512]{2,1,0:T(4,128)S(1)} %bitcast.22), channel_id=1, source_target_pairs={{0,12},{1,13},{2,14},{3,15},{4,8},{5,9},{6,10},{7,11},{8,4},{9,5},... | collective-permute-start | bytes 245768 | tf_op jit(solution)/shard_map/ppermute | solution.py:508
  44.9 6.5 %collective-permute-start.9 = (f32[10,4,512]{2,1,0:T(4,128)S(1)}, f32[10,4,512]{2,1,0:T(4,128)S(1)}, u32[]{:S(2)}, u32[]{:S(2)}) collective-permute-start(f32[10,4,512]{2,1,0:T(4,128)S(1)} %bitcast.23), channel_id=1, source_target_pairs={{0,4},{1,5},{2,6},{3,7},{4,0},{5,1},{6,2},{7,3},{8,12},{9,13},{10,... | collective-permute-start | bytes 245768 | tf_op jit(solution)/shard_map/ppermute | solution.py:508
  51.5 1.4 %collective-permute-start.12 = (f32[10,4,512]{2,1,0:T(4,128)S(1)}, f32[10,4,512]{2,1,0:T(4,128)S(1)}, u32[]{:S(2)}, u32[]{:S(2)}) collective-permute-start(f32[10,4,512]{2,1,0:T(4,128)S(1)} %bitcast.16), channel_id=1, source_target_pairs={{0,16},{32,48},{64,80},{96,112},{128,144},{160,176},{192,208},{224... | collective-permute-start | bytes 245768 | tf_op jit(solution)/shard_map/ppermute | solution.py:526
  52.9 7.8 %collective-permute-start.13 = (f32[2,10,4,512]{3,2,1,0:T(4,128)S(1)}, f32[2,10,4,512]{3,2,1,0:T(4,128)S(1)}, u32[]{:S(2)}, u32[]{:S(2)}) collective-permute-start(f32[2,10,4,512]{3,2,1,0:T(4,128)S(1)} %pad_maximum_fusion), channel_id=1, source_target_pairs={{0,32},{16,48},{64,96},{80,112},{128,160},{144,176},{192,224},{208... | collective-permute-start | bytes 491528 | tf_op jit(solution)/shard_map/ppermute | solution.py:528
  56.2 4.5 %collective-permute-start.14 = (f32[2,10,4,512]{3,2,1,0:T(4,128)S(1)}, f32[2,10,4,512]{3,2,1,0:T(4,128)S(1)}, u32[]{:S(2)}, u32[]{:S(2)}) collective-permute-start(f32[2,10,4,512]{3,2,1,0:T(4,128)S(1)} %pad_maximum_fusion), channel_id=1, source_target_pairs={{32,64},{48,80},{96,128},{112,144},{160,192},{176,208},{64,32},{80... | collective-permute-start | bytes 491528 | tf_op jit(solution)/shard_map/ppermute | solution.py:528

commit v7 on v6

--- a/solution.py
+++ b/solution.py
@@ -62,23 +62,18 @@
         out[:, 10 + 2 * c : 12 + 2 * c] = f[c, :, NY - 2 : NY]
 
 
-def pack(par, own, f, to_od, to_ev, sems):
-    copies = []
-    for n, (out, last) in enumerate(((to_od, par), (to_ev, 1 - par))):
-        copies.append(pltpu.make_async_copy(own.at[pl.ds(last, 3)], out.at[0:3], sems.at[3 * n]))
-        for c in range(2):
-            copies.append(
-                pltpu.make_async_copy(
-                    f.at[c, pl.ds(2 * last, 2)], out.at[3 + 2 * c : 5 + 2 * c], sems.at[1 + 3 * n + c]
-                )
-            )
-    return copies
-
-
-def corner_kernel(par_ref, own, od, ev, own_all, f_all, first, second, to_od, to_ev, low, high, sems):
-    copies = pack(par_ref[0], own_all, f_all, to_od, to_ev, sems)
-    for copy in copies:
-        copy.start()
+def pass_kernel(own, od_e, ev_e, out):
+    pass
+
+
+def pack(par, f, to_od, to_ev, sems):
+    return [
+        pltpu.make_async_copy(f.at[:, pl.ds(2 * last, 2)], out, sems.at[n])
+        for n, (out, last) in enumerate(((to_od, par), (to_ev, 1 - par)))
+    ]
+
+
+def corner_kernel(par_ref, own, od, ev, first, second, low, high):
     odd = par_ref[0] == 1
     below = lax.select(odd, ev[2:4], od[2:4])
     above = lax.select(odd, od[0:2], ev[0:2])
@@ -96,8 +91,6 @@
     odd = par_ref[2] == 1
     first[...] = lax.select(odd, low[...], high[...])
     second[...] = lax.select(odd, high[...], low[...])
-    for copy in copies:
-        copy.wait()
 
 
 def sides(odd, first, second):
@@ -106,8 +99,8 @@
 
 def fill_viscosity(par, v, own, od, ev, lo, hi, sems):
     copies = [pltpu.make_async_copy(own, v.at[3:7, LO:HI], sems.at[0])]
-    for n, at, x in ((1, par * 7, od), (2, 7 - par * 7, ev)):
-        copies.append(pltpu.make_async_copy(x.at[0:3], v.at[pl.ds(at, 3), LO:HI], sems.at[n]))
+    for n, at, last, x in ((1, par * 7, 1 - par, od), (2, 7 - par * 7, par, ev)):
+        copies.append(pltpu.make_async_copy(x.at[pl.ds(last, 3)], v.at[pl.ds(at, 3), LO:HI], sems.at[n]))
     for copy in copies:
         copy.start()
     for n in range(4):
@@ -139,10 +132,13 @@
     lax.fori_loop(0, 8, layer, 0)
 
 
-def stencil_kernel(par_ref, own, od, ev, first, second, f, out, v, d, fz, h0, ex, ez, ezm, acc, s_acc, sems):
+def stencil_kernel(par_ref, own, od, ev, first, second, f, out, to_od, to_ev, v, d, fz, h0, ex, ez, ezm, acc, s_acc, sems):
     par = par_ref[0]
     lo, hi = sides(par_ref[2] == 1, first, second)
     fill_viscosity(par, v, own, od, ev, lo, hi, sems)
+    packs = pack(par, f, to_od, to_ev, sems.at[pl.ds(3, 2)])
+    for copy in packs:
+        copy.start()
     fill_inverse(v, d, fz)
 
     ex[0] = E2 * d[0] * (v[1] + v[2]) * d[1]
@@ -232,6 +228,8 @@
     out[7:9] = e[0:8].reshape(2, 4, NZ)
     out[9, 0:1] = e[8:9]
     out[9, 1:4] = jnp.zeros((3, NZ), jnp.float32)
+    for copy in packs:
+        copy.wait()
 
 
 def krylov_kernel(par_ref, mine, mate, first, second, basis, dots, s_ref, g_ref):
@@ -320,7 +318,7 @@
     for at, x in ((par * 6, od), (6 - par * 6, ev)):
         dm = d[pl.ds(at, 2), LO:HI]
         for c in range(2):
-            u[c, pl.ds(at, 2), LO:HI] = dm * x[3 + 2 * c : 5 + 2 * c]
+            u[c, pl.ds(at, 2), LO:HI] = dm * x[c]
     for c in range(2):
         for n in range(4):
             u[c, 2 + n, LO - 2 : LO] = d[2 + n, LO - 2 : LO] * lo[7 * n + 3 + 2 * c : 7 * n + 5 + 2 * c]
@@ -418,7 +416,7 @@
 HBM = pl.BlockSpec(memory_space=pltpu.HBM)
 
 
-def call(kernel, out_shape, scratch, args, in_specs, out_specs=None, micros=1.0, sems=0, mib=16):
+def call(kernel, out_shape, scratch, args, in_specs, out_specs=None, micros=1.0, sems=0, mib=16, aliases={}):
     return pl.pallas_call(
         kernel,
         out_shape=out_shape,
@@ -426,6 +424,7 @@
         out_specs=out_specs or jax.tree.map(lambda _: VMEM, out_shape),
         scratch_shapes=[pltpu.VMEM(s, jnp.float32) for s in scratch]
         + ([pltpu.SemaphoreType.DMA((sems,))] if sems else []),
+        input_output_aliases=aliases,
         compiler_params=pltpu.CompilerParams(vmem_limit_bytes=mib * 1024 * 1024),
         cost_estimate=pl.CostEstimate(flops=0, transcendentals=0, bytes_accessed=int(micros * 3.6e6)),
     )(*args)
@@ -473,30 +472,39 @@
     )
     od_e = lax.ppermute(edges, "slab", others)
     ev_e = lax.ppermute(edges, "slab", mates)
-    layers = pltpu.VMEM((7, NY, NZ), jnp.float32)
-    first, second, to_od, to_ev = call(
+    late = call(
+        pass_kernel,
+        pltpu.VMEM(viscosity.shape, jnp.float32),
+        [],
+        (in_vmem(own), in_vmem(od_e), in_vmem(ev_e)),
+        in_specs=[VMEM] * 3,
+        mib=2,
+        aliases={0: 0},
+    )
+    od = lax.ppermute(late, "slab", others)
+    ev = lax.ppermute(late, "slab", mates)
+    rows = pltpu.VMEM((40, NZ), jnp.float32)
+    first, second = call(
         corner_kernel,
-        (f32(40, NZ), f32(40, NZ), layers, layers),
+        (rows, rows),
         [(40, NZ), (40, NZ)],
-        (where, in_vmem(edges), in_vmem(od_e), in_vmem(ev_e), in_vmem(own), in_vmem(f)),
-        in_specs=[SMEM] + [VMEM] * 5,
-        sems=6,
+        (where, in_vmem(edges), in_vmem(od_e), in_vmem(ev_e)),
+        in_specs=[SMEM] + [VMEM] * 3,
         mib=4,
     )
-    od = lax.ppermute(to_od, "slab", others)
-    ev = lax.ppermute(to_ev, "slab", mates)
     first = lax.ppermute(first, "cross", pairs(cross, 0))
     second = lax.ppermute(second, "cross", pairs(cross, 1))
 
     kept = (f32(10, FRAME, NZ), f32(8, FRAME, NZ), f32(8, FRAME, NZ)) + (f32(7, FRAME, NZ),) * 3
-    part, v, d, fz, h0, ex, ez = call(
+    layers = pltpu.VMEM((2, 2, NY, NZ), jnp.float32)
+    part, to_od, to_ev, v, d, fz, h0, ex, ez = call(
         stencil_kernel,
-        (f32(10, 4, NZ), *[pltpu.VMEM(x.shape, x.dtype) for x in kept]),
+        (f32(10, 4, NZ), layers, layers, *[pltpu.VMEM(x.shape, x.dtype) for x in kept]),
         [(7, FRAME, NZ), (5, 2, 8, 8, NZ), (7, ROWS, 8, NZ)],
-        (where, in_vmem(own), in_vmem(od), in_vmem(ev), first, second, in_vmem(f)),
+        (where, in_vmem(late), in_vmem(od), in_vmem(ev), in_vmem(first), in_vmem(second), in_vmem(f)),
         in_specs=[SMEM] + [VMEM] * 6,
         micros=6,
-        sems=4,
+        sems=5,
         mib=8,
     )
 
@@ -508,6 +516,8 @@
         return [lax.ppermute(x, "cross", [(i, i ^ (n * step)) for i in range(cross)]) for n in (1, 2, 3)]
 
     part, onehot = lax.optimization_barrier((part, onehot))
+    od_f = lax.ppermute(to_od, "slab", others)
+    ev_f = lax.ppermute(to_ev, "slab", mates)
     got = among(part, 1)
     part = part + got[0] + got[1] + got[2]
     got = among(part, 4)
@@ -515,7 +525,7 @@
         forced_kernel,
         pltpu.VMEM((2, ROWS, NY, NZ), jnp.float32),
         [(2, 8, FRAME, NZ)] * 2,
-        (where, in_vmem(f), in_vmem(od), in_vmem(ev), first, second, in_vmem(v), in_vmem(d), in_vmem(fz)),
+        (where, in_vmem(f), in_vmem(od_f), in_vmem(ev_f), in_vmem(first), in_vmem(second), in_vmem(v), in_vmem(d), in_vmem(fz)),
         in_specs=[SMEM] + [VMEM] * 8,
         micros=5,
         mib=8,

time: 87 us -> 85.1 us (0.978)
  starting transfers between devices: 27.7 us -> 30.5 us
  blocking collectives: 20.8 us -> 18.9 us
  Pallas kernels: 20.9 us -> 19.2 us
    ppermute x2 -> x4, starting transfers between devices: 5.28 us -> 9.31 us  [the longest x1 4.6 us: shards(): ev = lax.ppermute(late, 'slab', mates)]
    all_to_all x1, blocking collectives: 20.8 us -> 18.9 us  [shards(): lax.all_to_all(dots, 'slab', 0, 0, tiled=True, axis_index_groups=groups)]
    pallas_call x6 -> x7, Pallas kernels: 20.9 us -> 19.2 us  [call(): pl.pallas_call(kernel, out_shape=out_shape, in_specs=in_specs, out_specs=...]
    ppermute x1, starting transfers between devices: 3.29 us -> 2 us  [shards(): lax.ppermute(both, 'slab', first_chips)]
  transfers between devices with their start and end apart: 15 -> 17, of which waited for: 7 -> 6; matrix products, arithmetic and copies ran while one was open for 0% -> 0% of each run, Pallas kernels for 5% -> 6%
where the time goes in v7:
time: 85.1 us; the launch traced here: 84.8 us
  starting transfers between devices  30.5 us (36%)
  Pallas kernels  19.2 us (23%)
  blocking collectives  18.9 us (22%)
  waiting for transfers between devices  15.1 us (18%)
    pallas_call x7, Pallas kernels, call(): pl.pallas_call(kernel, out_shape=out_shape, in_specs=in_specs, out_specs=...  19.2 us
    all_to_all x1, blocking collectives, shards(): lax.all_to_all(dots, 'slab', 0, 0, tiled=True, axis_index_groups=groups)  18.9 us
    ppermute x6, starting transfers between devices, among(): lax.ppermute(x, 'cross', [(i, i ^ n * step) for i in range(cross)])  8.97 us
    ppermute x1, starting transfers between devices, shards(): ev = lax.ppermute(late, 'slab', mates)  4.6 us
    ppermute x1, waiting for transfers between devices, shards(): second = lax.ppermute(second, 'cross', pairs(cross, 1))  4.52 us
    ppermute x6, waiting for transfers between devices, among(): lax.ppermute(x, 'cross', [(i, i ^ n * step) for i in range(cross)])  4.48 us
    ppermute x1, starting transfers between devices, shards(): second = lax.ppermute(second, 'cross', pairs(cross, 1))  3.88 us
    ppermute x1, waiting for transfers between devices, shards(): lax.ppermute(both, 'slab', first_chips)  3.85 us
  transfers between devices with their start and end apart: 17, of which 6 were waited for; matrix products, arithmetic and copies ran while one was open for 0% of the time, Pallas kernels for 6%

profile of v7, /device:TPU:16, one launch (start us, length us, event | category | flops | bytes accessed | tf_op | source)
XLA Modules:
  0.0 84.8 jit_solution(13069778503854922451)
XLA Ops:
  0.6 1.4 %shard_map.50 = (f32[4,14,512]{2,1,0:T(8,128)S(1)}, f32[4,64,512]{2,1,0:T(8,128)S(1)}, f32[2,4,64,512]{3,2,1,0:T(8,128)S(1)}) custom-call(f32[4,64,512]{2,1,0:T(8,128)} %own_hbm.1, f32[2,4,64,512]{3,2,1,0:T(8,128)} %f_hbm.1), custom_call_target="tpu_custom_call" | custom-call | bytes 3600000 | tf_op jit(solution)/shard_map/pallas_call | solution.py:420
  2.7 3.4 %collective-permute-start.1 = (f32[4,14,512]{2,1,0:T(8,128)S(1)}, f32[4,14,512]{2,1,0:T(8,128)S(1)}, u32[]{:S(2)}, u32[]{:S(2)}) collective-permute-start(f32[4,14,512]{2,1,0:T(8,128)S(1)} %get-tuple-element.25.own), channel_id=1, source_target_pairs={{0,16},{32,48},{64,80},{96,112},{128,144},{160,176},{192,208},{224... | collective-permute-start | bytes 344072 | tf_op jit(solution)/shard_map/ppermute | solution.py:474
  6.1 1.0 %collective-permute-done.1.ev_e.ev = f32[4,14,512]{2,1,0:T(8,128)S(1)} collective-permute-done((f32[4,14,512]{2,1,0:T(8,128)S(1)}, f32[4,14,512]{2,1,0:T(8,128)S(1)}, u32[]{:S(2)}, u32[]{:S(2)}) %collective-permute-start.1) | collective-permute-done | bytes 114720 | tf_op jit(solution)/shard_map/ppermute | solution.py:474
  7.1 0.7 collective-permute-start.2
  7.8 4.6 %collective-permute-start.3 = (f32[4,64,512]{2,1,0:T(8,128)S(1)}, f32[4,64,512]{2,1,0:T(8,128)S(1)}, u32[]{:S(2)}, u32[]{:S(2)}) collective-permute-start(f32[4,64,512]{2,1,0:T(8,128)S(1)} %shard_map.51.own), channel_id=1, source_target_pairs={{0,16},{32,48},{64,80},{96,112},{128,144},{160,176},{192,208},{224... | collective-permute-start | bytes 1572872 | tf_op jit(solution)/shard_map/ppermute | solution.py:485
  13.1 1.6 %collective-permute-start.4 = (f32[40,512]{1,0:T(8,128)S(1)}, f32[40,512]{1,0:T(8,128)S(1)}, u32[]{:S(2)}, u32[]{:S(2)}) collective-permute-start(f32[40,512]{1,0:T(8,128)S(1)} %get-tuple-element.26), channel_id=1, source_target_pairs={{0,1},{2,3},{4,5},{6,7},{8,9},{10,11},{12,13},{14,15},{1,0},{3,2},... | collective-permute-start | bytes 245768 | tf_op jit(solution)/shard_map/ppermute | solution.py:495
  14.6 3.9 %collective-permute-start.5 = (f32[40,512]{1,0:T(8,128)S(1)}, f32[40,512]{1,0:T(8,128)S(1)}, u32[]{:S(2)}, u32[]{:S(2)}) collective-permute-start(f32[40,512]{1,0:T(8,128)S(1)} %get-tuple-element.27), channel_id=1, source_target_pairs={{1,2},{3,4},{5,6},{7,8},{9,10},{11,12},{13,14},{2,1},{4,3},{6,5},{... | collective-permute-start | bytes 245768 | tf_op jit(solution)/shard_map/ppermute | solution.py:496
  18.6 4.5 %collective-permute-done.5.second = f32[40,512]{1,0:T(8,128)S(1)} collective-permute-done((f32[40,512]{1,0:T(8,128)S(1)}, f32[40,512]{1,0:T(8,128)S(1)}, u32[]{:S(2)}, u32[]{:S(2)}) %collective-permute-start.5) | collective-permute-done | bytes 81952 | tf_op jit(solution)/shard_map/ppermute | solution.py:496
  23.1 7.5 %shard_map.53 = (f32[10,4,512]{2,1,0:T(4,128)S(1)}, f32[2,2,64,512]{3,2,1,0:T(8,128)S(1)}, f32[2,2,64,512]{3,2,1,0:T(8,128)S(1)}, f32[10,80,512]{2,1,0:T(8,128)S...) custom-call(s32[4]{0:T(128)S(1)} %pad_add_fusion.par_ref, ...), custom_call_target="tpu_custom_call" | custom-call | bytes 21600000 | tf_op jit(solution)/shard_map/pallas_call | solution.py:420
  30.6 0.7 collective-permute-start.12
  31.3 3.3 %collective-permute-start.13 = (f32[2,2,64,512]{3,2,1,0:T(8,128)S(1)}, f32[2,2,64,512]{3,2,1,0:T(8,128)S(1)}, u32[]{:S(2)}, u32[]{:S(2)}) collective-permute-start(f32[2,2,64,512]{3,2,1,0:T(8,128)S(1)} %get-tuple-element.32), channel_id=1, source_target_pairs={{0,16},{32,48},{64,80},{96,112},{128,144},{160,176},{192,208},{224... | collective-permute-start | bytes 1572872 | tf_op jit(solution)/shard_map/ppermute | solution.py:520
  34.8 2.2 %collective-permute-start.8 = (f32[10,4,512]{2,1,0:T(4,128)S(1)}, f32[10,4,512]{2,1,0:T(4,128)S(1)}, u32[]{:S(2)}, u32[]{:S(2)}) collective-permute-start(f32[10,4,512]{2,1,0:T(4,128)S(1)} %get-tuple-element.30), channel_id=1, source_target_pairs={{0,3},{1,2},{2,1},{3,0},{4,7},{5,6},{6,5},{7,4},{8,11},{9,10},{10,... | collective-permute-start | bytes 245768 | tf_op jit(solution)/shard_map/ppermute | solution.py:516
  36.9 2.0 %collective-permute-start.6 = (f32[10,4,512]{2,1,0:T(4,128)S(1)}, f32[10,4,512]{2,1,0:T(4,128)S(1)}, u32[]{:S(2)}, u32[]{:S(2)}) collective-permute-start(f32[10,4,512]{2,1,0:T(4,128)S(1)} %get-tuple-element.30), channel_id=1, source_target_pairs={{0,1},{1,0},{2,3},{3,2},{4,5},{5,4},{6,7},{7,6},{8,9},{9,8},{10,11... | collective-permute-start | bytes 245768 | tf_op jit(solution)/shard_map/ppermute | solution.py:516
  38.9 1.6 %collective-permute-done.8 = f32[10,4,512]{2,1,0:T(4,128)S(1)} collective-permute-done((f32[10,4,512]{2,1,0:T(4,128)S(1)}, f32[10,4,512]{2,1,0:T(4,128)S(1)}, u32[]{:S(2)}, u32[]{:S(2)}) %collective-permute-start.8) | collective-permute-done | bytes 81952 | tf_op jit(solution)/shard_map/ppermute | solution.py:516
  40.5 2.9 %collective-permute-done.7 = f32[10,4,512]{2,1,0:T(4,128)S(1)} collective-permute-done((f32[10,4,512]{2,1,0:T(4,128)S(1)}, f32[10,4,512]{2,1,0:T(4,128)S(1)}, u32[]{:S(2)}, u32[]{:S(2)}) %collective-permute-start.7) | collective-permute-done | bytes 81952 | tf_op jit(solution)/shard_map/ppermute | solution.py:516
  43.9 1.8 %collective-permute-start.11 = (f32[10,4,512]{2,1,0:T(4,128)S(1)}, f32[10,4,512]{2,1,0:T(4,128)S(1)}, u32[]{:S(2)}, u32[]{:S(2)}) collective-permute-start(f32[10,4,512]{2,1,0:T(4,128)S(1)} %bitcast.22), channel_id=1, source_target_pairs={{0,12},{1,13},{2,14},{3,15},{4,8},{5,9},{6,10},{7,11},{8,4},{9,5},... | collective-permute-start | bytes 245768 | tf_op jit(solution)/shard_map/ppermute | solution.py:516
  45.6 2.6 %collective-permute-start.9 = (f32[10,4,512]{2,1,0:T(4,128)S(1)}, f32[10,4,512]{2,1,0:T(4,128)S(1)}, u32[]{:S(2)}, u32[]{:S(2)}) collective-permute-start(f32[10,4,512]{2,1,0:T(4,128)S(1)} %bitcast.23), channel_id=1, source_target_pairs={{0,4},{1,5},{2,6},{3,7},{4,0},{5,1},{6,2},{7,3},{8,12},{9,13},{10,... | collective-permute-start | bytes 245768 | tf_op jit(solution)/shard_map/ppermute | solution.py:516
  48.2 4.5 %shard_map.54.forced = f32[2,4,64,512]{3,2,1,0:T(8,128)S(1)} custom-call(s32[4]{0:T(128)S(1)} %pad_add_fusion.par_ref, f32[2,4,64,512]{3,2,1,0:T(8,128)S(1)} %get-tuple-element.28.f, f32[2,2,64,512]{3,2,1,0:T(8,128)S(1)} %collective-permute-done.12.od, f32[2,2,64,512]{3,2,1,0:T(8,128)S(1)} %collective-permute-done.13.ev, ...), custom_call_target="tpu_custom_call" | custom-call | bytes 18000000 | tf_op jit(solution)/shard_map/pallas_call | solution.py:420
  52.9 1.3 %collective-permute-done.14.mate = f32[10,4,512]{2,1,0:T(4,128)S(1)} collective-permute-done((f32[10,4,512]{2,1,0:T(4,128)S(1)}, f32[10,4,512]{2,1,0:T(4,128)S(1)}, u32[]{:S(2)}, u32[]{:S(2)}) %collective-permute-start.14) | collective-permute-done | bytes 81952 | tf_op jit(solution)/shard_map/ppermute | solution.py:536
  54.2 2.0 %collective-permute-start.15 = (f32[2,10,4,512]{3,2,1,0:T(4,128)S(1)}, f32[2,10,4,512]{3,2,1,0:T(4,128)S(1)}, u32[]{:S(2)}, u32[]{:S(2)}) collective-permute-start(f32[2,10,4,512]{3,2,1,0:T(4,128)S(1)} %pad_maximum_fusion), channel_id=1, source_target_pairs={{0,32},{16,48},{64,96},{80,112},{128,160},{144,176},{192,224},{208... | collective-permute-start | bytes 491528 | tf_op jit(solution)/shard_map/ppermute | solution.py:538
  56.9 3.9 %collective-permute-done.15.first = f32[2,10,4,512]{3,2,1,0:T(4,128)S(1)} collective-permute-done((f32[2,10,4,512]{3,2,1,0:T(4,128)S(1)}, f32[2,10,4,512]{3,2,1,0:T(4,128)S(1)}, u32[]{:S(2)}, u32[]{:S(2)}) %collective-permute-start.15) | collective-permute-done | bytes 163872 | tf_op jit(solution)/shard_map/ppermute | solution.py:538
  60.8 1.2 %shard_map.55 = (f32[48,512]{1,0:T(8,128)S(1)}, f32[8,8,128]{2,1,0:T(8,128)S(1)}) custom-call(s32[4]{0:T(128)S(1)} %pad_add_fusion.par_ref, f32[10,4,512]{2,1,0:T(4,128)S(1)} %bitcast.18, f32[10,4,512]{2,1,0:T(4,128)S(1)} %collective-permute-done.14.mate, f32[2,10,4,512]{3,2,1,0:T(4,128)S(1)} %collective-permute-done.15.first, ...), custom_call_target="tpu_custom_call" | custom-call | bytes 3600000 | tf_op jit(solution)/shard_map/pallas_call | solution.py:420
  62.0 18.9 %all_to_all.5.dots = f32[8,8,128]{2,1,0:T(8,128)S(1)} all-to-all(f32[8,8,128]{2,1,0:T(8,128)S(1)} %get-tuple-element.40), channel_id=1, replica_groups={{0,32,64,96,128,160,192,224},{16,48,80,112,144,176,208,240},{1,33,65,97..., dimensions={0} | all-to-all | bytes 65536 | tf_op jit(solution)/shard_map/all_to_all | solution.py:548
  80.8 4.0 %shard_map.56 = (f32[2,4,64,512]{3,2,1,0:T(8,128)}, f32[4,32]{1,0:T(4,128)}) custom-call(f32[48,512]{1,0:T(8,128)S(1)} %get-tuple-element.39.basis, f32[8,8,128]{2,1,0:T(8,128)S(1)} %all_to_all.5.dots, f32[512,32]{1,0:T(8,128)S(1)} %compare_convert_fusion.onehot, f32[7,80,512]{2,1,0:T(8,128)S(1)} %get-tuple-element.42.h0, ...), custom_call_target="tpu_custom_call" | custom-call | bytes 14400000 | tf_op jit(solution)/shard_map/pallas_call | solution.py:420
  (26 shorter events, 2.8 us)
Async XLA Ops:
  2.1 4.0 %collective-permute-start = (f32[4,14,512]{2,1,0:T(8,128)S(1)}, f32[4,14,512]{2,1,0:T(8,128)S(1)}, u32[]{:S(2)}, u32[]{:S(2)}) collective-permute-start(f32[4,14,512]{2,1,0:T(8,128)S(1)} %get-tuple-element.25.own), channel_id=1, source_target_pairs={{16,32},{48,64},{80,96},{112,128},{144,160},{176,192},{208,224},{3... | collective-permute-start | bytes 344072 | tf_op jit(solution)/shard_map/ppermute | solution.py:473
  2.7 4.3 %collective-permute-start.1 = (f32[4,14,512]{2,1,0:T(8,128)S(1)}, f32[4,14,512]{2,1,0:T(8,128)S(1)}, u32[]{:S(2)}, u32[]{:S(2)}) collective-permute-start(f32[4,14,512]{2,1,0:T(8,128)S(1)} %get-tuple-element.25.own), channel_id=1, source_target_pairs={{0,16},{32,48},{64,80},{96,112},{128,144},{160,176},{192,208},{224... | collective-permute-start | bytes 344072 | tf_op jit(solution)/shard_map/ppermute | solution.py:474
  7.1 16.0 %collective-permute-start.2 = (f32[4,64,512]{2,1,0:T(8,128)S(1)}, f32[4,64,512]{2,1,0:T(8,128)S(1)}, u32[]{:S(2)}, u32[]{:S(2)}) collective-permute-start(f32[4,64,512]{2,1,0:T(8,128)S(1)} %shard_map.51.own), channel_id=1, source_target_pairs={{16,32},{48,64},{80,96},{112,128},{144,160},{176,192},{208,224},{3... | collective-permute-start | bytes 1572872 | tf_op jit(solution)/shard_map/ppermute | solution.py:484
  7.8 15.3 %collective-permute-start.3 = (f32[4,64,512]{2,1,0:T(8,128)S(1)}, f32[4,64,512]{2,1,0:T(8,128)S(1)}, u32[]{:S(2)}, u32[]{:S(2)}) collective-permute-start(f32[4,64,512]{2,1,0:T(8,128)S(1)} %shard_map.51.own), channel_id=1, source_target_pairs={{0,16},{32,48},{64,80},{96,112},{128,144},{160,176},{192,208},{224... | collective-permute-start | bytes 1572872 | tf_op jit(solution)/shard_map/ppermute | solution.py:485
  13.1 5.5 %collective-permute-start.4 = (f32[40,512]{1,0:T(8,128)S(1)}, f32[40,512]{1,0:T(8,128)S(1)}, u32[]{:S(2)}, u32[]{:S(2)}) collective-permute-start(f32[40,512]{1,0:T(8,128)S(1)} %get-tuple-element.26), channel_id=1, source_target_pairs={{0,1},{2,3},{4,5},{6,7},{8,9},{10,11},{12,13},{14,15},{1,0},{3,2},... | collective-permute-start | bytes 245768 | tf_op jit(solution)/shard_map/ppermute | solution.py:495
  14.6 8.4 %collective-permute-start.5 = (f32[40,512]{1,0:T(8,128)S(1)}, f32[40,512]{1,0:T(8,128)S(1)}, u32[]{:S(2)}, u32[]{:S(2)}) collective-permute-start(f32[40,512]{1,0:T(8,128)S(1)} %get-tuple-element.27), channel_id=1, source_target_pairs={{1,2},{3,4},{5,6},{7,8},{9,10},{11,12},{13,14},{2,1},{4,3},{6,5},{... | collective-permute-start | bytes 245768 | tf_op jit(solution)/shard_map/ppermute | solution.py:496
  23.1 11.5 %copy-start = (s32[512]{0:T(512)S(1)}, s32[512]{0:T(512)}, u32[]{:S(2)}) copy-start(s32[512]{0:T(512)} %param.5) | copy-start | bytes 6148
  30.6 17.7 %collective-permute-start.12 = (f32[2,2,64,512]{3,2,1,0:T(8,128)S(1)}, f32[2,2,64,512]{3,2,1,0:T(8,128)S(1)}, u32[]{:S(2)}, u32[]{:S(2)}) collective-permute-start(f32[2,2,64,512]{3,2,1,0:T(8,128)S(1)} %get-tuple-element.31), channel_id=1, source_target_pairs={{16,32},{48,64},{80,96},{112,128},{144,160},{176,192},{208,224},{3... | collective-permute-start | bytes 1572872 | tf_op jit(solution)/shard_map/ppermute | solution.py:519
  31.3 17.0 %collective-permute-start.13 = (f32[2,2,64,512]{3,2,1,0:T(8,128)S(1)}, f32[2,2,64,512]{3,2,1,0:T(8,128)S(1)}, u32[]{:S(2)}, u32[]{:S(2)}) collective-permute-start(f32[2,2,64,512]{3,2,1,0:T(8,128)S(1)} %get-tuple-element.32), channel_id=1, source_target_pairs={{0,16},{32,48},{64,80},{96,112},{128,144},{160,176},{192,208},{224... | collective-permute-start | bytes 1572872 | tf_op jit(solution)/shard_map/ppermute | solution.py:520
  34.8 5.7 %collective-permute-start.8 = (f32[10,4,512]{2,1,0:T(4,128)S(1)}, f32[10,4,512]{2,1,0:T(4,128)S(1)}, u32[]{:S(2)}, u32[]{:S(2)}) collective-permute-start(f32[10,4,512]{2,1,0:T(4,128)S(1)} %get-tuple-element.30), channel_id=1, source_target_pairs={{0,3},{1,2},{2,1},{3,0},{4,7},{5,6},{6,5},{7,4},{8,11},{9,10},{10,... | collective-permute-start | bytes 245768 | tf_op jit(solution)/shard_map/ppermute | solution.py:516
  36.9 6.5 %collective-permute-start.7 = (f32[10,4,512]{2,1,0:T(4,128)S(1)}, f32[10,4,512]{2,1,0:T(4,128)S(1)}, u32[]{:S(2)}, u32[]{:S(2)}) collective-permute-start(f32[10,4,512]{2,1,0:T(4,128)S(1)} %get-tuple-element.30), channel_id=1, source_target_pairs={{0,2},{1,3},{2,0},{3,1},{4,6},{5,7},{6,4},{7,5},{8,10},{9,11},{10,... | collective-permute-start | bytes 245768 | tf_op jit(solution)/shard_map/ppermute | solution.py:516
  36.9 6.5 %collective-permute-start.6 = (f32[10,4,512]{2,1,0:T(4,128)S(1)}, f32[10,4,512]{2,1,0:T(4,128)S(1)}, u32[]{:S(2)}, u32[]{:S(2)}) collective-permute-start(f32[10,4,512]{2,1,0:T(4,128)S(1)} %get-tuple-element.30), channel_id=1, source_target_pairs={{0,1},{1,0},{2,3},{3,2},{4,5},{5,4},{6,7},{7,6},{8,9},{9,8},{10,11... | collective-permute-start | bytes 245768 | tf_op jit(solution)/shard_map/ppermute | solution.py:516
  43.4 9.3 %collective-permute-start.10 = (f32[10,4,512]{2,1,0:T(4,128)S(1)}, f32[10,4,512]{2,1,0:T(4,128)S(1)}, u32[]{:S(2)}, u32[]{:S(2)}) collective-permute-start(f32[10,4,512]{2,1,0:T(4,128)S(1)} %bitcast.21), channel_id=1, source_target_pairs={{0,8},{1,9},{2,10},{3,11},{4,12},{5,13},{6,14},{7,15},{8,0},{9,1},... | collective-permute-start | bytes 245768 | tf_op jit(solution)/shard_map/ppermute | solution.py:516
  43.9 8.9 %collective-permute-start.11 = (f32[10,4,512]{2,1,0:T(4,128)S(1)}, f32[10,4,512]{2,1,0:T(4,128)S(1)}, u32[]{:S(2)}, u32[]{:S(2)}) collective-permute-start(f32[10,4,512]{2,1,0:T(4,128)S(1)} %bitcast.22), channel_id=1, source_target_pairs={{0,12},{1,13},{2,14},{3,15},{4,8},{5,9},{6,10},{7,11},{8,4},{9,5},... | collective-permute-start | bytes 245768 | tf_op jit(solution)/shard_map/ppermute | solution.py:516
  45.6 7.2 %collective-permute-start.9 = (f32[10,4,512]{2,1,0:T(4,128)S(1)}, f32[10,4,512]{2,1,0:T(4,128)S(1)}, u32[]{:S(2)}, u32[]{:S(2)}) collective-permute-start(f32[10,4,512]{2,1,0:T(4,128)S(1)} %bitcast.23), channel_id=1, source_target_pairs={{0,4},{1,5},{2,6},{3,7},{4,0},{5,1},{6,2},{7,3},{8,12},{9,13},{10,... | collective-permute-start | bytes 245768 | tf_op jit(solution)/shard_map/ppermute | solution.py:516
  52.8 1.4 %collective-permute-start.14 = (f32[10,4,512]{2,1,0:T(4,128)S(1)}, f32[10,4,512]{2,1,0:T(4,128)S(1)}, u32[]{:S(2)}, u32[]{:S(2)}) collective-permute-start(f32[10,4,512]{2,1,0:T(4,128)S(1)} %bitcast.16), channel_id=1, source_target_pairs={{0,16},{32,48},{64,80},{96,112},{128,144},{160,176},{192,208},{224... | collective-permute-start | bytes 245768 | tf_op jit(solution)/shard_map/ppermute | solution.py:536
  54.2 6.5 %collective-permute-start.15 = (f32[2,10,4,512]{3,2,1,0:T(4,128)S(1)}, f32[2,10,4,512]{3,2,1,0:T(4,128)S(1)}, u32[]{:S(2)}, u32[]{:S(2)}) collective-permute-start(f32[2,10,4,512]{3,2,1,0:T(4,128)S(1)} %pad_maximum_fusion), channel_id=1, source_target_pairs={{0,32},{16,48},{64,96},{80,112},{128,160},{144,176},{192,224},{208... | collective-permute-start | bytes 491528 | tf_op jit(solution)/shard_map/ppermute | solution.py:538
  56.3 4.5 %collective-permute-start.16 = (f32[2,10,4,512]{3,2,1,0:T(4,128)S(1)}, f32[2,10,4,512]{3,2,1,0:T(4,128)S(1)}, u32[]{:S(2)}, u32[]{:S(2)}) collective-permute-start(f32[2,10,4,512]{3,2,1,0:T(4,128)S(1)} %pad_maximum_fusion), channel_id=1, source_target_pairs={{32,64},{48,80},{96,128},{112,144},{160,192},{176,208},{64,32},{80... | collective-permute-start | bytes 491528 | tf_op jit(solution)/shard_map/ppermute | solution.py:538

commit v8 on v7

--- a/solution.py
+++ b/solution.py
@@ -232,7 +232,7 @@
         copy.wait()
 
 
-def krylov_kernel(par_ref, mine, mate, first, second, basis, dots, s_ref, g_ref):
+def krylov_kernel(par_ref, mine, mate, first, second, crossed, basis, dots, s_ref, g_ref):
     par, chip = par_ref[0], par_ref[1]
     odd = par == 1
 
@@ -240,8 +240,10 @@
         return lax.select(odd, b, a), lax.select(odd, a, b)
 
     slabs = []
-    below, above = sides(par_ref[3] == 1, first, second)
-    for a, b in ((below[0], below[1]), (mine[...], mate[...]), (above[0], above[1])):
+    high = par_ref[3] == 1
+    below, above = sides(high, first, second)
+    below_mate, above_mate = sides(high, crossed.at[0], crossed.at[1])
+    for a, b in ((below, below_mate), (mine[...], mate[...]), (above, above_mate)):
         slabs += pair(a, b)
     W = 24
     g_ref[...] = jnp.zeros_like(g_ref)
@@ -534,14 +536,14 @@
     part = part + got[0] + got[1] + got[2]
 
     mate = lax.ppermute(part, "slab", mates)
-    both = jnp.stack([part, mate])
-    window = (lax.ppermute(both, "slab", first_chips), lax.ppermute(both, "slab", second_chips))
+    near = (lax.ppermute(part, "slab", first_chips), lax.ppermute(part, "slab", second_chips))
+    crossed = lax.ppermute(jnp.stack(near), "slab", mates)
     basis, dots = call(
         krylov_kernel,
         (f32(48, NZ), f32(chips, 8, 128)),
         [(7, 24, NZ), (40, NZ)],
-        (where, part, mate, *window),
-        in_specs=[SMEM] + [VMEM] * 4,
+        (where, part, mate, *near, crossed),
+        in_specs=[SMEM] + [VMEM] * 5,
         mib=4,
     )
     groups = [[2 * z + c for z in range(chips)] for c in range(2)]

time: 85.1 us -> 84 us (0.987)
  waiting for transfers between devices: 15.1 us -> 12.9 us
    ppermute x2 -> x3, waiting for transfers between devices: 3.86 us -> 1.87 us  [the longest x1 1.86 us: shards(): lax.ppermute(part, 'slab', first_chips)]
    ppermute x2 -> x3, starting transfers between devices: 2.66 us -> 2.75 us  [the longest x1 2 us: shards(): lax.ppermute(part, 'slab', first_chips)]
  transfers between devices with their start and end apart: 17 -> 18, of which waited for: 6 -> 6; matrix products, arithmetic and copies ran while one was open for 0% -> 0% of each run, Pallas kernels for 6% -> 6%
where the time goes in v8:
time: 84 us; the launch traced here: 83.7 us
  starting transfers between devices  31 us (37%)
  blocking collectives  19.3 us (23%)
  Pallas kernels  19.2 us (23%)
  waiting for transfers between devices  12.9 us (15%)
  between operations  0.95 us (1%)
    all_to_all x1, blocking collectives, shards(): lax.all_to_all(dots, 'slab', 0, 0, tiled=True, axis_index_groups=groups)  19.3 us
    pallas_call x7, Pallas kernels, call(): pl.pallas_call(kernel, out_shape=out_shape, in_specs=in_specs, out_specs=...  19.2 us
    ppermute x6, starting transfers between devices, among(): lax.ppermute(x, 'cross', [(i, i ^ n * step) for i in range(cross)])  8.97 us
    ppermute x1, starting transfers between devices, shards(): ev = lax.ppermute(late, 'slab', mates)  4.6 us
    ppermute x1, waiting for transfers between devices, shards(): second = lax.ppermute(second, 'cross', pairs(cross, 1))  4.52 us
    ppermute x6, waiting for transfers between devices, among(): lax.ppermute(x, 'cross', [(i, i ^ n * step) for i in range(cross)])  4.48 us
    ppermute x1, starting transfers between devices, shards(): second = lax.ppermute(second, 'cross', pairs(cross, 1))  3.88 us
    ppermute x1, starting transfers between devices, shards(): ev_e = lax.ppermute(edges, 'slab', mates)  3.36 us
  transfers between devices with their start and end apart: 18, of which 6 were waited for; matrix products, arithmetic and copies ran while one was open for 0% of the time, Pallas kernels for 6%

profile of v8, /device:TPU:16, one launch (start us, length us, event | category | flops | bytes accessed | tf_op | source)
XLA Modules:
  0.0 83.7 jit_solution(16599965492462321259)
XLA Ops:
  0.6 1.4 %shard_map.50 = (f32[4,14,512]{2,1,0:T(8,128)S(1)}, f32[4,64,512]{2,1,0:T(8,128)S(1)}, f32[2,4,64,512]{3,2,1,0:T(8,128)S(1)}) custom-call(f32[4,64,512]{2,1,0:T(8,128)} %own_hbm.1, f32[2,4,64,512]{3,2,1,0:T(8,128)} %f_hbm.1), custom_call_target="tpu_custom_call" | custom-call | bytes 3600000 | tf_op jit(solution)/shard_map/pallas_call | solution.py:422
  2.7 3.4 %collective-permute-start.1 = (f32[4,14,512]{2,1,0:T(8,128)S(1)}, f32[4,14,512]{2,1,0:T(8,128)S(1)}, u32[]{:S(2)}, u32[]{:S(2)}) collective-permute-start(f32[4,14,512]{2,1,0:T(8,128)S(1)} %get-tuple-element.25.own), channel_id=1, source_target_pairs={{0,16},{32,48},{64,80},{96,112},{128,144},{160,176},{192,208},{224... | collective-permute-start | bytes 344072 | tf_op jit(solution)/shard_map/ppermute | solution.py:476
  6.1 1.0 %collective-permute-done.1.ev_e.ev = f32[4,14,512]{2,1,0:T(8,128)S(1)} collective-permute-done((f32[4,14,512]{2,1,0:T(8,128)S(1)}, f32[4,14,512]{2,1,0:T(8,128)S(1)}, u32[]{:S(2)}, u32[]{:S(2)}) %collective-permute-start.1) | collective-permute-done | bytes 114720 | tf_op jit(solution)/shard_map/ppermute | solution.py:476
  7.1 0.7 collective-permute-start.2
  7.8 4.6 %collective-permute-start.3 = (f32[4,64,512]{2,1,0:T(8,128)S(1)}, f32[4,64,512]{2,1,0:T(8,128)S(1)}, u32[]{:S(2)}, u32[]{:S(2)}) collective-permute-start(f32[4,64,512]{2,1,0:T(8,128)S(1)} %shard_map.51.own), channel_id=1, source_target_pairs={{0,16},{32,48},{64,80},{96,112},{128,144},{160,176},{192,208},{224... | collective-permute-start | bytes 1572872 | tf_op jit(solution)/shard_map/ppermute | solution.py:487
  13.1 1.6 %collective-permute-start.4 = (f32[40,512]{1,0:T(8,128)S(1)}, f32[40,512]{1,0:T(8,128)S(1)}, u32[]{:S(2)}, u32[]{:S(2)}) collective-permute-start(f32[40,512]{1,0:T(8,128)S(1)} %get-tuple-element.26), channel_id=1, source_target_pairs={{0,1},{2,3},{4,5},{6,7},{8,9},{10,11},{12,13},{14,15},{1,0},{3,2},... | collective-permute-start | bytes 245768 | tf_op jit(solution)/shard_map/ppermute | solution.py:497
  14.6 3.9 %collective-permute-start.5 = (f32[40,512]{1,0:T(8,128)S(1)}, f32[40,512]{1,0:T(8,128)S(1)}, u32[]{:S(2)}, u32[]{:S(2)}) collective-permute-start(f32[40,512]{1,0:T(8,128)S(1)} %get-tuple-element.27), channel_id=1, source_target_pairs={{1,2},{3,4},{5,6},{7,8},{9,10},{11,12},{13,14},{2,1},{4,3},{6,5},{... | collective-permute-start | bytes 245768 | tf_op jit(solution)/shard_map/ppermute | solution.py:498
  18.6 4.5 %collective-permute-done.5.second = f32[40,512]{1,0:T(8,128)S(1)} collective-permute-done((f32[40,512]{1,0:T(8,128)S(1)}, f32[40,512]{1,0:T(8,128)S(1)}, u32[]{:S(2)}, u32[]{:S(2)}) %collective-permute-start.5) | collective-permute-done | bytes 81952 | tf_op jit(solution)/shard_map/ppermute | solution.py:498
  23.1 7.5 %shard_map.53 = (f32[10,4,512]{2,1,0:T(4,128)S(1)}, f32[2,2,64,512]{3,2,1,0:T(8,128)S(1)}, f32[2,2,64,512]{3,2,1,0:T(8,128)S(1)}, f32[10,80,512]{2,1,0:T(8,128)S...) custom-call(s32[4]{0:T(128)S(1)} %pad_add_fusion.par_ref, ...), custom_call_target="tpu_custom_call" | custom-call | bytes 21600000 | tf_op jit(solution)/shard_map/pallas_call | solution.py:422
  30.6 0.7 collective-permute-start.12
  31.3 3.3 %collective-permute-start.13 = (f32[2,2,64,512]{3,2,1,0:T(8,128)S(1)}, f32[2,2,64,512]{3,2,1,0:T(8,128)S(1)}, u32[]{:S(2)}, u32[]{:S(2)}) collective-permute-start(f32[2,2,64,512]{3,2,1,0:T(8,128)S(1)} %get-tuple-element.32), channel_id=1, source_target_pairs={{0,16},{32,48},{64,80},{96,112},{128,144},{160,176},{192,208},{224... | collective-permute-start | bytes 1572872 | tf_op jit(solution)/shard_map/ppermute | solution.py:522
  34.8 2.2 %collective-permute-start.8 = (f32[10,4,512]{2,1,0:T(4,128)S(1)}, f32[10,4,512]{2,1,0:T(4,128)S(1)}, u32[]{:S(2)}, u32[]{:S(2)}) collective-permute-start(f32[10,4,512]{2,1,0:T(4,128)S(1)} %get-tuple-element.30), channel_id=1, source_target_pairs={{0,3},{1,2},{2,1},{3,0},{4,7},{5,6},{6,5},{7,4},{8,11},{9,10},{10,... | collective-permute-start | bytes 245768 | tf_op jit(solution)/shard_map/ppermute | solution.py:518
  36.9 2.0 %collective-permute-start.6 = (f32[10,4,512]{2,1,0:T(4,128)S(1)}, f32[10,4,512]{2,1,0:T(4,128)S(1)}, u32[]{:S(2)}, u32[]{:S(2)}) collective-permute-start(f32[10,4,512]{2,1,0:T(4,128)S(1)} %get-tuple-element.30), channel_id=1, source_target_pairs={{0,1},{1,0},{2,3},{3,2},{4,5},{5,4},{6,7},{7,6},{8,9},{9,8},{10,11... | collective-permute-start | bytes 245768 | tf_op jit(solution)/shard_map/ppermute | solution.py:518
  38.9 1.6 %collective-permute-done.8 = f32[10,4,512]{2,1,0:T(4,128)S(1)} collective-permute-done((f32[10,4,512]{2,1,0:T(4,128)S(1)}, f32[10,4,512]{2,1,0:T(4,128)S(1)}, u32[]{:S(2)}, u32[]{:S(2)}) %collective-permute-start.8) | collective-permute-done | bytes 81952 | tf_op jit(solution)/shard_map/ppermute | solution.py:518
  40.5 2.9 %collective-permute-done.7 = f32[10,4,512]{2,1,0:T(4,128)S(1)} collective-permute-done((f32[10,4,512]{2,1,0:T(4,128)S(1)}, f32[10,4,512]{2,1,0:T(4,128)S(1)}, u32[]{:S(2)}, u32[]{:S(2)}) %collective-permute-start.7) | collective-permute-done | bytes 81952 | tf_op jit(solution)/shard_map/ppermute | solution.py:518
  43.9 1.8 %collective-permute-start.11 = (f32[10,4,512]{2,1,0:T(4,128)S(1)}, f32[10,4,512]{2,1,0:T(4,128)S(1)}, u32[]{:S(2)}, u32[]{:S(2)}) collective-permute-start(f32[10,4,512]{2,1,0:T(4,128)S(1)} %bitcast.24), channel_id=1, source_target_pairs={{0,12},{1,13},{2,14},{3,15},{4,8},{5,9},{6,10},{7,11},{8,4},{9,5},... | collective-permute-start | bytes 245768 | tf_op jit(solution)/shard_map/ppermute | solution.py:518
  45.6 2.6 %collective-permute-start.9 = (f32[10,4,512]{2,1,0:T(4,128)S(1)}, f32[10,4,512]{2,1,0:T(4,128)S(1)}, u32[]{:S(2)}, u32[]{:S(2)}) collective-permute-start(f32[10,4,512]{2,1,0:T(4,128)S(1)} %bitcast.25), channel_id=1, source_target_pairs={{0,4},{1,5},{2,6},{3,7},{4,0},{5,1},{6,2},{7,3},{8,12},{9,13},{10,... | collective-permute-start | bytes 245768 | tf_op jit(solution)/shard_map/ppermute | solution.py:518
  48.2 4.5 %shard_map.54.forced = f32[2,4,64,512]{3,2,1,0:T(8,128)S(1)} custom-call(s32[4]{0:T(128)S(1)} %pad_add_fusion.par_ref, f32[2,4,64,512]{3,2,1,0:T(8,128)S(1)} %get-tuple-element.28.f, f32[2,2,64,512]{3,2,1,0:T(8,128)S(1)} %collective-permute-done.12.od, f32[2,2,64,512]{3,2,1,0:T(8,128)S(1)} %collective-permute-done.13.ev, ...), custom_call_target="tpu_custom_call" | custom-call | bytes 18000000 | tf_op jit(solution)/shard_map/pallas_call | solution.py:422
  52.8 2.0 %collective-permute-start.15 = (f32[10,4,512]{2,1,0:T(4,128)S(1)}, f32[10,4,512]{2,1,0:T(4,128)S(1)}, u32[]{:S(2)}, u32[]{:S(2)}) collective-permute-start(f32[10,4,512]{2,1,0:T(4,128)S(1)} %bitcast.18), channel_id=1, source_target_pairs={{0,32},{16,48},{64,96},{80,112},{128,160},{144,176},{192,224},{208... | collective-permute-start | bytes 245768 | tf_op jit(solution)/shard_map/ppermute | solution.py:539
  55.5 1.9 %collective-permute-done.15.first = f32[10,4,512]{2,1,0:T(4,128)S(1)} collective-permute-done((f32[10,4,512]{2,1,0:T(4,128)S(1)}, f32[10,4,512]{2,1,0:T(4,128)S(1)}, u32[]{:S(2)}, u32[]{:S(2)}) %collective-permute-start.15) | collective-permute-done | bytes 81952 | tf_op jit(solution)/shard_map/ppermute | solution.py:539
  58.0 1.0 %collective-permute-done.14.mate = f32[10,4,512]{2,1,0:T(4,128)S(1)} collective-permute-done((f32[10,4,512]{2,1,0:T(4,128)S(1)}, f32[10,4,512]{2,1,0:T(4,128)S(1)}, u32[]{:S(2)}, u32[]{:S(2)}) %collective-permute-start.14) | collective-permute-done | bytes 81952 | tf_op jit(solution)/shard_map/ppermute | solution.py:538
  59.1 1.2 %shard_map.55 = (f32[48,512]{1,0:T(8,128)S(1)}, f32[8,8,128]{2,1,0:T(8,128)S(1)}) custom-call(s32[4]{0:T(128)S(1)} %pad_add_fusion.par_ref, f32[10,4,512]{2,1,0:T(4,128)S(1)} %bitcast.21, f32[10,4,512]{2,1,0:T(4,128)S(1)} %collective-permute-done.14.mate, f32[10,4,512]{2,1,0:T(4,128)S(1)} %collective-permute-done.15.first, ...), custom_call_target="tpu_custom_call" | custom-call | bytes 3600000 | tf_op jit(solution)/shard_map/pallas_call | solution.py:422
  60.2 19.3 %all_to_all.5.dots = f32[8,8,128]{2,1,0:T(8,128)S(1)} all-to-all(f32[8,8,128]{2,1,0:T(8,128)S(1)} %get-tuple-element.40), channel_id=1, replica_groups={{0,32,64,96,128,160,192,224},{16,48,80,112,144,176,208,240},{1,33,65,97..., dimensions={0} | all-to-all | bytes 65536 | tf_op jit(solution)/shard_map/all_to_all | solution.py:550
  79.6 4.0 %shard_map.56 = (f32[2,4,64,512]{3,2,1,0:T(8,128)}, f32[4,32]{1,0:T(4,128)}) custom-call(f32[48,512]{1,0:T(8,128)S(1)} %get-tuple-element.39.basis, f32[8,8,128]{2,1,0:T(8,128)S(1)} %all_to_all.5.dots, f32[512,32]{1,0:T(8,128)S(1)} %compare_convert_fusion.onehot, f32[7,80,512]{2,1,0:T(8,128)S(1)} %get-tuple-element.42.h0, ...), custom_call_target="tpu_custom_call" | custom-call | bytes 14400000 | tf_op jit(solution)/shard_map/pallas_call | solution.py:422
  (28 shorter events, 3.3 us)
Async XLA Ops:
  2.1 4.0 %collective-permute-start = (f32[4,14,512]{2,1,0:T(8,128)S(1)}, f32[4,14,512]{2,1,0:T(8,128)S(1)}, u32[]{:S(2)}, u32[]{:S(2)}) collective-permute-start(f32[4,14,512]{2,1,0:T(8,128)S(1)} %get-tuple-element.25.own), channel_id=1, source_target_pairs={{16,32},{48,64},{80,96},{112,128},{144,160},{176,192},{208,224},{3... | collective-permute-start | bytes 344072 | tf_op jit(solution)/shard_map/ppermute | solution.py:475
  2.7 4.3 %collective-permute-start.1 = (f32[4,14,512]{2,1,0:T(8,128)S(1)}, f32[4,14,512]{2,1,0:T(8,128)S(1)}, u32[]{:S(2)}, u32[]{:S(2)}) collective-permute-start(f32[4,14,512]{2,1,0:T(8,128)S(1)} %get-tuple-element.25.own), channel_id=1, source_target_pairs={{0,16},{32,48},{64,80},{96,112},{128,144},{160,176},{192,208},{224... | collective-permute-start | bytes 344072 | tf_op jit(solution)/shard_map/ppermute | solution.py:476
  7.1 16.0 %collective-permute-start.2 = (f32[4,64,512]{2,1,0:T(8,128)S(1)}, f32[4,64,512]{2,1,0:T(8,128)S(1)}, u32[]{:S(2)}, u32[]{:S(2)}) collective-permute-start(f32[4,64,512]{2,1,0:T(8,128)S(1)} %shard_map.51.own), channel_id=1, source_target_pairs={{16,32},{48,64},{80,96},{112,128},{144,160},{176,192},{208,224},{3... | collective-permute-start | bytes 1572872 | tf_op jit(solution)/shard_map/ppermute | solution.py:486
  7.8 15.3 %collective-permute-start.3 = (f32[4,64,512]{2,1,0:T(8,128)S(1)}, f32[4,64,512]{2,1,0:T(8,128)S(1)}, u32[]{:S(2)}, u32[]{:S(2)}) collective-permute-start(f32[4,64,512]{2,1,0:T(8,128)S(1)} %shard_map.51.own), channel_id=1, source_target_pairs={{0,16},{32,48},{64,80},{96,112},{128,144},{160,176},{192,208},{224... | collective-permute-start | bytes 1572872 | tf_op jit(solution)/shard_map/ppermute | solution.py:487
  13.1 5.5 %collective-permute-start.4 = (f32[40,512]{1,0:T(8,128)S(1)}, f32[40,512]{1,0:T(8,128)S(1)}, u32[]{:S(2)}, u32[]{:S(2)}) collective-permute-start(f32[40,512]{1,0:T(8,128)S(1)} %get-tuple-element.26), channel_id=1, source_target_pairs={{0,1},{2,3},{4,5},{6,7},{8,9},{10,11},{12,13},{14,15},{1,0},{3,2},... | collective-permute-start | bytes 245768 | tf_op jit(solution)/shard_map/ppermute | solution.py:497
  14.6 8.4 %collective-permute-start.5 = (f32[40,512]{1,0:T(8,128)S(1)}, f32[40,512]{1,0:T(8,128)S(1)}, u32[]{:S(2)}, u32[]{:S(2)}) collective-permute-start(f32[40,512]{1,0:T(8,128)S(1)} %get-tuple-element.27), channel_id=1, source_target_pairs={{1,2},{3,4},{5,6},{7,8},{9,10},{11,12},{13,14},{2,1},{4,3},{6,5},{... | collective-permute-start | bytes 245768 | tf_op jit(solution)/shard_map/ppermute | solution.py:498
  23.1 11.5 %copy-start = (s32[512]{0:T(512)S(1)}, s32[512]{0:T(512)}, u32[]{:S(2)}) copy-start(s32[512]{0:T(512)} %param.5) | copy-start | bytes 6148
  30.6 17.7 %collective-permute-start.12 = (f32[2,2,64,512]{3,2,1,0:T(8,128)S(1)}, f32[2,2,64,512]{3,2,1,0:T(8,128)S(1)}, u32[]{:S(2)}, u32[]{:S(2)}) collective-permute-start(f32[2,2,64,512]{3,2,1,0:T(8,128)S(1)} %get-tuple-element.31), channel_id=1, source_target_pairs={{16,32},{48,64},{80,96},{112,128},{144,160},{176,192},{208,224},{3... | collective-permute-start | bytes 1572872 | tf_op jit(solution)/shard_map/ppermute | solution.py:521
  31.3 17.0 %collective-permute-start.13 = (f32[2,2,64,512]{3,2,1,0:T(8,128)S(1)}, f32[2,2,64,512]{3,2,1,0:T(8,128)S(1)}, u32[]{:S(2)}, u32[]{:S(2)}) collective-permute-start(f32[2,2,64,512]{3,2,1,0:T(8,128)S(1)} %get-tuple-element.32), channel_id=1, source_target_pairs={{0,16},{32,48},{64,80},{96,112},{128,144},{160,176},{192,208},{224... | collective-permute-start | bytes 1572872 | tf_op jit(solution)/shard_map/ppermute | solution.py:522
  34.8 5.7 %collective-permute-start.8 = (f32[10,4,512]{2,1,0:T(4,128)S(1)}, f32[10,4,512]{2,1,0:T(4,128)S(1)}, u32[]{:S(2)}, u32[]{:S(2)}) collective-permute-start(f32[10,4,512]{2,1,0:T(4,128)S(1)} %get-tuple-element.30), channel_id=1, source_target_pairs={{0,3},{1,2},{2,1},{3,0},{4,7},{5,6},{6,5},{7,4},{8,11},{9,10},{10,... | collective-permute-start | bytes 245768 | tf_op jit(solution)/shard_map/ppermute | solution.py:518
  36.9 6.5 %collective-permute-start.7 = (f32[10,4,512]{2,1,0:T(4,128)S(1)}, f32[10,4,512]{2,1,0:T(4,128)S(1)}, u32[]{:S(2)}, u32[]{:S(2)}) collective-permute-start(f32[10,4,512]{2,1,0:T(4,128)S(1)} %get-tuple-element.30), channel_id=1, source_target_pairs={{0,2},{1,3},{2,0},{3,1},{4,6},{5,7},{6,4},{7,5},{8,10},{9,11},{10,... | collective-permute-start | bytes 245768 | tf_op jit(solution)/shard_map/ppermute | solution.py:518
  36.9 6.5 %collective-permute-start.6 = (f32[10,4,512]{2,1,0:T(4,128)S(1)}, f32[10,4,512]{2,1,0:T(4,128)S(1)}, u32[]{:S(2)}, u32[]{:S(2)}) collective-permute-start(f32[10,4,512]{2,1,0:T(4,128)S(1)} %get-tuple-element.30), channel_id=1, source_target_pairs={{0,1},{1,0},{2,3},{3,2},{4,5},{5,4},{6,7},{7,6},{8,9},{9,8},{10,11... | collective-permute-start | bytes 245768 | tf_op jit(solution)/shard_map/ppermute | solution.py:518
  43.4 9.3 %collective-permute-start.10 = (f32[10,4,512]{2,1,0:T(4,128)S(1)}, f32[10,4,512]{2,1,0:T(4,128)S(1)}, u32[]{:S(2)}, u32[]{:S(2)}) collective-permute-start(f32[10,4,512]{2,1,0:T(4,128)S(1)} %bitcast.23), channel_id=1, source_target_pairs={{0,8},{1,9},{2,10},{3,11},{4,12},{5,13},{6,14},{7,15},{8,0},{9,1},... | collective-permute-start | bytes 245768 | tf_op jit(solution)/shard_map/ppermute | solution.py:518
  43.9 8.9 %collective-permute-start.11 = (f32[10,4,512]{2,1,0:T(4,128)S(1)}, f32[10,4,512]{2,1,0:T(4,128)S(1)}, u32[]{:S(2)}, u32[]{:S(2)}) collective-permute-start(f32[10,4,512]{2,1,0:T(4,128)S(1)} %bitcast.24), channel_id=1, source_target_pairs={{0,12},{1,13},{2,14},{3,15},{4,8},{5,9},{6,10},{7,11},{8,4},{9,5},... | collective-permute-start | bytes 245768 | tf_op jit(solution)/shard_map/ppermute | solution.py:518
  45.6 7.2 %collective-permute-start.9 = (f32[10,4,512]{2,1,0:T(4,128)S(1)}, f32[10,4,512]{2,1,0:T(4,128)S(1)}, u32[]{:S(2)}, u32[]{:S(2)}) collective-permute-start(f32[10,4,512]{2,1,0:T(4,128)S(1)} %bitcast.25), channel_id=1, source_target_pairs={{0,4},{1,5},{2,6},{3,7},{4,0},{5,1},{6,2},{7,3},{8,12},{9,13},{10,... | collective-permute-start | bytes 245768 | tf_op jit(solution)/shard_map/ppermute | solution.py:518
  52.8 4.5 %collective-permute-start.15 = (f32[10,4,512]{2,1,0:T(4,128)S(1)}, f32[10,4,512]{2,1,0:T(4,128)S(1)}, u32[]{:S(2)}, u32[]{:S(2)}) collective-permute-start(f32[10,4,512]{2,1,0:T(4,128)S(1)} %bitcast.18), channel_id=1, source_target_pairs={{0,32},{16,48},{64,96},{80,112},{128,160},{144,176},{192,224},{208... | collective-permute-start | bytes 245768 | tf_op jit(solution)/shard_map/ppermute | solution.py:539
  54.8 2.5 %collective-permute-start.16 = (f32[10,4,512]{2,1,0:T(4,128)S(1)}, f32[10,4,512]{2,1,0:T(4,128)S(1)}, u32[]{:S(2)}, u32[]{:S(2)}) collective-permute-start(f32[10,4,512]{2,1,0:T(4,128)S(1)} %bitcast.19), channel_id=1, source_target_pairs={{32,64},{48,80},{96,128},{112,144},{160,192},{176,208},{64,32},{80... | collective-permute-start | bytes 245768 | tf_op jit(solution)/shard_map/ppermute | solution.py:539
  57.4 1.6 %collective-permute-start.17 = (f32[2,10,4,512]{3,2,1,0:T(4,128)S(1)}, f32[2,10,4,512]{3,2,1,0:T(4,128)S(1)}, u32[]{:S(2)}, u32[]{:S(2)}) collective-permute-start(f32[2,10,4,512]{3,2,1,0:T(4,128)S(1)} %pad_maximum_fusion), channel_id=1, source_target_pairs={{0,16},{32,48},{64,80},{96,112},{128,144},{160,176},{192,208},{224... | collective-permute-start | bytes 491528 | tf_op jit(solution)/shard_map/ppermute | solution.py:540
  57.5 1.5 %collective-permute-start.14 = (f32[10,4,512]{2,1,0:T(4,128)S(1)}, f32[10,4,512]{2,1,0:T(4,128)S(1)}, u32[]{:S(2)}, u32[]{:S(2)}) collective-permute-start(f32[10,4,512]{2,1,0:T(4,128)S(1)} %bitcast.20), channel_id=1, source_target_pairs={{0,16},{32,48},{64,80},{96,112},{128,144},{160,176},{192,208},{224... | collective-permute-start | bytes 245768 | tf_op jit(solution)/shard_map/ppermute | solution.py:538

commit v9 on v8

--- a/solution.py
+++ b/solution.py
@@ -232,7 +232,7 @@
         copy.wait()
 
 
-def krylov_kernel(par_ref, mine, mate, first, second, crossed, basis, dots, s_ref, g_ref):
+def krylov_kernel(par_ref, mine, first, second, crossed, basis, dots, s_ref, g_ref):
     par, chip = par_ref[0], par_ref[1]
     odd = par == 1
 
@@ -243,7 +243,7 @@
     high = par_ref[3] == 1
     below, above = sides(high, first, second)
     below_mate, above_mate = sides(high, crossed.at[0], crossed.at[1])
-    for a, b in ((below, below_mate), (mine[...], mate[...]), (above, above_mate)):
+    for a, b in ((below, below_mate), (mine[...], crossed[2]), (above, above_mate)):
         slabs += pair(a, b)
     W = 24
     g_ref[...] = jnp.zeros_like(g_ref)
@@ -535,15 +535,14 @@
     got, forced = lax.optimization_barrier((got, forced))
     part = part + got[0] + got[1] + got[2]
 
-    mate = lax.ppermute(part, "slab", mates)
     near = (lax.ppermute(part, "slab", first_chips), lax.ppermute(part, "slab", second_chips))
-    crossed = lax.ppermute(jnp.stack(near), "slab", mates)
+    crossed = lax.ppermute(jnp.stack([*near, part]), "slab", mates)
     basis, dots = call(
         krylov_kernel,
         (f32(48, NZ), f32(chips, 8, 128)),
         [(7, 24, NZ), (40, NZ)],
-        (where, part, mate, *near, crossed),
-        in_specs=[SMEM] + [VMEM] * 5,
+        (where, part, *near, crossed),
+        in_specs=[SMEM] + [VMEM] * 4,
         mib=4,
     )
     groups = [[2 * z + c for z in range(chips)] for c in range(2)]

time: 84 us -> 83.4 us (level)
  transfers between devices with their start and end apart: 18 -> 17, of which waited for: 6 -> 7; matrix products, arithmetic and copies ran while one was open for 0% -> 0% of each run, Pallas kernels for 6% -> 6%
where the time goes in v9:
time: 83.4 us; the launch traced here: 83.1 us
  starting transfers between devices  30.5 us (37%)
  blocking collectives  19.3 us (23%)
  Pallas kernels  19.2 us (23%)
  waiting for transfers between devices  12.9 us (15%)
    all_to_all x1, blocking collectives, shards(): lax.all_to_all(dots, 'slab', 0, 0, tiled=True, axis_index_groups=groups)  19.3 us
    pallas_call x7, Pallas kernels, call(): pl.pallas_call(kernel, out_shape=out_shape, in_specs=in_specs, out_specs=...  19.2 us
    ppermute x6, starting transfers between devices, among(): lax.ppermute(x, 'cross', [(i, i ^ n * step) for i in range(cross)])  8.96 us
    ppermute x1, starting transfers between devices, shards(): ev = lax.ppermute(late, 'slab', mates)  4.6 us
    ppermute x1, waiting for transfers between devices, shards(): second = lax.ppermute(second, 'cross', pairs(cross, 1))  4.52 us
    ppermute x6, waiting for transfers between devices, among(): lax.ppermute(x, 'cross', [(i, i ^ n * step) for i in range(cross)])  4.05 us
    ppermute x1, starting transfers between devices, shards(): second = lax.ppermute(second, 'cross', pairs(cross, 1))  3.88 us
    ppermute x1, starting transfers between devices, shards(): ev_e = lax.ppermute(edges, 'slab', mates)  3.36 us
  transfers between devices with their start and end apart: 17, of which 7 were waited for; matrix products, arithmetic and copies ran while one was open for 0% of the time, Pallas kernels for 6%

profile of v9, /device:TPU:16, one launch (start us, length us, event | category | flops | bytes accessed | tf_op | source)
XLA Modules:
  0.0 83.1 jit_solution(2711320212382013583)
XLA Ops:
  0.6 1.4 %shard_map.50 = (f32[4,14,512]{2,1,0:T(8,128)S(1)}, f32[4,64,512]{2,1,0:T(8,128)S(1)}, f32[2,4,64,512]{3,2,1,0:T(8,128)S(1)}) custom-call(f32[4,64,512]{2,1,0:T(8,128)} %own_hbm.1, f32[2,4,64,512]{3,2,1,0:T(8,128)} %f_hbm.1), custom_call_target="tpu_custom_call" | custom-call | bytes 3600000 | tf_op jit(solution)/shard_map/pallas_call | solution.py:422
  2.7 3.4 %collective-permute-start.1 = (f32[4,14,512]{2,1,0:T(8,128)S(1)}, f32[4,14,512]{2,1,0:T(8,128)S(1)}, u32[]{:S(2)}, u32[]{:S(2)}) collective-permute-start(f32[4,14,512]{2,1,0:T(8,128)S(1)} %get-tuple-element.25.own), channel_id=1, source_target_pairs={{0,16},{32,48},{64,80},{96,112},{128,144},{160,176},{192,208},{224... | collective-permute-start | bytes 344072 | tf_op jit(solution)/shard_map/ppermute | solution.py:476
  6.1 1.0 %collective-permute-done.1.ev_e.ev = f32[4,14,512]{2,1,0:T(8,128)S(1)} collective-permute-done((f32[4,14,512]{2,1,0:T(8,128)S(1)}, f32[4,14,512]{2,1,0:T(8,128)S(1)}, u32[]{:S(2)}, u32[]{:S(2)}) %collective-permute-start.1) | collective-permute-done | bytes 114720 | tf_op jit(solution)/shard_map/ppermute | solution.py:476
  7.1 0.7 collective-permute-start.2
  7.8 4.6 %collective-permute-start.3 = (f32[4,64,512]{2,1,0:T(8,128)S(1)}, f32[4,64,512]{2,1,0:T(8,128)S(1)}, u32[]{:S(2)}, u32[]{:S(2)}) collective-permute-start(f32[4,64,512]{2,1,0:T(8,128)S(1)} %shard_map.51.own), channel_id=1, source_target_pairs={{0,16},{32,48},{64,80},{96,112},{128,144},{160,176},{192,208},{224... | collective-permute-start | bytes 1572872 | tf_op jit(solution)/shard_map/ppermute | solution.py:487
  13.1 1.6 %collective-permute-start.4 = (f32[40,512]{1,0:T(8,128)S(1)}, f32[40,512]{1,0:T(8,128)S(1)}, u32[]{:S(2)}, u32[]{:S(2)}) collective-permute-start(f32[40,512]{1,0:T(8,128)S(1)} %get-tuple-element.26), channel_id=1, source_target_pairs={{0,1},{2,3},{4,5},{6,7},{8,9},{10,11},{12,13},{14,15},{1,0},{3,2},... | collective-permute-start | bytes 245768 | tf_op jit(solution)/shard_map/ppermute | solution.py:497
  14.6 3.9 %collective-permute-start.5 = (f32[40,512]{1,0:T(8,128)S(1)}, f32[40,512]{1,0:T(8,128)S(1)}, u32[]{:S(2)}, u32[]{:S(2)}) collective-permute-start(f32[40,512]{1,0:T(8,128)S(1)} %get-tuple-element.27), channel_id=1, source_target_pairs={{1,2},{3,4},{5,6},{7,8},{9,10},{11,12},{13,14},{2,1},{4,3},{6,5},{... | collective-permute-start | bytes 245768 | tf_op jit(solution)/shard_map/ppermute | solution.py:498
  18.6 4.5 %collective-permute-done.5.second = f32[40,512]{1,0:T(8,128)S(1)} collective-permute-done((f32[40,512]{1,0:T(8,128)S(1)}, f32[40,512]{1,0:T(8,128)S(1)}, u32[]{:S(2)}, u32[]{:S(2)}) %collective-permute-start.5) | collective-permute-done | bytes 81952 | tf_op jit(solution)/shard_map/ppermute | solution.py:498
  23.1 7.5 %shard_map.53 = (f32[10,4,512]{2,1,0:T(4,128)S(1)}, f32[2,2,64,512]{3,2,1,0:T(8,128)S(1)}, f32[2,2,64,512]{3,2,1,0:T(8,128)S(1)}, f32[10,80,512]{2,1,0:T(8,128)S...) custom-call(s32[4]{0:T(128)S(1)} %pad_add_fusion.par_ref, ...), custom_call_target="tpu_custom_call" | custom-call | bytes 21600000 | tf_op jit(solution)/shard_map/pallas_call | solution.py:422
  30.6 0.7 collective-permute-start.12
  31.3 3.3 %collective-permute-start.13 = (f32[2,2,64,512]{3,2,1,0:T(8,128)S(1)}, f32[2,2,64,512]{3,2,1,0:T(8,128)S(1)}, u32[]{:S(2)}, u32[]{:S(2)}) collective-permute-start(f32[2,2,64,512]{3,2,1,0:T(8,128)S(1)} %get-tuple-element.32), channel_id=1, source_target_pairs={{0,16},{32,48},{64,80},{96,112},{128,144},{160,176},{192,208},{224... | collective-permute-start | bytes 1572872 | tf_op jit(solution)/shard_map/ppermute | solution.py:522
  34.9 2.2 %collective-permute-start.8 = (f32[10,4,512]{2,1,0:T(4,128)S(1)}, f32[10,4,512]{2,1,0:T(4,128)S(1)}, u32[]{:S(2)}, u32[]{:S(2)}) collective-permute-start(f32[10,4,512]{2,1,0:T(4,128)S(1)} %get-tuple-element.30), channel_id=1, source_target_pairs={{0,3},{1,2},{2,1},{3,0},{4,7},{5,6},{6,5},{7,4},{8,11},{9,10},{10,... | collective-permute-start | bytes 245768 | tf_op jit(solution)/shard_map/ppermute | solution.py:518
  37.0 1.9 %collective-permute-start.7 = (f32[10,4,512]{2,1,0:T(4,128)S(1)}, f32[10,4,512]{2,1,0:T(4,128)S(1)}, u32[]{:S(2)}, u32[]{:S(2)}) collective-permute-start(f32[10,4,512]{2,1,0:T(4,128)S(1)} %get-tuple-element.30), channel_id=1, source_target_pairs={{0,2},{1,3},{2,0},{3,1},{4,6},{5,7},{6,4},{7,5},{8,10},{9,11},{10,... | collective-permute-start | bytes 245768 | tf_op jit(solution)/shard_map/ppermute | solution.py:518
  39.3 1.5 %collective-permute-done.8 = f32[10,4,512]{2,1,0:T(4,128)S(1)} collective-permute-done((f32[10,4,512]{2,1,0:T(4,128)S(1)}, f32[10,4,512]{2,1,0:T(4,128)S(1)}, u32[]{:S(2)}, u32[]{:S(2)}) %collective-permute-start.8) | collective-permute-done | bytes 81952 | tf_op jit(solution)/shard_map/ppermute | solution.py:518
  40.8 2.2 %collective-permute-done.7 = f32[10,4,512]{2,1,0:T(4,128)S(1)} collective-permute-done((f32[10,4,512]{2,1,0:T(4,128)S(1)}, f32[10,4,512]{2,1,0:T(4,128)S(1)}, u32[]{:S(2)}, u32[]{:S(2)}) %collective-permute-start.7) | collective-permute-done | bytes 81952 | tf_op jit(solution)/shard_map/ppermute | solution.py:518
  43.4 1.7 %collective-permute-start.11 = (f32[10,4,512]{2,1,0:T(4,128)S(1)}, f32[10,4,512]{2,1,0:T(4,128)S(1)}, u32[]{:S(2)}, u32[]{:S(2)}) collective-permute-start(f32[10,4,512]{2,1,0:T(4,128)S(1)} %bitcast.25), channel_id=1, source_target_pairs={{0,12},{1,13},{2,14},{3,15},{4,8},{5,9},{6,10},{7,11},{8,4},{9,5},... | collective-permute-start | bytes 245768 | tf_op jit(solution)/shard_map/ppermute | solution.py:518
  45.1 2.7 %collective-permute-start.9 = (f32[10,4,512]{2,1,0:T(4,128)S(1)}, f32[10,4,512]{2,1,0:T(4,128)S(1)}, u32[]{:S(2)}, u32[]{:S(2)}) collective-permute-start(f32[10,4,512]{2,1,0:T(4,128)S(1)} %bitcast.26), channel_id=1, source_target_pairs={{0,4},{1,5},{2,6},{3,7},{4,0},{5,1},{6,2},{7,3},{8,12},{9,13},{10,... | collective-permute-start | bytes 245768 | tf_op jit(solution)/shard_map/ppermute | solution.py:518
  47.8 4.5 %shard_map.54.forced = f32[2,4,64,512]{3,2,1,0:T(8,128)S(1)} custom-call(s32[4]{0:T(128)S(1)} %pad_add_fusion.par_ref, f32[2,4,64,512]{3,2,1,0:T(8,128)S(1)} %get-tuple-element.28.f, f32[2,2,64,512]{3,2,1,0:T(8,128)S(1)} %collective-permute-done.12.od, f32[2,2,64,512]{3,2,1,0:T(8,128)S(1)} %collective-permute-done.13.ev, ...), custom_call_target="tpu_custom_call" | custom-call | bytes 18000000 | tf_op jit(solution)/shard_map/pallas_call | solution.py:422
  52.4 2.0 %collective-permute-start.14 = (f32[10,4,512]{2,1,0:T(4,128)S(1)}, f32[10,4,512]{2,1,0:T(4,128)S(1)}, u32[]{:S(2)}, u32[]{:S(2)}) collective-permute-start(f32[10,4,512]{2,1,0:T(4,128)S(1)} %bitcast.17), channel_id=1, source_target_pairs={{0,32},{16,48},{64,96},{80,112},{128,160},{144,176},{192,224},{208... | collective-permute-start | bytes 245768 | tf_op jit(solution)/shard_map/ppermute | solution.py:538
  55.1 1.9 %collective-permute-done.14.first = f32[10,4,512]{2,1,0:T(4,128)S(1)} collective-permute-done((f32[10,4,512]{2,1,0:T(4,128)S(1)}, f32[10,4,512]{2,1,0:T(4,128)S(1)}, u32[]{:S(2)}, u32[]{:S(2)}) %collective-permute-start.14) | collective-permute-done | bytes 81952 | tf_op jit(solution)/shard_map/ppermute | solution.py:538
  57.1 1.5 %collective-permute-done.16.crossed = f32[3,10,4,512]{3,2,1,0:T(4,128)S(1)} collective-permute-done((f32[3,10,4,512]{3,2,1,0:T(4,128)S(1)}, f32[3,10,4,512]{3,2,1,0:T(4,128)S(1)}, u32[]{:S(2)}, u32[]{:S(2)}) %collective-permute-start.16) | collective-permute-done | bytes 245792 | tf_op jit(solution)/shard_map/ppermute | solution.py:539
  58.6 1.2 %shard_map.55 = (f32[48,512]{1,0:T(8,128)S(1)}, f32[8,8,128]{2,1,0:T(8,128)S(1)}) custom-call(s32[4]{0:T(128)S(1)} %pad_add_fusion.par_ref, f32[10,4,512]{2,1,0:T(4,128)S(1)} %bitcast.20, f32[10,4,512]{2,1,0:T(4,128)S(1)} %collective-permute-done.14.first, f32[10,4,512]{2,1,0:T(4,128)S(1)} %collective-permute-done.15.second, ...), custom_call_target="tpu_custom_call" | custom-call | bytes 3600000 | tf_op jit(solution)/shard_map/pallas_call | solution.py:422
  59.8 19.3 %all_to_all.5.dots = f32[8,8,128]{2,1,0:T(8,128)S(1)} all-to-all(f32[8,8,128]{2,1,0:T(8,128)S(1)} %get-tuple-element.40), channel_id=1, replica_groups={{0,32,64,96,128,160,192,224},{16,48,80,112,144,176,208,240},{1,33,65,97..., dimensions={0} | all-to-all | bytes 65536 | tf_op jit(solution)/shard_map/all_to_all | solution.py:549
  79.1 4.0 %shard_map.56 = (f32[2,4,64,512]{3,2,1,0:T(8,128)}, f32[4,32]{1,0:T(4,128)}) custom-call(f32[48,512]{1,0:T(8,128)S(1)} %get-tuple-element.39.basis, f32[8,8,128]{2,1,0:T(8,128)S(1)} %all_to_all.5.dots, f32[512,32]{1,0:T(8,128)S(1)} %compare_convert_fusion.onehot, f32[7,80,512]{2,1,0:T(8,128)S(1)} %get-tuple-element.42.h0, ...), custom_call_target="tpu_custom_call" | custom-call | bytes 14400000 | tf_op jit(solution)/shard_map/pallas_call | solution.py:422
  (26 shorter events, 3.2 us)
Async XLA Ops:
  2.1 4.0 %collective-permute-start = (f32[4,14,512]{2,1,0:T(8,128)S(1)}, f32[4,14,512]{2,1,0:T(8,128)S(1)}, u32[]{:S(2)}, u32[]{:S(2)}) collective-permute-start(f32[4,14,512]{2,1,0:T(8,128)S(1)} %get-tuple-element.25.own), channel_id=1, source_target_pairs={{16,32},{48,64},{80,96},{112,128},{144,160},{176,192},{208,224},{3... | collective-permute-start | bytes 344072 | tf_op jit(solution)/shard_map/ppermute | solution.py:475
  2.7 4.3 %collective-permute-start.1 = (f32[4,14,512]{2,1,0:T(8,128)S(1)}, f32[4,14,512]{2,1,0:T(8,128)S(1)}, u32[]{:S(2)}, u32[]{:S(2)}) collective-permute-start(f32[4,14,512]{2,1,0:T(8,128)S(1)} %get-tuple-element.25.own), channel_id=1, source_target_pairs={{0,16},{32,48},{64,80},{96,112},{128,144},{160,176},{192,208},{224... | collective-permute-start | bytes 344072 | tf_op jit(solution)/shard_map/ppermute | solution.py:476
  7.1 16.0 %collective-permute-start.2 = (f32[4,64,512]{2,1,0:T(8,128)S(1)}, f32[4,64,512]{2,1,0:T(8,128)S(1)}, u32[]{:S(2)}, u32[]{:S(2)}) collective-permute-start(f32[4,64,512]{2,1,0:T(8,128)S(1)} %shard_map.51.own), channel_id=1, source_target_pairs={{16,32},{48,64},{80,96},{112,128},{144,160},{176,192},{208,224},{3... | collective-permute-start | bytes 1572872 | tf_op jit(solution)/shard_map/ppermute | solution.py:486
  7.8 15.3 %collective-permute-start.3 = (f32[4,64,512]{2,1,0:T(8,128)S(1)}, f32[4,64,512]{2,1,0:T(8,128)S(1)}, u32[]{:S(2)}, u32[]{:S(2)}) collective-permute-start(f32[4,64,512]{2,1,0:T(8,128)S(1)} %shard_map.51.own), channel_id=1, source_target_pairs={{0,16},{32,48},{64,80},{96,112},{128,144},{160,176},{192,208},{224... | collective-permute-start | bytes 1572872 | tf_op jit(solution)/shard_map/ppermute | solution.py:487
  13.1 5.5 %collective-permute-start.4 = (f32[40,512]{1,0:T(8,128)S(1)}, f32[40,512]{1,0:T(8,128)S(1)}, u32[]{:S(2)}, u32[]{:S(2)}) collective-permute-start(f32[40,512]{1,0:T(8,128)S(1)} %get-tuple-element.26), channel_id=1, source_target_pairs={{0,1},{2,3},{4,5},{6,7},{8,9},{10,11},{12,13},{14,15},{1,0},{3,2},... | collective-permute-start | bytes 245768 | tf_op jit(solution)/shard_map/ppermute | solution.py:497
  14.6 8.4 %collective-permute-start.5 = (f32[40,512]{1,0:T(8,128)S(1)}, f32[40,512]{1,0:T(8,128)S(1)}, u32[]{:S(2)}, u32[]{:S(2)}) collective-permute-start(f32[40,512]{1,0:T(8,128)S(1)} %get-tuple-element.27), channel_id=1, source_target_pairs={{1,2},{3,4},{5,6},{7,8},{9,10},{11,12},{13,14},{2,1},{4,3},{6,5},{... | collective-permute-start | bytes 245768 | tf_op jit(solution)/shard_map/ppermute | solution.py:498
  23.1 11.5 %copy-start = (s32[512]{0:T(512)S(1)}, s32[512]{0:T(512)}, u32[]{:S(2)}) copy-start(s32[512]{0:T(512)} %param.5) | copy-start | bytes 6148
  30.6 17.2 %collective-permute-start.12 = (f32[2,2,64,512]{3,2,1,0:T(8,128)S(1)}, f32[2,2,64,512]{3,2,1,0:T(8,128)S(1)}, u32[]{:S(2)}, u32[]{:S(2)}) collective-permute-start(f32[2,2,64,512]{3,2,1,0:T(8,128)S(1)} %get-tuple-element.31), channel_id=1, source_target_pairs={{16,32},{48,64},{80,96},{112,128},{144,160},{176,192},{208,224},{3... | collective-permute-start | bytes 1572872 | tf_op jit(solution)/shard_map/ppermute | solution.py:521
  31.3 16.5 %collective-permute-start.13 = (f32[2,2,64,512]{3,2,1,0:T(8,128)S(1)}, f32[2,2,64,512]{3,2,1,0:T(8,128)S(1)}, u32[]{:S(2)}, u32[]{:S(2)}) collective-permute-start(f32[2,2,64,512]{3,2,1,0:T(8,128)S(1)} %get-tuple-element.32), channel_id=1, source_target_pairs={{0,16},{32,48},{64,80},{96,112},{128,144},{160,176},{192,208},{224... | collective-permute-start | bytes 1572872 | tf_op jit(solution)/shard_map/ppermute | solution.py:522
  34.8 4.5 %collective-permute-start.6 = (f32[10,4,512]{2,1,0:T(4,128)S(1)}, f32[10,4,512]{2,1,0:T(4,128)S(1)}, u32[]{:S(2)}, u32[]{:S(2)}) collective-permute-start(f32[10,4,512]{2,1,0:T(4,128)S(1)} %get-tuple-element.30), channel_id=1, source_target_pairs={{0,1},{1,0},{2,3},{3,2},{4,5},{5,4},{6,7},{7,6},{8,9},{9,8},{10,11... | collective-permute-start | bytes 245768 | tf_op jit(solution)/shard_map/ppermute | solution.py:518
  34.9 5.9 %collective-permute-start.8 = (f32[10,4,512]{2,1,0:T(4,128)S(1)}, f32[10,4,512]{2,1,0:T(4,128)S(1)}, u32[]{:S(2)}, u32[]{:S(2)}) collective-permute-start(f32[10,4,512]{2,1,0:T(4,128)S(1)} %get-tuple-element.30), channel_id=1, source_target_pairs={{0,3},{1,2},{2,1},{3,0},{4,7},{5,6},{6,5},{7,4},{8,11},{9,10},{10,... | collective-permute-start | bytes 245768 | tf_op jit(solution)/shard_map/ppermute | solution.py:518
  37.0 5.9 %collective-permute-start.7 = (f32[10,4,512]{2,1,0:T(4,128)S(1)}, f32[10,4,512]{2,1,0:T(4,128)S(1)}, u32[]{:S(2)}, u32[]{:S(2)}) collective-permute-start(f32[10,4,512]{2,1,0:T(4,128)S(1)} %get-tuple-element.30), channel_id=1, source_target_pairs={{0,2},{1,3},{2,0},{3,1},{4,6},{5,7},{6,4},{7,5},{8,10},{9,11},{10,... | collective-permute-start | bytes 245768 | tf_op jit(solution)/shard_map/ppermute | solution.py:518
  43.0 9.3 %collective-permute-start.10 = (f32[10,4,512]{2,1,0:T(4,128)S(1)}, f32[10,4,512]{2,1,0:T(4,128)S(1)}, u32[]{:S(2)}, u32[]{:S(2)}) collective-permute-start(f32[10,4,512]{2,1,0:T(4,128)S(1)} %bitcast.24), channel_id=1, source_target_pairs={{0,8},{1,9},{2,10},{3,11},{4,12},{5,13},{6,14},{7,15},{8,0},{9,1},... | collective-permute-start | bytes 245768 | tf_op jit(solution)/shard_map/ppermute | solution.py:518
  43.4 8.9 %collective-permute-start.11 = (f32[10,4,512]{2,1,0:T(4,128)S(1)}, f32[10,4,512]{2,1,0:T(4,128)S(1)}, u32[]{:S(2)}, u32[]{:S(2)}) collective-permute-start(f32[10,4,512]{2,1,0:T(4,128)S(1)} %bitcast.25), channel_id=1, source_target_pairs={{0,12},{1,13},{2,14},{3,15},{4,8},{5,9},{6,10},{7,11},{8,4},{9,5},... | collective-permute-start | bytes 245768 | tf_op jit(solution)/shard_map/ppermute | solution.py:518
  45.1 7.2 %collective-permute-start.9 = (f32[10,4,512]{2,1,0:T(4,128)S(1)}, f32[10,4,512]{2,1,0:T(4,128)S(1)}, u32[]{:S(2)}, u32[]{:S(2)}) collective-permute-start(f32[10,4,512]{2,1,0:T(4,128)S(1)} %bitcast.26), channel_id=1, source_target_pairs={{0,4},{1,5},{2,6},{3,7},{4,0},{5,1},{6,2},{7,3},{8,12},{9,13},{10,... | collective-permute-start | bytes 245768 | tf_op jit(solution)/shard_map/ppermute | solution.py:518
  52.4 4.5 %collective-permute-start.14 = (f32[10,4,512]{2,1,0:T(4,128)S(1)}, f32[10,4,512]{2,1,0:T(4,128)S(1)}, u32[]{:S(2)}, u32[]{:S(2)}) collective-permute-start(f32[10,4,512]{2,1,0:T(4,128)S(1)} %bitcast.17), channel_id=1, source_target_pairs={{0,32},{16,48},{64,96},{80,112},{128,160},{144,176},{192,224},{208... | collective-permute-start | bytes 245768 | tf_op jit(solution)/shard_map/ppermute | solution.py:538
  54.4 2.5 %collective-permute-start.15 = (f32[10,4,512]{2,1,0:T(4,128)S(1)}, f32[10,4,512]{2,1,0:T(4,128)S(1)}, u32[]{:S(2)}, u32[]{:S(2)}) collective-permute-start(f32[10,4,512]{2,1,0:T(4,128)S(1)} %bitcast.18), channel_id=1, source_target_pairs={{32,64},{48,80},{96,128},{112,144},{160,192},{176,208},{64,32},{80... | collective-permute-start | bytes 245768 | tf_op jit(solution)/shard_map/ppermute | solution.py:538
  57.0 1.6 %collective-permute-start.16 = (f32[3,10,4,512]{3,2,1,0:T(4,128)S(1)}, f32[3,10,4,512]{3,2,1,0:T(4,128)S(1)}, u32[]{:S(2)}, u32[]{:S(2)}) collective-permute-start(f32[3,10,4,512]{3,2,1,0:T(4,128)S(1)} %pad_maximum_fusion), channel_id=1, source_target_pairs={{0,16},{32,48},{64,80},{96,112},{128,144},{160,176},{192,208},{224... | collective-permute-start | bytes 737288 | tf_op jit(solution)/shard_map/ppermute | solution.py:539

commit v10 on v9

--- a/solution.py
+++ b/solution.py
@@ -49,20 +49,24 @@
     return lax.broadcasted_iota(jnp.int32, shape, len(shape) - 1)
 
 
-def edge_kernel(own_hbm, f_hbm, out, own, f, sems):
+def edge_kernel(own_hbm, f_hbm, out, bundle, f, sems):
+    own = bundle.at[:, 0:NY]
     copies = [pltpu.make_async_copy(own_hbm, own, sems.at[0]), pltpu.make_async_copy(f_hbm, f, sems.at[1])]
     for copy in copies:
         copy.start()
     copies[0].wait()
-    out[:, 0:3] = own[:, 0:3]
-    out[:, 7:10] = own[:, NY - 3 : NY]
+    out[:, 0:3] = bundle[:, 0:3]
+    out[:, 7:10] = bundle[:, NY - 3 : NY]
     copies[1].wait()
     for c in range(2):
-        out[:, 3 + 2 * c : 5 + 2 * c] = f[c, :, 0:2]
-        out[:, 10 + 2 * c : 12 + 2 * c] = f[c, :, NY - 2 : NY]
-
-
-def pass_kernel(own, od_e, ev_e, out):
+        low, high = f[c, :, 0:2], f[c, :, NY - 2 : NY]
+        out[:, 3 + 2 * c : 5 + 2 * c] = low
+        out[:, 10 + 2 * c : 12 + 2 * c] = high
+        bundle[:, NY + 2 * c : NY + 2 * c + 2] = low
+        bundle[:, NY + 4 + 2 * c : NY + 6 + 2 * c] = high
+
+
+def pass_kernel(own, od_e, ev, out):
     pass
 
 
@@ -73,10 +77,14 @@
     ]
 
 
-def corner_kernel(par_ref, own, od, ev, first, second, low, high):
+def corner_kernel(par_ref, own, od, ev, first, second, low, high, mate):
     odd = par_ref[0] == 1
-    below = lax.select(odd, ev[2:4], od[2:4])
-    above = lax.select(odd, od[0:2], ev[0:2])
+    mate[:, 0:3] = ev[:, 0:3]
+    mate[:, 3:7] = ev[:, NY : NY + 4]
+    mate[:, 7:10] = ev[:, NY - 3 : NY]
+    mate[:, 10:14] = ev[:, NY + 4 : NY + 8]
+    below = lax.select(odd, mate[2:4], od[2:4])
+    above = lax.select(odd, od[0:2], mate[0:2])
     for out, near, forced, base in ((low, (0, 2), 0, 0), (high, (1, 3), 1, 7)):
         for n in range(4):
             out[7 * n : 7 * n + 7] = own[n, base : base + 7]
@@ -98,9 +106,9 @@
 
 
 def fill_viscosity(par, v, own, od, ev, lo, hi, sems):
-    copies = [pltpu.make_async_copy(own, v.at[3:7, LO:HI], sems.at[0])]
+    copies = [pltpu.make_async_copy(own.at[:, 0:NY], v.at[3:7, LO:HI], sems.at[0])]
     for n, at, last, x in ((1, par * 7, 1 - par, od), (2, 7 - par * 7, par, ev)):
-        copies.append(pltpu.make_async_copy(x.at[pl.ds(last, 3)], v.at[pl.ds(at, 3), LO:HI], sems.at[n]))
+        copies.append(pltpu.make_async_copy(x.at[pl.ds(last, 3), 0:NY], v.at[pl.ds(at, 3), LO:HI], sems.at[n]))
     for copy in copies:
         copy.start()
     for n in range(4):
@@ -463,7 +471,7 @@
         edge_kernel,
         (
             pltpu.VMEM((ROWS, 14, NZ), jnp.float32),
-            pltpu.VMEM(viscosity.shape, jnp.float32),
+            pltpu.VMEM((ROWS, NY + 8, NZ), jnp.float32),
             pltpu.VMEM(forcing.shape, jnp.float32),
         ),
         [],
@@ -473,24 +481,23 @@
         mib=4,
     )
     od_e = lax.ppermute(edges, "slab", others)
-    ev_e = lax.ppermute(edges, "slab", mates)
+    ev = lax.ppermute(own, "slab", mates)
     late = call(
         pass_kernel,
-        pltpu.VMEM(viscosity.shape, jnp.float32),
+        pltpu.VMEM((ROWS, NY + 8, NZ), jnp.float32),
         [],
-        (in_vmem(own), in_vmem(od_e), in_vmem(ev_e)),
+        (in_vmem(own), in_vmem(od_e), in_vmem(ev)),
         in_specs=[VMEM] * 3,
         mib=2,
         aliases={0: 0},
     )
     od = lax.ppermute(late, "slab", others)
-    ev = lax.ppermute(late, "slab", mates)
     rows = pltpu.VMEM((40, NZ), jnp.float32)
     first, second = call(
         corner_kernel,
         (rows, rows),
-        [(40, NZ), (40, NZ)],
-        (where, in_vmem(edges), in_vmem(od_e), in_vmem(ev_e)),
+        [(40, NZ), (40, NZ), (ROWS, 14, NZ)],
+        (where, in_vmem(edges), in_vmem(od_e), in_vmem(ev)),
         in_specs=[SMEM] + [VMEM] * 3,
         mib=4,
     )

time: 83.4 us -> 82.6 us (level); the launches traced: 83.1 us -> 81.2 us
  starting transfers between devices: 30.5 us -> 27.5 us
    ppermute x2 -> x1, starting transfers between devices: 7.96 us -> 0.09 us  [shards(): ev = lax.ppermute(own, 'slab', mates)]
    ppermute x1, starting transfers between devices: 3.33 us -> 9.39 us  [shards(): ev_f = lax.ppermute(to_ev, 'slab', mates)]
    ppermute x6, starting transfers between devices: 8.96 us -> 7.75 us  [among(): lax.ppermute(x, 'cross', [(i, i ^ n * step) for i in range(cross)])]
  transfers between devices with their start and end apart: 17 -> 16, of which waited for: 7 -> 7; matrix products, arithmetic and copies ran while one was open for 0% -> 0% of each run, Pallas kernels for 6% -> 6%
where the time goes in v10:
time: 82.6 us; the launch traced here: 81.2 us
  starting transfers between devices  27.5 us (33%)
  blocking collectives  20 us (24%)
  Pallas kernels  19.2 us (23%)
  waiting for transfers between devices  13.3 us (16%)
  between operations  0.85 us (1%)
    all_to_all x1, blocking collectives, shards(): lax.all_to_all(dots, 'slab', 0, 0, tiled=True, axis_index_groups=groups)  20 us
    pallas_call x7, Pallas kernels, call(): pl.pallas_call(kernel, out_shape=out_shape, in_specs=in_specs, out_specs=...  19.2 us
    ppermute x1, starting transfers between devices, shards(): ev_f = lax.ppermute(to_ev, 'slab', mates)  9.39 us
    ppermute x6, starting transfers between devices, among(): lax.ppermute(x, 'cross', [(i, i ^ n * step) for i in range(cross)])  7.75 us
    ppermute x1, waiting for transfers between devices, shards(): second = lax.ppermute(second, 'cross', pairs(cross, 1))  4.52 us
    ppermute x6, waiting for transfers between devices, among(): lax.ppermute(x, 'cross', [(i, i ^ n * step) for i in range(cross)])  4.05 us
    ppermute x1, starting transfers between devices, shards(): second = lax.ppermute(second, 'cross', pairs(cross, 1))  3.88 us
    ppermute x1, starting transfers between devices, shards(): lax.ppermute(part, 'slab', first_chips)  2 us
  transfers between devices with their start and end apart: 16, of which 7 were waited for; matrix products, arithmetic and copies ran while one was open for 0% of the time, Pallas kernels for 6%

profile of v10, /device:TPU:16, one launch (start us, length us, event | category | flops | bytes accessed | tf_op | source)
XLA Modules:
  0.0 81.2 jit_solution(5333457134419665220)
XLA Ops:
  0.6 1.5 %shard_map.50 = (f32[4,14,512]{2,1,0:T(8,128)S(1)}, f32[4,72,512]{2,1,0:T(8,128)S(1)}, f32[2,4,64,512]{3,2,1,0:T(8,128)S(1)}) custom-call(f32[4,64,512]{2,1,0:T(8,128)} %own_hbm.1, f32[2,4,64,512]{3,2,1,0:T(8,128)} %f_hbm.1), custom_call_target="tpu_custom_call" | custom-call | bytes 3600000 | tf_op jit(solution)/shard_map/pallas_call | solution.py:430
  2.2 0.7 collective-permute-start
  2.9 1.3 %collective-permute-done.1.ev = f32[4,72,512]{2,1,0:T(8,128)S(1)} collective-permute-done((f32[4,72,512]{2,1,0:T(8,128)S(1)}, f32[4,72,512]{2,1,0:T(8,128)S(1)}, u32[]{:S(2)}, u32[]{:S(2)}) %collective-permute-start.1) | collective-permute-done | bytes 589856 | tf_op jit(solution)/shard_map/ppermute | solution.py:484
  4.2 0.7 collective-permute-start.2
  5.6 1.6 %collective-permute-start.3 = (f32[40,512]{1,0:T(8,128)S(1)}, f32[40,512]{1,0:T(8,128)S(1)}, u32[]{:S(2)}, u32[]{:S(2)}) collective-permute-start(f32[40,512]{1,0:T(8,128)S(1)} %get-tuple-element.26), channel_id=1, source_target_pairs={{0,1},{2,3},{4,5},{6,7},{8,9},{10,11},{12,13},{14,15},{1,0},{3,2},... | collective-permute-start | bytes 245768 | tf_op jit(solution)/shard_map/ppermute | solution.py:504
  7.2 3.9 %collective-permute-start.4 = (f32[40,512]{1,0:T(8,128)S(1)}, f32[40,512]{1,0:T(8,128)S(1)}, u32[]{:S(2)}, u32[]{:S(2)}) collective-permute-start(f32[40,512]{1,0:T(8,128)S(1)} %get-tuple-element.27), channel_id=1, source_target_pairs={{1,2},{3,4},{5,6},{7,8},{9,10},{11,12},{13,14},{2,1},{4,3},{6,5},{... | collective-permute-start | bytes 245768 | tf_op jit(solution)/shard_map/ppermute | solution.py:505
  11.1 4.5 %collective-permute-done.4.second = f32[40,512]{1,0:T(8,128)S(1)} collective-permute-done((f32[40,512]{1,0:T(8,128)S(1)}, f32[40,512]{1,0:T(8,128)S(1)}, u32[]{:S(2)}, u32[]{:S(2)}) %collective-permute-start.4) | collective-permute-done | bytes 81952 | tf_op jit(solution)/shard_map/ppermute | solution.py:505
  15.6 7.5 %shard_map.53 = (f32[10,4,512]{2,1,0:T(4,128)S(1)}, f32[2,2,64,512]{3,2,1,0:T(8,128)S(1)}, f32[2,2,64,512]{3,2,1,0:T(8,128)S(1)}, f32[10,80,512]{2,1,0:T(8,128)S...) custom-call(s32[4]{0:T(128)S(1)} %pad_add_fusion.par_ref, ...), custom_call_target="tpu_custom_call" | custom-call | bytes 21600000 | tf_op jit(solution)/shard_map/pallas_call | solution.py:430
  23.1 0.7 collective-permute-start.11
  23.8 9.4 %collective-permute-start.12 = (f32[2,2,64,512]{3,2,1,0:T(8,128)S(1)}, f32[2,2,64,512]{3,2,1,0:T(8,128)S(1)}, u32[]{:S(2)}, u32[]{:S(2)}) collective-permute-start(f32[2,2,64,512]{3,2,1,0:T(8,128)S(1)} %get-tuple-element.32), channel_id=1, source_target_pairs={{0,16},{32,48},{64,80},{96,112},{128,144},{160,176},{192,208},{224... | collective-permute-start | bytes 1572872 | tf_op jit(solution)/shard_map/ppermute | solution.py:529
  33.5 2.2 %collective-permute-start.7 = (f32[10,4,512]{2,1,0:T(4,128)S(1)}, f32[10,4,512]{2,1,0:T(4,128)S(1)}, u32[]{:S(2)}, u32[]{:S(2)}) collective-permute-start(f32[10,4,512]{2,1,0:T(4,128)S(1)} %get-tuple-element.30), channel_id=1, source_target_pairs={{0,3},{1,2},{2,1},{3,0},{4,7},{5,6},{6,5},{7,4},{8,11},{9,10},{10,... | collective-permute-start | bytes 245768 | tf_op jit(solution)/shard_map/ppermute | solution.py:525
  35.7 1.9 %collective-permute-start.6 = (f32[10,4,512]{2,1,0:T(4,128)S(1)}, f32[10,4,512]{2,1,0:T(4,128)S(1)}, u32[]{:S(2)}, u32[]{:S(2)}) collective-permute-start(f32[10,4,512]{2,1,0:T(4,128)S(1)} %get-tuple-element.30), channel_id=1, source_target_pairs={{0,2},{1,3},{2,0},{3,1},{4,6},{5,7},{6,4},{7,5},{8,10},{9,11},{10,... | collective-permute-start | bytes 245768 | tf_op jit(solution)/shard_map/ppermute | solution.py:525
  37.9 1.5 %collective-permute-done.7 = f32[10,4,512]{2,1,0:T(4,128)S(1)} collective-permute-done((f32[10,4,512]{2,1,0:T(4,128)S(1)}, f32[10,4,512]{2,1,0:T(4,128)S(1)}, u32[]{:S(2)}, u32[]{:S(2)}) %collective-permute-start.7) | collective-permute-done | bytes 81952 | tf_op jit(solution)/shard_map/ppermute | solution.py:525
  39.4 2.2 %collective-permute-done.6 = f32[10,4,512]{2,1,0:T(4,128)S(1)} collective-permute-done((f32[10,4,512]{2,1,0:T(4,128)S(1)}, f32[10,4,512]{2,1,0:T(4,128)S(1)}, u32[]{:S(2)}, u32[]{:S(2)}) %collective-permute-start.6) | collective-permute-done | bytes 81952 | tf_op jit(solution)/shard_map/ppermute | solution.py:525
  42.2 1.1 %collective-permute-start.8 = (f32[10,4,512]{2,1,0:T(4,128)S(1)}, f32[10,4,512]{2,1,0:T(4,128)S(1)}, u32[]{:S(2)}, u32[]{:S(2)}) collective-permute-start(f32[10,4,512]{2,1,0:T(4,128)S(1)} %bitcast.25), channel_id=1, source_target_pairs={{0,4},{1,5},{2,6},{3,7},{4,0},{5,1},{6,2},{7,3},{8,12},{9,13},{10,... | collective-permute-start | bytes 245768 | tf_op jit(solution)/shard_map/ppermute | solution.py:525
  43.2 2.0 %collective-permute-start.9 = (f32[10,4,512]{2,1,0:T(4,128)S(1)}, f32[10,4,512]{2,1,0:T(4,128)S(1)}, u32[]{:S(2)}, u32[]{:S(2)}) collective-permute-start(f32[10,4,512]{2,1,0:T(4,128)S(1)} %bitcast.26), channel_id=1, source_target_pairs={{0,8},{1,9},{2,10},{3,11},{4,12},{5,13},{6,14},{7,15},{8,0},{9,1},... | collective-permute-start | bytes 245768 | tf_op jit(solution)/shard_map/ppermute | solution.py:525
  45.2 4.5 %shard_map.54.forced = f32[2,4,64,512]{3,2,1,0:T(8,128)S(1)} custom-call(s32[4]{0:T(128)S(1)} %pad_add_fusion.par_ref, f32[2,4,64,512]{3,2,1,0:T(8,128)S(1)} %get-tuple-element.28.f, f32[2,2,64,512]{3,2,1,0:T(8,128)S(1)} %collective-permute-done.11.od, f32[2,2,64,512]{3,2,1,0:T(8,128)S(1)} %collective-permute-done.12.ev, ...), custom_call_target="tpu_custom_call" | custom-call | bytes 18000000 | tf_op jit(solution)/shard_map/pallas_call | solution.py:430
  49.8 2.0 %collective-permute-start.13 = (f32[10,4,512]{2,1,0:T(4,128)S(1)}, f32[10,4,512]{2,1,0:T(4,128)S(1)}, u32[]{:S(2)}, u32[]{:S(2)}) collective-permute-start(f32[10,4,512]{2,1,0:T(4,128)S(1)} %bitcast.17), channel_id=1, source_target_pairs={{0,32},{16,48},{64,96},{80,112},{128,160},{144,176},{192,224},{208... | collective-permute-start | bytes 245768 | tf_op jit(solution)/shard_map/ppermute | solution.py:545
  51.8 0.7 collective-permute-start.14
  52.5 1.9 %collective-permute-done.13.first = f32[10,4,512]{2,1,0:T(4,128)S(1)} collective-permute-done((f32[10,4,512]{2,1,0:T(4,128)S(1)}, f32[10,4,512]{2,1,0:T(4,128)S(1)}, u32[]{:S(2)}, u32[]{:S(2)}) %collective-permute-start.13) | collective-permute-done | bytes 81952 | tf_op jit(solution)/shard_map/ppermute | solution.py:545
  54.5 1.5 %collective-permute-done.15.crossed = f32[3,10,4,512]{3,2,1,0:T(4,128)S(1)} collective-permute-done((f32[3,10,4,512]{3,2,1,0:T(4,128)S(1)}, f32[3,10,4,512]{3,2,1,0:T(4,128)S(1)}, u32[]{:S(2)}, u32[]{:S(2)}) %collective-permute-start.15) | collective-permute-done | bytes 245792 | tf_op jit(solution)/shard_map/ppermute | solution.py:546
  56.0 1.2 %shard_map.55 = (f32[48,512]{1,0:T(8,128)S(1)}, f32[8,8,128]{2,1,0:T(8,128)S(1)}) custom-call(s32[4]{0:T(128)S(1)} %pad_add_fusion.par_ref, f32[10,4,512]{2,1,0:T(4,128)S(1)} %bitcast.20, f32[10,4,512]{2,1,0:T(4,128)S(1)} %collective-permute-done.13.first, f32[10,4,512]{2,1,0:T(4,128)S(1)} %collective-permute-done.14.second, ...), custom_call_target="tpu_custom_call" | custom-call | bytes 3600000 | tf_op jit(solution)/shard_map/pallas_call | solution.py:430
  57.2 20.0 %all_to_all.5.dots = f32[8,8,128]{2,1,0:T(8,128)S(1)} all-to-all(f32[8,8,128]{2,1,0:T(8,128)S(1)} %get-tuple-element.40), channel_id=1, replica_groups={{0,32,64,96,128,160,192,224},{16,48,80,112,144,176,208,240},{1,33,65,97..., dimensions={0} | all-to-all | bytes 65536 | tf_op jit(solution)/shard_map/all_to_all | solution.py:556
  77.2 4.0 %shard_map.56 = (f32[2,4,64,512]{3,2,1,0:T(8,128)}, f32[4,32]{1,0:T(4,128)}) custom-call(f32[48,512]{1,0:T(8,128)S(1)} %get-tuple-element.39.basis, f32[8,8,128]{2,1,0:T(8,128)S(1)} %all_to_all.5.dots, f32[512,32]{1,0:T(8,128)S(1)} %compare_convert_fusion.onehot, f32[7,80,512]{2,1,0:T(8,128)S(1)} %get-tuple-element.42.h0, ...), custom_call_target="tpu_custom_call" | custom-call | bytes 14400000 | tf_op jit(solution)/shard_map/pallas_call | solution.py:430
  (24 shorter events, 2.1 us)
Async XLA Ops:
  2.1 2.1 %collective-permute-start.1 = (f32[4,72,512]{2,1,0:T(8,128)S(1)}, f32[4,72,512]{2,1,0:T(8,128)S(1)}, u32[]{:S(2)}, u32[]{:S(2)}) collective-permute-start(f32[4,72,512]{2,1,0:T(8,128)S(1)} %get-tuple-element.24.own), channel_id=1, source_target_pairs={{0,16},{32,48},{64,80},{96,112},{128,144},{160,176},{192,208},{224... | collective-permute-start | bytes 1769480 | tf_op jit(solution)/shard_map/ppermute | solution.py:484
  2.2 0.7 collective-permute-start
  4.2 11.5 %collective-permute-start.2 = (f32[4,72,512]{2,1,0:T(8,128)S(1)}, f32[4,72,512]{2,1,0:T(8,128)S(1)}, u32[]{:S(2)}, u32[]{:S(2)}) collective-permute-start(f32[4,72,512]{2,1,0:T(8,128)S(1)} %shard_map.51.own), channel_id=1, source_target_pairs={{16,32},{48,64},{80,96},{112,128},{144,160},{176,192},{208,224},{3... | collective-permute-start | bytes 1769480 | tf_op jit(solution)/shard_map/ppermute | solution.py:494
  5.6 5.5 %collective-permute-start.3 = (f32[40,512]{1,0:T(8,128)S(1)}, f32[40,512]{1,0:T(8,128)S(1)}, u32[]{:S(2)}, u32[]{:S(2)}) collective-permute-start(f32[40,512]{1,0:T(8,128)S(1)} %get-tuple-element.26), channel_id=1, source_target_pairs={{0,1},{2,3},{4,5},{6,7},{8,9},{10,11},{12,13},{14,15},{1,0},{3,2},... | collective-permute-start | bytes 245768 | tf_op jit(solution)/shard_map/ppermute | solution.py:504
  7.2 8.4 %collective-permute-start.4 = (f32[40,512]{1,0:T(8,128)S(1)}, f32[40,512]{1,0:T(8,128)S(1)}, u32[]{:S(2)}, u32[]{:S(2)}) collective-permute-start(f32[40,512]{1,0:T(8,128)S(1)} %get-tuple-element.27), channel_id=1, source_target_pairs={{1,2},{3,4},{5,6},{7,8},{9,10},{11,12},{13,14},{2,1},{4,3},{6,5},{... | collective-permute-start | bytes 245768 | tf_op jit(solution)/shard_map/ppermute | solution.py:505
  15.6 17.6 %copy-start = (s32[512]{0:T(512)S(1)}, s32[512]{0:T(512)}, u32[]{:S(2)}) copy-start(s32[512]{0:T(512)} %param.5) | copy-start | bytes 6148
  23.1 22.1 %collective-permute-start.11 = (f32[2,2,64,512]{3,2,1,0:T(8,128)S(1)}, f32[2,2,64,512]{3,2,1,0:T(8,128)S(1)}, u32[]{:S(2)}, u32[]{:S(2)}) collective-permute-start(f32[2,2,64,512]{3,2,1,0:T(8,128)S(1)} %get-tuple-element.31), channel_id=1, source_target_pairs={{16,32},{48,64},{80,96},{112,128},{144,160},{176,192},{208,224},{3... | collective-permute-start | bytes 1572872 | tf_op jit(solution)/shard_map/ppermute | solution.py:528
  23.8 21.4 %collective-permute-start.12 = (f32[2,2,64,512]{3,2,1,0:T(8,128)S(1)}, f32[2,2,64,512]{3,2,1,0:T(8,128)S(1)}, u32[]{:S(2)}, u32[]{:S(2)}) collective-permute-start(f32[2,2,64,512]{3,2,1,0:T(8,128)S(1)} %get-tuple-element.32), channel_id=1, source_target_pairs={{0,16},{32,48},{64,80},{96,112},{128,144},{160,176},{192,208},{224... | collective-permute-start | bytes 1572872 | tf_op jit(solution)/shard_map/ppermute | solution.py:529
  33.4 4.5 %collective-permute-start.5 = (f32[10,4,512]{2,1,0:T(4,128)S(1)}, f32[10,4,512]{2,1,0:T(4,128)S(1)}, u32[]{:S(2)}, u32[]{:S(2)}) collective-permute-start(f32[10,4,512]{2,1,0:T(4,128)S(1)} %get-tuple-element.30), channel_id=1, source_target_pairs={{0,1},{1,0},{2,3},{3,2},{4,5},{5,4},{6,7},{7,6},{8,9},{9,8},{10,11... | collective-permute-start | bytes 245768 | tf_op jit(solution)/shard_map/ppermute | solution.py:525
  33.5 5.9 %collective-permute-start.7 = (f32[10,4,512]{2,1,0:T(4,128)S(1)}, f32[10,4,512]{2,1,0:T(4,128)S(1)}, u32[]{:S(2)}, u32[]{:S(2)}) collective-permute-start(f32[10,4,512]{2,1,0:T(4,128)S(1)} %get-tuple-element.30), channel_id=1, source_target_pairs={{0,3},{1,2},{2,1},{3,0},{4,7},{5,6},{6,5},{7,4},{8,11},{9,10},{10,... | collective-permute-start | bytes 245768 | tf_op jit(solution)/shard_map/ppermute | solution.py:525
  35.7 5.9 %collective-permute-start.6 = (f32[10,4,512]{2,1,0:T(4,128)S(1)}, f32[10,4,512]{2,1,0:T(4,128)S(1)}, u32[]{:S(2)}, u32[]{:S(2)}) collective-permute-start(f32[10,4,512]{2,1,0:T(4,128)S(1)} %get-tuple-element.30), channel_id=1, source_target_pairs={{0,2},{1,3},{2,0},{3,1},{4,6},{5,7},{6,4},{7,5},{8,10},{9,11},{10,... | collective-permute-start | bytes 245768 | tf_op jit(solution)/shard_map/ppermute | solution.py:525
  41.6 8.1 %collective-permute-start.10 = (f32[10,4,512]{2,1,0:T(4,128)S(1)}, f32[10,4,512]{2,1,0:T(4,128)S(1)}, u32[]{:S(2)}, u32[]{:S(2)}) collective-permute-start(f32[10,4,512]{2,1,0:T(4,128)S(1)} %bitcast.24), channel_id=1, source_target_pairs={{0,12},{1,13},{2,14},{3,15},{4,8},{5,9},{6,10},{7,11},{8,4},{9,5},... | collective-permute-start | bytes 245768 | tf_op jit(solution)/shard_map/ppermute | solution.py:525
  42.2 7.6 %collective-permute-start.8 = (f32[10,4,512]{2,1,0:T(4,128)S(1)}, f32[10,4,512]{2,1,0:T(4,128)S(1)}, u32[]{:S(2)}, u32[]{:S(2)}) collective-permute-start(f32[10,4,512]{2,1,0:T(4,128)S(1)} %bitcast.25), channel_id=1, source_target_pairs={{0,4},{1,5},{2,6},{3,7},{4,0},{5,1},{6,2},{7,3},{8,12},{9,13},{10,... | collective-permute-start | bytes 245768 | tf_op jit(solution)/shard_map/ppermute | solution.py:525
  43.2 6.5 %collective-permute-start.9 = (f32[10,4,512]{2,1,0:T(4,128)S(1)}, f32[10,4,512]{2,1,0:T(4,128)S(1)}, u32[]{:S(2)}, u32[]{:S(2)}) collective-permute-start(f32[10,4,512]{2,1,0:T(4,128)S(1)} %bitcast.26), channel_id=1, source_target_pairs={{0,8},{1,9},{2,10},{3,11},{4,12},{5,13},{6,14},{7,15},{8,0},{9,1},... | collective-permute-start | bytes 245768 | tf_op jit(solution)/shard_map/ppermute | solution.py:525
  49.8 4.5 %collective-permute-start.13 = (f32[10,4,512]{2,1,0:T(4,128)S(1)}, f32[10,4,512]{2,1,0:T(4,128)S(1)}, u32[]{:S(2)}, u32[]{:S(2)}) collective-permute-start(f32[10,4,512]{2,1,0:T(4,128)S(1)} %bitcast.17), channel_id=1, source_target_pairs={{0,32},{16,48},{64,96},{80,112},{128,160},{144,176},{192,224},{208... | collective-permute-start | bytes 245768 | tf_op jit(solution)/shard_map/ppermute | solution.py:545
  51.8 2.5 %collective-permute-start.14 = (f32[10,4,512]{2,1,0:T(4,128)S(1)}, f32[10,4,512]{2,1,0:T(4,128)S(1)}, u32[]{:S(2)}, u32[]{:S(2)}) collective-permute-start(f32[10,4,512]{2,1,0:T(4,128)S(1)} %bitcast.18), channel_id=1, source_target_pairs={{32,64},{48,80},{96,128},{112,144},{160,192},{176,208},{64,32},{80... | collective-permute-start | bytes 245768 | tf_op jit(solution)/shard_map/ppermute | solution.py:545
  54.4 1.6 %collective-permute-start.15 = (f32[3,10,4,512]{3,2,1,0:T(4,128)S(1)}, f32[3,10,4,512]{3,2,1,0:T(4,128)S(1)}, u32[]{:S(2)}, u32[]{:S(2)}) collective-permute-start(f32[3,10,4,512]{3,2,1,0:T(4,128)S(1)} %pad_maximum_fusion), channel_id=1, source_target_pairs={{0,16},{32,48},{64,80},{96,112},{128,144},{160,176},{192,208},{224... | collective-permute-start | bytes 737288 | tf_op jit(solution)/shard_map/ppermute | solution.py:546

commit v11 on v10

--- a/solution.py
+++ b/solution.py
@@ -49,8 +49,11 @@
     return lax.broadcasted_iota(jnp.int32, shape, len(shape) - 1)
 
 
-def edge_kernel(own_hbm, f_hbm, out, bundle, f, sems):
+def edge_kernel(par_ref, own_hbm, f_hbm, out, bundle, three, f, sems):
+    par = par_ref[0]
     own = bundle.at[:, 0:NY]
+    extra = pltpu.make_async_copy(own_hbm.at[pl.ds(par, 3)], three.at[:, 0:NY], sems.at[2])
+    extra.start()
     copies = [pltpu.make_async_copy(own_hbm, own, sems.at[0]), pltpu.make_async_copy(f_hbm, f, sems.at[1])]
     for copy in copies:
         copy.start()
@@ -64,10 +67,9 @@
         out[:, 10 + 2 * c : 12 + 2 * c] = high
         bundle[:, NY + 2 * c : NY + 2 * c + 2] = low
         bundle[:, NY + 4 + 2 * c : NY + 6 + 2 * c] = high
-
-
-def pass_kernel(own, od_e, ev, out):
-    pass
+        three[:, NY + 2 * c : NY + 2 * c + 2] = f[c, pl.ds(par, 3), 0:2]
+        three[:, NY + 4 + 2 * c : NY + 6 + 2 * c] = f[c, pl.ds(par, 3), NY - 2 : NY]
+    extra.wait()
 
 
 def pack(par, f, to_od, to_ev, sems):
@@ -77,14 +79,15 @@
     ]
 
 
-def corner_kernel(par_ref, own, od, ev, first, second, low, high, mate):
+def corner_kernel(par_ref, own, od, ev, first, second, low, high, mate, other):
     odd = par_ref[0] == 1
-    mate[:, 0:3] = ev[:, 0:3]
-    mate[:, 3:7] = ev[:, NY : NY + 4]
-    mate[:, 7:10] = ev[:, NY - 3 : NY]
-    mate[:, 10:14] = ev[:, NY + 4 : NY + 8]
-    below = lax.select(odd, mate[2:4], od[2:4])
-    above = lax.select(odd, od[0:2], mate[0:2])
+    for rows, x in ((mate, ev), (other, od)):
+        rows[:, 0:3] = x[:, 0:3]
+        rows[:, 3:7] = x[:, NY : NY + 4]
+        rows[:, 7:10] = x[:, NY - 3 : NY]
+        rows[:, 10:14] = x[:, NY + 4 : NY + 8]
+    below = lax.select(odd, mate[2:4], other[1:3])
+    above = lax.select(odd, other[0:2], mate[0:2])
     for out, near, forced, base in ((low, (0, 2), 0, 0), (high, (1, 3), 1, 7)):
         for n in range(4):
             out[7 * n : 7 * n + 7] = own[n, base : base + 7]
@@ -107,7 +110,7 @@
 
 def fill_viscosity(par, v, own, od, ev, lo, hi, sems):
     copies = [pltpu.make_async_copy(own.at[:, 0:NY], v.at[3:7, LO:HI], sems.at[0])]
-    for n, at, last, x in ((1, par * 7, 1 - par, od), (2, 7 - par * 7, par, ev)):
+    for n, at, last, x in ((1, par * 7, 0, od), (2, 7 - par * 7, par, ev)):
         copies.append(pltpu.make_async_copy(x.at[pl.ds(last, 3), 0:NY], v.at[pl.ds(at, 3), LO:HI], sems.at[n]))
     for copy in copies:
         copy.start()
@@ -467,37 +470,28 @@
     first_chips = [(2 * a + c, 2 * b + c) for a, b in pairs(chips, 0) for c in range(2)]
     second_chips = [(2 * a + c, 2 * b + c) for a, b in pairs(chips, 1) for c in range(2)]
 
-    edges, own, f = call(
+    edges, own, three, f = call(
         edge_kernel,
         (
             pltpu.VMEM((ROWS, 14, NZ), jnp.float32),
             pltpu.VMEM((ROWS, NY + 8, NZ), jnp.float32),
+            pltpu.VMEM((3, NY + 8, NZ), jnp.float32),
             pltpu.VMEM(forcing.shape, jnp.float32),
         ),
         [],
-        (in_hbm(viscosity), in_hbm(forcing)),
-        in_specs=[ANY, ANY],
-        sems=2,
+        (where, in_hbm(viscosity), in_hbm(forcing)),
+        in_specs=[SMEM, ANY, ANY],
+        sems=3,
         mib=4,
     )
-    od_e = lax.ppermute(edges, "slab", others)
+    od = lax.ppermute(three, "slab", others)
     ev = lax.ppermute(own, "slab", mates)
-    late = call(
-        pass_kernel,
-        pltpu.VMEM((ROWS, NY + 8, NZ), jnp.float32),
-        [],
-        (in_vmem(own), in_vmem(od_e), in_vmem(ev)),
-        in_specs=[VMEM] * 3,
-        mib=2,
-        aliases={0: 0},
-    )
-    od = lax.ppermute(late, "slab", others)
     rows = pltpu.VMEM((40, NZ), jnp.float32)
     first, second = call(
         corner_kernel,
         (rows, rows),
-        [(40, NZ), (40, NZ), (ROWS, 14, NZ)],
-        (where, in_vmem(edges), in_vmem(od_e), in_vmem(ev)),
+        [(40, NZ), (40, NZ), (ROWS, 14, NZ), (3, 14, NZ)],
+        (where, in_vmem(edges), in_vmem(od), in_vmem(ev)),
         in_specs=[SMEM] + [VMEM] * 3,
         mib=4,
     )
@@ -510,7 +504,7 @@
         stencil_kernel,
         (f32(10, 4, NZ), layers, layers, *[pltpu.VMEM(x.shape, x.dtype) for x in kept]),
         [(7, FRAME, NZ), (5, 2, 8, 8, NZ), (7, ROWS, 8, NZ)],
-        (where, in_vmem(late), in_vmem(od), in_vmem(ev), in_vmem(first), in_vmem(second), in_vmem(f)),
+        (where, in_vmem(own), in_vmem(od), in_vmem(ev), in_vmem(first), in_vmem(second), in_vmem(f)),
         in_specs=[SMEM] + [VMEM] * 6,
         micros=6,
         sems=5,

time: 82.6 us -> 83.7 us (1.013)
  starting transfers between devices: 27.5 us -> 28.5 us
    ppermute x1, starting transfers between devices: 9.39 us -> 11.1 us  [shards(): ev_f = lax.ppermute(to_ev, 'slab', mates)]
    pallas_call x7 -> x6, Pallas kernels: 19.2 us -> 19.9 us  [call(): pl.pallas_call(kernel, out_shape=out_shape, in_specs=in_specs, out_specs=...]
  transfers between devices with their start and end apart: 16 -> 15, of which waited for: 7 -> 7; matrix products, arithmetic and copies ran while one was open for 0% -> 0% of each run, Pallas kernels for 6% -> 5%
where the time goes in v11:
time: 83.7 us; the launch traced here: 82.4 us
  starting transfers between devices  28.5 us (34%)
  Pallas kernels  19.9 us (24%)
  blocking collectives  19.5 us (23%)
  waiting for transfers between devices  13.2 us (16%)
  between operations  0.84 us (1%)
    pallas_call x6, Pallas kernels, call(): pl.pallas_call(kernel, out_shape=out_shape, in_specs=in_specs, out_specs=...  19.9 us
    all_to_all x1, blocking collectives, shards(): lax.all_to_all(dots, 'slab', 0, 0, tiled=True, axis_index_groups=groups)  19.5 us
    ppermute x1, starting transfers between devices, shards(): ev_f = lax.ppermute(to_ev, 'slab', mates)  11.1 us
    ppermute x6, starting transfers between devices, among(): lax.ppermute(x, 'cross', [(i, i ^ n * step) for i in range(cross)])  7.75 us
    ppermute x1, waiting for transfers between devices, shards(): second = lax.ppermute(second, 'cross', pairs(cross, 1))  4.52 us
    ppermute x6, waiting for transfers between devices, among(): lax.ppermute(x, 'cross', [(i, i ^ n * step) for i in range(cross)])  4.05 us
    ppermute x1, starting transfers between devices, shards(): second = lax.ppermute(second, 'cross', pairs(cross, 1))  3.88 us
    ppermute x1, starting transfers between devices, shards(): lax.ppermute(part, 'slab', first_chips)  2 us
  transfers between devices with their start and end apart: 15, of which 7 were waited for; matrix products, arithmetic and copies ran while one was open for 0% of the time, Pallas kernels for 5%

profile of v11, /device:TPU:16, one launch (start us, length us, event | category | flops | bytes accessed | tf_op | source)
XLA Modules:
  0.0 82.4 jit_solution(8961629036592219281)
XLA Ops:
  0.7 2.1 %shard_map.50 = (f32[4,14,512]{2,1,0:T(8,128)S(1)}, f32[4,72,512]{2,1,0:T(8,128)S(1)}, f32[3,72,512]{2,1,0:T(8,128)S(1)}, f32[2,4,64,512]{3,2,1,0:T(8,128)S(1)}) custom-call(s32[4]{0:T(128)S(1)} %pad_add_fusion.par_ref, f32[4,64,512]{2,1,0:T(8,128)} %own_hbm.1, f32[2,4,64,512]{3,2,1,0:T(8,128)} %f_hbm.1), custom_call_target="tpu_custom_call" | custom-call | bytes 3600000 | tf_op jit(solution)/shard_map/pallas_call | solution.py:433
  3.0 0.7 collective-permute-start
  3.7 1.3 %collective-permute-done.1.ev = f32[4,72,512]{2,1,0:T(8,128)S(1)} collective-permute-done((f32[4,72,512]{2,1,0:T(8,128)S(1)}, f32[4,72,512]{2,1,0:T(8,128)S(1)}, u32[]{:S(2)}, u32[]{:S(2)}) %collective-permute-start.1) | collective-permute-done | bytes 589856 | tf_op jit(solution)/shard_map/ppermute | solution.py:488
  5.6 1.6 %collective-permute-start.2 = (f32[40,512]{1,0:T(8,128)S(1)}, f32[40,512]{1,0:T(8,128)S(1)}, u32[]{:S(2)}, u32[]{:S(2)}) collective-permute-start(f32[40,512]{1,0:T(8,128)S(1)} %get-tuple-element.28), channel_id=1, source_target_pairs={{0,1},{2,3},{4,5},{6,7},{8,9},{10,11},{12,13},{14,15},{1,0},{3,2},... | collective-permute-start | bytes 245768 | tf_op jit(solution)/shard_map/ppermute | solution.py:498
  7.2 3.9 %collective-permute-start.3 = (f32[40,512]{1,0:T(8,128)S(1)}, f32[40,512]{1,0:T(8,128)S(1)}, u32[]{:S(2)}, u32[]{:S(2)}) collective-permute-start(f32[40,512]{1,0:T(8,128)S(1)} %get-tuple-element.29), channel_id=1, source_target_pairs={{1,2},{3,4},{5,6},{7,8},{9,10},{11,12},{13,14},{2,1},{4,3},{6,5},{... | collective-permute-start | bytes 245768 | tf_op jit(solution)/shard_map/ppermute | solution.py:499
  11.1 4.5 %collective-permute-done.3.second = f32[40,512]{1,0:T(8,128)S(1)} collective-permute-done((f32[40,512]{1,0:T(8,128)S(1)}, f32[40,512]{1,0:T(8,128)S(1)}, u32[]{:S(2)}, u32[]{:S(2)}) %collective-permute-start.3) | collective-permute-done | bytes 81952 | tf_op jit(solution)/shard_map/ppermute | solution.py:499
  15.7 7.5 %shard_map.52 = (f32[10,4,512]{2,1,0:T(4,128)S(1)}, f32[2,2,64,512]{3,2,1,0:T(8,128)S(1)}, f32[2,2,64,512]{3,2,1,0:T(8,128)S(1)}, f32[10,80,512]{2,1,0:T(8,128)S...) custom-call(s32[4]{0:T(128)S(1)} %pad_add_fusion.par_ref, ...), custom_call_target="tpu_custom_call" | custom-call | bytes 21600000 | tf_op jit(solution)/shard_map/pallas_call | solution.py:433
  23.1 0.7 collective-permute-start.10
  23.8 11.1 %collective-permute-start.11 = (f32[2,2,64,512]{3,2,1,0:T(8,128)S(1)}, f32[2,2,64,512]{3,2,1,0:T(8,128)S(1)}, u32[]{:S(2)}, u32[]{:S(2)}) collective-permute-start(f32[2,2,64,512]{3,2,1,0:T(8,128)S(1)} %get-tuple-element.34), channel_id=1, source_target_pairs={{0,16},{32,48},{64,80},{96,112},{128,144},{160,176},{192,208},{224... | collective-permute-start | bytes 1572872 | tf_op jit(solution)/shard_map/ppermute | solution.py:523
  35.2 2.2 %collective-permute-start.6 = (f32[10,4,512]{2,1,0:T(4,128)S(1)}, f32[10,4,512]{2,1,0:T(4,128)S(1)}, u32[]{:S(2)}, u32[]{:S(2)}) collective-permute-start(f32[10,4,512]{2,1,0:T(4,128)S(1)} %get-tuple-element.32), channel_id=1, source_target_pairs={{0,3},{1,2},{2,1},{3,0},{4,7},{5,6},{6,5},{7,4},{8,11},{9,10},{10,... | collective-permute-start | bytes 245768 | tf_op jit(solution)/shard_map/ppermute | solution.py:519
  37.3 1.9 %collective-permute-start.5 = (f32[10,4,512]{2,1,0:T(4,128)S(1)}, f32[10,4,512]{2,1,0:T(4,128)S(1)}, u32[]{:S(2)}, u32[]{:S(2)}) collective-permute-start(f32[10,4,512]{2,1,0:T(4,128)S(1)} %get-tuple-element.32), channel_id=1, source_target_pairs={{0,2},{1,3},{2,0},{3,1},{4,6},{5,7},{6,4},{7,5},{8,10},{9,11},{10,... | collective-permute-start | bytes 245768 | tf_op jit(solution)/shard_map/ppermute | solution.py:519
  39.6 1.5 %collective-permute-done.6 = f32[10,4,512]{2,1,0:T(4,128)S(1)} collective-permute-done((f32[10,4,512]{2,1,0:T(4,128)S(1)}, f32[10,4,512]{2,1,0:T(4,128)S(1)}, u32[]{:S(2)}, u32[]{:S(2)}) %collective-permute-start.6) | collective-permute-done | bytes 81952 | tf_op jit(solution)/shard_map/ppermute | solution.py:519
  41.1 2.2 %collective-permute-done.5 = f32[10,4,512]{2,1,0:T(4,128)S(1)} collective-permute-done((f32[10,4,512]{2,1,0:T(4,128)S(1)}, f32[10,4,512]{2,1,0:T(4,128)S(1)}, u32[]{:S(2)}, u32[]{:S(2)}) %collective-permute-start.5) | collective-permute-done | bytes 81952 | tf_op jit(solution)/shard_map/ppermute | solution.py:519
  43.3 0.7 collective-permute-start.7
  44.0 1.3 %collective-permute-start.8 = (f32[10,4,512]{2,1,0:T(4,128)S(1)}, f32[10,4,512]{2,1,0:T(4,128)S(1)}, u32[]{:S(2)}, u32[]{:S(2)}) collective-permute-start(f32[10,4,512]{2,1,0:T(4,128)S(1)} %bitcast.25), channel_id=1, source_target_pairs={{0,8},{1,9},{2,10},{3,11},{4,12},{5,13},{6,14},{7,15},{8,0},{9,1},... | collective-permute-start | bytes 245768 | tf_op jit(solution)/shard_map/ppermute | solution.py:519
  45.3 1.6 %collective-permute-start.9 = (f32[10,4,512]{2,1,0:T(4,128)S(1)}, f32[10,4,512]{2,1,0:T(4,128)S(1)}, u32[]{:S(2)}, u32[]{:S(2)}) collective-permute-start(f32[10,4,512]{2,1,0:T(4,128)S(1)} %bitcast.26), channel_id=1, source_target_pairs={{0,12},{1,13},{2,14},{3,15},{4,8},{5,9},{6,10},{7,11},{8,4},{9,5},... | collective-permute-start | bytes 245768 | tf_op jit(solution)/shard_map/ppermute | solution.py:519
  46.9 4.5 %shard_map.53.forced = f32[2,4,64,512]{3,2,1,0:T(8,128)S(1)} custom-call(s32[4]{0:T(128)S(1)} %pad_add_fusion.par_ref, f32[2,4,64,512]{3,2,1,0:T(8,128)S(1)} %get-tuple-element.30.f, f32[2,2,64,512]{3,2,1,0:T(8,128)S(1)} %collective-permute-done.10.od, f32[2,2,64,512]{3,2,1,0:T(8,128)S(1)} %collective-permute-done.11.ev, ...), custom_call_target="tpu_custom_call" | custom-call | bytes 18000000 | tf_op jit(solution)/shard_map/pallas_call | solution.py:433
  51.5 2.0 %collective-permute-start.12 = (f32[10,4,512]{2,1,0:T(4,128)S(1)}, f32[10,4,512]{2,1,0:T(4,128)S(1)}, u32[]{:S(2)}, u32[]{:S(2)}) collective-permute-start(f32[10,4,512]{2,1,0:T(4,128)S(1)} %bitcast.17), channel_id=1, source_target_pairs={{0,32},{16,48},{64,96},{80,112},{128,160},{144,176},{192,224},{208... | collective-permute-start | bytes 245768 | tf_op jit(solution)/shard_map/ppermute | solution.py:539
  53.5 0.7 collective-permute-start.13
  54.2 1.9 %collective-permute-done.12.first = f32[10,4,512]{2,1,0:T(4,128)S(1)} collective-permute-done((f32[10,4,512]{2,1,0:T(4,128)S(1)}, f32[10,4,512]{2,1,0:T(4,128)S(1)}, u32[]{:S(2)}, u32[]{:S(2)}) %collective-permute-start.12) | collective-permute-done | bytes 81952 | tf_op jit(solution)/shard_map/ppermute | solution.py:539
  56.2 1.5 %collective-permute-done.14.crossed = f32[3,10,4,512]{3,2,1,0:T(4,128)S(1)} collective-permute-done((f32[3,10,4,512]{3,2,1,0:T(4,128)S(1)}, f32[3,10,4,512]{3,2,1,0:T(4,128)S(1)}, u32[]{:S(2)}, u32[]{:S(2)}) %collective-permute-start.14) | collective-permute-done | bytes 245792 | tf_op jit(solution)/shard_map/ppermute | solution.py:540
  57.7 1.2 %shard_map.54 = (f32[48,512]{1,0:T(8,128)S(1)}, f32[8,8,128]{2,1,0:T(8,128)S(1)}) custom-call(s32[4]{0:T(128)S(1)} %pad_add_fusion.par_ref, f32[10,4,512]{2,1,0:T(4,128)S(1)} %bitcast.20, f32[10,4,512]{2,1,0:T(4,128)S(1)} %collective-permute-done.12.first, f32[10,4,512]{2,1,0:T(4,128)S(1)} %collective-permute-done.13.second, ...), custom_call_target="tpu_custom_call" | custom-call | bytes 3600000 | tf_op jit(solution)/shard_map/pallas_call | solution.py:433
  58.9 19.5 %all_to_all.5.dots = f32[8,8,128]{2,1,0:T(8,128)S(1)} all-to-all(f32[8,8,128]{2,1,0:T(8,128)S(1)} %get-tuple-element.42), channel_id=1, replica_groups={{0,32,64,96,128,160,192,224},{16,48,80,112,144,176,208,240},{1,33,65,97..., dimensions={0} | all-to-all | bytes 65536 | tf_op jit(solution)/shard_map/all_to_all | solution.py:550
  78.4 4.0 %shard_map.55 = (f32[2,4,64,512]{3,2,1,0:T(8,128)}, f32[4,32]{1,0:T(4,128)}) custom-call(f32[48,512]{1,0:T(8,128)S(1)} %get-tuple-element.41.basis, f32[8,8,128]{2,1,0:T(8,128)S(1)} %all_to_all.5.dots, f32[512,32]{1,0:T(8,128)S(1)} %compare_convert_fusion.onehot, f32[7,80,512]{2,1,0:T(8,128)S(1)} %get-tuple-element.44.h0, ...), custom_call_target="tpu_custom_call" | custom-call | bytes 14400000 | tf_op jit(solution)/shard_map/pallas_call | solution.py:433
  (21 shorter events, 1.6 us)
Async XLA Ops:
  2.9 2.1 %collective-permute-start.1 = (f32[4,72,512]{2,1,0:T(8,128)S(1)}, f32[4,72,512]{2,1,0:T(8,128)S(1)}, u32[]{:S(2)}, u32[]{:S(2)}) collective-permute-start(f32[4,72,512]{2,1,0:T(8,128)S(1)} %get-tuple-element.25.own), channel_id=1, source_target_pairs={{0,16},{32,48},{64,80},{96,112},{128,144},{160,176},{192,208},{224... | collective-permute-start | bytes 1769480 | tf_op jit(solution)/shard_map/ppermute | solution.py:488
  3.0 0.7 collective-permute-start
  5.6 5.5 %collective-permute-start.2 = (f32[40,512]{1,0:T(8,128)S(1)}, f32[40,512]{1,0:T(8,128)S(1)}, u32[]{:S(2)}, u32[]{:S(2)}) collective-permute-start(f32[40,512]{1,0:T(8,128)S(1)} %get-tuple-element.28), channel_id=1, source_target_pairs={{0,1},{2,3},{4,5},{6,7},{8,9},{10,11},{12,13},{14,15},{1,0},{3,2},... | collective-permute-start | bytes 245768 | tf_op jit(solution)/shard_map/ppermute | solution.py:498
  7.2 8.4 %collective-permute-start.3 = (f32[40,512]{1,0:T(8,128)S(1)}, f32[40,512]{1,0:T(8,128)S(1)}, u32[]{:S(2)}, u32[]{:S(2)}) collective-permute-start(f32[40,512]{1,0:T(8,128)S(1)} %get-tuple-element.29), channel_id=1, source_target_pairs={{1,2},{3,4},{5,6},{7,8},{9,10},{11,12},{13,14},{2,1},{4,3},{6,5},{... | collective-permute-start | bytes 245768 | tf_op jit(solution)/shard_map/ppermute | solution.py:499
  15.6 19.3 %copy-start = (s32[512]{0:T(512)S(1)}, s32[512]{0:T(512)}, u32[]{:S(2)}) copy-start(s32[512]{0:T(512)} %param.5) | copy-start | bytes 6148
  23.1 23.8 %collective-permute-start.10 = (f32[2,2,64,512]{3,2,1,0:T(8,128)S(1)}, f32[2,2,64,512]{3,2,1,0:T(8,128)S(1)}, u32[]{:S(2)}, u32[]{:S(2)}) collective-permute-start(f32[2,2,64,512]{3,2,1,0:T(8,128)S(1)} %get-tuple-element.33), channel_id=1, source_target_pairs={{16,32},{48,64},{80,96},{112,128},{144,160},{176,192},{208,224},{3... | collective-permute-start | bytes 1572872 | tf_op jit(solution)/shard_map/ppermute | solution.py:522
  23.8 23.1 %collective-permute-start.11 = (f32[2,2,64,512]{3,2,1,0:T(8,128)S(1)}, f32[2,2,64,512]{3,2,1,0:T(8,128)S(1)}, u32[]{:S(2)}, u32[]{:S(2)}) collective-permute-start(f32[2,2,64,512]{3,2,1,0:T(8,128)S(1)} %get-tuple-element.34), channel_id=1, source_target_pairs={{0,16},{32,48},{64,80},{96,112},{128,144},{160,176},{192,208},{224... | collective-permute-start | bytes 1572872 | tf_op jit(solution)/shard_map/ppermute | solution.py:523
  35.1 4.5 %collective-permute-start.4 = (f32[10,4,512]{2,1,0:T(4,128)S(1)}, f32[10,4,512]{2,1,0:T(4,128)S(1)}, u32[]{:S(2)}, u32[]{:S(2)}) collective-permute-start(f32[10,4,512]{2,1,0:T(4,128)S(1)} %get-tuple-element.32), channel_id=1, source_target_pairs={{0,1},{1,0},{2,3},{3,2},{4,5},{5,4},{6,7},{7,6},{8,9},{9,8},{10,11... | collective-permute-start | bytes 245768 | tf_op jit(solution)/shard_map/ppermute | solution.py:519
  35.2 5.9 %collective-permute-start.6 = (f32[10,4,512]{2,1,0:T(4,128)S(1)}, f32[10,4,512]{2,1,0:T(4,128)S(1)}, u32[]{:S(2)}, u32[]{:S(2)}) collective-permute-start(f32[10,4,512]{2,1,0:T(4,128)S(1)} %get-tuple-element.32), channel_id=1, source_target_pairs={{0,3},{1,2},{2,1},{3,0},{4,7},{5,6},{6,5},{7,4},{8,11},{9,10},{10,... | collective-permute-start | bytes 245768 | tf_op jit(solution)/shard_map/ppermute | solution.py:519
  37.3 5.9 %collective-permute-start.5 = (f32[10,4,512]{2,1,0:T(4,128)S(1)}, f32[10,4,512]{2,1,0:T(4,128)S(1)}, u32[]{:S(2)}, u32[]{:S(2)}) collective-permute-start(f32[10,4,512]{2,1,0:T(4,128)S(1)} %get-tuple-element.32), channel_id=1, source_target_pairs={{0,2},{1,3},{2,0},{3,1},{4,6},{5,7},{6,4},{7,5},{8,10},{9,11},{10,... | collective-permute-start | bytes 245768 | tf_op jit(solution)/shard_map/ppermute | solution.py:519
  43.3 8.1 %collective-permute-start.7 = (f32[10,4,512]{2,1,0:T(4,128)S(1)}, f32[10,4,512]{2,1,0:T(4,128)S(1)}, u32[]{:S(2)}, u32[]{:S(2)}) collective-permute-start(f32[10,4,512]{2,1,0:T(4,128)S(1)} %bitcast.24), channel_id=1, source_target_pairs={{0,4},{1,5},{2,6},{3,7},{4,0},{5,1},{6,2},{7,3},{8,12},{9,13},{10,... | collective-permute-start | bytes 245768 | tf_op jit(solution)/shard_map/ppermute | solution.py:519
  44.0 7.5 %collective-permute-start.8 = (f32[10,4,512]{2,1,0:T(4,128)S(1)}, f32[10,4,512]{2,1,0:T(4,128)S(1)}, u32[]{:S(2)}, u32[]{:S(2)}) collective-permute-start(f32[10,4,512]{2,1,0:T(4,128)S(1)} %bitcast.25), channel_id=1, source_target_pairs={{0,8},{1,9},{2,10},{3,11},{4,12},{5,13},{6,14},{7,15},{8,0},{9,1},... | collective-permute-start | bytes 245768 | tf_op jit(solution)/shard_map/ppermute | solution.py:519
  45.3 6.1 %collective-permute-start.9 = (f32[10,4,512]{2,1,0:T(4,128)S(1)}, f32[10,4,512]{2,1,0:T(4,128)S(1)}, u32[]{:S(2)}, u32[]{:S(2)}) collective-permute-start(f32[10,4,512]{2,1,0:T(4,128)S(1)} %bitcast.26), channel_id=1, source_target_pairs={{0,12},{1,13},{2,14},{3,15},{4,8},{5,9},{6,10},{7,11},{8,4},{9,5},... | collective-permute-start | bytes 245768 | tf_op jit(solution)/shard_map/ppermute | solution.py:519
  51.5 4.5 %collective-permute-start.12 = (f32[10,4,512]{2,1,0:T(4,128)S(1)}, f32[10,4,512]{2,1,0:T(4,128)S(1)}, u32[]{:S(2)}, u32[]{:S(2)}) collective-permute-start(f32[10,4,512]{2,1,0:T(4,128)S(1)} %bitcast.17), channel_id=1, source_target_pairs={{0,32},{16,48},{64,96},{80,112},{128,160},{144,176},{192,224},{208... | collective-permute-start | bytes 245768 | tf_op jit(solution)/shard_map/ppermute | solution.py:539
  53.5 2.5 %collective-permute-start.13 = (f32[10,4,512]{2,1,0:T(4,128)S(1)}, f32[10,4,512]{2,1,0:T(4,128)S(1)}, u32[]{:S(2)}, u32[]{:S(2)}) collective-permute-start(f32[10,4,512]{2,1,0:T(4,128)S(1)} %bitcast.18), channel_id=1, source_target_pairs={{32,64},{48,80},{96,128},{112,144},{160,192},{176,208},{64,32},{80... | collective-permute-start | bytes 245768 | tf_op jit(solution)/shard_map/ppermute | solution.py:539
  56.1 1.6 %collective-permute-start.14 = (f32[3,10,4,512]{3,2,1,0:T(4,128)S(1)}, f32[3,10,4,512]{3,2,1,0:T(4,128)S(1)}, u32[]{:S(2)}, u32[]{:S(2)}) collective-permute-start(f32[3,10,4,512]{3,2,1,0:T(4,128)S(1)} %pad_maximum_fusion), channel_id=1, source_target_pairs={{0,16},{32,48},{64,80},{96,112},{128,144},{160,176},{192,208},{224... | collective-permute-start | bytes 737288 | tf_op jit(solution)/shard_map/ppermute | solution.py:540

commit v12 on v11

--- a/solution.py
+++ b/solution.py
@@ -72,11 +72,16 @@
     extra.wait()
 
 
-def pack(par, f, to_od, to_ev, sems):
-    return [
+def pack_kernel(par_ref, f, three, to_od, to_ev, sems):
+    par = par_ref[0]
+    copies = [
         pltpu.make_async_copy(f.at[:, pl.ds(2 * last, 2)], out, sems.at[n])
         for n, (out, last) in enumerate(((to_od, par), (to_ev, 1 - par)))
     ]
+    for copy in copies:
+        copy.start()
+    for copy in copies:
+        copy.wait()
 
 
 def corner_kernel(par_ref, own, od, ev, first, second, low, high, mate, other):
@@ -143,13 +148,10 @@
     lax.fori_loop(0, 8, layer, 0)
 
 
-def stencil_kernel(par_ref, own, od, ev, first, second, f, out, to_od, to_ev, v, d, fz, h0, ex, ez, ezm, acc, s_acc, sems):
+def stencil_kernel(par_ref, own, od, ev, first, second, f, out, v, d, fz, h0, ex, ez, ezm, acc, s_acc, sems):
     par = par_ref[0]
     lo, hi = sides(par_ref[2] == 1, first, second)
     fill_viscosity(par, v, own, od, ev, lo, hi, sems)
-    packs = pack(par, f, to_od, to_ev, sems.at[pl.ds(3, 2)])
-    for copy in packs:
-        copy.start()
     fill_inverse(v, d, fz)
 
     ex[0] = E2 * d[0] * (v[1] + v[2]) * d[1]
@@ -239,8 +241,6 @@
     out[7:9] = e[0:8].reshape(2, 4, NZ)
     out[9, 0:1] = e[8:9]
     out[9, 1:4] = jnp.zeros((3, NZ), jnp.float32)
-    for copy in packs:
-        copy.wait()
 
 
 def krylov_kernel(par_ref, mine, first, second, crossed, basis, dots, s_ref, g_ref):
@@ -486,6 +486,19 @@
     )
     od = lax.ppermute(three, "slab", others)
     ev = lax.ppermute(own, "slab", mates)
+    layers = pltpu.VMEM((2, 2, NY, NZ), jnp.float32)
+    to_od, to_ev = call(
+        pack_kernel,
+        (layers, layers),
+        [],
+        (where, in_vmem(f), in_vmem(three)),
+        in_specs=[SMEM, VMEM, VMEM],
+        micros=4,
+        sems=2,
+        mib=2,
+    )
+    od_f = lax.ppermute(to_od, "slab", others)
+    ev_f = lax.ppermute(to_ev, "slab", mates)
     rows = pltpu.VMEM((40, NZ), jnp.float32)
     first, second = call(
         corner_kernel,
@@ -499,10 +512,9 @@
     second = lax.ppermute(second, "cross", pairs(cross, 1))
 
     kept = (f32(10, FRAME, NZ), f32(8, FRAME, NZ), f32(8, FRAME, NZ)) + (f32(7, FRAME, NZ),) * 3
-    layers = pltpu.VMEM((2, 2, NY, NZ), jnp.float32)
-    part, to_od, to_ev, v, d, fz, h0, ex, ez = call(
+    part, v, d, fz, h0, ex, ez = call(
         stencil_kernel,
-        (f32(10, 4, NZ), layers, layers, *[pltpu.VMEM(x.shape, x.dtype) for x in kept]),
+        (f32(10, 4, NZ), *[pltpu.VMEM(x.shape, x.dtype) for x in kept]),
         [(7, FRAME, NZ), (5, 2, 8, 8, NZ), (7, ROWS, 8, NZ)],
         (where, in_vmem(own), in_vmem(od), in_vmem(ev), in_vmem(first), in_vmem(second), in_vmem(f)),
         in_specs=[SMEM] + [VMEM] * 6,
@@ -519,8 +531,6 @@
         return [lax.ppermute(x, "cross", [(i, i ^ (n * step)) for i in range(cross)]) for n in (1, 2, 3)]
 
     part, onehot = lax.optimization_barrier((part, onehot))
-    od_f = lax.ppermute(to_od, "slab", others)
-    ev_f = lax.ppermute(to_ev, "slab", mates)
     got = among(part, 1)
     part = part + got[0] + got[1] + got[2]
     got = among(part, 4)

time: 83.7 us -> 82.2 us (0.982)
  starting transfers between devices: 28.5 us -> 23.8 us
  Pallas kernels: 19.9 us -> 23.3 us
  waiting for transfers between devices: 13.2 us -> 12 us
  blocking collectives: 19.5 us -> 20.5 us
    ppermute x1, starting transfers between devices: 11.1 us -> 4.78 us  [shards(): ev_f = lax.ppermute(to_ev, 'slab', mates)]
    pallas_call x6 -> x7, Pallas kernels: 19.9 us -> 23.3 us  [call(): pl.pallas_call(kernel, out_shape=out_shape, in_specs=in_specs, out_specs=...]
    ppermute x1, starting transfers between devices: 2 us -> 3.62 us  [shards(): lax.ppermute(part, 'slab', first_chips)]
    ppermute x1, waiting for transfers between devices: 1.28 us -> 0.01 us  [shards(): ev = lax.ppermute(own, 'slab', mates)]
    all_to_all x1, blocking collectives: 19.5 us -> 20.5 us  [shards(): lax.all_to_all(dots, 'slab', 0, 0, tiled=True, axis_index_groups=groups)]
  transfers between devices with their start and end apart: 15 -> 15, of which waited for: 7 -> 6; matrix products, arithmetic and copies ran while one was open for 0% -> 0% of each run, Pallas kernels for 5% -> 19%
where the time goes in v12:
time: 82.2 us; the launch traced here: 80.9 us
  starting transfers between devices  23.8 us (29%)
  Pallas kernels  23.3 us (28%)
  blocking collectives  20.5 us (25%)
  waiting for transfers between devices  12 us (15%)
  between operations  0.85 us (1%)
    pallas_call x7, Pallas kernels, call(): pl.pallas_call(kernel, out_shape=out_shape, in_specs=in_specs, out_specs=...  23.3 us
    all_to_all x1, blocking collectives, shards(): lax.all_to_all(dots, 'slab', 0, 0, tiled=True, axis_index_groups=groups)  20.5 us
    ppermute x6, starting transfers between devices, among(): lax.ppermute(x, 'cross', [(i, i ^ n * step) for i in range(cross)])  7.75 us
    ppermute x1, starting transfers between devices, shards(): ev_f = lax.ppermute(to_ev, 'slab', mates)  4.78 us
    ppermute x1, waiting for transfers between devices, shards(): second = lax.ppermute(second, 'cross', pairs(cross, 1))  4.52 us
    ppermute x6, waiting for transfers between devices, among(): lax.ppermute(x, 'cross', [(i, i ^ n * step) for i in range(cross)])  4.24 us
    ppermute x1, starting transfers between devices, shards(): second = lax.ppermute(second, 'cross', pairs(cross, 1))  3.88 us
    ppermute x1, starting transfers between devices, shards(): lax.ppermute(part, 'slab', first_chips)  3.62 us
  transfers between devices with their start and end apart: 15, of which 6 were waited for; matrix products, arithmetic and copies ran while one was open for 0% of the time, Pallas kernels for 19%

profile of v12, /device:TPU:16, one launch (start us, length us, event | category | flops | bytes accessed | tf_op | source)
XLA Modules:
  0.0 80.9 jit_solution(4853455723803290384)
XLA Ops:
  0.7 2.9 %shard_map.50 = (f32[4,14,512]{2,1,0:T(8,128)S(1)}, f32[4,72,512]{2,1,0:T(8,128)S(1)}, f32[3,72,512]{2,1,0:T(8,128)}, f32[2,4,64,512]{3,2,1,0:T(8,128)S(1)}) custom-call(s32[4]{0:T(128)S(1)} %pad_add_fusion.par_ref, f32[4,64,512]{2,1,0:T(8,128)} %own_hbm.1, f32[2,4,64,512]{3,2,1,0:T(8,128)} %f_hbm.1), custom_call_target="tpu_custom_call" | custom-call | bytes 3600000 | tf_op jit(solution)/shard_map/pallas_call | solution.py:433
  3.8 0.7 collective-permute-start
  4.5 2.1 %shard_map.53 = (f32[2,2,64,512]{3,2,1,0:T(8,128)}, f32[2,2,64,512]{3,2,1,0:T(8,128)}) custom-call(s32[4]{0:T(128)S(1)} %pad_add_fusion.par_ref, f32[2,4,64,512]{3,2,1,0:T(8,128)S(1)} %get-tuple-element.30.f, f32[3,72,512]{2,1,0:T(8,128)} %get-tuple-element.26.three), custom_call_target="tpu_custom_call" | custom-call | bytes 14400000 | tf_op jit(solution)/shard_map/pallas_call | solution.py:433
  6.6 0.7 collective-permute-start.10
  7.3 4.8 %collective-permute-start.11 = (f32[2,2,64,512]{3,2,1,0:T(8,128)}, f32[2,2,64,512]{3,2,1,0:T(8,128)}, u32[]{:S(2)}, u32[]{:S(2)}) collective-permute-start(f32[2,2,64,512]{3,2,1,0:T(8,128)} %get-tuple-element.34), channel_id=1, source_target_pairs={{0,16},{32,48},{64,80},{96,112},{128,144},{160,176},{192,208},{224... | collective-permute-start | bytes 1572872 | tf_op jit(solution)/shard_map/ppermute | solution.py:501
  12.7 1.6 %collective-permute-start.2 = (f32[40,512]{1,0:T(8,128)S(1)}, f32[40,512]{1,0:T(8,128)S(1)}, u32[]{:S(2)}, u32[]{:S(2)}) collective-permute-start(f32[40,512]{1,0:T(8,128)S(1)} %get-tuple-element.28), channel_id=1, source_target_pairs={{0,1},{2,3},{4,5},{6,7},{8,9},{10,11},{12,13},{14,15},{1,0},{3,2},... | collective-permute-start | bytes 245768 | tf_op jit(solution)/shard_map/ppermute | solution.py:511
  14.3 3.9 %collective-permute-start.3 = (f32[40,512]{1,0:T(8,128)S(1)}, f32[40,512]{1,0:T(8,128)S(1)}, u32[]{:S(2)}, u32[]{:S(2)}) collective-permute-start(f32[40,512]{1,0:T(8,128)S(1)} %get-tuple-element.29), channel_id=1, source_target_pairs={{1,2},{3,4},{5,6},{7,8},{9,10},{11,12},{13,14},{2,1},{4,3},{6,5},{... | collective-permute-start | bytes 245768 | tf_op jit(solution)/shard_map/ppermute | solution.py:512
  18.4 4.5 %collective-permute-done.3.second = f32[40,512]{1,0:T(8,128)S(1)} collective-permute-done((f32[40,512]{1,0:T(8,128)S(1)}, f32[40,512]{1,0:T(8,128)S(1)}, u32[]{:S(2)}, u32[]{:S(2)}) %collective-permute-start.3) | collective-permute-done | bytes 81952 | tf_op jit(solution)/shard_map/ppermute | solution.py:512
  22.9 7.5 %shard_map.52 = (f32[10,4,512]{2,1,0:T(4,128)S(1)}, f32[10,80,512]{2,1,0:T(8,128)S(1)}, f32[8,80,512]{2,1,0:T(8,128)S(1)}, f32[8,80,512]{2,1,0:T(8,128)S(1)}, f3...) custom-call(s32[4]{0:T(128)S(1)} %pad_add_fusion.par_ref, ...), custom_call_target="tpu_custom_call" | custom-call | bytes 21600000 | tf_op jit(solution)/shard_map/pallas_call | solution.py:433
  30.5 2.2 %collective-permute-start.6 = (f32[10,4,512]{2,1,0:T(4,128)S(1)}, f32[10,4,512]{2,1,0:T(4,128)S(1)}, u32[]{:S(2)}, u32[]{:S(2)}) collective-permute-start(f32[10,4,512]{2,1,0:T(4,128)S(1)} %get-tuple-element.32), channel_id=1, source_target_pairs={{0,3},{1,2},{2,1},{3,0},{4,7},{5,6},{6,5},{7,4},{8,11},{9,10},{10,... | collective-permute-start | bytes 245768 | tf_op jit(solution)/shard_map/ppermute | solution.py:531
  32.6 1.9 %collective-permute-start.5 = (f32[10,4,512]{2,1,0:T(4,128)S(1)}, f32[10,4,512]{2,1,0:T(4,128)S(1)}, u32[]{:S(2)}, u32[]{:S(2)}) collective-permute-start(f32[10,4,512]{2,1,0:T(4,128)S(1)} %get-tuple-element.32), channel_id=1, source_target_pairs={{0,2},{1,3},{2,0},{3,1},{4,6},{5,7},{6,4},{7,5},{8,10},{9,11},{10,... | collective-permute-start | bytes 245768 | tf_op jit(solution)/shard_map/ppermute | solution.py:531
  34.5 0.8 %collective-permute-done.4 = f32[10,4,512]{2,1,0:T(4,128)S(1)} collective-permute-done((f32[10,4,512]{2,1,0:T(4,128)S(1)}, f32[10,4,512]{2,1,0:T(4,128)S(1)}, u32[]{:S(2)}, u32[]{:S(2)}) %collective-permute-start.4) | collective-permute-done | bytes 81952 | tf_op jit(solution)/shard_map/ppermute | solution.py:531
  35.4 1.5 %collective-permute-done.6 = f32[10,4,512]{2,1,0:T(4,128)S(1)} collective-permute-done((f32[10,4,512]{2,1,0:T(4,128)S(1)}, f32[10,4,512]{2,1,0:T(4,128)S(1)}, u32[]{:S(2)}, u32[]{:S(2)}) %collective-permute-start.6) | collective-permute-done | bytes 81952 | tf_op jit(solution)/shard_map/ppermute | solution.py:531
  36.9 1.9 %collective-permute-done.5 = f32[10,4,512]{2,1,0:T(4,128)S(1)} collective-permute-done((f32[10,4,512]{2,1,0:T(4,128)S(1)}, f32[10,4,512]{2,1,0:T(4,128)S(1)}, u32[]{:S(2)}, u32[]{:S(2)}) %collective-permute-start.5) | collective-permute-done | bytes 81952 | tf_op jit(solution)/shard_map/ppermute | solution.py:531
  38.8 1.0 %collective-permute-start.7 = (f32[10,4,512]{2,1,0:T(4,128)S(1)}, f32[10,4,512]{2,1,0:T(4,128)S(1)}, u32[]{:S(2)}, u32[]{:S(2)}) collective-permute-start(f32[10,4,512]{2,1,0:T(4,128)S(1)} %bitcast.24), channel_id=1, source_target_pairs={{0,4},{1,5},{2,6},{3,7},{4,0},{5,1},{6,2},{7,3},{8,12},{9,13},{10,... | collective-permute-start | bytes 245768 | tf_op jit(solution)/shard_map/ppermute | solution.py:531
  39.8 1.0 %collective-permute-start.8 = (f32[10,4,512]{2,1,0:T(4,128)S(1)}, f32[10,4,512]{2,1,0:T(4,128)S(1)}, u32[]{:S(2)}, u32[]{:S(2)}) collective-permute-start(f32[10,4,512]{2,1,0:T(4,128)S(1)} %bitcast.25), channel_id=1, source_target_pairs={{0,8},{1,9},{2,10},{3,11},{4,12},{5,13},{6,14},{7,15},{8,0},{9,1},... | collective-permute-start | bytes 245768 | tf_op jit(solution)/shard_map/ppermute | solution.py:531
  40.8 1.6 %collective-permute-start.9 = (f32[10,4,512]{2,1,0:T(4,128)S(1)}, f32[10,4,512]{2,1,0:T(4,128)S(1)}, u32[]{:S(2)}, u32[]{:S(2)}) collective-permute-start(f32[10,4,512]{2,1,0:T(4,128)S(1)} %bitcast.26), channel_id=1, source_target_pairs={{0,12},{1,13},{2,14},{3,15},{4,8},{5,9},{6,10},{7,11},{8,4},{9,5},... | collective-permute-start | bytes 245768 | tf_op jit(solution)/shard_map/ppermute | solution.py:531
  42.4 5.0 %shard_map.54.forced = f32[2,4,64,512]{3,2,1,0:T(8,128)S(1)} custom-call(s32[4]{0:T(128)S(1)} %pad_add_fusion.par_ref, f32[2,4,64,512]{3,2,1,0:T(8,128)S(1)} %get-tuple-element.30.f, f32[2,2,64,512]{3,2,1,0:T(8,128)S(1)} %collective-permute-done.10.od, f32[2,2,64,512]{3,2,1,0:T(8,128)} %collective-permute-done.11.ev, ...), custom_call_target="tpu_custom_call" | custom-call | bytes 18000000 | tf_op jit(solution)/shard_map/pallas_call | solution.py:433
  47.5 3.6 %collective-permute-start.12 = (f32[10,4,512]{2,1,0:T(4,128)S(1)}, f32[10,4,512]{2,1,0:T(4,128)S(1)}, u32[]{:S(2)}, u32[]{:S(2)}) collective-permute-start(f32[10,4,512]{2,1,0:T(4,128)S(1)} %bitcast.17), channel_id=1, source_target_pairs={{0,32},{16,48},{64,96},{80,112},{128,160},{144,176},{192,224},{208... | collective-permute-start | bytes 245768 | tf_op jit(solution)/shard_map/ppermute | solution.py:549
  51.8 1.8 %collective-permute-done.12.first = f32[10,4,512]{2,1,0:T(4,128)S(1)} collective-permute-done((f32[10,4,512]{2,1,0:T(4,128)S(1)}, f32[10,4,512]{2,1,0:T(4,128)S(1)}, u32[]{:S(2)}, u32[]{:S(2)}) %collective-permute-start.12) | collective-permute-done | bytes 81952 | tf_op jit(solution)/shard_map/ppermute | solution.py:549
  53.7 1.5 %collective-permute-done.14.crossed = f32[3,10,4,512]{3,2,1,0:T(4,128)S(1)} collective-permute-done((f32[3,10,4,512]{3,2,1,0:T(4,128)S(1)}, f32[3,10,4,512]{3,2,1,0:T(4,128)S(1)}, u32[]{:S(2)}, u32[]{:S(2)}) %collective-permute-start.14) | collective-permute-done | bytes 245792 | tf_op jit(solution)/shard_map/ppermute | solution.py:550
  55.2 1.2 %shard_map.55 = (f32[48,512]{1,0:T(8,128)S(1)}, f32[8,8,128]{2,1,0:T(8,128)S(1)}) custom-call(s32[4]{0:T(128)S(1)} %pad_add_fusion.par_ref, f32[10,4,512]{2,1,0:T(4,128)S(1)} %bitcast.20, f32[10,4,512]{2,1,0:T(4,128)S(1)} %collective-permute-done.12.first, f32[10,4,512]{2,1,0:T(4,128)S(1)} %collective-permute-done.13.second, ...), custom_call_target="tpu_custom_call" | custom-call | bytes 3600000 | tf_op jit(solution)/shard_map/pallas_call | solution.py:433
  56.4 20.5 %all_to_all.5.dots = f32[8,8,128]{2,1,0:T(8,128)S(1)} all-to-all(f32[8,8,128]{2,1,0:T(8,128)S(1)} %get-tuple-element.42), channel_id=1, replica_groups={{0,32,64,96,128,160,192,224},{16,48,80,112,144,176,208,240},{1,33,65,97..., dimensions={0} | all-to-all | bytes 65536 | tf_op jit(solution)/shard_map/all_to_all | solution.py:560
  76.9 4.0 %shard_map.56 = (f32[2,4,64,512]{3,2,1,0:T(8,128)}, f32[4,32]{1,0:T(4,128)}) custom-call(f32[48,512]{1,0:T(8,128)S(1)} %get-tuple-element.41.basis, f32[8,8,128]{2,1,0:T(8,128)S(1)} %all_to_all.5.dots, f32[512,32]{1,0:T(8,128)S(1)} %compare_convert_fusion.onehot, f32[7,80,512]{2,1,0:T(8,128)S(1)} %get-tuple-element.44.h0, ...), custom_call_target="tpu_custom_call" | custom-call | bytes 14400000 | tf_op jit(solution)/shard_map/pallas_call | solution.py:433
  (22 shorter events, 1.9 us)
Async XLA Ops:
  3.7 8.4 %collective-permute-start.1 = (f32[4,72,512]{2,1,0:T(8,128)S(1)}, f32[4,72,512]{2,1,0:T(8,128)S(1)}, u32[]{:S(2)}, u32[]{:S(2)}) collective-permute-start(f32[4,72,512]{2,1,0:T(8,128)S(1)} %get-tuple-element.25.own), channel_id=1, source_target_pairs={{0,16},{32,48},{64,80},{96,112},{128,144},{160,176},{192,208},{224... | collective-permute-start | bytes 1769480 | tf_op jit(solution)/shard_map/ppermute | solution.py:488
  3.8 8.3 %collective-permute-start = (f32[3,72,512]{2,1,0:T(8,128)}, f32[3,72,512]{2,1,0:T(8,128)S(1)}, u32[]{:S(2)}, u32[]{:S(2)}) collective-permute-start(f32[3,72,512]{2,1,0:T(8,128)} %get-tuple-element.26.three), channel_id=1, source_target_pairs={{16,32},{48,64},{80,96},{112,128},{144,160},{176,192},{208,224},{3... | collective-permute-start | bytes 1327112 | tf_op jit(solution)/shard_map/ppermute | solution.py:487
  4.5 13.7 %copy-start = (s32[512]{0:T(512)S(1)}, s32[512]{0:T(512)}, u32[]{:S(2)}) copy-start(s32[512]{0:T(512)} %param.5) | copy-start | bytes 6148
  6.6 35.8 %collective-permute-start.10 = (f32[2,2,64,512]{3,2,1,0:T(8,128)}, f32[2,2,64,512]{3,2,1,0:T(8,128)S(1)}, u32[]{:S(2)}, u32[]{:S(2)}) collective-permute-start(f32[2,2,64,512]{3,2,1,0:T(8,128)} %get-tuple-element.33), channel_id=1, source_target_pairs={{16,32},{48,64},{80,96},{112,128},{144,160},{176,192},{208,224},{3... | collective-permute-start | bytes 1572872 | tf_op jit(solution)/shard_map/ppermute | solution.py:500
  7.3 35.1 %collective-permute-start.11 = (f32[2,2,64,512]{3,2,1,0:T(8,128)}, f32[2,2,64,512]{3,2,1,0:T(8,128)}, u32[]{:S(2)}, u32[]{:S(2)}) collective-permute-start(f32[2,2,64,512]{3,2,1,0:T(8,128)} %get-tuple-element.34), channel_id=1, source_target_pairs={{0,16},{32,48},{64,80},{96,112},{128,144},{160,176},{192,208},{224... | collective-permute-start | bytes 1572872 | tf_op jit(solution)/shard_map/ppermute | solution.py:501
  12.7 5.6 %collective-permute-start.2 = (f32[40,512]{1,0:T(8,128)S(1)}, f32[40,512]{1,0:T(8,128)S(1)}, u32[]{:S(2)}, u32[]{:S(2)}) collective-permute-start(f32[40,512]{1,0:T(8,128)S(1)} %get-tuple-element.28), channel_id=1, source_target_pairs={{0,1},{2,3},{4,5},{6,7},{8,9},{10,11},{12,13},{14,15},{1,0},{3,2},... | collective-permute-start | bytes 245768 | tf_op jit(solution)/shard_map/ppermute | solution.py:511
  14.3 8.6 %collective-permute-start.3 = (f32[40,512]{1,0:T(8,128)S(1)}, f32[40,512]{1,0:T(8,128)S(1)}, u32[]{:S(2)}, u32[]{:S(2)}) collective-permute-start(f32[40,512]{1,0:T(8,128)S(1)} %get-tuple-element.29), channel_id=1, source_target_pairs={{1,2},{3,4},{5,6},{7,8},{9,10},{11,12},{13,14},{2,1},{4,3},{6,5},{... | collective-permute-start | bytes 245768 | tf_op jit(solution)/shard_map/ppermute | solution.py:512
  30.4 5.0 %collective-permute-start.4 = (f32[10,4,512]{2,1,0:T(4,128)S(1)}, f32[10,4,512]{2,1,0:T(4,128)S(1)}, u32[]{:S(2)}, u32[]{:S(2)}) collective-permute-start(f32[10,4,512]{2,1,0:T(4,128)S(1)} %get-tuple-element.32), channel_id=1, source_target_pairs={{0,1},{1,0},{2,3},{3,2},{4,5},{5,4},{6,7},{7,6},{8,9},{9,8},{10,11... | collective-permute-start | bytes 245768 | tf_op jit(solution)/shard_map/ppermute | solution.py:531
  30.5 6.4 %collective-permute-start.6 = (f32[10,4,512]{2,1,0:T(4,128)S(1)}, f32[10,4,512]{2,1,0:T(4,128)S(1)}, u32[]{:S(2)}, u32[]{:S(2)}) collective-permute-start(f32[10,4,512]{2,1,0:T(4,128)S(1)} %get-tuple-element.32), channel_id=1, source_target_pairs={{0,3},{1,2},{2,1},{3,0},{4,7},{5,6},{6,5},{7,4},{8,11},{9,10},{10,... | collective-permute-start | bytes 245768 | tf_op jit(solution)/shard_map/ppermute | solution.py:531
  32.6 6.1 %collective-permute-start.5 = (f32[10,4,512]{2,1,0:T(4,128)S(1)}, f32[10,4,512]{2,1,0:T(4,128)S(1)}, u32[]{:S(2)}, u32[]{:S(2)}) collective-permute-start(f32[10,4,512]{2,1,0:T(4,128)S(1)} %get-tuple-element.32), channel_id=1, source_target_pairs={{0,2},{1,3},{2,0},{3,1},{4,6},{5,7},{6,4},{7,5},{8,10},{9,11},{10,... | collective-permute-start | bytes 245768 | tf_op jit(solution)/shard_map/ppermute | solution.py:531
  38.8 8.6 %collective-permute-start.7 = (f32[10,4,512]{2,1,0:T(4,128)S(1)}, f32[10,4,512]{2,1,0:T(4,128)S(1)}, u32[]{:S(2)}, u32[]{:S(2)}) collective-permute-start(f32[10,4,512]{2,1,0:T(4,128)S(1)} %bitcast.24), channel_id=1, source_target_pairs={{0,4},{1,5},{2,6},{3,7},{4,0},{5,1},{6,2},{7,3},{8,12},{9,13},{10,... | collective-permute-start | bytes 245768 | tf_op jit(solution)/shard_map/ppermute | solution.py:531
  39.8 7.6 %collective-permute-start.8 = (f32[10,4,512]{2,1,0:T(4,128)S(1)}, f32[10,4,512]{2,1,0:T(4,128)S(1)}, u32[]{:S(2)}, u32[]{:S(2)}) collective-permute-start(f32[10,4,512]{2,1,0:T(4,128)S(1)} %bitcast.25), channel_id=1, source_target_pairs={{0,8},{1,9},{2,10},{3,11},{4,12},{5,13},{6,14},{7,15},{8,0},{9,1},... | collective-permute-start | bytes 245768 | tf_op jit(solution)/shard_map/ppermute | solution.py:531
  40.8 6.6 %collective-permute-start.9 = (f32[10,4,512]{2,1,0:T(4,128)S(1)}, f32[10,4,512]{2,1,0:T(4,128)S(1)}, u32[]{:S(2)}, u32[]{:S(2)}) collective-permute-start(f32[10,4,512]{2,1,0:T(4,128)S(1)} %bitcast.26), channel_id=1, source_target_pairs={{0,12},{1,13},{2,14},{3,15},{4,8},{5,9},{6,10},{7,11},{8,4},{9,5},... | collective-permute-start | bytes 245768 | tf_op jit(solution)/shard_map/ppermute | solution.py:531
  47.5 6.0 %collective-permute-start.12 = (f32[10,4,512]{2,1,0:T(4,128)S(1)}, f32[10,4,512]{2,1,0:T(4,128)S(1)}, u32[]{:S(2)}, u32[]{:S(2)}) collective-permute-start(f32[10,4,512]{2,1,0:T(4,128)S(1)} %bitcast.17), channel_id=1, source_target_pairs={{0,32},{16,48},{64,96},{80,112},{128,160},{144,176},{192,224},{208... | collective-permute-start | bytes 245768 | tf_op jit(solution)/shard_map/ppermute | solution.py:549
  51.1 2.4 %collective-permute-start.13 = (f32[10,4,512]{2,1,0:T(4,128)S(1)}, f32[10,4,512]{2,1,0:T(4,128)S(1)}, u32[]{:S(2)}, u32[]{:S(2)}) collective-permute-start(f32[10,4,512]{2,1,0:T(4,128)S(1)} %bitcast.18), channel_id=1, source_target_pairs={{32,64},{48,80},{96,128},{112,144},{160,192},{176,208},{64,32},{80... | collective-permute-start | bytes 245768 | tf_op jit(solution)/shard_map/ppermute | solution.py:549
  53.6 1.6 %collective-permute-start.14 = (f32[3,10,4,512]{3,2,1,0:T(4,128)S(1)}, f32[3,10,4,512]{3,2,1,0:T(4,128)S(1)}, u32[]{:S(2)}, u32[]{:S(2)}) collective-permute-start(f32[3,10,4,512]{3,2,1,0:T(4,128)S(1)} %pad_maximum_fusion), channel_id=1, source_target_pairs={{0,16},{32,48},{64,80},{96,112},{128,144},{160,176},{192,208},{224... | collective-permute-start | bytes 737288 | tf_op jit(solution)/shard_map/ppermute | solution.py:550

commit v13 on v12

--- a/solution.py
+++ b/solution.py
@@ -72,7 +72,7 @@
     extra.wait()
 
 
-def pack_kernel(par_ref, f, three, to_od, to_ev, sems):
+def pack_kernel(par_ref, f, ev, to_od, to_ev, sems):
     par = par_ref[0]
     copies = [
         pltpu.make_async_copy(f.at[:, pl.ds(2 * last, 2)], out, sems.at[n])
@@ -491,7 +491,7 @@
         pack_kernel,
         (layers, layers),
         [],
-        (where, in_vmem(f), in_vmem(three)),
+        (where, in_vmem(f), in_vmem(ev)),
         in_specs=[SMEM, VMEM, VMEM],
         micros=4,
         sems=2,

time: 82.2 us -> 80.5 us (0.979)
  starting transfers between devices: 23.8 us -> 28.4 us
  waiting for transfers between devices: 12 us -> 8.67 us
  Pallas kernels: 23.3 us -> 20.6 us
    ppermute x1, starting transfers between devices: 4.78 us -> 11 us  [shards(): ev_f = lax.ppermute(to_ev, 'slab', mates)]
    ppermute x1, waiting for transfers between devices: 4.52 us -> 0.01 us  [shards(): second = lax.ppermute(second, 'cross', pairs(cross, 1))]
    pallas_call x7, Pallas kernels: 23.3 us -> 20.6 us  [call(): pl.pallas_call(kernel, out_shape=out_shape, in_specs=in_specs, out_specs=...]
    ppermute x1, starting transfers between devices: 3.62 us -> 2 us  [shards(): lax.ppermute(part, 'slab', first_chips)]
    ppermute x1, waiting for transfers between devices: 0.01 us -> 1.27 us  [shards(): ev = lax.ppermute(own, 'slab', mates)]
  transfers between devices with their start and end apart: 15 -> 15, of which waited for: 6 -> 5; matrix products, arithmetic and copies ran while one was open for 0% -> 0% of each run, Pallas kernels for 19% -> 16%
where the time goes in v13:
time: 80.5 us; the launch traced here: 79.2 us
  starting transfers between devices  28.4 us (35%)
  Pallas kernels  20.6 us (26%)
  blocking collectives  20.3 us (25%)
  waiting for transfers between devices  8.67 us (11%)
  between operations  0.85 us (1%)
    pallas_call x7, Pallas kernels, call(): pl.pallas_call(kernel, out_shape=out_shape, in_specs=in_specs, out_specs=...  20.6 us
    all_to_all x1, blocking collectives, shards(): lax.all_to_all(dots, 'slab', 0, 0, tiled=True, axis_index_groups=groups)  20.3 us
    ppermute x1, starting transfers between devices, shards(): ev_f = lax.ppermute(to_ev, 'slab', mates)  11 us
    ppermute x6, starting transfers between devices, among(): lax.ppermute(x, 'cross', [(i, i ^ n * step) for i in range(cross)])  7.75 us
    ppermute x6, waiting for transfers between devices, among(): lax.ppermute(x, 'cross', [(i, i ^ n * step) for i in range(cross)])  4.03 us
    ppermute x1, starting transfers between devices, shards(): second = lax.ppermute(second, 'cross', pairs(cross, 1))  3.88 us
    ppermute x1, starting transfers between devices, shards(): lax.ppermute(part, 'slab', first_chips)  2 us
    ppermute x1, waiting for transfers between devices, shards(): lax.ppermute(part, 'slab', first_chips)  1.86 us
  transfers between devices with their start and end apart: 15, of which 5 were waited for; matrix products, arithmetic and copies ran while one was open for 0% of the time, Pallas kernels for 16%

profile of v13, /device:TPU:16, one launch (start us, length us, event | category | flops | bytes accessed | tf_op | source)
XLA Modules:
  0.0 79.2 jit_solution(1305070397180537000)
XLA Ops:
  0.7 2.1 %shard_map.50 = (f32[4,14,512]{2,1,0:T(8,128)S(1)}, f32[4,72,512]{2,1,0:T(8,128)S(1)}, f32[3,72,512]{2,1,0:T(8,128)S(1)}, f32[2,4,64,512]{3,2,1,0:T(8,128)S(1)}) custom-call(s32[4]{0:T(128)S(1)} %pad_add_fusion.par_ref, f32[4,64,512]{2,1,0:T(8,128)} %own_hbm.1, f32[2,4,64,512]{3,2,1,0:T(8,128)} %f_hbm.1), custom_call_target="tpu_custom_call" | custom-call | bytes 3600000 | tf_op jit(solution)/shard_map/pallas_call | solution.py:433
  3.0 0.7 collective-permute-start
  3.7 1.3 %collective-permute-done.1.ev = f32[4,72,512]{2,1,0:T(8,128)S(1)} collective-permute-done((f32[4,72,512]{2,1,0:T(8,128)S(1)}, f32[4,72,512]{2,1,0:T(8,128)S(1)}, u32[]{:S(2)}, u32[]{:S(2)}) %collective-permute-start.1) | collective-permute-done | bytes 589856 | tf_op jit(solution)/shard_map/ppermute | solution.py:488
  5.0 0.6 shard_map.51
  5.6 1.6 %collective-permute-start.2 = (f32[40,512]{1,0:T(8,128)S(1)}, f32[40,512]{1,0:T(8,128)S(1)}, u32[]{:S(2)}, u32[]{:S(2)}) collective-permute-start(f32[40,512]{1,0:T(8,128)S(1)} %get-tuple-element.28), channel_id=1, source_target_pairs={{0,1},{2,3},{4,5},{6,7},{8,9},{10,11},{12,13},{14,15},{1,0},{3,2},... | collective-permute-start | bytes 245768 | tf_op jit(solution)/shard_map/ppermute | solution.py:511
  7.2 3.9 %collective-permute-start.3 = (f32[40,512]{1,0:T(8,128)S(1)}, f32[40,512]{1,0:T(8,128)S(1)}, u32[]{:S(2)}, u32[]{:S(2)}) collective-permute-start(f32[40,512]{1,0:T(8,128)S(1)} %get-tuple-element.29), channel_id=1, source_target_pairs={{1,2},{3,4},{5,6},{7,8},{9,10},{11,12},{13,14},{2,1},{4,3},{6,5},{... | collective-permute-start | bytes 245768 | tf_op jit(solution)/shard_map/ppermute | solution.py:512
  11.8 0.7 collective-permute-start.10
  12.5 11.0 %collective-permute-start.11 = (f32[2,2,64,512]{3,2,1,0:T(8,128)S(1)}, f32[2,2,64,512]{3,2,1,0:T(8,128)S(1)}, u32[]{:S(2)}, u32[]{:S(2)}) collective-permute-start(f32[2,2,64,512]{3,2,1,0:T(8,128)S(1)} %get-tuple-element.34), channel_id=1, source_target_pairs={{0,16},{32,48},{64,80},{96,112},{128,144},{160,176},{192,208},{224... | collective-permute-start | bytes 1572872 | tf_op jit(solution)/shard_map/ppermute | solution.py:501
  23.6 7.5 %shard_map.52 = (f32[10,4,512]{2,1,0:T(4,128)S(1)}, f32[10,80,512]{2,1,0:T(8,128)S(1)}, f32[8,80,512]{2,1,0:T(8,128)S(1)}, f32[8,80,512]{2,1,0:T(8,128)S(1)}, f3...) custom-call(s32[4]{0:T(128)S(1)} %pad_add_fusion.par_ref, ...), custom_call_target="tpu_custom_call" | custom-call | bytes 21600000 | tf_op jit(solution)/shard_map/pallas_call | solution.py:433
  31.1 0.8 %collective-permute-start.4 = (f32[10,4,512]{2,1,0:T(4,128)S(1)}, f32[10,4,512]{2,1,0:T(4,128)S(1)}, u32[]{:S(2)}, u32[]{:S(2)}) collective-permute-start(f32[10,4,512]{2,1,0:T(4,128)S(1)} %get-tuple-element.32), channel_id=1, source_target_pairs={{0,1},{1,0},{2,3},{3,2},{4,5},{5,4},{6,7},{7,6},{8,9},{9,8},{10,11... | collective-permute-start | bytes 245768 | tf_op jit(solution)/shard_map/ppermute | solution.py:531
  31.9 1.4 %collective-permute-start.6 = (f32[10,4,512]{2,1,0:T(4,128)S(1)}, f32[10,4,512]{2,1,0:T(4,128)S(1)}, u32[]{:S(2)}, u32[]{:S(2)}) collective-permute-start(f32[10,4,512]{2,1,0:T(4,128)S(1)} %get-tuple-element.32), channel_id=1, source_target_pairs={{0,3},{1,2},{2,1},{3,0},{4,7},{5,6},{6,5},{7,4},{8,11},{9,10},{10,... | collective-permute-start | bytes 245768 | tf_op jit(solution)/shard_map/ppermute | solution.py:531
  33.2 2.0 %collective-permute-start.5 = (f32[10,4,512]{2,1,0:T(4,128)S(1)}, f32[10,4,512]{2,1,0:T(4,128)S(1)}, u32[]{:S(2)}, u32[]{:S(2)}) collective-permute-start(f32[10,4,512]{2,1,0:T(4,128)S(1)} %get-tuple-element.32), channel_id=1, source_target_pairs={{0,2},{1,3},{2,0},{3,1},{4,6},{5,7},{6,4},{7,5},{8,10},{9,11},{10,... | collective-permute-start | bytes 245768 | tf_op jit(solution)/shard_map/ppermute | solution.py:531
  35.6 3.7 %collective-permute-done.6 = f32[10,4,512]{2,1,0:T(4,128)S(1)} collective-permute-done((f32[10,4,512]{2,1,0:T(4,128)S(1)}, f32[10,4,512]{2,1,0:T(4,128)S(1)}, u32[]{:S(2)}, u32[]{:S(2)}) %collective-permute-start.6) | collective-permute-done | bytes 81952 | tf_op jit(solution)/shard_map/ppermute | solution.py:531
  39.3 1.0 %collective-permute-start.7 = (f32[10,4,512]{2,1,0:T(4,128)S(1)}, f32[10,4,512]{2,1,0:T(4,128)S(1)}, u32[]{:S(2)}, u32[]{:S(2)}) collective-permute-start(f32[10,4,512]{2,1,0:T(4,128)S(1)} %bitcast.24), channel_id=1, source_target_pairs={{0,4},{1,5},{2,6},{3,7},{4,0},{5,1},{6,2},{7,3},{8,12},{9,13},{10,... | collective-permute-start | bytes 245768 | tf_op jit(solution)/shard_map/ppermute | solution.py:531
  40.3 1.2 %collective-permute-start.8 = (f32[10,4,512]{2,1,0:T(4,128)S(1)}, f32[10,4,512]{2,1,0:T(4,128)S(1)}, u32[]{:S(2)}, u32[]{:S(2)}) collective-permute-start(f32[10,4,512]{2,1,0:T(4,128)S(1)} %bitcast.25), channel_id=1, source_target_pairs={{0,8},{1,9},{2,10},{3,11},{4,12},{5,13},{6,14},{7,15},{8,0},{9,1},... | collective-permute-start | bytes 245768 | tf_op jit(solution)/shard_map/ppermute | solution.py:531
  41.5 1.4 %collective-permute-start.9 = (f32[10,4,512]{2,1,0:T(4,128)S(1)}, f32[10,4,512]{2,1,0:T(4,128)S(1)}, u32[]{:S(2)}, u32[]{:S(2)}) collective-permute-start(f32[10,4,512]{2,1,0:T(4,128)S(1)} %bitcast.26), channel_id=1, source_target_pairs={{0,12},{1,13},{2,14},{3,15},{4,8},{5,9},{6,10},{7,11},{8,4},{9,5},... | collective-permute-start | bytes 245768 | tf_op jit(solution)/shard_map/ppermute | solution.py:531
  42.9 4.5 %shard_map.54.forced = f32[2,4,64,512]{3,2,1,0:T(8,128)S(1)} custom-call(s32[4]{0:T(128)S(1)} %pad_add_fusion.par_ref, f32[2,4,64,512]{3,2,1,0:T(8,128)S(1)} %get-tuple-element.30.f, f32[2,2,64,512]{3,2,1,0:T(8,128)S(1)} %collective-permute-done.10.od, f32[2,2,64,512]{3,2,1,0:T(8,128)S(1)} %collective-permute-done.11.ev, ...), custom_call_target="tpu_custom_call" | custom-call | bytes 18000000 | tf_op jit(solution)/shard_map/pallas_call | solution.py:433
  47.5 2.0 %collective-permute-start.12 = (f32[10,4,512]{2,1,0:T(4,128)S(1)}, f32[10,4,512]{2,1,0:T(4,128)S(1)}, u32[]{:S(2)}, u32[]{:S(2)}) collective-permute-start(f32[10,4,512]{2,1,0:T(4,128)S(1)} %bitcast.17), channel_id=1, source_target_pairs={{0,32},{16,48},{64,96},{80,112},{128,160},{144,176},{192,224},{208... | collective-permute-start | bytes 245768 | tf_op jit(solution)/shard_map/ppermute | solution.py:549
  49.5 0.7 collective-permute-start.13
  50.1 1.9 %collective-permute-done.12.first = f32[10,4,512]{2,1,0:T(4,128)S(1)} collective-permute-done((f32[10,4,512]{2,1,0:T(4,128)S(1)}, f32[10,4,512]{2,1,0:T(4,128)S(1)}, u32[]{:S(2)}, u32[]{:S(2)}) %collective-permute-start.12) | collective-permute-done | bytes 81952 | tf_op jit(solution)/shard_map/ppermute | solution.py:549
  52.2 1.5 %collective-permute-done.14.crossed = f32[3,10,4,512]{3,2,1,0:T(4,128)S(1)} collective-permute-done((f32[3,10,4,512]{3,2,1,0:T(4,128)S(1)}, f32[3,10,4,512]{3,2,1,0:T(4,128)S(1)}, u32[]{:S(2)}, u32[]{:S(2)}) %collective-permute-start.14) | collective-permute-done | bytes 245792 | tf_op jit(solution)/shard_map/ppermute | solution.py:550
  53.7 1.2 %shard_map.55 = (f32[48,512]{1,0:T(8,128)S(1)}, f32[8,8,128]{2,1,0:T(8,128)S(1)}) custom-call(s32[4]{0:T(128)S(1)} %pad_add_fusion.par_ref, f32[10,4,512]{2,1,0:T(4,128)S(1)} %bitcast.20, f32[10,4,512]{2,1,0:T(4,128)S(1)} %collective-permute-done.12.first, f32[10,4,512]{2,1,0:T(4,128)S(1)} %collective-permute-done.13.second, ...), custom_call_target="tpu_custom_call" | custom-call | bytes 3600000 | tf_op jit(solution)/shard_map/pallas_call | solution.py:433
  54.8 20.3 %all_to_all.5.dots = f32[8,8,128]{2,1,0:T(8,128)S(1)} all-to-all(f32[8,8,128]{2,1,0:T(8,128)S(1)} %get-tuple-element.42), channel_id=1, replica_groups={{0,32,64,96,128,160,192,224},{16,48,80,112,144,176,208,240},{1,33,65,97..., dimensions={0} | all-to-all | bytes 65536 | tf_op jit(solution)/shard_map/all_to_all | solution.py:560
  75.2 4.0 %shard_map.56 = (f32[2,4,64,512]{3,2,1,0:T(8,128)}, f32[4,32]{1,0:T(4,128)}) custom-call(f32[48,512]{1,0:T(8,128)S(1)} %get-tuple-element.41.basis, f32[8,8,128]{2,1,0:T(8,128)S(1)} %all_to_all.5.dots, f32[512,32]{1,0:T(8,128)S(1)} %compare_convert_fusion.onehot, f32[7,80,512]{2,1,0:T(8,128)S(1)} %get-tuple-element.44.h0, ...), custom_call_target="tpu_custom_call" | custom-call | bytes 14400000 | tf_op jit(solution)/shard_map/pallas_call | solution.py:433
  (22 shorter events, 1.5 us)
Async XLA Ops:
  2.9 2.1 %collective-permute-start.1 = (f32[4,72,512]{2,1,0:T(8,128)S(1)}, f32[4,72,512]{2,1,0:T(8,128)S(1)}, u32[]{:S(2)}, u32[]{:S(2)}) collective-permute-start(f32[4,72,512]{2,1,0:T(8,128)S(1)} %get-tuple-element.25.own), channel_id=1, source_target_pairs={{0,16},{32,48},{64,80},{96,112},{128,144},{160,176},{192,208},{224... | collective-permute-start | bytes 1769480 | tf_op jit(solution)/shard_map/ppermute | solution.py:488
  3.0 0.7 collective-permute-start
  5.0 18.4 %copy-start = (s32[512]{0:T(512)S(1)}, s32[512]{0:T(512)}, u32[]{:S(2)}) copy-start(s32[512]{0:T(512)} %param.5) | copy-start | bytes 6148
  5.6 17.9 %collective-permute-start.2 = (f32[40,512]{1,0:T(8,128)S(1)}, f32[40,512]{1,0:T(8,128)S(1)}, u32[]{:S(2)}, u32[]{:S(2)}) collective-permute-start(f32[40,512]{1,0:T(8,128)S(1)} %get-tuple-element.28), channel_id=1, source_target_pairs={{0,1},{2,3},{4,5},{6,7},{8,9},{10,11},{12,13},{14,15},{1,0},{3,2},... | collective-permute-start | bytes 245768 | tf_op jit(solution)/shard_map/ppermute | solution.py:511
  7.2 16.4 %collective-permute-start.3 = (f32[40,512]{1,0:T(8,128)S(1)}, f32[40,512]{1,0:T(8,128)S(1)}, u32[]{:S(2)}, u32[]{:S(2)}) collective-permute-start(f32[40,512]{1,0:T(8,128)S(1)} %get-tuple-element.29), channel_id=1, source_target_pairs={{1,2},{3,4},{5,6},{7,8},{9,10},{11,12},{13,14},{2,1},{4,3},{6,5},{... | collective-permute-start | bytes 245768 | tf_op jit(solution)/shard_map/ppermute | solution.py:512
  11.8 31.1 %collective-permute-start.10 = (f32[2,2,64,512]{3,2,1,0:T(8,128)S(1)}, f32[2,2,64,512]{3,2,1,0:T(8,128)S(1)}, u32[]{:S(2)}, u32[]{:S(2)}) collective-permute-start(f32[2,2,64,512]{3,2,1,0:T(8,128)S(1)} %get-tuple-element.33), channel_id=1, source_target_pairs={{16,32},{48,64},{80,96},{112,128},{144,160},{176,192},{208,224},{3... | collective-permute-start | bytes 1572872 | tf_op jit(solution)/shard_map/ppermute | solution.py:500
  12.5 30.4 %collective-permute-start.11 = (f32[2,2,64,512]{3,2,1,0:T(8,128)S(1)}, f32[2,2,64,512]{3,2,1,0:T(8,128)S(1)}, u32[]{:S(2)}, u32[]{:S(2)}) collective-permute-start(f32[2,2,64,512]{3,2,1,0:T(8,128)S(1)} %get-tuple-element.34), channel_id=1, source_target_pairs={{0,16},{32,48},{64,80},{96,112},{128,144},{160,176},{192,208},{224... | collective-permute-start | bytes 1572872 | tf_op jit(solution)/shard_map/ppermute | solution.py:501
  31.1 4.5 %collective-permute-start.4 = (f32[10,4,512]{2,1,0:T(4,128)S(1)}, f32[10,4,512]{2,1,0:T(4,128)S(1)}, u32[]{:S(2)}, u32[]{:S(2)}) collective-permute-start(f32[10,4,512]{2,1,0:T(4,128)S(1)} %get-tuple-element.32), channel_id=1, source_target_pairs={{0,1},{1,0},{2,3},{3,2},{4,5},{5,4},{6,7},{7,6},{8,9},{9,8},{10,11... | collective-permute-start | bytes 245768 | tf_op jit(solution)/shard_map/ppermute | solution.py:531
  31.9 7.4 %collective-permute-start.6 = (f32[10,4,512]{2,1,0:T(4,128)S(1)}, f32[10,4,512]{2,1,0:T(4,128)S(1)}, u32[]{:S(2)}, u32[]{:S(2)}) collective-permute-start(f32[10,4,512]{2,1,0:T(4,128)S(1)} %get-tuple-element.32), channel_id=1, source_target_pairs={{0,3},{1,2},{2,1},{3,0},{4,7},{5,6},{6,5},{7,4},{8,11},{9,10},{10,... | collective-permute-start | bytes 245768 | tf_op jit(solution)/shard_map/ppermute | solution.py:531
  33.2 6.0 %collective-permute-start.5 = (f32[10,4,512]{2,1,0:T(4,128)S(1)}, f32[10,4,512]{2,1,0:T(4,128)S(1)}, u32[]{:S(2)}, u32[]{:S(2)}) collective-permute-start(f32[10,4,512]{2,1,0:T(4,128)S(1)} %get-tuple-element.32), channel_id=1, source_target_pairs={{0,2},{1,3},{2,0},{3,1},{4,6},{5,7},{6,4},{7,5},{8,10},{9,11},{10,... | collective-permute-start | bytes 245768 | tf_op jit(solution)/shard_map/ppermute | solution.py:531
  39.3 8.1 %collective-permute-start.7 = (f32[10,4,512]{2,1,0:T(4,128)S(1)}, f32[10,4,512]{2,1,0:T(4,128)S(1)}, u32[]{:S(2)}, u32[]{:S(2)}) collective-permute-start(f32[10,4,512]{2,1,0:T(4,128)S(1)} %bitcast.24), channel_id=1, source_target_pairs={{0,4},{1,5},{2,6},{3,7},{4,0},{5,1},{6,2},{7,3},{8,12},{9,13},{10,... | collective-permute-start | bytes 245768 | tf_op jit(solution)/shard_map/ppermute | solution.py:531
  40.3 7.1 %collective-permute-start.8 = (f32[10,4,512]{2,1,0:T(4,128)S(1)}, f32[10,4,512]{2,1,0:T(4,128)S(1)}, u32[]{:S(2)}, u32[]{:S(2)}) collective-permute-start(f32[10,4,512]{2,1,0:T(4,128)S(1)} %bitcast.25), channel_id=1, source_target_pairs={{0,8},{1,9},{2,10},{3,11},{4,12},{5,13},{6,14},{7,15},{8,0},{9,1},... | collective-permute-start | bytes 245768 | tf_op jit(solution)/shard_map/ppermute | solution.py:531
  41.5 5.9 %collective-permute-start.9 = (f32[10,4,512]{2,1,0:T(4,128)S(1)}, f32[10,4,512]{2,1,0:T(4,128)S(1)}, u32[]{:S(2)}, u32[]{:S(2)}) collective-permute-start(f32[10,4,512]{2,1,0:T(4,128)S(1)} %bitcast.26), channel_id=1, source_target_pairs={{0,12},{1,13},{2,14},{3,15},{4,8},{5,9},{6,10},{7,11},{8,4},{9,5},... | collective-permute-start | bytes 245768 | tf_op jit(solution)/shard_map/ppermute | solution.py:531
  47.5 4.5 %collective-permute-start.12 = (f32[10,4,512]{2,1,0:T(4,128)S(1)}, f32[10,4,512]{2,1,0:T(4,128)S(1)}, u32[]{:S(2)}, u32[]{:S(2)}) collective-permute-start(f32[10,4,512]{2,1,0:T(4,128)S(1)} %bitcast.17), channel_id=1, source_target_pairs={{0,32},{16,48},{64,96},{80,112},{128,160},{144,176},{192,224},{208... | collective-permute-start | bytes 245768 | tf_op jit(solution)/shard_map/ppermute | solution.py:549
  49.5 2.5 %collective-permute-start.13 = (f32[10,4,512]{2,1,0:T(4,128)S(1)}, f32[10,4,512]{2,1,0:T(4,128)S(1)}, u32[]{:S(2)}, u32[]{:S(2)}) collective-permute-start(f32[10,4,512]{2,1,0:T(4,128)S(1)} %bitcast.18), channel_id=1, source_target_pairs={{32,64},{48,80},{96,128},{112,144},{160,192},{176,208},{64,32},{80... | collective-permute-start | bytes 245768 | tf_op jit(solution)/shard_map/ppermute | solution.py:549
  52.1 1.6 %collective-permute-start.14 = (f32[3,10,4,512]{3,2,1,0:T(4,128)S(1)}, f32[3,10,4,512]{3,2,1,0:T(4,128)S(1)}, u32[]{:S(2)}, u32[]{:S(2)}) collective-permute-start(f32[3,10,4,512]{3,2,1,0:T(4,128)S(1)} %pad_maximum_fusion), channel_id=1, source_target_pairs={{0,16},{32,48},{64,80},{96,112},{128,144},{160,176},{192,208},{224... | collective-permute-start | bytes 737288 | tf_op jit(solution)/shard_map/ppermute | solution.py:550
